TPU v7x, 256 devices: a whole 4x4x8 slice. The times are simulated.
256 devices in a mesh: seq: 32 (over y, z), exp: 8 (over x, core).
Axes of the slice: x: 4, y: 4, z: 8, core: 2. Of those that a mesh axis runs over, the one named last changes fastest.
Arguments:
- block_in: bfloat16 [49152, 1024], P(('seq', 'exp')), may hold values from -24 to 24
- out_grad: bfloat16 [49152, 1024], P(('seq', 'exp')), may hold values from -6 to 6
- gate_values: bfloat16 [49152, 2], P(('seq', 'exp')), may hold values from 0.099609375 to 1
- expert_ids: int32 [49152, 2], P(('seq', 'exp')), may hold values from 0 to 7, all different within a row; in each aligned block of 192 rows (0 to 191, 192 to 383, ...) at most 60 rows name the same one
- conv_kernel: bfloat16 [31, 1024], replicated, may hold values from -1 to 1
- expert_weights: bfloat16 [8, 1024, 6144], P('exp', 'seq'), may hold values from -0.1875 to 0.1875
Outputs:
- input_grad: bfloat16 [49152, 1024], P(('seq', 'exp'))
- weight_grad: bfloat16 [8, 1024, 6144], P('exp', 'seq')
- gate_grad: bfloat16 [49152, 2], P(('seq', 'exp'))
Inputs may be any that keep to these rules, and one draw needn't show every extreme that they name: `expert_ids`: each frame names two different experts. Among the frames of one device (aligned blocks of 192 frames) no expert is named more than 60 times, a bound that some block reaches.
All inputs are finite; a program needn't handle non-finite values.
Results may differ from a plain program's by a relative error of at most 0.02.
Values may be sent and summed in bfloat16 or wider, within the bound.
No kernel may reach another device: no remote copies, remote signals or barrier semaphores. Data moves between devices by JAX's collectives and lax.ppermute only.
A program may use at most 128 MiB of HBM per device.

v0:
```python
import jax
import jax.numpy as jnp
from jax import lax
from jax.sharding import PartitionSpec as P


def with_halo(block, sides, width):
    for axis, dim in sides:
        count = lax.axis_size(axis)
        forward = [(i, i + 1) for i in range(count - 1)]
        backward = [(target, source) for source, target in forward]
        low = lax.ppermute(
            lax.slice_in_dim(block, block.shape[dim] - width, None, axis=dim), axis, forward
        )
        high = lax.ppermute(lax.slice_in_dim(block, 0, width, axis=dim), axis, backward)
        block = jnp.concatenate([low, block, high], axis=dim)
    return block


def silu_pair(inputs):
    sigmoid = jax.nn.sigmoid(inputs)
    return (inputs * sigmoid, sigmoid * (1.0 + inputs * (1.0 - sigmoid)))


def expert_backward(rows_in, rows_grad, rows_gate, weights):
    hidden_width = weights.shape[1] // 3
    in_weights = weights[:, : 2 * hidden_width]
    down_weights = weights[:, 2 * hidden_width :]
    projected = jnp.dot(rows_in, in_weights, preferred_element_type=jnp.float32)
    gate_input = projected[:, :hidden_width]
    up_input = projected[:, hidden_width:]
    activated, derivative = silu_pair(gate_input)
    hidden = (activated * up_input).astype(jnp.bfloat16)
    expert_out = lax.dot_general(
        hidden, down_weights, (((1,), (1,)), ((), ())), preferred_element_type=jnp.float32
    )
    gate_grad = jnp.sum(rows_grad.astype(jnp.float32) * expert_out, axis=1).astype(jnp.bfloat16)
    out_scaled = (rows_gate.astype(jnp.float32)[:, None] * rows_grad.astype(jnp.float32)).astype(
        jnp.bfloat16
    )
    hidden_grad = jnp.dot(out_scaled, down_weights, preferred_element_type=jnp.float32)
    pre_grads = jnp.concatenate(
        [
            (hidden_grad * up_input * derivative).astype(jnp.bfloat16),
            (hidden_grad * activated).astype(jnp.bfloat16),
        ],
        axis=1,
    )
    row_grad = lax.dot_general(
        pre_grads, in_weights, (((1,), (1,)), ((), ())), preferred_element_type=jnp.float32
    ).astype(jnp.bfloat16)
    return (row_grad, gate_grad, pre_grads, out_scaled, hidden)


def local(block_in, out_grad, gate_values, expert_ids, conv_kernel, expert_weights):
    experts = lax.axis_size("exp")
    frames = block_in.shape[0]
    model_width = block_in.shape[1]
    capacity = 5 * frames // (2 * experts)
    owners = expert_ids.reshape(-1)
    one_hot = (owners[:, None] == jnp.arange(experts, dtype=jnp.int32)[None, :]).astype(jnp.int32)
    ranks = jnp.sum(jnp.cumsum(one_hot, axis=0) * one_hot, axis=1) - 1
    targets = owners * capacity + ranks
    placing = (targets[None, :] == jnp.arange(experts * capacity, dtype=jnp.int32)[:, None]).astype(
        jnp.bfloat16
    )
    placing_frames = placing.reshape(experts * capacity, frames, 2).sum(axis=2)
    sent_in = jnp.dot(placing_frames, block_in, preferred_element_type=jnp.float32).astype(
        jnp.bfloat16
    )
    sent_grad = jnp.dot(placing_frames, out_grad, preferred_element_type=jnp.float32).astype(
        jnp.bfloat16
    )
    sent_gate = jnp.dot(placing, gate_values.reshape(-1, 1), preferred_element_type=jnp.float32)[
        :, 0
    ].astype(jnp.bfloat16)
    arrived_in, arrived_grad, arrived_gate = (
        lax.all_to_all(
            sent_in.reshape(experts, capacity, model_width),
            "exp",
            split_axis=0,
            concat_axis=0,
            tiled=True,
        ),
        lax.all_to_all(
            sent_grad.reshape(experts, capacity, model_width),
            "exp",
            split_axis=0,
            concat_axis=0,
            tiled=True,
        ),
        lax.all_to_all(
            sent_gate.reshape(experts, capacity), "exp", split_axis=0, concat_axis=0, tiled=True
        ),
    )
    weights = lax.all_gather(expert_weights, "seq", axis=1, tiled=True)[0]
    rows_in = arrived_in.reshape(-1, model_width)
    row_grad, gate_grad, pre_grads, out_scaled, hidden = expert_backward(
        rows_in, arrived_grad.reshape(-1, model_width), arrived_gate.reshape(-1), weights
    )
    contract = (((0,), (0,)), ((), ()))
    full_term = jnp.concatenate(
        [
            lax.dot_general(rows_in, pre_grads, contract, preferred_element_type=jnp.float32),
            lax.dot_general(out_scaled, hidden, contract, preferred_element_type=jnp.float32),
        ],
        axis=1,
    )
    shard_sum = lax.psum_scatter(
        full_term.astype(jnp.bfloat16), "seq", scatter_dimension=0, tiled=True
    )
    weight_grad = shard_sum[None]
    returned_grad, returned_gate = (
        lax.all_to_all(
            row_grad.reshape(experts, capacity, model_width),
            "exp",
            split_axis=0,
            concat_axis=0,
            tiled=True,
        ),
        lax.all_to_all(
            gate_grad.reshape(experts, capacity), "exp", split_axis=0, concat_axis=0, tiled=True
        ),
    )
    frame_grad = out_grad.astype(jnp.float32) + lax.dot_general(
        placing_frames,
        returned_grad.reshape(-1, model_width),
        contract,
        preferred_element_type=jnp.float32,
    )
    gate_out = jnp.dot(returned_gate.reshape(1, -1), placing, preferred_element_type=jnp.float32)[0]
    gate_out = gate_out.reshape(frames, 2).astype(jnp.bfloat16)
    tap_count = conv_kernel.shape[0]
    half_width = (tap_count - 1) // 2
    kernel_rows = conv_kernel.astype(jnp.float32)
    padded = with_halo(frame_grad.astype(jnp.bfloat16), ((("seq", "exp"), 0),), half_width).astype(
        frame_grad.dtype
    )
    conv_part = jnp.zeros((frames, model_width), jnp.float32)
    for offset in range(tap_count):
        conv_part = (
            conv_part
            + kernel_rows[offset]
            * padded[2 * half_width - offset : 2 * half_width - offset + frames]
        )
    input_grad = (frame_grad + conv_part).astype(jnp.bfloat16)
    return (input_grad, weight_grad, gate_out)


def solution(mesh):
    in_specs = (
        P(("seq", "exp"), None),
        P(("seq", "exp"), None),
        P(("seq", "exp"), None),
        P(("seq", "exp"), None),
        P(),
        P("exp", "seq", None),
    )
    out_specs = (P(("seq", "exp"), None), P("exp", "seq", None), P(("seq", "exp"), None))
    return jax.shard_map(local, mesh=mesh, in_specs=in_specs, out_specs=out_specs, check_vma=False)
```

profile of v0, /device:TPU:8, one launch (start us, length us, event | category | flops | bytes accessed | tf_op | source)
XLA Modules:
  0.0 407.6 jit_solution(1151771117352911082)
XLA Ops:
  7.2 0.0 copy-start
  7.2 0.0 copy-start.3
  7.2 0.0 all-gather.2.cloned.1.call-start
  7.2 0.7 all-gather.2.cloned.1.call-update
  7.9 0.8 copy.41
  8.7 0.1 eq.79
  8.9 0.1 eq.83
  9.0 0.8 copy.44
  9.8 0.2 reshape.154
  10.0 0.9 reduce-window.6
  10.9 0.2 slice_reduce_fusion
  11.1 0.1 fusion.56
  11.2 0.4 fusion.50
  11.6 0.6 copy.45
  12.3 4.3 %all-to-all-start = ((bf16[8,1,60]{2,1,0:T(2,128)(2,1)}), bf16[8,1,60]{2,1,0:T(2,128)(2,1)S(1)}, u32[]{:S(2)}, u32[]{:S(2)}) async-start(bf16[8,1,60]{2,1,0:T(2,128)(2,1)} %copy.45), calls=%async_computation | async-start | bytes 8192 | tf_op jit(solution)/shard_map/all_to_all | solution.py:92
  16.6 0.1 sub.10
  16.7 0.1 copy.43
  16.8 0.7 multiply_add_fusion.2
  17.5 0.1 fusion.52
  17.6 0.5 convolution_convert_fusion.2
  18.1 1.1 reshape.147
  19.2 2.5 all-to-all-done
  21.7 3.6 all-to-all-start.2
  25.3 0.5 convolution_convert_fusion.3
  25.8 1.2 reshape.146
  27.0 14.2 %all-to-all-done.2 = bf16[8,60,1024]{2,1,0:T(8,128)(2,1)S(1)} async-done(((bf16[8,60,1024]{2,1,0:T(8,128)(2,1)}), bf16[8,60,1024]{2,1,0:T(8,128)(2,1)S(1)}, u32[]{:S(2)}, u32[]{:S(2)}) %all-to-all-start.2) | async-done | bytes 983072 | tf_op jit(solution)/shard_map/all_to_all | solution.py:78
  41.2 3.6 all-to-all-start.1
  44.8 0.2 reduce-scatter.2.cloned.1.call-start
  45.0 0.1 reshape.152
  45.1 1.1 reshape.148
  46.2 14.4 %all-to-all-done.1 = bf16[8,60,1024]{2,1,0:T(8,128)(2,1)S(1)} async-done(((bf16[8,60,1024]{2,1,0:T(8,128)(2,1)}), bf16[8,60,1024]{2,1,0:T(8,128)(2,1)S(1)}, u32[]{:S(2)}, u32[]{:S(2)}) %all-to-all-start.1) | async-done | bytes 983072 | tf_op jit(solution)/shard_map/all_to_all | solution.py:85
  60.6 1.5 reshape.153
  62.1 69.8 %all-gather.2.cloned.1.call-done = bf16[1,1024,6144]{2,1,0:T(8,128)(2,1)} async-done(((bf16[1,32,6144]{2,1,0:T(8,128)(2,1)}), bf16[1,1024,6144]{2,1,0:T(8,128)(2,1)}) %all-gather.2.cloned.1.call-update) | async-done | bytes 12582928 | tf_op jit(solution)/shard_map/all_gather | solution.py:96
  131.9 7.0 %fusion.2 = f32[480,4096]{1,0:T(8,128)S(1)} fusion(bf16[480,1024]{1,0:T(8,128)(2,1)} %reshape.148, bf16[1024,6144]{1,0:T(8,128)(2,1)} %bitcast.96), kind=kOutput, calls=%fused_computation.4 | convolution fusion | flops 4026531840 | bytes 17235968 | tf_op jit(solution)/shard_map/dot_general | solution.py:29
  139.0 7.2 %multiply_convert_fusion.2 = (bf16[480,2048]{1,0:T(8,128)(2,1)}, bf16[480,2048]{1,0:T(8,128)(2,1)}, bf16[480,2048]{1,0:T(8,128)(2,1)S(1)}) fusion(f32[480,4096]{1,0:T(8,128)S(1)} %fusion.2, bf16[1024,6144]{1,0:T(8,128)(2,1)} %bitcast.97, f32[480,1024]{1,0:T(8,128)S(1)} %copy-done.2, f32[480]{0:T(512)S(1)} %reshape.152), kind=kOutput, calls=%fused_computation.9 | convolution fusion | flops 2028994560 | bytes 19924864 | tf_op jit(solution)/shard_map/dot_general | solution.py:41
  146.2 2.5 convolution_convert_fusion.1
  148.7 0.0 copy-done.4
  148.7 7.0 %convolution_convert_fusion = bf16[1024,4096]{1,0:T(8,128)(2,1)S(1)} fusion(bf16[480,1024]{1,0:T(8,128)(2,1)S(1)} %copy-done.4, bf16[480,2048]{1,0:T(8,128)(2,1)} %get-tuple-element.4, bf16[480,2048]{1,0:T(8,128)(2,1)} %get-tuple-element.3), kind=kOutput, calls=%fused_computation.1 | convolution fusion | flops 4038590464 | bytes 13303808 | tf_op jit(solution)/shard_map/dot_general | solution.py:104
  155.7 0.0 copy-done.6
  155.7 9.2 %pad_maximum_fusion = bf16[1024,6144]{1,0:T(8,128)(2,1)} fusion(bf16[1024,2048]{1,0:T(8,128)(2,1)S(1)} %convolution_convert_fusion.1, bf16[1024,4096]{1,0:T(8,128)(2,1)S(1)} %convolution_convert_fusion), kind=kLoop, calls=%fused_computation | loop fusion | flops 25165824 | bytes 25165824 | tf_op jit(solution)/shard_map/concatenate | solution.py:102
  164.8 0.0 reduce-scatter.2.cloned.1.call-update
  164.9 5.1 %multiply_reduce_fusion = bf16[480]{0:T(512)(128)(2,1)S(1)} fusion(f32[480,1024]{1,0:T(8,128)S(1)} %copy-done.2, bf16[480,2048]{1,0:T(8,128)(2,1)} %copy-done.6, bf16[1024,6144]{1,0:T(8,128)(2,1)} %bitcast.98), kind=kOutput, calls=%fused_computation.17 | convolution fusion | flops 2014248448 | bytes 8127424 | tf_op jit(solution)/shard_map/dot_general | solution.py:34
  170.0 0.7 convert_element_type.115
  170.7 4.2 %all-to-all-start.4 = ((bf16[8,1,60]{2,1,0:T(2,128)(2,1)}), bf16[8,1,60]{2,1,0:T(2,128)(2,1)S(1)}, u32[]{:S(2)}, u32[]{:S(2)}) async-start(bf16[8,1,60]{2,1,0:T(2,128)(2,1)} %convert_element_type.115), calls=%async_computation.5 | async-start | bytes 8192 | tf_op jit(solution)/shard_map/all_to_all | solution.py:121
  174.9 8.9 %fusion.11 = bf16[480,1024]{1,0:T(8,128)(2,1)S(1)} fusion(bf16[1024,6144]{1,0:T(8,128)(2,1)} %bitcast.99, bf16[480,2048]{1,0:T(8,128)(2,1)} %get-tuple-element.4, bf16[480,2048]{1,0:T(8,128)(2,1)} %get-tuple-element.3), kind=kOutput, calls=%fused_computation.19 | convolution fusion | flops 4034887680 | bytes 13303808 | tf_op jit(solution)/shard_map/dot_general | solution.py:49
  183.8 0.0 copy-start.5
  183.8 1.1 reshape.149
  185.0 0.0 all-to-all-done.4
  185.0 4.7 %all-to-all-start.3 = ((bf16[8,60,1024]{2,1,0:T(8,128)(2,1)}), bf16[8,60,1024]{2,1,0:T(8,128)(2,1)S(1)}, u32[]{:S(2)}, u32[]{:S(2)}) async-start(bf16[8,60,1024]{2,1,0:T(8,128)(2,1)} %reshape.149), calls=%async_computation.3 | async-start | bytes 2097152 | tf_op jit(solution)/shard_map/all_to_all | solution.py:114
  189.8 0.1 fusion.61
  189.8 0.1 reshape.156
  189.9 15.7 %all-to-all-done.3 = bf16[8,60,1024]{2,1,0:T(8,128)(2,1)S(1)} async-done(((bf16[8,60,1024]{2,1,0:T(8,128)(2,1)}), bf16[8,60,1024]{2,1,0:T(8,128)(2,1)S(1)}, u32[]{:S(2)}, u32[]{:S(2)}) %all-to-all-start.3) | async-done | bytes 983072 | tf_op jit(solution)/shard_map/all_to_all | solution.py:114
  205.7 0.2 reshape.150
  205.9 0.4 fusion.63
  206.3 1.9 collective-permute-start
  208.2 7.9 %collective-permute-start.1 = (bf16[15,1024]{1,0:T(8,128)(2,1)S(1)}, bf16[15,1024]{1,0:T(8,128)(2,1)S(1)}, u32[]{:S(2)}, u32[]{:S(2)}) collective-permute-start(bf16[15,1024]{1,0:T(8,128)(2,1)S(1)} %get-tuple-element.7), channel_id=1, source_target_pairs={{1,0},{2,1},{3,2},{4,3},{5,4},{6,5},{7,6},{8,7},{9,8},{10,9},{11,1... | collective-permute-start | bytes 92168 | tf_op jit(solution)/shard_map/ppermute | solution.py:15
  216.1 0.3 fusion.48
  216.4 0.7 copy.48
  217.0 0.0 collective-permute-done
  217.0 0.6 collective-permute-done.1
  217.7 0.1 maximum_convert_fusion
  217.8 0.0 copy-start.1
  217.8 3.8 fusion.16
  221.6 179.2 %reduce-scatter.2.cloned.1.call-done = bf16[32,6144]{1,0:T(8,128)(2,1)} async-done(((bf16[1024,6144]{1,0:T(8,128)(2,1)}), bf16[32,6144]{1,0:T(8,128)(2,1)}) %reduce-scatter.2.cloned.1.call-update) | async-done | bytes 393232 | tf_op jit(solution)/shard_map/reduce_scatter | solution.py:109
  (17 shorter events, 0.2 us)
Async XLA Ops:
  7.2 10.5 %copy-start = (bf16[192,1024]{1,0:T(8,128)(2,1)S(1)}, bf16[192,1024]{1,0:T(8,128)(2,1)}, u32[]{:S(2)}) copy-start(bf16[192,1024]{1,0:T(8,128)(2,1)} %param.6) | copy-start | bytes 1179652
  7.2 18.1 %copy-start.3 = (bf16[192,1024]{1,0:T(8,128)(2,1)S(1)}, bf16[192,1024]{1,0:T(8,128)(2,1)}, u32[]{:S(2)}) copy-start(bf16[192,1024]{1,0:T(8,128)(2,1)} %param.7) | copy-start | bytes 1179652
  7.2 124.8 %all-gather.2.cloned.1.call-start = ((), (), s32[]{:S(2)}) async-start(), calls=%async_computation.6 | async-start | bytes 12976128 | tf_op jit(solution)/shard_map/all_gather | solution.py:96
  12.3 9.5 %all-to-all-start = ((bf16[8,1,60]{2,1,0:T(2,128)(2,1)}), bf16[8,1,60]{2,1,0:T(2,128)(2,1)S(1)}, u32[]{:S(2)}, u32[]{:S(2)}) async-start(bf16[8,1,60]{2,1,0:T(2,128)(2,1)} %copy.45), calls=%async_computation | async-start | bytes 8192 | tf_op jit(solution)/shard_map/all_to_all | solution.py:92
  21.7 19.4 %all-to-all-start.2 = ((bf16[8,60,1024]{2,1,0:T(8,128)(2,1)}), bf16[8,60,1024]{2,1,0:T(8,128)(2,1)S(1)}, u32[]{:S(2)}, u32[]{:S(2)}) async-start(bf16[8,60,1024]{2,1,0:T(8,128)(2,1)} %reshape.147), calls=%async_computation.2 | async-start | bytes 2097152 | tf_op jit(solution)/shard_map/all_to_all | solution.py:78
  41.2 19.5 %all-to-all-start.1 = ((bf16[8,60,1024]{2,1,0:T(8,128)(2,1)}), bf16[8,60,1024]{2,1,0:T(8,128)(2,1)S(1)}, u32[]{:S(2)}, u32[]{:S(2)}) async-start(bf16[8,60,1024]{2,1,0:T(8,128)(2,1)} %reshape.146), calls=%async_computation.1 | async-start | bytes 2097152 | tf_op jit(solution)/shard_map/all_to_all | solution.py:85
  44.8 356.0 %reduce-scatter.2.cloned.1.call-start = ((), (), s32[]{:S(2)}) async-start(), calls=%async_computation.7 | async-start | bytes 12976128 | tf_op jit(solution)/shard_map/reduce_scatter | solution.py:109
  131.9 7.1 %copy-start.2 = (f32[480,1024]{1,0:T(8,128)S(1)}, f32[480,1024]{1,0:T(8,128)}, u32[]{:S(2)}) copy-start(f32[480,1024]{1,0:T(8,128)} %reshape.153) | copy-start | bytes 5898244
  146.2 9.5 %copy-start.6 = (bf16[480,2048]{1,0:T(8,128)(2,1)}, bf16[480,2048]{1,0:T(8,128)(2,1)S(1)}, u32[]{:S(2)}) copy-start(bf16[480,2048]{1,0:T(8,128)(2,1)S(1)} %get-tuple-element.5) | copy-start | bytes 5898244
  146.2 2.5 copy-start.4
  170.7 14.3 %all-to-all-start.4 = ((bf16[8,1,60]{2,1,0:T(2,128)(2,1)}), bf16[8,1,60]{2,1,0:T(2,128)(2,1)S(1)}, u32[]{:S(2)}, u32[]{:S(2)}) async-start(bf16[8,1,60]{2,1,0:T(2,128)(2,1)} %convert_element_type.115), calls=%async_computation.5 | async-start | bytes 8192 | tf_op jit(solution)/shard_map/all_to_all | solution.py:121
  183.8 5.9 %copy-start.5 = (bf16[31,1024]{1,0:T(8,128)(2,1)S(1)}, bf16[31,1024]{1,0:T(8,128)(2,1)}, u32[]{:S(2)}) copy-start(bf16[31,1024]{1,0:T(8,128)(2,1)} %param.10) | copy-start | bytes 190468
  185.0 20.7 %all-to-all-start.3 = ((bf16[8,60,1024]{2,1,0:T(8,128)(2,1)}), bf16[8,60,1024]{2,1,0:T(8,128)(2,1)S(1)}, u32[]{:S(2)}, u32[]{:S(2)}) async-start(bf16[8,60,1024]{2,1,0:T(8,128)(2,1)} %reshape.149), calls=%async_computation.3 | async-start | bytes 2097152 | tf_op jit(solution)/shard_map/all_to_all | solution.py:114
  206.3 10.8 %collective-permute-start = (bf16[15,1024]{1,0:T(8,128)(2,1)S(1)}, bf16[15,1024]{1,0:T(8,128)(2,1)S(1)}, u32[]{:S(2)}, u32[]{:S(2)}) collective-permute-start(bf16[15,1024]{1,0:T(8,128)(2,1)S(1)} %get-tuple-element.6), channel_id=1, source_target_pairs={{0,1},{1,2},{2,3},{3,4},{4,5},{5,6},{6,7},{7,8},{8,9},{9,10},{10,1... | collective-permute-start | bytes 92168 | tf_op jit(solution)/shard_map/ppermute | solution.py:12
  208.2 9.5 %collective-permute-start.1 = (bf16[15,1024]{1,0:T(8,128)(2,1)S(1)}, bf16[15,1024]{1,0:T(8,128)(2,1)S(1)}, u32[]{:S(2)}, u32[]{:S(2)}) collective-permute-start(bf16[15,1024]{1,0:T(8,128)(2,1)S(1)} %get-tuple-element.7), channel_id=1, source_target_pairs={{1,0},{2,1},{3,2},{4,3},{5,4},{6,5},{7,6},{8,7},{9,8},{10,9},{11,1... | collective-permute-start | bytes 92168 | tf_op jit(solution)/shard_map/ppermute | solution.py:15
  217.8 182.9 %copy-start.1 = (bf16[192,1024]{1,0:T(8,128)(2,1)S(1)}, bf16[192,1024]{1,0:T(8,128)(2,1)}, u32[]{:S(2)}) copy-start(bf16[192,1024]{1,0:T(8,128)(2,1)} %param.6) | copy-start | bytes 1179652
Sparse Core Ops, SparseCore 0:
  10.6 121.2 all-gather.1
  165.0 235.6 reduce-scatter.1
where the time goes:
time: 409 us; the launch traced here: 408 us
  waiting for transfers between devices  297 us (73%)
  matrix products  39.6 us (10%)
  starting transfers between devices  30.4 us (7%)
  other arithmetic  15 us (4%)
  between operations  14.3 us (3%)
  local copies, waits for them, and re-layouts  11.1 us (3%)
    reduce_scatter x1, waiting for transfers between devices, local(): lax.psum_scatter(full_term.astype(jnp.bfloat16), 'seq', scatter_dimension...  179 us
    all_gather x1, waiting for transfers between devices, local(): weights = lax.all_gather(expert_weights, 'seq', axis=1, tiled=True)[0]  69.8 us
    all_to_all x1, waiting for transfers between devices, local(): lax.all_to_all(row_grad.reshape(experts, capacity, model_width), 'exp', s...  15.7 us
    all_to_all x1, waiting for transfers between devices, local(): lax.all_to_all(sent_grad.reshape(experts, capacity, model_width), 'exp',...  14.4 us
    all_to_all x1, waiting for transfers between devices, local(): lax.all_to_all(sent_in.reshape(experts, capacity, model_width), 'exp', sp...  14.2 us
    concatenate x1, other arithmetic, local(): jnp.concatenate([lax.dot_general(rows_in, pre_grads, contract, preferred_...  9.18 us
    dot_general x1, matrix products, expert_backward(): lax.dot_general(pre_grads, in_weights, (((1,), (1,)), ((), ())), preferre...  8.91 us
  transfers between devices with their start and end apart: 9, of which 7 were waited for; matrix products, arithmetic and copies ran while one was open for 8% of the time, Pallas kernels for 0%

commit v1 on v0

v1 whole, which is shorter than its diff:
```python
import jax
import jax.numpy as jnp
from jax import lax
from jax.sharding import Mesh, PartitionSpec as P

BF = jnp.bfloat16
F32 = jnp.float32
SLOTS = 64
SPARE = 60
META = 16


def dot(a, b, contract, batch=((), ())):
    return lax.dot_general(a, b, (contract, batch), preferred_element_type=F32)


def ring_gather(shard, axis, place, buffer):
    count = lax.axis_size(axis)
    me = lax.axis_index(axis)
    up = [(i, (i + 1) % count) for i in range(count)]
    down = [(target, source) for source, target in up]
    buffer = place(buffer, shard, me)
    right = left = shard
    for step in range(1, count // 2 + 1):
        right = lax.ppermute(right, axis, up)
        buffer = place(buffer, right, (me - step) % count)
        if step < count - step:
            left = lax.ppermute(left, axis, down)
            buffer = place(buffer, left, (me + step) % count)
    return buffer


def gather_weights(expert_weights):
    ny, nz = lax.axis_size("y"), lax.axis_size("z")
    rows, width = expert_weights.shape[1], expert_weights.shape[2]
    part = width // (3 * ny)
    sliced = expert_weights[0].reshape(rows, 3, ny, part).transpose(2, 0, 1, 3)
    sliced = sliced.reshape(ny, rows, 3 * part)
    mine = lax.all_to_all(sliced, "y", 0, 0, tiled=True)

    def place(buffer, shard, z):
        return lax.dynamic_update_slice(buffer, shard[:, None], (0, z, 0, 0))

    buffer = ring_gather(mine, "z", place, jnp.zeros((ny, nz, rows, 3 * part), BF))
    return buffer.reshape(ny * nz * rows, 3 * part)


def scatter_weight_grad(term):
    ny, nz = lax.axis_size("y"), lax.axis_size("z")
    rows = term.shape[0] // (ny * nz)
    part = term.shape[1] // 3
    blocks = term.reshape(ny, nz, rows, 3 * part).transpose(1, 0, 2, 3)
    mine = lax.psum_scatter(blocks.reshape(nz * ny * rows, 3 * part), "z", scatter_dimension=0, tiled=True)
    back = lax.all_to_all(mine.reshape(ny, rows, 3 * part), "y", 0, 0, tiled=True)
    back = back.reshape(ny, rows, 3, part).transpose(1, 2, 0, 3)
    return back.reshape(1, rows, 3 * ny * part)


def slots_of(chosen):
    frames = chosen.shape[-1]
    before = (jnp.arange(frames)[:, None] < jnp.arange(frames)[None, :]).astype(BF)
    ranks = dot(chosen.astype(BF), before, ((chosen.ndim - 1,), (0,))).astype(jnp.int32)
    return chosen[..., None, :] & (ranks[..., None, :] == jnp.arange(SLOTS)[:, None])


def with_halo(block, width):
    axes = ("y", "z", "x", "c")
    count = 1
    for axis in axes:
        count *= lax.axis_size(axis)
    forward = [(i, i + 1) for i in range(count - 1)]
    backward = [(target, source) for source, target in forward]
    low = lax.ppermute(block[block.shape[0] - width :], axes, forward)
    high = lax.ppermute(block[:width], axes, backward)
    return jnp.concatenate([low, block, high], axis=0)


def local(block_in, out_grad, gate_values, expert_ids, conv_kernel, expert_weights):
    frames, width = block_in.shape
    ny, experts = lax.axis_size("y"), lax.axis_size("x") * lax.axis_size("c")
    group = ("y", "x", "c")
    expert = lax.axis_index("x") * lax.axis_size("c") + lax.axis_index("c")

    meta = jnp.concatenate([expert_ids.astype(BF).T, gate_values.T], axis=0)
    meta = jnp.pad(meta, ((0, META - 4), (0, width - frames)))
    packed = jnp.concatenate([block_in, meta], axis=0)
    all_in = lax.all_gather(packed, group, axis=0, tiled=False)
    all_grad = lax.all_gather(out_grad, group, axis=0, tiled=False)
    blocks = all_in.shape[0]
    weights = gather_weights(expert_weights)
    part = weights.shape[1] // 3
    in_weights, down_weights = weights[:, : 2 * part], weights[:, 2 * part :]

    ids = all_in[:, frames : frames + 2, :frames].astype(jnp.int32) == expert
    gates = all_in[:, frames + 2 : frames + 4, :frames]
    gate = jnp.where(ids[:, 0], gates[:, 0], gates[:, 1])
    chosen = slots_of(ids[:, 0] | ids[:, 1])
    placing = chosen.astype(BF)
    placing_gate = jnp.where(chosen, gate[:, None, :], jnp.zeros((), BF))

    rows_in = dot(placing, all_in[:, :frames], ((2,), (1,)), ((0,), (0,))).astype(BF)
    rows_in = rows_in.reshape(blocks * SLOTS, width)
    projected = dot(rows_in, in_weights, ((1,), (0,)))
    gate_in, up_in = projected[:, :part], projected[:, part:]
    sigmoid = jax.nn.sigmoid(gate_in)
    activated = gate_in * sigmoid
    derivative = sigmoid * (1.0 + gate_in * (1.0 - sigmoid))
    hidden = (activated * up_in).astype(BF)

    rows_q = dot(placing_gate, all_grad, ((2,), (1,)), ((0,), (0,))).astype(BF)
    rows_q = rows_q.reshape(blocks * SLOTS, width)
    hidden_grad = dot(rows_q, down_weights, ((1,), (0,)))
    gate_part = jnp.sum(hidden.astype(F32) * hidden_grad, axis=1).reshape(blocks, 1, SLOTS)
    pre_grads = jnp.concatenate(
        [(hidden_grad * up_in * derivative).astype(BF), (hidden_grad * activated).astype(BF)], axis=1
    )
    row_grad = dot(pre_grads, in_weights, ((1,), (1,))).reshape(blocks, SLOTS, width)
    gate_rows = jnp.pad(gate_part, ((0, 0), (0, 0), (0, width - SLOTS)))
    spare = (jnp.arange(SLOTS) == SPARE)[None, :, None]
    row_grad = jnp.where(spare, gate_rows, row_grad).astype(BF)

    parts = lax.all_to_all(row_grad.reshape(ny, experts * SLOTS, width), "y", 0, 0, tiled=True)
    summed = jnp.sum(parts.astype(F32), axis=0).astype(BF)
    returned = lax.all_to_all(summed.reshape(experts, SLOTS, width), ("x", "c"), 0, 0, tiled=True)

    term = jnp.concatenate(
        [dot(rows_in, pre_grads, ((0,), (0,))), dot(rows_q, hidden, ((0,), (0,)))], axis=1
    ).astype(BF)
    weight_grad = scatter_weight_grad(term)

    own_ids = expert_ids.T[None] == jnp.arange(experts, dtype=jnp.int32)[:, None, None]
    own = slots_of(own_ids[:, 0] | own_ids[:, 1])
    own_placing = own.astype(BF)
    flat = own_placing.reshape(experts * SLOTS, frames)
    frame_grad = out_grad.astype(F32) + dot(
        flat, returned.reshape(experts * SLOTS, width), ((0,), (0,))
    )
    gate_sums = jnp.einsum(
        "es,est,ekt->tk",
        returned[:, SPARE, :SLOTS].astype(F32),
        own.astype(F32),
        own_ids.astype(F32),
        precision="highest",
    )
    gate_out = (gate_sums / gate_values.astype(F32)).astype(BF)

    taps = conv_kernel.shape[0]
    half = (taps - 1) // 2
    kernel_rows = conv_kernel.astype(F32)
    padded = with_halo(frame_grad.astype(BF), half).astype(F32)
    conv_part = jnp.zeros((frames, width), F32)
    for offset in range(taps):
        conv_part = conv_part + kernel_rows[offset] * padded[2 * half - offset : 2 * half - offset + frames]
    input_grad = (frame_grad + conv_part).astype(BF)
    return input_grad, weight_grad, gate_out


def solution(mesh):
    grid = Mesh(mesh.devices.reshape(4, 8, 4, 2), ("y", "z", "x", "c"))
    frames = P(("y", "z", "x", "c"), None)
    weights = P(("x", "c"), ("y", "z"), None)
    in_specs = (frames, frames, frames, frames, P(), weights)
    out_specs = (frames, weights, frames)
    return jax.shard_map(local, mesh=grid, in_specs=in_specs, out_specs=out_specs, check_vma=False)
```

time: 409 us -> 314 us (0.77)
  waiting for transfers between devices: 297 us -> 122 us
  blocking collectives: 0 us -> 52.5 us
  local copies, waits for them, and re-layouts: 11.1 us -> 24 us
  matrix products: 39.6 us -> 47.2 us
  starting transfers between devices: 30.4 us -> 36.8 us
    reduce_scatter x1, waiting for transfers between devices: 179 us -> 0.02 us  [scatter_weight_grad(): lax.psum_scatter(blocks.reshape(nz * ny * rows, 3 * part), 'z', scatter_d...]
    all_to_all x0 -> x1, blocking collectives: none -> 52.5 us  [local(): lax.all_to_all(row_grad.reshape(ny, experts * SLOTS, width), 'y', 0, 0, t...]
    ppermute x2 -> x9, waiting for transfers between devices: 0.63 us -> 31.8 us  [the longest x4 18.4 us: ring_gather(): right = lax.ppermute(right, axis, up)]
    all_to_all x5 -> x3, waiting for transfers between devices: 46.9 us -> 23.7 us  [the longest x1 15.7 us: local(): lax.all_to_all(summed.reshape(experts, SLOTS, width), ('x', 'c'), 0, 0, t...]
    ppermute x2 -> x9, starting transfers between devices: 9.78 us -> 23 us  [the longest x3 13.2 us: ring_gather(): left = lax.ppermute(left, axis, down)]
    dot_general x1 -> x2, local copies, waits for them, and re-layouts: 0.67 us -> 13.2 us  [dot(): return lax.dot_general(a, b, (contract, batch), preferred_element_type=F32)]
    dot_general x11, matrix products: 39.6 us -> 47.2 us  [the longest x10 47 us: dot(): return lax.dot_general(a, b, (contract, batch), preferred_element_type=F32)]
    concatenate x1 -> x2, other arithmetic: 9.18 us -> 2.47 us  [the longest x1 1.79 us: local(): packed = jnp.concatenate([block_in, meta], axis=0)]
  transfers between devices with their start and end apart: 9 -> 15, of which waited for: 7 -> 10; matrix products, arithmetic and copies ran while one was open for 8% -> 13% of each run, Pallas kernels for 0% -> 0%
where the time goes in v1:
time: 314 us; the launch traced here: 312 us
  waiting for transfers between devices  122 us (39%)
  blocking collectives  52.5 us (17%)
  matrix products  47.2 us (15%)
  starting transfers between devices  36.8 us (12%)
  local copies, waits for them, and re-layouts  24 us (8%)
  other arithmetic  15.4 us (5%)
  between operations  14.1 us (4%)
    all_to_all x1, blocking collectives, local(): lax.all_to_all(row_grad.reshape(ny, experts * SLOTS, width), 'y', 0, 0, t...  52.5 us
    all_gather x1, waiting for transfers between devices, local(): all_grad = lax.all_gather(out_grad, group, axis=0, tiled=False)  52.2 us
    dot_general x10, matrix products, dot(): return lax.dot_general(a, b, (contract, batch), preferred_element_type=F32)  47 us
    ppermute x4, waiting for transfers between devices, ring_gather(): right = lax.ppermute(right, axis, up)  18.4 us
    all_to_all x1, waiting for transfers between devices, local(): lax.all_to_all(summed.reshape(experts, SLOTS, width), ('x', 'c'), 0, 0, t...  15.7 us
    ppermute x3, starting transfers between devices, ring_gather(): left = lax.ppermute(left, axis, down)  13.2 us
    dot_general x2, local copies, waits for them, and re-layouts, dot(): return lax.dot_general(a, b, (contract, batch), preferred_element_type=F32)  13.2 us
    all_gather x1, waiting for transfers between devices, local(): all_in = lax.all_gather(packed, group, axis=0, tiled=False)  13.2 us
  transfers between devices with their start and end apart: 15, of which 10 were waited for; matrix products, arithmetic and copies ran while one was open for 13% of the time, Pallas kernels for 0%

profile of v1, /device:TPU:8, one launch (start us, length us, event | category | flops | bytes accessed | tf_op | source)
XLA Modules:
  0.0 311.7 jit_solution(12913092034407135313)
XLA Ops:
  7.2 0.0 all-gather.5.cloned.1.call-start
  7.2 0.7 convert_bitcast_fusion
  7.9 0.7 fusion.79
  8.6 1.8 pad_maximum_fusion.3
  10.4 0.0 all-gather.5.cloned.1.call-update
  10.4 0.0 all-gather.7.cloned.1.call-start
  10.4 0.7 all-gather.7.cloned.1.call-update
  11.2 1.3 reshape_squeeze.3
  12.4 0.2 copy.62
  12.7 1.3 reshape.61
  13.9 5.6 %all-to-all-start = ((bf16[4,32,1536]{2,1,0:T(8,128)(2,1)}), bf16[4,32,1536]{2,1,0:T(8,128)(2,1)S(1)}, u32[]{:S(2)}, u32[]{:S(2)}) async-start(bf16[4,32,1536]{2,1,0:T(8,128)(2,1)} %reshape.61), calls=%async_computation | async-start | bytes 786432 | tf_op jit(solution)/shard_map/all_to_all | solution.py:39
  19.6 0.1 broadcast_in_dim.78
  19.6 5.8 %all-to-all-done = bf16[4,32,1536]{2,1,0:T(8,128)(2,1)S(1)} async-done(((bf16[4,32,1536]{2,1,0:T(8,128)(2,1)}), bf16[4,32,1536]{2,1,0:T(8,128)(2,1)S(1)}, u32[]{:S(2)}, u32[]{:S(2)}) %all-to-all-start) | async-done | bytes 393248 | tf_op jit(solution)/shard_map/all_to_all | solution.py:39
  25.5 5.8 %collective-permute-start.1 = (bf16[4,32,1536]{2,1,0:T(8,128)(2,1)S(1)}, bf16[4,32,1536]{2,1,0:T(8,128)(2,1)S(1)}, u32[]{:S(2)}, u32[]{:S(2)}) collective-permute-start(bf16[4,32,1536]{2,1,0:T(8,128)(2,1)S(1)} %all-to-all-done), channel_id=1, source_target_pairs={{8,0},{16,8},{24,16},{32,24},{40,32},{48,40},{56,48},{0,56},{9,1},... | collective-permute-start | bytes 1179656 | tf_op jit(solution)/shard_map/ppermute | solution.py:28
  31.3 0.3 broadcast_in_dim.80
  31.7 6.5 %collective-permute-done.1 = bf16[4,32,1536]{2,1,0:T(8,128)(2,1)S(1)} collective-permute-done((bf16[4,32,1536]{2,1,0:T(8,128)(2,1)S(1)}, bf16[4,32,1536]{2,1,0:T(8,128)(2,1)S(1)}, u32[]{:S(2)}, u32[]{:S(2)}) %collective-permute-start.1) | collective-permute-done | bytes 393248 | tf_op jit(solution)/shard_map/ppermute | solution.py:28
  38.2 3.7 %collective-permute-start.3 = (bf16[4,32,1536]{2,1,0:T(8,128)(2,1)S(1)}, bf16[4,32,1536]{2,1,0:T(8,128)(2,1)S(1)}, u32[]{:S(2)}, u32[]{:S(2)}) collective-permute-start(bf16[4,32,1536]{2,1,0:T(8,128)(2,1)S(1)} %collective-permute-done.1), channel_id=1, source_target_pairs={{8,0},{16,8},{24,16},{32,24},{40,32},{48,40},{56,48},{0,56},{9,1},... | collective-permute-start | bytes 1179656 | tf_op jit(solution)/shard_map/ppermute | solution.py:28
  42.0 6.0 %collective-permute-done.3 = bf16[4,32,1536]{2,1,0:T(8,128)(2,1)S(1)} collective-permute-done((bf16[4,32,1536]{2,1,0:T(8,128)(2,1)S(1)}, bf16[4,32,1536]{2,1,0:T(8,128)(2,1)S(1)}, u32[]{:S(2)}, u32[]{:S(2)}) %collective-permute-start.3) | collective-permute-done | bytes 393248 | tf_op jit(solution)/shard_map/ppermute | solution.py:28
  48.0 3.7 %collective-permute-start.5 = (bf16[4,32,1536]{2,1,0:T(8,128)(2,1)S(1)}, bf16[4,32,1536]{2,1,0:T(8,128)(2,1)S(1)}, u32[]{:S(2)}, u32[]{:S(2)}) collective-permute-start(bf16[4,32,1536]{2,1,0:T(8,128)(2,1)S(1)} %collective-permute-done.3), channel_id=1, source_target_pairs={{8,0},{16,8},{24,16},{32,24},{40,32},{48,40},{56,48},{0,56},{9,1},... | collective-permute-start | bytes 1179656 | tf_op jit(solution)/shard_map/ppermute | solution.py:28
  51.7 9.5 %collective-permute-done.4 = bf16[4,32,1536]{2,1,0:T(8,128)(2,1)S(1)} collective-permute-done((bf16[4,32,1536]{2,1,0:T(8,128)(2,1)S(1)}, bf16[4,32,1536]{2,1,0:T(8,128)(2,1)S(1)}, u32[]{:S(2)}, u32[]{:S(2)}) %collective-permute-start.4) | collective-permute-done | bytes 393248 | tf_op jit(solution)/shard_map/ppermute | solution.py:25
  61.3 8.9 %collective-permute-done.6 = bf16[4,32,1536]{2,1,0:T(8,128)(2,1)S(1)} collective-permute-done((bf16[4,32,1536]{2,1,0:T(8,128)(2,1)S(1)}, bf16[4,32,1536]{2,1,0:T(8,128)(2,1)S(1)}, u32[]{:S(2)}, u32[]{:S(2)}) %collective-permute-start.6) | collective-permute-done | bytes 393248 | tf_op jit(solution)/shard_map/ppermute | solution.py:25
  70.2 13.2 %all-gather.5.cloned.1.call-done = bf16[6656,1024]{1,0:T(8,128)(2,1)} async-done(((bf16[208,1024]{1,0:T(8,128)(2,1)}), bf16[6656,1024]{1,0:T(8,128)(2,1)}) %all-gather.5.cloned.1.call-update) | async-done | bytes 13631504 | tf_op jit(solution)/shard_map/all_gather | solution.py:87
  83.4 1.0 convert_compare_fusion
  84.3 0.1 slice_or_fusion
  84.4 1.1 slice_select_fusion
  85.6 0.1 convolution_convert_fusion.1
  85.7 9.0 %fusion.7 = bf16[32,64,1024]{2,1,0:T(8,128)(2,1)} fusion(bf16[32,208,1024]{2,1,0:T(8,128)(2,1)} %bitcast.146, s32[32,192]{1,0:T(8,128)S(1)} %convolution_convert_fusion.1, pred[32,192]{1,0:T(8,128)(4,1)S(1)} %copy.75), kind=kOutput, calls=%fused_computation.15 | convolution fusion | flops 808189952 | bytes 16807936 | tf_op jit(solution)/shard_map/dot_general | solution.py:14
  94.7 6.6 %copy.35 = bf16[1024,2048]{1,0:T(8,128)(2,1)} copy(bf16[1024,2048]{0,1:T(8,128)(2,1)} %bitcast.141) | data formatting | bytes 8388608 | tf_op jit(solution)/shard_map/dot_general | solution.py:14
  101.3 52.2 %all-gather.7.cloned.1.call-done = bf16[6144,1024]{1,0:T(8,128)(2,1)} async-done(((bf16[192,1024]{1,0:T(8,128)(2,1)}), bf16[6144,1024]{1,0:T(8,128)(2,1)}) %all-gather.7.cloned.1.call-update) | async-done | bytes 12582928 | tf_op jit(solution)/shard_map/all_gather | solution.py:88
  153.5 9.0 %convolution_convert_fusion = bf16[32,64,1024]{2,1,0:T(8,128)(2,1)} fusion(bf16[32,192,1024]{2,1,0:T(8,128)(2,1)} %bitcast.137, s32[32,192]{1,0:T(8,128)S(1)} %convolution_convert_fusion.1, pred[32,192]{1,0:T(8,128)(4,1)S(1)} %copy.75, bf16[32,192]{1,0:T(8,128)(2,1)S(1)} %bitcast.156), kind=kOutput, calls=%fused_computation.16 | convolution fusion | flops 808583168 | bytes 16820224 | tf_op jit(solution)/shard_map/dot_general | solution.py:14
  162.5 6.6 %copy.37 = bf16[1024,2048]{1,0:T(8,128)(2,1)} copy(bf16[1024,2048]{0,1:T(8,128)(2,1)} %bitcast.138) | data formatting | bytes 8388608 | tf_op jit(solution)/shard_map/dot_general | solution.py:14
  169.1 6.7 %fusion.19 = f32[2048,1024]{0,1:T(8,128)S(1)} fusion(bf16[2048,1024]{1,0:T(8,128)(2,1)} %bitcast.142, bf16[1024,1536]{1,0:T(8,128)(2,1)S(1)} %bitcast.150), kind=kOutput, calls=%fused_computation.24 | convolution fusion | flops 4294967296 | bytes 14680064 | tf_op jit(solution)/shard_map/dot_general | solution.py:14
  175.8 4.7 %multiply_reduce_fusion = (bf16[2048]{0:T(1024)(128)(2,1)S(1)}, bf16[2048,512]{0,1:T(8,128)(2,1)S(1)}, bf16[2048,512]{0,1:T(8,128)(2,1)S(1)}, bf16[2048,512]{0,1:T(8,128)(2,1)S(1)}) fusion(f32[2048,1024]{0,1:T(8,128)S(1)} %fusion.19, bf16[2048,1024]{1,0:T(8,128)(2,1)S(1)} %bitcast.139, bf16[1024,1536]{1,0:T(8,128)(2,1)S(1)} %bitcast.151), kind=kOutput, calls=%fused_computation.9 | convolution fusion | flops 2166355968 | bytes 19927040 | tf_op jit(solution)/shard_map/dot_general | solution.py:14
  180.6 2.4 fusion.21
  183.0 1.3 copy-done.1
  184.3 6.0 %fusion.15 = bf16[4,8,32,1024]{3,2,1,0:T(8,128)(2,1)S(1)} fusion(bf16[4,8,32,2048]{3,2,1,0:T(8,128)(2,1)S(1)} %bitcast.147, bf16[2048,512]{0,1:T(8,128)(2,1)S(1)} %get-tuple-element.5, bf16[2048,512]{0,1:T(8,128)(2,1)S(1)} %get-tuple-element.6), kind=kOutput, calls=%fused_computation.22 | convolution fusion | flops 4304404480 | bytes 10485760 | tf_op jit(solution)/shard_map/dot_general | solution.py:14
  190.3 0.2 maximum_bitcast_fusion
  190.5 2.0 copy.39
  192.5 0.0 reduce-scatter.2.cloned.1.call-update
  192.5 8.5 %fusion.6 = bf16[2048,1024]{1,0:T(8,128)(2,1)} fusion(bf16[2048,512]{0,1:T(8,128)(2,1)} %copy-done.8, bf16[2048,512]{0,1:T(8,128)(2,1)} %copy-done.9, bf16[1024,1536]{1,0:T(8,128)(2,1)S(1)} %bitcast.152), kind=kOutput, calls=%fused_computation.14 | convolution fusion | flops 4303355904 | bytes 10485760 | tf_op jit(solution)/shard_map/dot_general | solution.py:14
  201.0 0.1 reshape.64
  201.1 0.5 broadcast_in_dim.93
  201.6 1.6 copy-done.2
  203.3 0.9 fusion.2
  204.2 52.5 %all_to_all.20 = bf16[4,512,1024]{2,1,0:T(8,128)(2,1)} all-to-all(bf16[4,512,1024]{2,1,0:T(8,128)(2,1)S(1)} %fusion.2), channel_id=1, replica_groups=mesh['y'=4,'z'=8,'x'=4,'c'=2] {'y'}, dimensions={0} | all-to-all | bytes 8388608 | tf_op jit(solution)/shard_map/all_to_all | solution.py:122
  256.7 4.5 %reduce_sum.22 = bf16[512,1024]{1,0:T(8,128)(2,1)} reduce(bf16[4,512,1024]{2,1,0:T(8,128)(2,1)} %all_to_all.20, bf16[]{:T(256)} %constant.61.clone.1), dimensions={0}, to_apply=%region_1.2 | reduce | flops 1572864 | bytes 5242882 | tf_op jit(solution)/shard_map/reduce_sum | solution.py:123
  261.2 4.2 %all-to-all-start.2 = ((bf16[8,64,1024]{2,1,0:T(8,128)(2,1)}), bf16[8,64,1024]{2,1,0:T(8,128)(2,1)S(1)}, u32[]{:S(2)}, u32[]{:S(2)}) async-start(bf16[8,64,1024]{2,1,0:T(8,128)(2,1)} %bitcast.31), calls=%async_computation.2 | async-start | bytes 2097152 | tf_op jit(solution)/shard_map/all_to_all | solution.py:124
  265.5 0.1 convolution_convert_fusion.2
  265.7 0.1 fusion.86
  265.8 15.7 %all-to-all-done.2 = bf16[8,64,1024]{2,1,0:T(8,128)(2,1)S(1)} async-done(((bf16[8,64,1024]{2,1,0:T(8,128)(2,1)}), bf16[8,64,1024]{2,1,0:T(8,128)(2,1)S(1)}, u32[]{:S(2)}, u32[]{:S(2)}) %all-to-all-start.2) | async-done | bytes 1048608 | tf_op jit(solution)/shard_map/all_to_all | solution.py:124
  281.4 0.2 fusion.67
  281.7 0.4 fusion.88
  282.1 1.9 collective-permute-start.7
  284.0 7.9 %collective-permute-start.8 = (bf16[15,1024]{1,0:T(8,128)(2,1)S(1)}, bf16[15,1024]{1,0:T(8,128)(2,1)S(1)}, u32[]{:S(2)}, u32[]{:S(2)}) collective-permute-start(bf16[15,1024]{1,0:T(8,128)(2,1)S(1)} %get-tuple-element.8), channel_id=1, source_target_pairs={{1,0},{2,1},{3,2},{4,3},{5,4},{6,5},{7,6},{8,7},{9,8},{10,9},{11,1... | collective-permute-start | bytes 92168 | tf_op jit(solution)/shard_map/ppermute | solution.py:74
  292.0 0.6 fusion.81
  292.5 1.0 collective-permute-done.8
  293.5 0.1 maximum_convert_fusion
  293.6 0.0 reduce-scatter.2.cloned.1.call-done
  293.6 3.9 %all-to-all-start.3 = ((bf16[4,32,1536]{2,1,0:T(8,128)(2,1)}), bf16[4,32,1536]{2,1,0:T(8,128)(2,1)S(1)}, u32[]{:S(2)}, u32[]{:S(2)}) async-start(bf16[4,32,1536]{2,1,0:T(8,128)(2,1)} %bitcast.155), calls=%async_computation.4 | async-start | bytes 786432 | tf_op jit(solution)/shard_map/all_to_all | solution.py:54
  297.6 3.7 %fusion.34 = bf16[192,1024]{1,0:T(8,128)(2,1)} fusion(f32[192,1024]{1,0:T(8,128)S(1)} %get-tuple-element.41, f32[222,1024]{1,0:T(8,128)S(1)} %maximum_convert_fusion, f32[1024]{0:T(1024)S(1)} %bitcast.173, f32[1024]{0:T(1024)S(1)} %bitcast.172, f32[1024]{0:T(1024)S(1)} %bitcast.171, f32[1024]{0:T(1024)S(1)} %bitcast.170, f32[1024]{0:T(1024)S(1)} %bitcast.169, ...), kind=kLoop, calls=%fused_computation.40 | loop fusion | flops 12386304 | bytes 25686016 | tf_op jit(solution)/shard_map/convert_element_type | solution.py:154
  301.2 2.2 all-to-all-done.3
  303.5 0.3 reshape.69
  303.7 0.4 copy.40
  304.1 1.0 reshape.70
  (47 shorter events, 0.4 us)
Async XLA Ops:
  7.2 76.2 %all-gather.5.cloned.1.call-start = ((), (), s32[]{:S(2)}) async-start(), calls=%async_computation.6 | async-start | bytes 14057472 | tf_op jit(solution)/shard_map/all_gather | solution.py:87
  10.4 143.1 %all-gather.7.cloned.1.call-start = ((), (), s32[]{:S(2)}) async-start(), calls=%async_computation.7 | async-start | bytes 12976128 | tf_op jit(solution)/shard_map/all_gather | solution.py:88
  13.9 11.5 %all-to-all-start = ((bf16[4,32,1536]{2,1,0:T(8,128)(2,1)}), bf16[4,32,1536]{2,1,0:T(8,128)(2,1)S(1)}, u32[]{:S(2)}, u32[]{:S(2)}) async-start(bf16[4,32,1536]{2,1,0:T(8,128)(2,1)} %reshape.61), calls=%async_computation | async-start | bytes 786432 | tf_op jit(solution)/shard_map/all_to_all | solution.py:39
  19.5 274.1 %reduce-scatter.2.cloned.1.call-start = ((), (), s32[]{:S(2)}) async-start(), calls=%async_computation.5 | async-start | bytes 3538944 | tf_op jit(solution)/shard_map/reduce_scatter | solution.py:53
  25.5 12.7 %collective-permute-start.1 = (bf16[4,32,1536]{2,1,0:T(8,128)(2,1)S(1)}, bf16[4,32,1536]{2,1,0:T(8,128)(2,1)S(1)}, u32[]{:S(2)}, u32[]{:S(2)}) collective-permute-start(bf16[4,32,1536]{2,1,0:T(8,128)(2,1)S(1)} %all-to-all-done), channel_id=1, source_target_pairs={{8,0},{16,8},{24,16},{32,24},{40,32},{48,40},{56,48},{0,56},{9,1},... | collective-permute-start | bytes 1179656 | tf_op jit(solution)/shard_map/ppermute | solution.py:28
  31.3 10.6 %collective-permute-start = (bf16[4,32,1536]{2,1,0:T(8,128)(2,1)S(1)}, bf16[4,32,1536]{2,1,0:T(8,128)(2,1)S(1)}, u32[]{:S(2)}, u32[]{:S(2)}) collective-permute-start(bf16[4,32,1536]{2,1,0:T(8,128)(2,1)S(1)} %all-to-all-done), channel_id=1, source_target_pairs={{0,8},{8,16},{16,24},{24,32},{32,40},{40,48},{48,56},{56,0},{1,9},... | collective-permute-start | bytes 1179656 | tf_op jit(solution)/shard_map/ppermute | solution.py:25
  38.2 9.8 %collective-permute-start.3 = (bf16[4,32,1536]{2,1,0:T(8,128)(2,1)S(1)}, bf16[4,32,1536]{2,1,0:T(8,128)(2,1)S(1)}, u32[]{:S(2)}, u32[]{:S(2)}) collective-permute-start(bf16[4,32,1536]{2,1,0:T(8,128)(2,1)S(1)} %collective-permute-done.1), channel_id=1, source_target_pairs={{8,0},{16,8},{24,16},{32,24},{40,32},{48,40},{56,48},{0,56},{9,1},... | collective-permute-start | bytes 1179656 | tf_op jit(solution)/shard_map/ppermute | solution.py:28
  41.9 9.8 %collective-permute-start.2 = (bf16[4,32,1536]{2,1,0:T(8,128)(2,1)S(1)}, bf16[4,32,1536]{2,1,0:T(8,128)(2,1)S(1)}, u32[]{:S(2)}, u32[]{:S(2)}) collective-permute-start(bf16[4,32,1536]{2,1,0:T(8,128)(2,1)S(1)} %collective-permute-done), channel_id=1, source_target_pairs={{0,8},{8,16},{16,24},{24,32},{32,40},{40,48},{48,56},{56,0},{1,9},... | collective-permute-start | bytes 1179656 | tf_op jit(solution)/shard_map/ppermute | solution.py:25
  48.0 13.3 %collective-permute-start.5 = (bf16[4,32,1536]{2,1,0:T(8,128)(2,1)S(1)}, bf16[4,32,1536]{2,1,0:T(8,128)(2,1)S(1)}, u32[]{:S(2)}, u32[]{:S(2)}) collective-permute-start(bf16[4,32,1536]{2,1,0:T(8,128)(2,1)S(1)} %collective-permute-done.3), channel_id=1, source_target_pairs={{8,0},{16,8},{24,16},{32,24},{40,32},{48,40},{56,48},{0,56},{9,1},... | collective-permute-start | bytes 1179656 | tf_op jit(solution)/shard_map/ppermute | solution.py:28
  51.7 9.5 %collective-permute-start.4 = (bf16[4,32,1536]{2,1,0:T(8,128)(2,1)S(1)}, bf16[4,32,1536]{2,1,0:T(8,128)(2,1)S(1)}, u32[]{:S(2)}, u32[]{:S(2)}) collective-permute-start(bf16[4,32,1536]{2,1,0:T(8,128)(2,1)S(1)} %collective-permute-done.2), channel_id=1, source_target_pairs={{0,8},{8,16},{16,24},{24,32},{32,40},{40,48},{48,56},{56,0},{1,9},... | collective-permute-start | bytes 1179656 | tf_op jit(solution)/shard_map/ppermute | solution.py:25
  61.2 9.0 %collective-permute-start.6 = (bf16[4,32,1536]{2,1,0:T(8,128)(2,1)S(1)}, bf16[4,32,1536]{2,1,0:T(8,128)(2,1)S(1)}, u32[]{:S(2)}, u32[]{:S(2)}) collective-permute-start(bf16[4,32,1536]{2,1,0:T(8,128)(2,1)S(1)} %collective-permute-done.4), channel_id=1, source_target_pairs={{0,8},{8,16},{16,24},{24,32},{32,40},{40,48},{48,56},{56,0},{1,9},... | collective-permute-start | bytes 1179656 | tf_op jit(solution)/shard_map/ppermute | solution.py:25
  169.1 6.7 %copy-start = (bf16[32,64,1024]{2,1,0:T(8,128)(2,1)S(1)}, bf16[32,64,1024]{2,1,0:T(8,128)(2,1)}, u32[]{:S(2)}) copy-start(bf16[32,64,1024]{2,1,0:T(8,128)(2,1)} %convolution_convert_fusion) | copy-start | bytes 12582916
  175.8 4.8 %copy-start.3 = (bf16[1024,2048]{1,0:T(8,128)(2,1)S(1)}, bf16[1024,2048]{1,0:T(8,128)(2,1)}, u32[]{:S(2)}) copy-start(bf16[1024,2048]{1,0:T(8,128)(2,1)} %copy.37) | copy-start | bytes 12582916
  180.6 2.4 copy-start.8
  180.6 2.4 copy-start.9
  180.6 3.7 %copy-start.1 = (bf16[1024,2048]{1,0:T(8,128)(2,1)S(1)}, bf16[1024,2048]{1,0:T(8,128)(2,1)}, u32[]{:S(2)}) copy-start(bf16[1024,2048]{1,0:T(8,128)(2,1)} %copy.35) | copy-start | bytes 12582916
  201.1 2.2 copy-start.2
  256.7 8.8 %copy-start.6 = (s32[192,2]{0,1:T(2,128)S(1)}, s32[192,2]{0,1:T(2,128)}, u32[]{:S(2)}) copy-start(s32[192,2]{0,1:T(2,128)} %param.9) | copy-start | bytes 4612
  256.7 8.9 %copy-start.5 = (bf16[31,1024]{1,0:T(8,128)(2,1)S(1)}, bf16[31,1024]{1,0:T(8,128)(2,1)}, u32[]{:S(2)}) copy-start(bf16[31,1024]{1,0:T(8,128)(2,1)} %param.10) | copy-start | bytes 190468
  256.7 25.0 %copy-start.4 = (bf16[192,1024]{1,0:T(8,128)(2,1)S(1)}, bf16[192,1024]{1,0:T(8,128)(2,1)}, u32[]{:S(2)}) copy-start(bf16[192,1024]{1,0:T(8,128)(2,1)} %param.7) | copy-start | bytes 1179652
  261.2 30.7 %copy-start.7 = (bf16[192,2]{0,1:T(2,128)(2,1)S(1)}, bf16[192,2]{0,1:T(2,128)(2,1)}, u32[]{:S(2)}) copy-start(bf16[192,2]{0,1:T(2,128)(2,1)} %param.8) | copy-start | bytes 2308
  261.2 20.2 %all-to-all-start.2 = ((bf16[8,64,1024]{2,1,0:T(8,128)(2,1)}), bf16[8,64,1024]{2,1,0:T(8,128)(2,1)S(1)}, u32[]{:S(2)}, u32[]{:S(2)}) async-start(bf16[8,64,1024]{2,1,0:T(8,128)(2,1)} %bitcast.31), calls=%async_computation.2 | async-start | bytes 2097152 | tf_op jit(solution)/shard_map/all_to_all | solution.py:124
  282.1 10.4 %collective-permute-start.7 = (bf16[15,1024]{1,0:T(8,128)(2,1)S(1)}, bf16[15,1024]{1,0:T(8,128)(2,1)S(1)}, u32[]{:S(2)}, u32[]{:S(2)}) collective-permute-start(bf16[15,1024]{1,0:T(8,128)(2,1)S(1)} %get-tuple-element.7), channel_id=1, source_target_pairs={{0,1},{1,2},{2,3},{3,4},{4,5},{5,6},{6,7},{7,8},{8,9},{9,10},{10,1... | collective-permute-start | bytes 92168 | tf_op jit(solution)/shard_map/ppermute | solution.py:73
  284.0 9.4 %collective-permute-start.8 = (bf16[15,1024]{1,0:T(8,128)(2,1)S(1)}, bf16[15,1024]{1,0:T(8,128)(2,1)S(1)}, u32[]{:S(2)}, u32[]{:S(2)}) collective-permute-start(bf16[15,1024]{1,0:T(8,128)(2,1)S(1)} %get-tuple-element.8), channel_id=1, source_target_pairs={{1,0},{2,1},{3,2},{4,3},{5,4},{6,5},{7,6},{8,7},{9,8},{10,9},{11,1... | collective-permute-start | bytes 92168 | tf_op jit(solution)/shard_map/ppermute | solution.py:74
  293.6 9.8 %all-to-all-start.3 = ((bf16[4,32,1536]{2,1,0:T(8,128)(2,1)}), bf16[4,32,1536]{2,1,0:T(8,128)(2,1)S(1)}, u32[]{:S(2)}, u32[]{:S(2)}) async-start(bf16[4,32,1536]{2,1,0:T(8,128)(2,1)} %bitcast.155), calls=%async_computation.4 | async-start | bytes 786432 | tf_op jit(solution)/shard_map/all_to_all | solution.py:54
Sparse Core Ops, SparseCore 0:
  10.5 72.7 all-gather.4
  85.9 67.5 all-gather.6
  192.6 46.5 reduce-scatter.1

commit v2 on v1

--- a/solution.py
+++ b/solution.py
@@ -1,13 +1,16 @@
 import jax
 import jax.numpy as jnp
 from jax import lax
+from jax.experimental import pallas as pl
+from jax.experimental.pallas import tpu as pltpu
 from jax.sharding import Mesh, PartitionSpec as P
 
 BF = jnp.bfloat16
 F32 = jnp.float32
 SLOTS = 64
 SPARE = 60
-META = 16
+META = 8
+STEP = 4
 
 
 def dot(a, b, contract, batch=((), ())):
@@ -75,6 +78,75 @@
     return jnp.concatenate([low, block, high], axis=0)
 
 
+def rows_kernel(expert, x_ref, w_ref, wt_ref, r_ref, u_ref, q_ref, pre_ref, h_ref):
+    steps, rows, wide = x_ref.shape
+    frames, width = rows - META, wide // 2
+    part = h_ref.shape[1]
+    name = expert[0].astype(F32)
+    earlier = lax.broadcasted_iota(jnp.int32, (frames, frames), 0)
+    before = (earlier < lax.broadcasted_iota(jnp.int32, (frames, frames), 1)).astype(F32).astype(BF)
+    slot = lax.broadcasted_iota(jnp.int32, (SLOTS, frames), 0).astype(F32)
+    for j in range(steps):
+        meta = x_ref[j, frames:rows, :frames].astype(F32)
+        named = (meta == name).astype(F32)
+        chosen = named[0:1] + named[1:2]
+        ranks = dot(jnp.broadcast_to(chosen, (8, frames)).astype(BF), before, ((1,), (0,)))[0:1]
+        gate = named[0:1] * meta[2:3] + named[1:2] * meta[3:4]
+        here = jnp.where((slot == ranks) & (chosen > 0.0), 1.0, 0.0)
+        place = pl.ds(j * SLOTS, SLOTS)
+        u = dot(here.astype(BF), x_ref[j, :frames, :width], ((1,), (0,)))
+        u_ref[place] = u.astype(BF)
+        q = dot((here * gate).astype(BF), x_ref[j, :frames, width:], ((1,), (0,)))
+        q_ref[place] = q.astype(BF)
+    projected = dot(u_ref[...], w_ref[:, : 2 * part], ((1,), (0,)))
+    hidden_grad = dot(q_ref[...], w_ref[:, 2 * part :], ((1,), (0,)))
+    gate_in, up_in = projected[:, :part], projected[:, part:]
+    sigmoid = jax.nn.sigmoid(gate_in)
+    activated = gate_in * sigmoid
+    hidden = (activated * up_in).astype(BF)
+    h_ref[...] = hidden
+    pre_ref[:, :part] = (hidden_grad * up_in * (sigmoid * (1.0 + gate_in * (1.0 - sigmoid)))).astype(BF)
+    pre_ref[:, part:] = (hidden_grad * activated).astype(BF)
+    gate_part = jnp.sum(hidden.astype(F32) * hidden_grad, axis=1, keepdims=True)
+    r_ref[...] = dot(pre_ref[...], wt_ref[...], ((1,), (0,))).astype(BF)
+    row = lax.broadcasted_iota(jnp.int32, (SLOTS, 128), 0)
+    lane = lax.broadcasted_iota(jnp.int32, (SLOTS, 128), 1)
+    for j in range(steps):
+        place = pl.ds(j * SLOTS, SLOTS)
+        diagonal = jnp.where(row == lane, gate_part[j * SLOTS : (j + 1) * SLOTS], 0.0)
+        line = jnp.sum(diagonal, axis=0, keepdims=True)
+        r_ref[place, :128] = jnp.where(row == SPARE, line, r_ref[place, :128].astype(F32)).astype(BF)
+
+
+def expert_rows(expert, everything, weights):
+    blocks, rows, wide = everything.shape
+    width, part = wide // 2, weights.shape[1] // 3
+    turned = weights[:, : 2 * part].T
+    rows_step = STEP * SLOTS
+    total = blocks * SLOTS
+
+    def rowwise(columns):
+        return pl.BlockSpec((rows_step, columns), lambda i: (i, 0))
+
+    def whole(array):
+        return pl.BlockSpec(array.shape, lambda i: (0, 0))
+
+    widths = (width, width, width, 2 * part, part)
+    return pl.pallas_call(
+        rows_kernel,
+        grid=(blocks // STEP,),
+        in_specs=[
+            pl.BlockSpec(memory_space=pltpu.SMEM),
+            pl.BlockSpec((STEP, rows, wide), lambda i: (i, 0, 0)),
+            whole(weights),
+            whole(turned),
+        ],
+        out_specs=[rowwise(columns) for columns in widths],
+        out_shape=[jax.ShapeDtypeStruct((total, columns), BF) for columns in widths],
+        compiler_params=pltpu.CompilerParams(vmem_limit_bytes=52 * 1024 * 1024),
+    )(expert.reshape(1).astype(jnp.int32), everything, weights, turned)
+
+
 def local(block_in, out_grad, gate_values, expert_ids, conv_kernel, expert_weights):
     frames, width = block_in.shape
     ny, experts = lax.axis_size("y"), lax.axis_size("x") * lax.axis_size("c")
@@ -82,42 +154,11 @@
     expert = lax.axis_index("x") * lax.axis_size("c") + lax.axis_index("c")
 
     meta = jnp.concatenate([expert_ids.astype(BF).T, gate_values.T], axis=0)
-    meta = jnp.pad(meta, ((0, META - 4), (0, width - frames)))
-    packed = jnp.concatenate([block_in, meta], axis=0)
-    all_in = lax.all_gather(packed, group, axis=0, tiled=False)
-    all_grad = lax.all_gather(out_grad, group, axis=0, tiled=False)
-    blocks = all_in.shape[0]
+    meta = jnp.pad(meta, ((0, META - 4), (0, 2 * width - frames)))
+    packed = jnp.concatenate([jnp.concatenate([block_in, out_grad], axis=1), meta], axis=0)
+    everything = lax.all_gather(packed, group, axis=0, tiled=False)
     weights = gather_weights(expert_weights)
-    part = weights.shape[1] // 3
-    in_weights, down_weights = weights[:, : 2 * part], weights[:, 2 * part :]
-
-    ids = all_in[:, frames : frames + 2, :frames].astype(jnp.int32) == expert
-    gates = all_in[:, frames + 2 : frames + 4, :frames]
-    gate = jnp.where(ids[:, 0], gates[:, 0], gates[:, 1])
-    chosen = slots_of(ids[:, 0] | ids[:, 1])
-    placing = chosen.astype(BF)
-    placing_gate = jnp.where(chosen, gate[:, None, :], jnp.zeros((), BF))
-
-    rows_in = dot(placing, all_in[:, :frames], ((2,), (1,)), ((0,), (0,))).astype(BF)
-    rows_in = rows_in.reshape(blocks * SLOTS, width)
-    projected = dot(rows_in, in_weights, ((1,), (0,)))
-    gate_in, up_in = projected[:, :part], projected[:, part:]
-    sigmoid = jax.nn.sigmoid(gate_in)
-    activated = gate_in * sigmoid
-    derivative = sigmoid * (1.0 + gate_in * (1.0 - sigmoid))
-    hidden = (activated * up_in).astype(BF)
-
-    rows_q = dot(placing_gate, all_grad, ((2,), (1,)), ((0,), (0,))).astype(BF)
-    rows_q = rows_q.reshape(blocks * SLOTS, width)
-    hidden_grad = dot(rows_q, down_weights, ((1,), (0,)))
-    gate_part = jnp.sum(hidden.astype(F32) * hidden_grad, axis=1).reshape(blocks, 1, SLOTS)
-    pre_grads = jnp.concatenate(
-        [(hidden_grad * up_in * derivative).astype(BF), (hidden_grad * activated).astype(BF)], axis=1
-    )
-    row_grad = dot(pre_grads, in_weights, ((1,), (1,))).reshape(blocks, SLOTS, width)
-    gate_rows = jnp.pad(gate_part, ((0, 0), (0, 0), (0, width - SLOTS)))
-    spare = (jnp.arange(SLOTS) == SPARE)[None, :, None]
-    row_grad = jnp.where(spare, gate_rows, row_grad).astype(BF)
+    row_grad, rows_in, rows_q, pre_grads, hidden = expert_rows(expert, everything, weights)
 
     parts = lax.all_to_all(row_grad.reshape(ny, experts * SLOTS, width), "y", 0, 0, tiled=True)
     summed = jnp.sum(parts.astype(F32), axis=0).astype(BF)

time: 314 us -> 265 us (0.84)
  matrix products: 47.2 us -> 11.3 us
  waiting for transfers between devices: 122 us -> 93.4 us
  Pallas kernels: 0 us -> 27.1 us
  local copies, waits for them, and re-layouts: 24 us -> 13.2 us
    dot_general x10 -> x4, matrix products: 47 us -> 11.1 us  [dot(): return lax.dot_general(a, b, (contract, batch), preferred_element_type=F32)]
    pallas_call x0 -> x1, Pallas kernels: none -> 27.1 us  [expert_rows(): pl.pallas_call(rows_kernel, grid=(blocks // STEP,), in_specs=[pl.BlockSpe...]
    all_gather x2 -> x1, waiting for transfers between devices: 65.3 us -> 40 us  [local(): everything = lax.all_gather(packed, group, axis=0, tiled=False)]
    dot_general x2 -> x0, local copies, waits for them, and re-layouts: 13.2 us -> none  [dot(): return lax.dot_general(a, b, (contract, batch), preferred_element_type=F32)]
    ppermute x3, waiting for transfers between devices: 12.5 us -> 0.01 us  [ring_gather(): left = lax.ppermute(left, axis, down)]
    ppermute x4, waiting for transfers between devices: 18.4 us -> 28.8 us  [ring_gather(): right = lax.ppermute(right, axis, up)]
  transfers between devices with their start and end apart: 15 -> 14, of which waited for: 10 -> 9; matrix products, arithmetic and copies ran while one was open for 13% -> 7% of each run, Pallas kernels for 0% -> 0%
where the time goes in v2:
time: 265 us; the launch traced here: 263 us
  waiting for transfers between devices  93.4 us (35%)
  blocking collectives  54.9 us (21%)
  starting transfers between devices  36 us (14%)
  Pallas kernels  27.1 us (10%)
  between operations  14.3 us (5%)
  local copies, waits for them, and re-layouts  13.2 us (5%)
  other arithmetic  12.7 us (5%)
  matrix products  11.3 us (4%)
    all_to_all x1, blocking collectives, local(): lax.all_to_all(row_grad.reshape(ny, experts * SLOTS, width), 'y', 0, 0, t...  54.9 us
    all_gather x1, waiting for transfers between devices, local(): everything = lax.all_gather(packed, group, axis=0, tiled=False)  40 us
    ppermute x4, waiting for transfers between devices, ring_gather(): right = lax.ppermute(right, axis, up)  28.8 us
    pallas_call x1, Pallas kernels, expert_rows(): pl.pallas_call(rows_kernel, grid=(blocks // STEP,), in_specs=[pl.BlockSpe...  27.1 us
    all_to_all x1, waiting for transfers between devices, local(): lax.all_to_all(summed.reshape(experts, SLOTS, width), ('x', 'c'), 0, 0, t...  15.7 us
    dot_general x4, matrix products, dot(): return lax.dot_general(a, b, (contract, batch), preferred_element_type=F32)  11.1 us
    ppermute x3, starting transfers between devices, ring_gather(): left = lax.ppermute(left, axis, down)  10.4 us
    ppermute x1, starting transfers between devices, with_halo(): high = lax.ppermute(block[:width], axes, backward)  7.86 us
  transfers between devices with their start and end apart: 14, of which 9 were waited for; matrix products, arithmetic and copies ran while one was open for 7% of the time, Pallas kernels for 0%

profile of v2, /device:TPU:8, one launch (start us, length us, event | category | flops | bytes accessed | tf_op | source)
XLA Modules:
  0.0 262.9 jit_solution(1929578170220102648)
XLA Ops:
  7.2 0.0 all-gather.3.cloned.1.call-start
  7.2 0.7 convert_bitcast_fusion
  7.9 0.7 fusion.46
  8.6 2.1 pad_maximum_fusion.1
  10.7 0.0 all-gather.3.cloned.1.call-update
  10.7 1.3 reshape_squeeze.3
  12.0 0.2 copy.58
  12.2 1.3 reshape.44
  13.5 5.6 %all-to-all-start = ((bf16[4,32,1536]{2,1,0:T(8,128)(2,1)}), bf16[4,32,1536]{2,1,0:T(8,128)(2,1)S(1)}, u32[]{:S(2)}, u32[]{:S(2)}) async-start(bf16[4,32,1536]{2,1,0:T(8,128)(2,1)} %reshape.44), calls=%async_computation | async-start | bytes 786432 | tf_op jit(solution)/shard_map/all_to_all | solution.py:42
  19.1 0.0 reduce-scatter.2.cloned.1.call-start
  19.1 5.9 %all-to-all-done = bf16[4,32,1536]{2,1,0:T(8,128)(2,1)S(1)} async-done(((bf16[4,32,1536]{2,1,0:T(8,128)(2,1)}), bf16[4,32,1536]{2,1,0:T(8,128)(2,1)S(1)}, u32[]{:S(2)}, u32[]{:S(2)}) %all-to-all-start) | async-done | bytes 393248 | tf_op jit(solution)/shard_map/all_to_all | solution.py:42
  25.0 1.9 collective-permute-start
  26.9 3.9 %collective-permute-start.1 = (bf16[4,32,1536]{2,1,0:T(8,128)(2,1)S(1)}, bf16[4,32,1536]{2,1,0:T(8,128)(2,1)S(1)}, u32[]{:S(2)}, u32[]{:S(2)}) collective-permute-start(bf16[4,32,1536]{2,1,0:T(8,128)(2,1)S(1)} %all-to-all-done), channel_id=1, source_target_pairs={{8,0},{16,8},{24,16},{32,24},{40,32},{48,40},{56,48},{0,56},{9,1},... | collective-permute-start | bytes 1179656 | tf_op jit(solution)/shard_map/ppermute | solution.py:31
  30.9 0.3 broadcast_in_dim.33
  31.3 7.2 %collective-permute-done = bf16[4,32,1536]{2,1,0:T(8,128)(2,1)S(1)} collective-permute-done((bf16[4,32,1536]{2,1,0:T(8,128)(2,1)S(1)}, bf16[4,32,1536]{2,1,0:T(8,128)(2,1)S(1)}, u32[]{:S(2)}, u32[]{:S(2)}) %collective-permute-start) | collective-permute-done | bytes 393248 | tf_op jit(solution)/shard_map/ppermute | solution.py:28
  38.5 0.0 collective-permute-start.2
  38.5 0.0 collective-permute-done.1
  38.5 3.2 %collective-permute-start.3 = (bf16[4,32,1536]{2,1,0:T(8,128)(2,1)S(1)}, bf16[4,32,1536]{2,1,0:T(8,128)(2,1)S(1)}, u32[]{:S(2)}, u32[]{:S(2)}) collective-permute-start(bf16[4,32,1536]{2,1,0:T(8,128)(2,1)S(1)} %collective-permute-done.1), channel_id=1, source_target_pairs={{8,0},{16,8},{24,16},{32,24},{40,32},{48,40},{56,48},{0,56},{9,1},... | collective-permute-start | bytes 1179656 | tf_op jit(solution)/shard_map/ppermute | solution.py:31
  41.8 6.7 %collective-permute-done.2 = bf16[4,32,1536]{2,1,0:T(8,128)(2,1)S(1)} collective-permute-done((bf16[4,32,1536]{2,1,0:T(8,128)(2,1)S(1)}, bf16[4,32,1536]{2,1,0:T(8,128)(2,1)S(1)}, u32[]{:S(2)}, u32[]{:S(2)}) %collective-permute-start.2) | collective-permute-done | bytes 393248 | tf_op jit(solution)/shard_map/ppermute | solution.py:28
  48.6 0.0 collective-permute-start.4
  48.6 0.0 collective-permute-done.3
  48.6 3.2 %collective-permute-start.5 = (bf16[4,32,1536]{2,1,0:T(8,128)(2,1)S(1)}, bf16[4,32,1536]{2,1,0:T(8,128)(2,1)S(1)}, u32[]{:S(2)}, u32[]{:S(2)}) collective-permute-start(bf16[4,32,1536]{2,1,0:T(8,128)(2,1)S(1)} %collective-permute-done.3), channel_id=1, source_target_pairs={{8,0},{16,8},{24,16},{32,24},{40,32},{48,40},{56,48},{0,56},{9,1},... | collective-permute-start | bytes 1179656 | tf_op jit(solution)/shard_map/ppermute | solution.py:31
  51.9 6.0 %collective-permute-done.4 = bf16[4,32,1536]{2,1,0:T(8,128)(2,1)S(1)} collective-permute-done((bf16[4,32,1536]{2,1,0:T(8,128)(2,1)S(1)}, bf16[4,32,1536]{2,1,0:T(8,128)(2,1)S(1)}, u32[]{:S(2)}, u32[]{:S(2)}) %collective-permute-start.4) | collective-permute-done | bytes 393248 | tf_op jit(solution)/shard_map/ppermute | solution.py:28
  57.8 0.0 collective-permute-start.6
  57.9 0.0 collective-permute-done.5
  57.9 8.9 %collective-permute-done.6 = bf16[4,32,1536]{2,1,0:T(8,128)(2,1)S(1)} collective-permute-done((bf16[4,32,1536]{2,1,0:T(8,128)(2,1)S(1)}, bf16[4,32,1536]{2,1,0:T(8,128)(2,1)S(1)}, u32[]{:S(2)}, u32[]{:S(2)}) %collective-permute-start.6) | collective-permute-done | bytes 393248 | tf_op jit(solution)/shard_map/ppermute | solution.py:28
  66.9 0.0 copy-start
  66.9 1.9 slice.274
  68.7 4.2 %copy.53 = bf16[1024,1024]{0,1:T(8,128)(2,1)} copy(bf16[1024,1024]{1,0:T(8,128)(2,1)} %slice.274) | data formatting | bytes 4194304
  72.9 40.0 %all-gather.3.cloned.1.call-done = bf16[6400,2048]{1,0:T(8,128)(2,1)} async-done(((bf16[200,2048]{1,0:T(8,128)(2,1)}), bf16[6400,2048]{1,0:T(8,128)(2,1)}) %all-gather.3.cloned.1.call-update) | async-done | bytes 26214416 | tf_op jit(solution)/shard_map/all_gather | solution.py:159
  112.9 27.1 %shard_map.85 = (bf16[2048,1024]{1,0:T(8,128)(2,1)}, bf16[2048,1024]{1,0:T(8,128)(2,1)}, bf16[2048,1024]{1,0:T(8,128)(2,1)}, bf16[2048,1024]{1,0:T(8,128)(2,1)}, bf16[2048,512]{1,0:T(8,128)(2,1)}) custom-call(s32[1]{0:T(128)} %bitcast.4.expert, bf16[32,200,2048]{2,1,0:T(8,128)(2,1)} %bitcast.107, bf16[1024,1536]{1,0:T(8,128)(2,1)} %bitcast.109, ...), custom_call_target="tpu_custom_call" | custom-call | tf_op jit(solution)/shard_map/pallas_call | solution.py:135
  139.9 0.0 copy-start.5
  139.9 0.0 copy-start.6
  140.0 8.2 %convolution_convert_fusion = bf16[1024,1024]{1,0:T(8,128)(2,1)S(1)} fusion(bf16[2048,1024]{1,0:T(8,128)(2,1)} %get-tuple-element.9, bf16[2048,1024]{1,0:T(8,128)(2,1)} %get-tuple-element.10), kind=kOutput, calls=%fused_computation.1 | convolution fusion | flops 4296015872 | bytes 10485760 | tf_op jit(solution)/shard_map/dot_general | solution.py:17
  148.1 0.0 copy-done.5
  148.2 0.0 copy-done.6
  148.2 2.4 convolution_convert_fusion.1
  150.5 0.3 pad_maximum_fusion
  150.8 2.0 copy.51
  152.9 0.0 reduce-scatter.2.cloned.1.call-update
  152.9 54.9 %all_to_all.20 = bf16[4,512,1024]{2,1,0:T(8,128)(2,1)} all-to-all(bf16[4,512,1024]{2,1,0:T(8,128)(2,1)} %bitcast.112), channel_id=1, replica_groups=mesh['y'=4,'z'=8,'x'=4,'c'=2] {'y'}, dimensions={0} | all-to-all | bytes 8388608 | tf_op jit(solution)/shard_map/all_to_all | solution.py:163
  207.8 4.5 %reduce_sum.12 = bf16[512,1024]{1,0:T(8,128)(2,1)} reduce(bf16[4,512,1024]{2,1,0:T(8,128)(2,1)} %all_to_all.20, bf16[]{:T(256)} %constant.59.clone.1), dimensions={0}, to_apply=%region_0.1 | reduce | flops 1572864 | bytes 5242882 | tf_op jit(solution)/shard_map/reduce_sum | solution.py:164
  212.3 4.4 %all-to-all-start.2 = ((bf16[8,64,1024]{2,1,0:T(8,128)(2,1)}), bf16[8,64,1024]{2,1,0:T(8,128)(2,1)S(1)}, u32[]{:S(2)}, u32[]{:S(2)}) async-start(bf16[8,64,1024]{2,1,0:T(8,128)(2,1)} %bitcast.28), calls=%async_computation.2 | async-start | bytes 2097152 | tf_op jit(solution)/shard_map/all_to_all | solution.py:165
  216.7 0.1 convolution_convert_fusion.2
  216.8 0.0 copy-done.2
  216.9 0.1 fusion.50
  216.9 15.7 %all-to-all-done.2 = bf16[8,64,1024]{2,1,0:T(8,128)(2,1)S(1)} async-done(((bf16[8,64,1024]{2,1,0:T(8,128)(2,1)}), bf16[8,64,1024]{2,1,0:T(8,128)(2,1)S(1)}, u32[]{:S(2)}, u32[]{:S(2)}) %all-to-all-start.2) | async-done | bytes 1048608 | tf_op jit(solution)/shard_map/all_to_all | solution.py:165
  232.6 0.0 copy-done.1
  232.6 0.4 fusion.52
  233.1 1.9 collective-permute-start.7
  235.0 7.9 %collective-permute-start.8 = (bf16[15,1024]{1,0:T(8,128)(2,1)S(1)}, bf16[15,1024]{1,0:T(8,128)(2,1)S(1)}, u32[]{:S(2)}, u32[]{:S(2)}) collective-permute-start(bf16[15,1024]{1,0:T(8,128)(2,1)S(1)} %get-tuple-element.14), channel_id=1, source_target_pairs={{1,0},{2,1},{3,2},{4,3},{5,4},{6,5},{7,6},{8,7},{9,8},{10,9},{11,1... | collective-permute-start | bytes 92168 | tf_op jit(solution)/shard_map/ppermute | solution.py:77
  242.9 0.2 fusion.34
  243.1 0.0 copy-done.4
  243.1 0.6 fusion.48
  243.7 0.0 collective-permute-done.7
  243.7 0.7 collective-permute-done.8
  244.4 0.1 maximum_convert_fusion
  244.6 0.0 reduce-scatter.2.cloned.1.call-done
  244.6 3.9 %all-to-all-start.3 = ((bf16[4,32,1536]{2,1,0:T(8,128)(2,1)}), bf16[4,32,1536]{2,1,0:T(8,128)(2,1)S(1)}, u32[]{:S(2)}, u32[]{:S(2)}) async-start(bf16[4,32,1536]{2,1,0:T(8,128)(2,1)} %bitcast.117), calls=%async_computation.4 | async-start | bytes 786432 | tf_op jit(solution)/shard_map/all_to_all | solution.py:57
  248.5 3.7 %fusion.3 = bf16[192,1024]{1,0:T(8,128)(2,1)} fusion(f32[192,1024]{1,0:T(8,128)S(1)} %get-tuple-element.47, f32[222,1024]{1,0:T(8,128)S(1)} %maximum_convert_fusion, f32[1024]{0:T(1024)S(1)} %bitcast.132, f32[1024]{0:T(1024)S(1)} %bitcast.131, f32[1024]{0:T(1024)S(1)} %bitcast.130, f32[1024]{0:T(1024)S(1)} %bitcast.129, f32[1024]{0:T(1024)S(1)} %bitcast.128, ...), kind=kLoop, calls=%fused_computation.10 | loop fusion | flops 12386304 | bytes 25686016 | tf_op jit(solution)/shard_map/convert_element_type | solution.py:195
  252.2 2.2 all-to-all-done.3
  254.4 0.3 reshape.50
  254.7 0.4 copy.42
  255.1 1.0 reshape.51
  (20 shorter events, 0.4 us)
Async XLA Ops:
  7.2 105.7 %all-gather.3.cloned.1.call-start = ((), (), s32[]{:S(2)}) async-start(), calls=%async_computation.6 | async-start | bytes 27033600 | tf_op jit(solution)/shard_map/all_gather | solution.py:159
  13.5 11.5 %all-to-all-start = ((bf16[4,32,1536]{2,1,0:T(8,128)(2,1)}), bf16[4,32,1536]{2,1,0:T(8,128)(2,1)S(1)}, u32[]{:S(2)}, u32[]{:S(2)}) async-start(bf16[4,32,1536]{2,1,0:T(8,128)(2,1)} %reshape.44), calls=%async_computation | async-start | bytes 786432 | tf_op jit(solution)/shard_map/all_to_all | solution.py:42
  19.1 225.5 %reduce-scatter.2.cloned.1.call-start = ((), (), s32[]{:S(2)}) async-start(), calls=%async_computation.5 | async-start | bytes 3538944 | tf_op jit(solution)/shard_map/reduce_scatter | solution.py:56
  25.0 13.5 %collective-permute-start = (bf16[4,32,1536]{2,1,0:T(8,128)(2,1)S(1)}, bf16[4,32,1536]{2,1,0:T(8,128)(2,1)S(1)}, u32[]{:S(2)}, u32[]{:S(2)}) collective-permute-start(bf16[4,32,1536]{2,1,0:T(8,128)(2,1)S(1)} %all-to-all-done), channel_id=1, source_target_pairs={{0,8},{8,16},{16,24},{24,32},{32,40},{40,48},{48,56},{56,0},{1,9},... | collective-permute-start | bytes 1179656 | tf_op jit(solution)/shard_map/ppermute | solution.py:28
  26.9 11.6 %collective-permute-start.1 = (bf16[4,32,1536]{2,1,0:T(8,128)(2,1)S(1)}, bf16[4,32,1536]{2,1,0:T(8,128)(2,1)S(1)}, u32[]{:S(2)}, u32[]{:S(2)}) collective-permute-start(bf16[4,32,1536]{2,1,0:T(8,128)(2,1)S(1)} %all-to-all-done), channel_id=1, source_target_pairs={{8,0},{16,8},{24,16},{32,24},{40,32},{48,40},{56,48},{0,56},{9,1},... | collective-permute-start | bytes 1179656 | tf_op jit(solution)/shard_map/ppermute | solution.py:31
  38.5 10.0 %collective-permute-start.2 = (bf16[4,32,1536]{2,1,0:T(8,128)(2,1)S(1)}, bf16[4,32,1536]{2,1,0:T(8,128)(2,1)S(1)}, u32[]{:S(2)}, u32[]{:S(2)}) collective-permute-start(bf16[4,32,1536]{2,1,0:T(8,128)(2,1)S(1)} %collective-permute-done), channel_id=1, source_target_pairs={{0,8},{8,16},{16,24},{24,32},{32,40},{40,48},{48,56},{56,0},{1,9},... | collective-permute-start | bytes 1179656 | tf_op jit(solution)/shard_map/ppermute | solution.py:28
  38.5 10.0 %collective-permute-start.3 = (bf16[4,32,1536]{2,1,0:T(8,128)(2,1)S(1)}, bf16[4,32,1536]{2,1,0:T(8,128)(2,1)S(1)}, u32[]{:S(2)}, u32[]{:S(2)}) collective-permute-start(bf16[4,32,1536]{2,1,0:T(8,128)(2,1)S(1)} %collective-permute-done.1), channel_id=1, source_target_pairs={{8,0},{16,8},{24,16},{32,24},{40,32},{48,40},{56,48},{0,56},{9,1},... | collective-permute-start | bytes 1179656 | tf_op jit(solution)/shard_map/ppermute | solution.py:31
  48.6 9.3 %collective-permute-start.4 = (bf16[4,32,1536]{2,1,0:T(8,128)(2,1)S(1)}, bf16[4,32,1536]{2,1,0:T(8,128)(2,1)S(1)}, u32[]{:S(2)}, u32[]{:S(2)}) collective-permute-start(bf16[4,32,1536]{2,1,0:T(8,128)(2,1)S(1)} %collective-permute-done.2), channel_id=1, source_target_pairs={{0,8},{8,16},{16,24},{24,32},{32,40},{40,48},{48,56},{56,0},{1,9},... | collective-permute-start | bytes 1179656 | tf_op jit(solution)/shard_map/ppermute | solution.py:28
  48.6 9.3 %collective-permute-start.5 = (bf16[4,32,1536]{2,1,0:T(8,128)(2,1)S(1)}, bf16[4,32,1536]{2,1,0:T(8,128)(2,1)S(1)}, u32[]{:S(2)}, u32[]{:S(2)}) collective-permute-start(bf16[4,32,1536]{2,1,0:T(8,128)(2,1)S(1)} %collective-permute-done.3), channel_id=1, source_target_pairs={{8,0},{16,8},{24,16},{32,24},{40,32},{48,40},{56,48},{0,56},{9,1},... | collective-permute-start | bytes 1179656 | tf_op jit(solution)/shard_map/ppermute | solution.py:31
  57.8 9.0 %collective-permute-start.6 = (bf16[4,32,1536]{2,1,0:T(8,128)(2,1)S(1)}, bf16[4,32,1536]{2,1,0:T(8,128)(2,1)S(1)}, u32[]{:S(2)}, u32[]{:S(2)}) collective-permute-start(bf16[4,32,1536]{2,1,0:T(8,128)(2,1)S(1)} %collective-permute-done.4), channel_id=1, source_target_pairs={{0,8},{8,16},{16,24},{24,32},{32,40},{40,48},{48,56},{56,0},{1,9},... | collective-permute-start | bytes 1179656 | tf_op jit(solution)/shard_map/ppermute | solution.py:28
  66.9 6.0 %copy-start = (bf16[4,8,32,1536]{3,2,1,0:T(8,128)(2,1)}, bf16[4,8,32,1536]{3,2,1,0:T(8,128)(2,1)S(1)}, u32[]{:S(2)}) copy-start(bf16[4,8,32,1536]{3,2,1,0:T(8,128)(2,1)S(1)} %bitcast_dynamic-update-slice_fusion) | copy-start | bytes 9437188
  139.9 8.2 %copy-start.5 = (bf16[2048,1024]{1,0:T(8,128)(2,1)S(1)}, bf16[2048,1024]{1,0:T(8,128)(2,1)}, u32[]{:S(2)}) copy-start(bf16[2048,1024]{1,0:T(8,128)(2,1)} %get-tuple-element.11) | copy-start | bytes 12582916
  139.9 8.2 %copy-start.6 = (bf16[2048,512]{1,0:T(8,128)(2,1)S(1)}, bf16[2048,512]{1,0:T(8,128)(2,1)}, u32[]{:S(2)}) copy-start(bf16[2048,512]{1,0:T(8,128)(2,1)} %get-tuple-element.12) | copy-start | bytes 6291460
  207.8 8.9 %copy-start.3 = (s32[192,2]{0,1:T(2,128)S(1)}, s32[192,2]{0,1:T(2,128)}, u32[]{:S(2)}) copy-start(s32[192,2]{0,1:T(2,128)} %param.9) | copy-start | bytes 4612
  207.8 9.1 %copy-start.2 = (bf16[31,1024]{1,0:T(8,128)(2,1)S(1)}, bf16[31,1024]{1,0:T(8,128)(2,1)}, u32[]{:S(2)}) copy-start(bf16[31,1024]{1,0:T(8,128)(2,1)} %param.10) | copy-start | bytes 190468
  207.8 24.9 %copy-start.1 = (bf16[192,1024]{1,0:T(8,128)(2,1)S(1)}, bf16[192,1024]{1,0:T(8,128)(2,1)}, u32[]{:S(2)}) copy-start(bf16[192,1024]{1,0:T(8,128)(2,1)} %param.7) | copy-start | bytes 1179652
  212.3 30.8 %copy-start.4 = (bf16[192,2]{0,1:T(2,128)(2,1)S(1)}, bf16[192,2]{0,1:T(2,128)(2,1)}, u32[]{:S(2)}) copy-start(bf16[192,2]{0,1:T(2,128)(2,1)} %param.8) | copy-start | bytes 2308
  212.3 20.3 %all-to-all-start.2 = ((bf16[8,64,1024]{2,1,0:T(8,128)(2,1)}), bf16[8,64,1024]{2,1,0:T(8,128)(2,1)S(1)}, u32[]{:S(2)}, u32[]{:S(2)}) async-start(bf16[8,64,1024]{2,1,0:T(8,128)(2,1)} %bitcast.28), calls=%async_computation.2 | async-start | bytes 2097152 | tf_op jit(solution)/shard_map/all_to_all | solution.py:165
  233.1 10.6 %collective-permute-start.7 = (bf16[15,1024]{1,0:T(8,128)(2,1)S(1)}, bf16[15,1024]{1,0:T(8,128)(2,1)S(1)}, u32[]{:S(2)}, u32[]{:S(2)}) collective-permute-start(bf16[15,1024]{1,0:T(8,128)(2,1)S(1)} %get-tuple-element.13), channel_id=1, source_target_pairs={{0,1},{1,2},{2,3},{3,4},{4,5},{5,6},{6,7},{7,8},{8,9},{9,10},{10,1... | collective-permute-start | bytes 92168 | tf_op jit(solution)/shard_map/ppermute | solution.py:76
  235.0 9.4 %collective-permute-start.8 = (bf16[15,1024]{1,0:T(8,128)(2,1)S(1)}, bf16[15,1024]{1,0:T(8,128)(2,1)S(1)}, u32[]{:S(2)}, u32[]{:S(2)}) collective-permute-start(bf16[15,1024]{1,0:T(8,128)(2,1)S(1)} %get-tuple-element.14), channel_id=1, source_target_pairs={{1,0},{2,1},{3,2},{4,3},{5,4},{6,5},{7,6},{8,7},{9,8},{10,9},{11,1... | collective-permute-start | bytes 92168 | tf_op jit(solution)/shard_map/ppermute | solution.py:77
  244.6 9.8 %all-to-all-start.3 = ((bf16[4,32,1536]{2,1,0:T(8,128)(2,1)}), bf16[4,32,1536]{2,1,0:T(8,128)(2,1)S(1)}, u32[]{:S(2)}, u32[]{:S(2)}) async-start(bf16[4,32,1536]{2,1,0:T(8,128)(2,1)} %bitcast.117), calls=%async_computation.4 | async-start | bytes 786432 | tf_op jit(solution)/shard_map/all_to_all | solution.py:57
Sparse Core Ops, SparseCore 0:
  10.8 101.9 all-gather.2
  153.0 46.5 reduce-scatter.1

commit v3 on v2

--- a/solution.py
+++ b/solution.py
@@ -78,11 +78,12 @@
     return jnp.concatenate([low, block, high], axis=0)
 
 
-def rows_kernel(expert, x_ref, w_ref, wt_ref, r_ref, u_ref, q_ref, pre_ref, h_ref):
+def rows_kernel(info, x_ref, w_ref, wt_ref, *refs):
+    low_ref, high_ref, u_ref, q_ref, pre_ref, h_ref = refs[-6:]
     steps, rows, wide = x_ref.shape
     frames, width = rows - META, wide // 2
-    part = h_ref.shape[1]
-    name = expert[0].astype(F32)
+    part, half = h_ref.shape[1], low_ref.shape[1]
+    name = info[0].astype(F32)
     earlier = lax.broadcasted_iota(jnp.int32, (frames, frames), 0)
     before = (earlier < lax.broadcasted_iota(jnp.int32, (frames, frames), 1)).astype(F32).astype(BF)
     slot = lax.broadcasted_iota(jnp.int32, (SLOTS, frames), 0).astype(F32)
@@ -108,43 +109,85 @@
     pre_ref[:, :part] = (hidden_grad * up_in * (sigmoid * (1.0 + gate_in * (1.0 - sigmoid)))).astype(BF)
     pre_ref[:, part:] = (hidden_grad * activated).astype(BF)
     gate_part = jnp.sum(hidden.astype(F32) * hidden_grad, axis=1, keepdims=True)
-    r_ref[...] = dot(pre_ref[...], wt_ref[...], ((1,), (0,))).astype(BF)
+    row_grad = dot(pre_ref[...], wt_ref[...], ((1,), (0,))).astype(BF)
+    low_ref[...] = row_grad[:, :half]
+    high_ref[...] = row_grad[:, half:]
     row = lax.broadcasted_iota(jnp.int32, (SLOTS, 128), 0)
     lane = lax.broadcasted_iota(jnp.int32, (SLOTS, 128), 1)
     for j in range(steps):
         place = pl.ds(j * SLOTS, SLOTS)
         diagonal = jnp.where(row == lane, gate_part[j * SLOTS : (j + 1) * SLOTS], 0.0)
         line = jnp.sum(diagonal, axis=0, keepdims=True)
-        r_ref[place, :128] = jnp.where(row == SPARE, line, r_ref[place, :128].astype(F32)).astype(BF)
-
-
-def expert_rows(expert, everything, weights):
+        low_ref[place, :128] = jnp.where(row == SPARE, line, low_ref[place, :128].astype(F32)).astype(BF)
+
+
+def expert_rows(expert, group, turn, everything, weights, turned, kept):
     blocks, rows, wide = everything.shape
+    groups = lax.axis_size("y")
     width, part = wide // 2, weights.shape[1] // 3
-    turned = weights[:, : 2 * part].T
     rows_step = STEP * SLOTS
-    total = blocks * SLOTS
-
-    def rowwise(columns):
-        return pl.BlockSpec((rows_step, columns), lambda i: (i, 0))
+    steps = blocks // (groups * STEP)
+    total, mine = blocks * SLOTS, blocks * SLOTS // groups
+    info = jnp.stack([expert, group * steps]).astype(jnp.int32)
+
+    def rowwise(columns, first):
+        return pl.BlockSpec((rows_step, columns), lambda i, info: (i + first, 0))
 
     def whole(array):
-        return pl.BlockSpec(array.shape, lambda i: (0, 0))
-
-    widths = (width, width, width, 2 * part, part)
-    return pl.pallas_call(
+        return pl.BlockSpec(array.shape, lambda i, info: (0, 0))
+
+    widths = (width, width, 2 * part, part)
+    shapes = [jax.ShapeDtypeStruct((mine, width // 2), BF)] * 2
+    shapes += [jax.ShapeDtypeStruct((total, columns), BF) for columns in widths]
+    low, high, *kept = pl.pallas_call(
         rows_kernel,
-        grid=(blocks // STEP,),
-        in_specs=[
-            pl.BlockSpec(memory_space=pltpu.SMEM),
-            pl.BlockSpec((STEP, rows, wide), lambda i: (i, 0, 0)),
-            whole(weights),
-            whole(turned),
-        ],
-        out_specs=[rowwise(columns) for columns in widths],
-        out_shape=[jax.ShapeDtypeStruct((total, columns), BF) for columns in widths],
+        grid_spec=pltpu.PrefetchScalarGridSpec(
+            num_scalar_prefetch=1,
+            grid=(steps,),
+            in_specs=[
+                pl.BlockSpec((STEP, rows, wide), lambda i, info: (info[1] + i, 0, 0)),
+                whole(weights),
+                whole(turned),
+            ]
+            + [pl.BlockSpec(memory_space=pl.ANY) for _ in kept],
+            out_specs=[rowwise(width // 2, 0)] * 2 + [rowwise(columns, turn * steps) for columns in widths],
+        ),
+        out_shape=shapes,
+        input_output_aliases={4 + k: 2 + k for k in range(len(kept))},
         compiler_params=pltpu.CompilerParams(vmem_limit_bytes=52 * 1024 * 1024),
-    )(expert.reshape(1).astype(jnp.int32), everything, weights, turned)
+    )(info, everything, weights, turned, *kept)
+    return low, high, kept
+
+
+def add(*parts):
+    return sum(part.astype(F32) for part in parts)
+
+
+def rows_backward(expert, everything, weights):
+    ny = lax.axis_size("y")
+    me = lax.axis_index("y")
+    up = [(i, (i + 1) % ny) for i in range(ny)]
+    down = [(target, source) for source, target in up]
+    turned = weights[:, : 2 * (weights.shape[1] // 3)].T
+
+    def send(rows, way):
+        return lax.ppermute(rows, "y", way)
+
+    def run(offset, turn, kept):
+        return expert_rows(expert, (me + offset) % ny, turn, everything, weights, turned, kept)
+
+    far_low, far_high, kept = run(2, 0, [])
+    low_via, high_via = send(far_low, up), send(far_high, down)
+    up_low, up_high, kept = run(1, 1, kept)
+    from_below_high = send(up_high, up)
+    down_low, down_high, kept = run(ny - 1, 2, kept)
+    from_above_low = send(down_low, down)
+    from_below_low = send(add(up_low, low_via).astype(BF), up)
+    from_above_high = send(add(down_high, high_via).astype(BF), down)
+    own_low, own_high, kept = run(0, 3, kept)
+    low = add(own_low, from_below_low, from_above_low).astype(BF)
+    high = add(own_high, from_below_high, from_above_high).astype(BF)
+    return jnp.concatenate([low, high], axis=1), kept
 
 
 def local(block_in, out_grad, gate_values, expert_ids, conv_kernel, expert_weights):
@@ -158,10 +201,8 @@
     packed = jnp.concatenate([jnp.concatenate([block_in, out_grad], axis=1), meta], axis=0)
     everything = lax.all_gather(packed, group, axis=0, tiled=False)
     weights = gather_weights(expert_weights)
-    row_grad, rows_in, rows_q, pre_grads, hidden = expert_rows(expert, everything, weights)
-
-    parts = lax.all_to_all(row_grad.reshape(ny, experts * SLOTS, width), "y", 0, 0, tiled=True)
-    summed = jnp.sum(parts.astype(F32), axis=0).astype(BF)
+    summed, (rows_in, rows_q, pre_grads, hidden) = rows_backward(expert, everything, weights)
+
     returned = lax.all_to_all(summed.reshape(experts, SLOTS, width), ("x", "c"), 0, 0, tiled=True)
 
     term = jnp.concatenate(

time: 265 us -> 264 us (level)
  blocking collectives: 54.9 us -> 0 us
  waiting for transfers between devices: 93.4 us -> 125 us
  Pallas kernels: 27.1 us -> 40.7 us
  starting transfers between devices: 36 us -> 44.9 us
    all_to_all x1 -> x0, blocking collectives: 54.9 us -> none  [local(): lax.all_to_all(row_grad.reshape(ny, experts * SLOTS, width), 'y', 0, 0, t...]
    ppermute x0 -> x6, waiting for transfers between devices: none -> 31.1 us  [send(): return lax.ppermute(rows, 'y', way)]
    pallas_call x1 -> x4, Pallas kernels: 27.1 us -> 40.7 us  [expert_rows(): pl.pallas_call(rows_kernel, grid_spec=pltpu.PrefetchScalarGridSpec(num_sc...]
    ppermute x3, waiting for transfers between devices: 0.01 us -> 12.5 us  [ring_gather(): left = lax.ppermute(left, axis, down)]
    ppermute x4, waiting for transfers between devices: 28.8 us -> 18.8 us  [ring_gather(): right = lax.ppermute(right, axis, up)]
    ppermute x0 -> x6, starting transfers between devices: none -> 8.15 us  [send(): return lax.ppermute(rows, 'y', way)]
    reduce_sum x1 -> x0, other arithmetic: 4.5 us -> none  [local(): summed = jnp.sum(parts.astype(F32), axis=0).astype(BF)]
    ppermute x3, starting transfers between devices: 10.4 us -> 13.2 us  [ring_gather(): left = lax.ppermute(left, axis, down)]
  transfers between devices with their start and end apart: 14 -> 20, of which waited for: 9 -> 13; matrix products, arithmetic and copies ran while one was open for 7% -> 5% of each run, Pallas kernels for 0% -> 0%
where the time goes in v3:
time: 264 us; the launch traced here: 260 us
  waiting for transfers between devices  125 us (47%)
  starting transfers between devices  44.9 us (17%)
  Pallas kernels  40.7 us (15%)
  between operations  14.3 us (5%)
  matrix products  13.3 us (5%)
  local copies, waits for them, and re-layouts  11.7 us (4%)
  other arithmetic  10.1 us (4%)
    pallas_call x4, Pallas kernels, expert_rows(): pl.pallas_call(rows_kernel, grid_spec=pltpu.PrefetchScalarGridSpec(num_sc...  40.7 us
    all_gather x1, waiting for transfers between devices, local(): everything = lax.all_gather(packed, group, axis=0, tiled=False)  38.2 us
    ppermute x6, waiting for transfers between devices, send(): return lax.ppermute(rows, 'y', way)  31.1 us
    ppermute x4, waiting for transfers between devices, ring_gather(): right = lax.ppermute(right, axis, up)  18.8 us
    all_to_all x1, waiting for transfers between devices, local(): lax.all_to_all(summed.reshape(experts, SLOTS, width), ('x', 'c'), 0, 0, t...  15.7 us
    ppermute x3, starting transfers between devices, ring_gather(): left = lax.ppermute(left, axis, down)  13.2 us
    dot_general x4, matrix products, dot(): return lax.dot_general(a, b, (contract, batch), preferred_element_type=F32)  13.1 us
    ppermute x3, waiting for transfers between devices, ring_gather(): left = lax.ppermute(left, axis, down)  12.5 us
  transfers between devices with their start and end apart: 20, of which 13 were waited for; matrix products, arithmetic and copies ran while one was open for 5% of the time, Pallas kernels for 0%

profile of v3, /device:TPU:8, one launch (start us, length us, event | category | flops | bytes accessed | tf_op | source)
XLA Modules:
  0.0 260.5 jit_solution(8878548921215068556)
XLA Ops:
  7.2 0.0 all-gather.3.cloned.1.call-start
  7.2 0.7 convert_bitcast_fusion
  7.9 0.7 fusion.46
  8.6 2.1 pad_maximum_fusion.2
  10.7 1.3 reshape_squeeze.3
  12.0 0.2 copy.73
  12.2 1.3 reshape.37
  13.5 5.6 %all-to-all-start = ((bf16[4,32,1536]{2,1,0:T(8,128)(2,1)}), bf16[4,32,1536]{2,1,0:T(8,128)(2,1)S(1)}, u32[]{:S(2)}, u32[]{:S(2)}) async-start(bf16[4,32,1536]{2,1,0:T(8,128)(2,1)} %reshape.37), calls=%async_computation | async-start | bytes 786432 | tf_op jit(solution)/shard_map/all_to_all | solution.py:42
  19.1 0.1 pad_add_fusion.2
  19.2 0.1 pad_add_fusion
  19.2 5.8 %all-to-all-done = bf16[4,32,1536]{2,1,0:T(8,128)(2,1)S(1)} async-done(((bf16[4,32,1536]{2,1,0:T(8,128)(2,1)}), bf16[4,32,1536]{2,1,0:T(8,128)(2,1)S(1)}, u32[]{:S(2)}, u32[]{:S(2)}) %all-to-all-start) | async-done | bytes 393248 | tf_op jit(solution)/shard_map/all_to_all | solution.py:42
  25.0 5.8 %collective-permute-start.1 = (bf16[4,32,1536]{2,1,0:T(8,128)(2,1)S(1)}, bf16[4,32,1536]{2,1,0:T(8,128)(2,1)S(1)}, u32[]{:S(2)}, u32[]{:S(2)}) collective-permute-start(bf16[4,32,1536]{2,1,0:T(8,128)(2,1)S(1)} %all-to-all-done), channel_id=1, source_target_pairs={{8,0},{16,8},{24,16},{32,24},{40,32},{48,40},{56,48},{0,56},{9,1},... | collective-permute-start | bytes 1179656 | tf_op jit(solution)/shard_map/ppermute | solution.py:31
  30.9 0.3 broadcast_in_dim.33
  31.3 6.5 %collective-permute-done.1 = bf16[4,32,1536]{2,1,0:T(8,128)(2,1)S(1)} collective-permute-done((bf16[4,32,1536]{2,1,0:T(8,128)(2,1)S(1)}, bf16[4,32,1536]{2,1,0:T(8,128)(2,1)S(1)}, u32[]{:S(2)}, u32[]{:S(2)}) %collective-permute-start.1) | collective-permute-done | bytes 393248 | tf_op jit(solution)/shard_map/ppermute | solution.py:31
  37.8 3.7 %collective-permute-start.3 = (bf16[4,32,1536]{2,1,0:T(8,128)(2,1)S(1)}, bf16[4,32,1536]{2,1,0:T(8,128)(2,1)S(1)}, u32[]{:S(2)}, u32[]{:S(2)}) collective-permute-start(bf16[4,32,1536]{2,1,0:T(8,128)(2,1)S(1)} %collective-permute-done.1), channel_id=1, source_target_pairs={{8,0},{16,8},{24,16},{32,24},{40,32},{48,40},{56,48},{0,56},{9,1},... | collective-permute-start | bytes 1179656 | tf_op jit(solution)/shard_map/ppermute | solution.py:31
  41.5 6.0 %collective-permute-done.3 = bf16[4,32,1536]{2,1,0:T(8,128)(2,1)S(1)} collective-permute-done((bf16[4,32,1536]{2,1,0:T(8,128)(2,1)S(1)}, bf16[4,32,1536]{2,1,0:T(8,128)(2,1)S(1)}, u32[]{:S(2)}, u32[]{:S(2)}) %collective-permute-start.3) | collective-permute-done | bytes 393248 | tf_op jit(solution)/shard_map/ppermute | solution.py:31
  47.5 3.7 %collective-permute-start.5 = (bf16[4,32,1536]{2,1,0:T(8,128)(2,1)S(1)}, bf16[4,32,1536]{2,1,0:T(8,128)(2,1)S(1)}, u32[]{:S(2)}, u32[]{:S(2)}) collective-permute-start(bf16[4,32,1536]{2,1,0:T(8,128)(2,1)S(1)} %collective-permute-done.3), channel_id=1, source_target_pairs={{8,0},{16,8},{24,16},{32,24},{40,32},{48,40},{56,48},{0,56},{9,1},... | collective-permute-start | bytes 1179656 | tf_op jit(solution)/shard_map/ppermute | solution.py:31
  51.3 9.9 %collective-permute-done.4 = bf16[4,32,1536]{2,1,0:T(8,128)(2,1)S(1)} collective-permute-done((bf16[4,32,1536]{2,1,0:T(8,128)(2,1)S(1)}, bf16[4,32,1536]{2,1,0:T(8,128)(2,1)S(1)}, u32[]{:S(2)}, u32[]{:S(2)}) %collective-permute-start.4) | collective-permute-done | bytes 393248 | tf_op jit(solution)/shard_map/ppermute | solution.py:28
  61.2 8.9 %collective-permute-done.6 = bf16[4,32,1536]{2,1,0:T(8,128)(2,1)S(1)} collective-permute-done((bf16[4,32,1536]{2,1,0:T(8,128)(2,1)S(1)}, bf16[4,32,1536]{2,1,0:T(8,128)(2,1)S(1)}, u32[]{:S(2)}, u32[]{:S(2)}) %collective-permute-start.6) | collective-permute-done | bytes 393248 | tf_op jit(solution)/shard_map/ppermute | solution.py:28
  70.2 1.7 copy-done.2
  71.9 0.2 slice.274
  72.1 2.6 copy.68
  74.7 38.2 %all-gather.3.cloned.1.call-done = bf16[6400,2048]{1,0:T(8,128)(2,1)} async-done(((bf16[200,2048]{1,0:T(8,128)(2,1)}), bf16[6400,2048]{1,0:T(8,128)(2,1)}) %all-gather.3.cloned.1.call-update) | async-done | bytes 26214416 | tf_op jit(solution)/shard_map/all_gather | solution.py:202
  112.9 10.4 %shard_map.85 = (bf16[512,512]{1,0:T(8,128)(2,1)S(1)}, bf16[512,512]{1,0:T(8,128)(2,1)S(1)}, bf16[2048,1024]{1,0:T(8,128)(2,1)}, bf16[2048,1024]{1,0:T(8,128)(2,...) custom-call(s32[2]{0:T(128)S(1)} %get-tuple-element.89.info, bf16[32,200,2048]{2,1,0:T(8,128)(2,1)} %bitcast.110, ...), custom_call_target="tpu_custom_call" | custom-call | tf_op jit(solution)/shard_map/pallas_call | solution.py:142
  123.3 10.1 %shard_map.86 = (bf16[512,512]{1,0:T(8,128)(2,1)S(1)}, bf16[512,512]{1,0:T(8,128)(2,1)S(1)}, bf16[2048,1024]{1,0:T(8,128)(2,1)}, bf16[2048,1024]{1,0:T(8,128)(2,...) custom-call(s32[2]{0:T(128)S(1)} %get-tuple-element.88.info, ...), custom_call_target="tpu_custom_call", output_to_operand_aliasing={{2}: (4, {}), {3}: (5, {}), {4}: (6, {}), {5}: (7, {})} | custom-call | tf_op jit(solution)/shard_map/pallas_call | solution.py:142
  133.4 10.1 %shard_map.87 = (bf16[512,512]{1,0:T(8,128)(2,1)S(1)}, bf16[512,512]{1,0:T(8,128)(2,1)S(1)}, bf16[2048,1024]{1,0:T(8,128)(2,1)}, bf16[2048,1024]{1,0:T(8,128)(2,...) custom-call(s32[2]{0:T(128)S(1)} %get-tuple-element.87.info, ...), custom_call_target="tpu_custom_call", output_to_operand_aliasing={{2}: (4, {}), {3}: (5, {}), {4}: (6, {}), {5}: (7, {})} | custom-call | tf_op jit(solution)/shard_map/pallas_call | solution.py:142
  143.5 10.1 %shard_map.88 = (bf16[512,512]{1,0:T(8,128)(2,1)S(1)}, bf16[512,512]{1,0:T(8,128)(2,1)S(1)}, bf16[2048,1024]{1,0:T(8,128)(2,1)}, bf16[2048,1024]{1,0:T(8,128)(2,...) custom-call(s32[2]{0:T(128)S(1)} %get-tuple-element.86.info, ...), custom_call_target="tpu_custom_call", output_to_operand_aliasing={{2}: (4, {}), {3}: (5, {}), {4}: (6, {}), {5}: (7, {})} | custom-call | tf_op jit(solution)/shard_map/pallas_call | solution.py:142
  153.6 5.4 %convolution_convert_fusion.1 = bf16[1024,512]{1,0:T(8,128)(2,1)S(1)} fusion(bf16[2048,1024]{1,0:T(8,128)(2,1)} %get-tuple-element.49, bf16[2048,512]{1,0:T(8,128)(2,1)} %get-tuple-element.50), kind=kOutput, calls=%fused_computation.2 | convolution fusion | flops 2148007936 | bytes 7340032 | tf_op jit(solution)/shard_map/dot_general | solution.py:17
  158.9 7.2 %convolution_convert_fusion = bf16[1024,1024]{1,0:T(8,128)(2,1)S(1)} fusion(bf16[2048,1024]{1,0:T(8,128)(2,1)S(1)} %copy-done.3, bf16[2048,1024]{1,0:T(8,128)(2,1)} %get-tuple-element.48), kind=kOutput, calls=%fused_computation.1 | convolution fusion | flops 4296015872 | bytes 10485760 | tf_op jit(solution)/shard_map/dot_general | solution.py:17
  166.1 0.3 pad_maximum_fusion
  166.4 2.0 copy.66
  168.4 1.6 collective-permute-start.7
  170.0 0.5 collective-permute-start.11
  170.6 2.4 collective-permute-start.9
  172.9 9.9 %collective-permute-done.7 = bf16[512,512]{1,0:T(8,128)(2,1)S(1)} collective-permute-done((bf16[512,512]{1,0:T(8,128)(2,1)}, bf16[512,512]{1,0:T(8,128)(2,1)S(1)}, u32[]{:S(2)}, u32[]{:S(2)}) %collective-permute-start.7) | collective-permute-done | bytes 524320 | tf_op jit(solution)/shard_map/ppermute | solution.py:174
  182.8 0.1 add_convert_fusion.3
  183.0 1.6 collective-permute-start.8
  184.5 1.2 collective-permute-start.10
  185.7 0.1 add_convert_fusion.1
  185.9 0.9 collective-permute-start.12
  186.8 9.2 %collective-permute-done.9 = bf16[512,512]{1,0:T(8,128)(2,1)S(1)} collective-permute-done((bf16[512,512]{1,0:T(8,128)(2,1)}, bf16[512,512]{1,0:T(8,128)(2,1)S(1)}, u32[]{:S(2)}, u32[]{:S(2)}) %collective-permute-start.9) | collective-permute-done | bytes 524320 | tf_op jit(solution)/shard_map/ppermute | solution.py:174
  196.0 2.2 collective-permute-done.8
  198.2 0.2 add_convert_fusion.2
  198.4 9.8 %collective-permute-done.10 = bf16[512,512]{1,0:T(8,128)(2,1)S(1)} collective-permute-done((bf16[512,512]{1,0:T(8,128)(2,1)S(1)}, bf16[512,512]{1,0:T(8,128)(2,1)S(1)}, u32[]{:S(2)}, u32[]{:S(2)}) %collective-permute-start.10) | collective-permute-done | bytes 524320 | tf_op jit(solution)/shard_map/ppermute | solution.py:174
  208.2 0.2 add_convert_fusion
  208.4 1.1 pad_maximum_fusion.1
  209.5 4.4 %all-to-all-start.1 = ((bf16[8,64,1024]{2,1,0:T(8,128)(2,1)}), bf16[8,64,1024]{2,1,0:T(8,128)(2,1)S(1)}, u32[]{:S(2)}, u32[]{:S(2)}) async-start(bf16[8,64,1024]{2,1,0:T(8,128)(2,1)} %bitcast.31), calls=%async_computation.1 | async-start | bytes 2097152 | tf_op jit(solution)/shard_map/all_to_all | solution.py:206
  213.9 0.1 convolution_convert_fusion.2
  214.1 0.1 fusion.50
  214.2 15.7 %all-to-all-done.1 = bf16[8,64,1024]{2,1,0:T(8,128)(2,1)S(1)} async-done(((bf16[8,64,1024]{2,1,0:T(8,128)(2,1)}), bf16[8,64,1024]{2,1,0:T(8,128)(2,1)S(1)}, u32[]{:S(2)}, u32[]{:S(2)}) %all-to-all-start.1) | async-done | bytes 1048608 | tf_op jit(solution)/shard_map/all_to_all | solution.py:206
  229.9 0.2 fusion.34
  230.1 0.4 fusion.52
  230.5 1.9 collective-permute-start.13
  232.5 7.9 %collective-permute-start.14 = (bf16[15,1024]{1,0:T(8,128)(2,1)S(1)}, bf16[15,1024]{1,0:T(8,128)(2,1)S(1)}, u32[]{:S(2)}, u32[]{:S(2)}) collective-permute-start(bf16[15,1024]{1,0:T(8,128)(2,1)S(1)} %get-tuple-element.52), channel_id=1, source_target_pairs={{1,0},{2,1},{3,2},{4,3},{5,4},{6,5},{7,6},{8,7},{9,8},{10,9},{11,1... | collective-permute-start | bytes 92168 | tf_op jit(solution)/shard_map/ppermute | solution.py:77
  240.4 0.6 fusion.48
  240.9 1.0 collective-permute-done.14
  241.9 0.1 maximum_convert_fusion
  242.0 0.0 reduce-scatter.2.cloned.1.call-done
  242.1 3.8 %all-to-all-start.2 = ((bf16[4,32,1536]{2,1,0:T(8,128)(2,1)}), bf16[4,32,1536]{2,1,0:T(8,128)(2,1)S(1)}, u32[]{:S(2)}, u32[]{:S(2)}) async-start(bf16[4,32,1536]{2,1,0:T(8,128)(2,1)} %bitcast.128), calls=%async_computation.3 | async-start | bytes 786432 | tf_op jit(solution)/shard_map/all_to_all | solution.py:57
  245.8 3.7 %fusion.3 = bf16[192,1024]{1,0:T(8,128)(2,1)} fusion(f32[192,1024]{1,0:T(8,128)S(1)} %get-tuple-element.85, f32[222,1024]{1,0:T(8,128)S(1)} %maximum_convert_fusion, f32[1024]{0:T(1024)S(1)} %bitcast.143, f32[1024]{0:T(1024)S(1)} %bitcast.142, f32[1024]{0:T(1024)S(1)} %bitcast.141, f32[1024]{0:T(1024)S(1)} %bitcast.140, f32[1024]{0:T(1024)S(1)} %bitcast.139, ...), kind=kLoop, calls=%fused_computation.15 | loop fusion | flops 12386304 | bytes 25686016 | tf_op jit(solution)/shard_map/convert_element_type | solution.py:236
  249.5 2.5 all-to-all-done.2
  252.0 0.3 reshape.42
  252.2 0.4 copy.57
  252.6 1.0 reshape.43
  (42 shorter events, 0.4 us)
Async XLA Ops:
  7.2 105.7 %all-gather.3.cloned.1.call-start = ((), (), s32[]{:S(2)}) async-start(), calls=%async_computation.5 | async-start | bytes 27033600 | tf_op jit(solution)/shard_map/all_gather | solution.py:202
  13.5 11.5 %all-to-all-start = ((bf16[4,32,1536]{2,1,0:T(8,128)(2,1)}), bf16[4,32,1536]{2,1,0:T(8,128)(2,1)S(1)}, u32[]{:S(2)}, u32[]{:S(2)}) async-start(bf16[4,32,1536]{2,1,0:T(8,128)(2,1)} %reshape.37), calls=%async_computation | async-start | bytes 786432 | tf_op jit(solution)/shard_map/all_to_all | solution.py:42
  19.1 223.0 %reduce-scatter.2.cloned.1.call-start = ((), (), s32[]{:S(2)}) async-start(), calls=%async_computation.4 | async-start | bytes 3538944 | tf_op jit(solution)/shard_map/reduce_scatter | solution.py:56
  25.0 12.7 %collective-permute-start.1 = (bf16[4,32,1536]{2,1,0:T(8,128)(2,1)S(1)}, bf16[4,32,1536]{2,1,0:T(8,128)(2,1)S(1)}, u32[]{:S(2)}, u32[]{:S(2)}) collective-permute-start(bf16[4,32,1536]{2,1,0:T(8,128)(2,1)S(1)} %all-to-all-done), channel_id=1, source_target_pairs={{8,0},{16,8},{24,16},{32,24},{40,32},{48,40},{56,48},{0,56},{9,1},... | collective-permute-start | bytes 1179656 | tf_op jit(solution)/shard_map/ppermute | solution.py:31
  30.9 10.6 %collective-permute-start = (bf16[4,32,1536]{2,1,0:T(8,128)(2,1)S(1)}, bf16[4,32,1536]{2,1,0:T(8,128)(2,1)S(1)}, u32[]{:S(2)}, u32[]{:S(2)}) collective-permute-start(bf16[4,32,1536]{2,1,0:T(8,128)(2,1)S(1)} %all-to-all-done), channel_id=1, source_target_pairs={{0,8},{8,16},{16,24},{24,32},{32,40},{40,48},{48,56},{56,0},{1,9},... | collective-permute-start | bytes 1179656 | tf_op jit(solution)/shard_map/ppermute | solution.py:28
  37.8 9.8 %collective-permute-start.3 = (bf16[4,32,1536]{2,1,0:T(8,128)(2,1)S(1)}, bf16[4,32,1536]{2,1,0:T(8,128)(2,1)S(1)}, u32[]{:S(2)}, u32[]{:S(2)}) collective-permute-start(bf16[4,32,1536]{2,1,0:T(8,128)(2,1)S(1)} %collective-permute-done.1), channel_id=1, source_target_pairs={{8,0},{16,8},{24,16},{32,24},{40,32},{48,40},{56,48},{0,56},{9,1},... | collective-permute-start | bytes 1179656 | tf_op jit(solution)/shard_map/ppermute | solution.py:31
  41.4 9.8 %collective-permute-start.2 = (bf16[4,32,1536]{2,1,0:T(8,128)(2,1)S(1)}, bf16[4,32,1536]{2,1,0:T(8,128)(2,1)S(1)}, u32[]{:S(2)}, u32[]{:S(2)}) collective-permute-start(bf16[4,32,1536]{2,1,0:T(8,128)(2,1)S(1)} %collective-permute-done), channel_id=1, source_target_pairs={{0,8},{8,16},{16,24},{24,32},{32,40},{40,48},{48,56},{56,0},{1,9},... | collective-permute-start | bytes 1179656 | tf_op jit(solution)/shard_map/ppermute | solution.py:28
  47.5 13.7 %collective-permute-start.5 = (bf16[4,32,1536]{2,1,0:T(8,128)(2,1)S(1)}, bf16[4,32,1536]{2,1,0:T(8,128)(2,1)S(1)}, u32[]{:S(2)}, u32[]{:S(2)}) collective-permute-start(bf16[4,32,1536]{2,1,0:T(8,128)(2,1)S(1)} %collective-permute-done.3), channel_id=1, source_target_pairs={{8,0},{16,8},{24,16},{32,24},{40,32},{48,40},{56,48},{0,56},{9,1},... | collective-permute-start | bytes 1179656 | tf_op jit(solution)/shard_map/ppermute | solution.py:31
  51.2 9.9 %collective-permute-start.4 = (bf16[4,32,1536]{2,1,0:T(8,128)(2,1)S(1)}, bf16[4,32,1536]{2,1,0:T(8,128)(2,1)S(1)}, u32[]{:S(2)}, u32[]{:S(2)}) collective-permute-start(bf16[4,32,1536]{2,1,0:T(8,128)(2,1)S(1)} %collective-permute-done.2), channel_id=1, source_target_pairs={{0,8},{8,16},{16,24},{24,32},{32,40},{40,48},{48,56},{56,0},{1,9},... | collective-permute-start | bytes 1179656 | tf_op jit(solution)/shard_map/ppermute | solution.py:28
  61.1 9.0 %collective-permute-start.6 = (bf16[4,32,1536]{2,1,0:T(8,128)(2,1)S(1)}, bf16[4,32,1536]{2,1,0:T(8,128)(2,1)S(1)}, u32[]{:S(2)}, u32[]{:S(2)}) collective-permute-start(bf16[4,32,1536]{2,1,0:T(8,128)(2,1)S(1)} %collective-permute-done.4), channel_id=1, source_target_pairs={{0,8},{8,16},{16,24},{24,32},{32,40},{40,48},{48,56},{56,0},{1,9},... | collective-permute-start | bytes 1179656 | tf_op jit(solution)/shard_map/ppermute | solution.py:28
  70.2 1.7 copy-start.2
  123.3 10.1 %copy-start.1 = (bf16[512,512]{1,0:T(8,128)(2,1)}, bf16[512,512]{1,0:T(8,128)(2,1)S(1)}, u32[]{:S(2)}) copy-start(bf16[512,512]{1,0:T(8,128)(2,1)S(1)} %get-tuple-element.41) | copy-start | bytes 1572868
  143.5 10.1 %copy-start = (bf16[512,512]{1,0:T(8,128)(2,1)}, bf16[512,512]{1,0:T(8,128)(2,1)S(1)}, u32[]{:S(2)}) copy-start(bf16[512,512]{1,0:T(8,128)(2,1)S(1)} %get-tuple-element.42) | copy-start | bytes 1572868
  153.6 5.4 %copy-start.3 = (bf16[2048,1024]{1,0:T(8,128)(2,1)S(1)}, bf16[2048,1024]{1,0:T(8,128)(2,1)}, u32[]{:S(2)}) copy-start(bf16[2048,1024]{1,0:T(8,128)(2,1)} %get-tuple-element.47) | copy-start | bytes 12582916
  168.4 14.4 %collective-permute-start.7 = (bf16[512,512]{1,0:T(8,128)(2,1)}, bf16[512,512]{1,0:T(8,128)(2,1)S(1)}, u32[]{:S(2)}, u32[]{:S(2)}) collective-permute-start(bf16[512,512]{1,0:T(8,128)(2,1)} %copy-done.1), channel_id=1, source_target_pairs={{0,64},{64,128},{128,192},{192,0},{1,65},{65,129},{129,193},{193,1... | collective-permute-start | bytes 1572872 | tf_op jit(solution)/shard_map/ppermute | solution.py:174
  170.0 15.7 %collective-permute-start.11 = (bf16[512,512]{1,0:T(8,128)(2,1)S(1)}, bf16[512,512]{1,0:T(8,128)(2,1)S(1)}, u32[]{:S(2)}, u32[]{:S(2)}) collective-permute-start(bf16[512,512]{1,0:T(8,128)(2,1)S(1)} %get-tuple-element.46), channel_id=1, source_target_pairs={{64,0},{128,64},{192,128},{0,192},{65,1},{129,65},{193,129},{1,193... | collective-permute-start | bytes 1572872 | tf_op jit(solution)/shard_map/ppermute | solution.py:174
  170.6 25.5 %collective-permute-start.9 = (bf16[512,512]{1,0:T(8,128)(2,1)}, bf16[512,512]{1,0:T(8,128)(2,1)S(1)}, u32[]{:S(2)}, u32[]{:S(2)}) collective-permute-start(bf16[512,512]{1,0:T(8,128)(2,1)} %copy-done), channel_id=1, source_target_pairs={{64,0},{128,64},{192,128},{0,192},{65,1},{129,65},{193,129},{1,193... | collective-permute-start | bytes 1572872 | tf_op jit(solution)/shard_map/ppermute | solution.py:174
  183.0 15.3 %collective-permute-start.8 = (bf16[512,512]{1,0:T(8,128)(2,1)S(1)}, bf16[512,512]{1,0:T(8,128)(2,1)S(1)}, u32[]{:S(2)}, u32[]{:S(2)}) collective-permute-start(bf16[512,512]{1,0:T(8,128)(2,1)S(1)} %add_convert_fusion.3), channel_id=1, source_target_pairs={{0,64},{64,128},{128,192},{192,0},{1,65},{65,129},{129,193},{193,1... | collective-permute-start | bytes 1572872 | tf_op jit(solution)/shard_map/ppermute | solution.py:174
  184.5 23.6 %collective-permute-start.10 = (bf16[512,512]{1,0:T(8,128)(2,1)S(1)}, bf16[512,512]{1,0:T(8,128)(2,1)S(1)}, u32[]{:S(2)}, u32[]{:S(2)}) collective-permute-start(bf16[512,512]{1,0:T(8,128)(2,1)S(1)} %get-tuple-element.44), channel_id=1, source_target_pairs={{0,64},{64,128},{128,192},{192,0},{1,65},{65,129},{129,193},{193,1... | collective-permute-start | bytes 1572872 | tf_op jit(solution)/shard_map/ppermute | solution.py:174
  185.9 22.3 %collective-permute-start.12 = (bf16[512,512]{1,0:T(8,128)(2,1)S(1)}, bf16[512,512]{1,0:T(8,128)(2,1)S(1)}, u32[]{:S(2)}, u32[]{:S(2)}) collective-permute-start(bf16[512,512]{1,0:T(8,128)(2,1)S(1)} %add_convert_fusion.1), channel_id=1, source_target_pairs={{64,0},{128,64},{192,128},{0,192},{65,1},{129,65},{193,129},{1,193... | collective-permute-start | bytes 1572872 | tf_op jit(solution)/shard_map/ppermute | solution.py:174
  208.2 5.7 %copy-start.6 = (s32[192,2]{0,1:T(2,128)S(1)}, s32[192,2]{0,1:T(2,128)}, u32[]{:S(2)}) copy-start(s32[192,2]{0,1:T(2,128)} %param.9) | copy-start | bytes 4612
  208.2 5.9 %copy-start.5 = (bf16[31,1024]{1,0:T(8,128)(2,1)S(1)}, bf16[31,1024]{1,0:T(8,128)(2,1)}, u32[]{:S(2)}) copy-start(bf16[31,1024]{1,0:T(8,128)(2,1)} %param.10) | copy-start | bytes 190468
  208.2 21.9 %copy-start.4 = (bf16[192,1024]{1,0:T(8,128)(2,1)S(1)}, bf16[192,1024]{1,0:T(8,128)(2,1)}, u32[]{:S(2)}) copy-start(bf16[192,1024]{1,0:T(8,128)(2,1)} %param.7) | copy-start | bytes 1179652
  209.5 30.8 %copy-start.7 = (bf16[192,2]{0,1:T(2,128)(2,1)S(1)}, bf16[192,2]{0,1:T(2,128)(2,1)}, u32[]{:S(2)}) copy-start(bf16[192,2]{0,1:T(2,128)(2,1)} %param.8) | copy-start | bytes 2308
  209.5 20.3 %all-to-all-start.1 = ((bf16[8,64,1024]{2,1,0:T(8,128)(2,1)}), bf16[8,64,1024]{2,1,0:T(8,128)(2,1)S(1)}, u32[]{:S(2)}, u32[]{:S(2)}) async-start(bf16[8,64,1024]{2,1,0:T(8,128)(2,1)} %bitcast.31), calls=%async_computation.1 | async-start | bytes 2097152 | tf_op jit(solution)/shard_map/all_to_all | solution.py:206
  230.5 10.4 %collective-permute-start.13 = (bf16[15,1024]{1,0:T(8,128)(2,1)S(1)}, bf16[15,1024]{1,0:T(8,128)(2,1)S(1)}, u32[]{:S(2)}, u32[]{:S(2)}) collective-permute-start(bf16[15,1024]{1,0:T(8,128)(2,1)S(1)} %get-tuple-element.51), channel_id=1, source_target_pairs={{0,1},{1,2},{2,3},{3,4},{4,5},{5,6},{6,7},{7,8},{8,9},{9,10},{10,1... | collective-permute-start | bytes 92168 | tf_op jit(solution)/shard_map/ppermute | solution.py:76
  232.5 9.4 %collective-permute-start.14 = (bf16[15,1024]{1,0:T(8,128)(2,1)S(1)}, bf16[15,1024]{1,0:T(8,128)(2,1)S(1)}, u32[]{:S(2)}, u32[]{:S(2)}) collective-permute-start(bf16[15,1024]{1,0:T(8,128)(2,1)S(1)} %get-tuple-element.52), channel_id=1, source_target_pairs={{1,0},{2,1},{3,2},{4,3},{5,4},{6,5},{7,6},{8,7},{9,8},{10,9},{11,1... | collective-permute-start | bytes 92168 | tf_op jit(solution)/shard_map/ppermute | solution.py:77
  242.1 9.9 %all-to-all-start.2 = ((bf16[4,32,1536]{2,1,0:T(8,128)(2,1)}), bf16[4,32,1536]{2,1,0:T(8,128)(2,1)S(1)}, u32[]{:S(2)}, u32[]{:S(2)}) async-start(bf16[4,32,1536]{2,1,0:T(8,128)(2,1)} %bitcast.128), calls=%async_computation.3 | async-start | bytes 786432 | tf_op jit(solution)/shard_map/all_to_all | solution.py:57
Sparse Core Ops, SparseCore 0:
  10.8 101.9 all-gather.2
  168.6 46.7 reduce-scatter.1

commit v4 on v3

--- a/solution.py
+++ b/solution.py
@@ -121,21 +121,21 @@
         low_ref[place, :128] = jnp.where(row == SPARE, line, low_ref[place, :128].astype(F32)).astype(BF)
 
 
-def expert_rows(expert, group, turn, everything, weights, turned, kept):
+def expert_rows(expert, targets, turn, everything, weights, turned, kept):
     blocks, rows, wide = everything.shape
     groups = lax.axis_size("y")
     width, part = wide // 2, weights.shape[1] // 3
     rows_step = STEP * SLOTS
     steps = blocks // (groups * STEP)
-    total, mine = blocks * SLOTS, blocks * SLOTS // groups
-    info = jnp.stack([expert, group * steps]).astype(jnp.int32)
+    count = len(targets) * steps
+    total, mine = blocks * SLOTS, len(targets) * blocks * SLOTS // groups
+    firsts = [target * steps + step for target in targets for step in range(steps)]
+    info = jnp.stack([expert] + firsts).astype(jnp.int32)
 
     def rowwise(columns, first):
         return pl.BlockSpec((rows_step, columns), lambda i, info: (i + first, 0))
 
-    def whole(array):
-        return pl.BlockSpec(array.shape, lambda i, info: (0, 0))
-
+    whole = pl.BlockSpec(memory_space=pltpu.VMEM)
     widths = (width, width, 2 * part, part)
     shapes = [jax.ShapeDtypeStruct((mine, width // 2), BF)] * 2
     shapes += [jax.ShapeDtypeStruct((total, columns), BF) for columns in widths]
@@ -143,11 +143,11 @@
         rows_kernel,
         grid_spec=pltpu.PrefetchScalarGridSpec(
             num_scalar_prefetch=1,
-            grid=(steps,),
+            grid=(count,),
             in_specs=[
-                pl.BlockSpec((STEP, rows, wide), lambda i, info: (info[1] + i, 0, 0)),
-                whole(weights),
-                whole(turned),
+                pl.BlockSpec((STEP, rows, wide), lambda i, info: (info[1 + i], 0, 0)),
+                whole,
+                whole,
             ]
             + [pl.BlockSpec(memory_space=pl.ANY) for _ in kept],
             out_specs=[rowwise(width // 2, 0)] * 2 + [rowwise(columns, turn * steps) for columns in widths],
@@ -173,21 +173,26 @@
     def send(rows, way):
         return lax.ppermute(rows, "y", way)
 
-    def run(offset, turn, kept):
-        return expert_rows(expert, (me + offset) % ny, turn, everything, weights, turned, kept)
-
-    far_low, far_high, kept = run(2, 0, [])
+    def run(offsets, turn, kept):
+        return expert_rows(expert, [(me + offset) % ny for offset in offsets], turn, everything, weights, turned, kept)
+
+    far_low, far_high, kept = run([2], 0, [])
     low_via, high_via = send(far_low, up), send(far_high, down)
-    up_low, up_high, kept = run(1, 1, kept)
-    from_below_high = send(up_high, up)
-    down_low, down_high, kept = run(ny - 1, 2, kept)
-    from_above_low = send(down_low, down)
-    from_below_low = send(add(up_low, low_via).astype(BF), up)
-    from_above_high = send(add(down_high, high_via).astype(BF), down)
-    own_low, own_high, kept = run(0, 3, kept)
-    low = add(own_low, from_below_low, from_above_low).astype(BF)
-    high = add(own_high, from_below_high, from_above_high).astype(BF)
-    return jnp.concatenate([low, high], axis=1), kept
+    near_low, near_high, kept = run([1, ny - 1], 1, kept)
+    low_via, high_via, kept = lax.optimization_barrier((low_via, high_via, kept))
+    rows = far_low.shape[0]
+    below_high, above_low = send(near_high[:rows], up), send(near_low[rows:], down)
+    below_low = send(add(near_low[:rows], low_via).astype(BF), up)
+    above_high = send(add(near_high[rows:], high_via).astype(BF), down)
+    own_low, own_high, kept = run([0], 3, kept)
+    rows_in, rows_q, pre_grads, hidden = kept
+    first = dot(rows_in, pre_grads, ((0,), (0,))).astype(BF)
+    rows_q, below_high, above_low, first = lax.optimization_barrier((rows_q, below_high, above_low, first))
+    second = dot(rows_q, hidden, ((0,), (0,))).astype(BF)
+    term = jnp.concatenate([first, second], axis=1)
+    low = add(own_low, below_low, above_low).astype(BF)
+    high = add(own_high, below_high, above_high).astype(BF)
+    return low, high, term
 
 
 def local(block_in, out_grad, gate_values, expert_ids, conv_kernel, expert_weights):
@@ -201,14 +206,14 @@
     packed = jnp.concatenate([jnp.concatenate([block_in, out_grad], axis=1), meta], axis=0)
     everything = lax.all_gather(packed, group, axis=0, tiled=False)
     weights = gather_weights(expert_weights)
-    summed, (rows_in, rows_q, pre_grads, hidden) = rows_backward(expert, everything, weights)
-
-    returned = lax.all_to_all(summed.reshape(experts, SLOTS, width), ("x", "c"), 0, 0, tiled=True)
-
-    term = jnp.concatenate(
-        [dot(rows_in, pre_grads, ((0,), (0,))), dot(rows_q, hidden, ((0,), (0,)))], axis=1
-    ).astype(BF)
+    low, high, term = rows_backward(expert, everything, weights)
     weight_grad = scatter_weight_grad(term)
+
+    def give_back(rows):
+        return lax.all_to_all(rows.reshape(experts, SLOTS, width // 2), ("x", "c"), 0, 0, tiled=True)
+
+    back_low, back_high = give_back(low), give_back(high)
+    returned = jnp.concatenate([back_low, back_high], axis=2)
 
     own_ids = expert_ids.T[None] == jnp.arange(experts, dtype=jnp.int32)[:, None, None]
     own = slots_of(own_ids[:, 0] | own_ids[:, 1])

time: 264 us -> 248 us (0.939)
  waiting for transfers between devices: 125 us -> 108 us
  Pallas kernels: 40.7 us -> 37.1 us
    ppermute x6, waiting for transfers between devices: 31.1 us -> 9.9 us  [send(): return lax.ppermute(rows, 'y', way)]
    ppermute x3, waiting for transfers between devices: 12.5 us -> 0.01 us  [ring_gather(): left = lax.ppermute(left, axis, down)]
    ppermute x4, waiting for transfers between devices: 18.8 us -> 28.8 us  [ring_gather(): right = lax.ppermute(right, axis, up)]
    convert_element_type x4, other arithmetic: 0.69 us -> 4.46 us  [the longest x1 1.29 us: rows_backward(): below_low = send(add(near_low[:rows], low_via).astype(BF), up)]
    all_to_all x1 -> x2, waiting for transfers between devices: 15.7 us -> 19.3 us  [give_back(): lax.all_to_all(rows.reshape(experts, SLOTS, width // 2), ('x', 'c'), 0, 0...]
    pallas_call x4 -> x3, Pallas kernels: 40.7 us -> 37.1 us  [expert_rows(): pl.pallas_call(rows_kernel, grid_spec=pltpu.PrefetchScalarGridSpec(num_sc...]
    all_to_all x1 -> x2, starting transfers between devices: 4.36 us -> 7.7 us  [give_back(): lax.all_to_all(rows.reshape(experts, SLOTS, width // 2), ('x', 'c'), 0, 0...]
    all_gather x1, waiting for transfers between devices: 38.2 us -> 41.4 us  [local(): everything = lax.all_gather(packed, group, axis=0, tiled=False)]
  transfers between devices with their start and end apart: 20 -> 21, of which waited for: 13 -> 11; matrix products, arithmetic and copies ran while one was open for 5% -> 10% of each run, Pallas kernels for 0% -> 11%
where the time goes in v4:
time: 248 us; the launch traced here: 244 us
  waiting for transfers between devices  108 us (44%)
  starting transfers between devices  47.5 us (19%)
  Pallas kernels  37.1 us (15%)
  between operations  14.4 us (6%)
  local copies, waits for them, and re-layouts  12.9 us (5%)
  other arithmetic  12.7 us (5%)
  matrix products  11.3 us (5%)
    all_gather x1, waiting for transfers between devices, local(): everything = lax.all_gather(packed, group, axis=0, tiled=False)  41.4 us
    pallas_call x3, Pallas kernels, expert_rows(): pl.pallas_call(rows_kernel, grid_spec=pltpu.PrefetchScalarGridSpec(num_sc...  37.1 us
    ppermute x4, waiting for transfers between devices, ring_gather(): right = lax.ppermute(right, axis, up)  28.8 us
    all_to_all x2, waiting for transfers between devices, give_back(): lax.all_to_all(rows.reshape(experts, SLOTS, width // 2), ('x', 'c'), 0, 0...  19.3 us
    dot_general x4, matrix products, dot(): return lax.dot_general(a, b, (contract, batch), preferred_element_type=F32)  11.1 us
    ppermute x3, starting transfers between devices, ring_gather(): left = lax.ppermute(left, axis, down)  10.4 us
    ppermute x6, waiting for transfers between devices, send(): return lax.ppermute(rows, 'y', way)  9.9 us
    ppermute x1, starting transfers between devices, with_halo(): high = lax.ppermute(block[:width], axes, backward)  8.08 us
  transfers between devices with their start and end apart: 21, of which 11 were waited for; matrix products, arithmetic and copies ran while one was open for 10% of the time, Pallas kernels for 11%

profile of v4, /device:TPU:8, one launch (start us, length us, event | category | flops | bytes accessed | tf_op | source)
XLA Modules:
  0.0 244.3 jit_solution(5187479717966591360)
XLA Ops:
  7.2 0.0 all-gather.3.cloned.1.call-start
  7.2 0.7 convert_bitcast_fusion
  7.9 0.7 fusion.49
  8.6 2.1 pad_maximum_fusion.1
  10.7 0.0 all-gather.3.cloned.1.call-update
  10.7 1.3 reshape_squeeze.3
  12.0 0.2 copy.69
  12.2 1.3 reshape.38
  13.5 5.6 %all-to-all-start = ((bf16[4,32,1536]{2,1,0:T(8,128)(2,1)}), bf16[4,32,1536]{2,1,0:T(8,128)(2,1)S(1)}, u32[]{:S(2)}, u32[]{:S(2)}) async-start(bf16[4,32,1536]{2,1,0:T(8,128)(2,1)} %reshape.38), calls=%async_computation | async-start | bytes 786432 | tf_op jit(solution)/shard_map/all_to_all | solution.py:42
  19.1 0.1 pad_add_fusion
  19.2 5.8 %all-to-all-done = bf16[4,32,1536]{2,1,0:T(8,128)(2,1)S(1)} async-done(((bf16[4,32,1536]{2,1,0:T(8,128)(2,1)}), bf16[4,32,1536]{2,1,0:T(8,128)(2,1)S(1)}, u32[]{:S(2)}, u32[]{:S(2)}) %all-to-all-start) | async-done | bytes 393248 | tf_op jit(solution)/shard_map/all_to_all | solution.py:42
  25.0 1.9 collective-permute-start
  26.9 3.9 %collective-permute-start.1 = (bf16[4,32,1536]{2,1,0:T(8,128)(2,1)S(1)}, bf16[4,32,1536]{2,1,0:T(8,128)(2,1)S(1)}, u32[]{:S(2)}, u32[]{:S(2)}) collective-permute-start(bf16[4,32,1536]{2,1,0:T(8,128)(2,1)S(1)} %all-to-all-done), channel_id=1, source_target_pairs={{8,0},{16,8},{24,16},{32,24},{40,32},{48,40},{56,48},{0,56},{9,1},... | collective-permute-start | bytes 1179656 | tf_op jit(solution)/shard_map/ppermute | solution.py:31
  30.9 0.3 broadcast_in_dim.33
  31.3 7.2 %collective-permute-done = bf16[4,32,1536]{2,1,0:T(8,128)(2,1)S(1)} collective-permute-done((bf16[4,32,1536]{2,1,0:T(8,128)(2,1)S(1)}, bf16[4,32,1536]{2,1,0:T(8,128)(2,1)S(1)}, u32[]{:S(2)}, u32[]{:S(2)}) %collective-permute-start) | collective-permute-done | bytes 393248 | tf_op jit(solution)/shard_map/ppermute | solution.py:28
  38.5 3.2 %collective-permute-start.3 = (bf16[4,32,1536]{2,1,0:T(8,128)(2,1)S(1)}, bf16[4,32,1536]{2,1,0:T(8,128)(2,1)S(1)}, u32[]{:S(2)}, u32[]{:S(2)}) collective-permute-start(bf16[4,32,1536]{2,1,0:T(8,128)(2,1)S(1)} %collective-permute-done.1), channel_id=1, source_target_pairs={{8,0},{16,8},{24,16},{32,24},{40,32},{48,40},{56,48},{0,56},{9,1},... | collective-permute-start | bytes 1179656 | tf_op jit(solution)/shard_map/ppermute | solution.py:31
  41.8 6.7 %collective-permute-done.2 = bf16[4,32,1536]{2,1,0:T(8,128)(2,1)S(1)} collective-permute-done((bf16[4,32,1536]{2,1,0:T(8,128)(2,1)S(1)}, bf16[4,32,1536]{2,1,0:T(8,128)(2,1)S(1)}, u32[]{:S(2)}, u32[]{:S(2)}) %collective-permute-start.2) | collective-permute-done | bytes 393248 | tf_op jit(solution)/shard_map/ppermute | solution.py:28
  48.6 3.2 %collective-permute-start.5 = (bf16[4,32,1536]{2,1,0:T(8,128)(2,1)S(1)}, bf16[4,32,1536]{2,1,0:T(8,128)(2,1)S(1)}, u32[]{:S(2)}, u32[]{:S(2)}) collective-permute-start(bf16[4,32,1536]{2,1,0:T(8,128)(2,1)S(1)} %collective-permute-done.3), channel_id=1, source_target_pairs={{8,0},{16,8},{24,16},{32,24},{40,32},{48,40},{56,48},{0,56},{9,1},... | collective-permute-start | bytes 1179656 | tf_op jit(solution)/shard_map/ppermute | solution.py:31
  51.9 6.0 %collective-permute-done.4 = bf16[4,32,1536]{2,1,0:T(8,128)(2,1)S(1)} collective-permute-done((bf16[4,32,1536]{2,1,0:T(8,128)(2,1)S(1)}, bf16[4,32,1536]{2,1,0:T(8,128)(2,1)S(1)}, u32[]{:S(2)}, u32[]{:S(2)}) %collective-permute-start.4) | collective-permute-done | bytes 393248 | tf_op jit(solution)/shard_map/ppermute | solution.py:28
  57.9 8.9 %collective-permute-done.6 = bf16[4,32,1536]{2,1,0:T(8,128)(2,1)S(1)} collective-permute-done((bf16[4,32,1536]{2,1,0:T(8,128)(2,1)S(1)}, bf16[4,32,1536]{2,1,0:T(8,128)(2,1)S(1)}, u32[]{:S(2)}, u32[]{:S(2)}) %collective-permute-start.6) | collective-permute-done | bytes 393248 | tf_op jit(solution)/shard_map/ppermute | solution.py:28
  66.9 1.7 copy-done
  68.5 0.3 slice.290
  68.9 2.6 %copy.64 = bf16[1024,1024]{0,1:T(8,128)(2,1)} copy(bf16[1024,1024]{1,0:T(8,128)(2,1)S(1)} %slice.290) | data formatting | bytes 4194304
  71.4 41.4 %all-gather.3.cloned.1.call-done = bf16[6400,2048]{1,0:T(8,128)(2,1)} async-done(((bf16[200,2048]{1,0:T(8,128)(2,1)}), bf16[6400,2048]{1,0:T(8,128)(2,1)}) %all-gather.3.cloned.1.call-update) | async-done | bytes 26214416 | tf_op jit(solution)/shard_map/all_gather | solution.py:207
  112.9 10.7 %shard_map.85 = (bf16[512,512]{1,0:T(8,128)(2,1)S(1)}, bf16[512,512]{1,0:T(8,128)(2,1)S(1)}, bf16[2048,1024]{1,0:T(8,128)(2,1)}, bf16[2048,1024]{1,0:T(8,128)(2,...) custom-call(s32[3]{0:T(128)S(1)} %get-tuple-element.95.info, bf16[32,200,2048]{2,1,0:T(8,128)(2,1)} %bitcast.113, ...), custom_call_target="tpu_custom_call" | custom-call | tf_op jit(solution)/shard_map/pallas_call | solution.py:142
  123.6 1.5 collective-permute-start.7
  125.1 0.5 collective-permute-start.8
  125.6 0.1 stack.49.info
  125.7 16.2 %shard_map.86 = (bf16[1024,512]{1,0:T(8,128)(2,1)S(1)}, bf16[1024,512]{1,0:T(8,128)(2,1)}, bf16[2048,1024]{1,0:T(8,128)(2,1)}, bf16[2048,1024]{1,0:T(8,128)(2,1)...) custom-call(s32[5]{0:T(128)S(1)} %stack.49.info, ...), custom_call_target="tpu_custom_call", output_to_operand_aliasing={{2}: (4, {}), {3}: (5, {}), {4}: (6, {}), {5}: (7, {})} | custom-call | tf_op jit(solution)/shard_map/pallas_call | solution.py:142
  141.9 1.1 slice.220
  143.0 1.6 collective-permute-start.10
  144.6 1.0 collective-permute-start.11
  145.6 10.2 %shard_map.87 = (bf16[512,512]{1,0:T(8,128)(2,1)S(1)}, bf16[512,512]{1,0:T(8,128)(2,1)S(1)}, bf16[2048,1024]{1,0:T(8,128)(2,1)}, bf16[2048,1024]{1,0:T(8,128)(2,...) custom-call(s32[3]{0:T(128)S(1)} %get-tuple-element.94.info, ...), custom_call_target="tpu_custom_call", output_to_operand_aliasing={{2}: (4, {}), {3}: (5, {}), {4}: (6, {}), {5}: (7, {})} | custom-call | tf_op jit(solution)/shard_map/pallas_call | solution.py:142
  155.8 8.2 %convolution_convert_fusion = bf16[1024,1024]{1,0:T(8,128)(2,1)S(1)} fusion(bf16[2048,1024]{1,0:T(8,128)(2,1)} %get-tuple-element.50, bf16[2048,1024]{1,0:T(8,128)(2,1)} %get-tuple-element.51), kind=kOutput, calls=%fused_computation.1 | convolution fusion | flops 4296015872 | bytes 10485760 | tf_op jit(solution)/shard_map/dot_general | solution.py:17
  164.1 2.4 convolution_convert_fusion.1
  166.5 0.2 pad_maximum_fusion
  166.7 2.0 copy.52
  168.7 1.3 add_convert_fusion.3
  170.0 1.2 collective-permute-start.9
  171.2 1.2 add_convert_fusion.1
  172.4 2.2 collective-permute-start.12
  174.7 9.9 %collective-permute-done.9 = bf16[512,512]{1,0:T(8,128)(2,1)S(1)} collective-permute-done((bf16[512,512]{1,0:T(8,128)(2,1)S(1)}, bf16[512,512]{1,0:T(8,128)(2,1)S(1)}, u32[]{:S(2)}, u32[]{:S(2)}) %collective-permute-start.9) | collective-permute-done | bytes 524320 | tf_op jit(solution)/shard_map/ppermute | solution.py:174
  184.6 1.0 add_convert_fusion.2
  185.6 4.2 %all-to-all-start.1 = ((bf16[8,64,512]{2,1,0:T(8,128)(2,1)}), bf16[8,64,512]{2,1,0:T(8,128)(2,1)S(1)}, u32[]{:S(2)}, u32[]{:S(2)}) async-start(bf16[8,64,512]{2,1,0:T(8,128)(2,1)} %bitcast.35), calls=%async_computation.1 | async-start | bytes 1048576 | tf_op jit(solution)/shard_map/all_to_all | solution.py:213
  189.8 1.0 add_convert_fusion
  190.8 9.3 %all-to-all-done.1 = bf16[8,64,512]{2,1,0:T(8,128)(2,1)S(1)} async-done(((bf16[8,64,512]{2,1,0:T(8,128)(2,1)}), bf16[8,64,512]{2,1,0:T(8,128)(2,1)S(1)}, u32[]{:S(2)}, u32[]{:S(2)}) %all-to-all-start.1) | async-done | bytes 524320 | tf_op jit(solution)/shard_map/all_to_all | solution.py:213
  200.1 3.5 %all-to-all-start.2 = ((bf16[8,64,512]{2,1,0:T(8,128)(2,1)}), bf16[8,64,512]{2,1,0:T(8,128)(2,1)S(1)}, u32[]{:S(2)}, u32[]{:S(2)}) async-start(bf16[8,64,512]{2,1,0:T(8,128)(2,1)} %bitcast.36), calls=%async_computation.2 | async-start | bytes 1048576 | tf_op jit(solution)/shard_map/all_to_all | solution.py:213
  203.6 0.1 convolution_convert_fusion.2
  203.8 0.1 fusion.54
  203.9 10.0 %all-to-all-done.2 = bf16[8,64,512]{2,1,0:T(8,128)(2,1)S(1)} async-done(((bf16[8,64,512]{2,1,0:T(8,128)(2,1)}), bf16[8,64,512]{2,1,0:T(8,128)(2,1)S(1)}, u32[]{:S(2)}, u32[]{:S(2)}) %all-to-all-start.2) | async-done | bytes 524320 | tf_op jit(solution)/shard_map/all_to_all | solution.py:213
  213.9 0.4 fusion.56
  214.3 1.9 collective-permute-start.13
  216.3 8.1 %collective-permute-start.14 = (bf16[15,1024]{1,0:T(8,128)(2,1)S(1)}, bf16[15,1024]{1,0:T(8,128)(2,1)S(1)}, u32[]{:S(2)}, u32[]{:S(2)}) collective-permute-start(bf16[15,1024]{1,0:T(8,128)(2,1)S(1)} %get-tuple-element.60), channel_id=1, source_target_pairs={{1,0},{2,1},{3,2},{4,3},{5,4},{6,5},{7,6},{8,7},{9,8},{10,9},{11,1... | collective-permute-start | bytes 92168 | tf_op jit(solution)/shard_map/ppermute | solution.py:77
  224.4 0.2 fusion.37
  224.6 0.6 fusion.51
  225.2 0.5 collective-permute-done.14
  225.7 0.1 maximum_convert_fusion
  225.8 0.0 reduce-scatter.2.cloned.1.call-done
  225.9 3.8 %all-to-all-start.3 = ((bf16[4,32,1536]{2,1,0:T(8,128)(2,1)}), bf16[4,32,1536]{2,1,0:T(8,128)(2,1)S(1)}, u32[]{:S(2)}, u32[]{:S(2)}) async-start(bf16[4,32,1536]{2,1,0:T(8,128)(2,1)} %bitcast.127), calls=%async_computation.4 | async-start | bytes 786432 | tf_op jit(solution)/shard_map/all_to_all | solution.py:57
  229.6 3.7 %fusion.6 = bf16[192,1024]{1,0:T(8,128)(2,1)} fusion(f32[192,1024]{1,0:T(8,128)S(1)} %get-tuple-element.93, f32[222,1024]{1,0:T(8,128)S(1)} %maximum_convert_fusion, f32[1024]{0:T(1024)S(1)} %bitcast.142, f32[1024]{0:T(1024)S(1)} %bitcast.141, f32[1024]{0:T(1024)S(1)} %bitcast.140, f32[1024]{0:T(1024)S(1)} %bitcast.139, f32[1024]{0:T(1024)S(1)} %bitcast.138, ...), kind=kLoop, calls=%fused_computation.17 | loop fusion | flops 12386304 | bytes 25686016 | tf_op jit(solution)/shard_map/convert_element_type | solution.py:241
  233.3 2.5 %all-to-all-done.3 = bf16[4,32,1536]{2,1,0:T(8,128)(2,1)S(1)} async-done(((bf16[4,32,1536]{2,1,0:T(8,128)(2,1)}), bf16[4,32,1536]{2,1,0:T(8,128)(2,1)S(1)}, u32[]{:S(2)}, u32[]{:S(2)}) %all-to-all-start.3) | async-done | bytes 393248 | tf_op jit(solution)/shard_map/all_to_all | solution.py:57
  235.8 0.3 reshape.45
  236.1 0.4 copy.53
  236.4 1.0 reshape.46
  (56 shorter events, 0.5 us)
Async XLA Ops:
  7.2 105.7 %all-gather.3.cloned.1.call-start = ((), (), s32[]{:S(2)}) async-start(), calls=%async_computation.6 | async-start | bytes 27033600 | tf_op jit(solution)/shard_map/all_gather | solution.py:207
  13.5 11.5 %all-to-all-start = ((bf16[4,32,1536]{2,1,0:T(8,128)(2,1)}), bf16[4,32,1536]{2,1,0:T(8,128)(2,1)S(1)}, u32[]{:S(2)}, u32[]{:S(2)}) async-start(bf16[4,32,1536]{2,1,0:T(8,128)(2,1)} %reshape.38), calls=%async_computation | async-start | bytes 786432 | tf_op jit(solution)/shard_map/all_to_all | solution.py:42
  19.1 206.7 %reduce-scatter.2.cloned.1.call-start = ((), (), s32[]{:S(2)}) async-start(), calls=%async_computation.5 | async-start | bytes 3538944 | tf_op jit(solution)/shard_map/reduce_scatter | solution.py:56
  25.0 13.5 %collective-permute-start = (bf16[4,32,1536]{2,1,0:T(8,128)(2,1)S(1)}, bf16[4,32,1536]{2,1,0:T(8,128)(2,1)S(1)}, u32[]{:S(2)}, u32[]{:S(2)}) collective-permute-start(bf16[4,32,1536]{2,1,0:T(8,128)(2,1)S(1)} %all-to-all-done), channel_id=1, source_target_pairs={{0,8},{8,16},{16,24},{24,32},{32,40},{40,48},{48,56},{56,0},{1,9},... | collective-permute-start | bytes 1179656 | tf_op jit(solution)/shard_map/ppermute | solution.py:28
  26.9 11.6 %collective-permute-start.1 = (bf16[4,32,1536]{2,1,0:T(8,128)(2,1)S(1)}, bf16[4,32,1536]{2,1,0:T(8,128)(2,1)S(1)}, u32[]{:S(2)}, u32[]{:S(2)}) collective-permute-start(bf16[4,32,1536]{2,1,0:T(8,128)(2,1)S(1)} %all-to-all-done), channel_id=1, source_target_pairs={{8,0},{16,8},{24,16},{32,24},{40,32},{48,40},{56,48},{0,56},{9,1},... | collective-permute-start | bytes 1179656 | tf_op jit(solution)/shard_map/ppermute | solution.py:31
  38.5 10.0 %collective-permute-start.2 = (bf16[4,32,1536]{2,1,0:T(8,128)(2,1)S(1)}, bf16[4,32,1536]{2,1,0:T(8,128)(2,1)S(1)}, u32[]{:S(2)}, u32[]{:S(2)}) collective-permute-start(bf16[4,32,1536]{2,1,0:T(8,128)(2,1)S(1)} %collective-permute-done), channel_id=1, source_target_pairs={{0,8},{8,16},{16,24},{24,32},{32,40},{40,48},{48,56},{56,0},{1,9},... | collective-permute-start | bytes 1179656 | tf_op jit(solution)/shard_map/ppermute | solution.py:28
  38.5 10.0 %collective-permute-start.3 = (bf16[4,32,1536]{2,1,0:T(8,128)(2,1)S(1)}, bf16[4,32,1536]{2,1,0:T(8,128)(2,1)S(1)}, u32[]{:S(2)}, u32[]{:S(2)}) collective-permute-start(bf16[4,32,1536]{2,1,0:T(8,128)(2,1)S(1)} %collective-permute-done.1), channel_id=1, source_target_pairs={{8,0},{16,8},{24,16},{32,24},{40,32},{48,40},{56,48},{0,56},{9,1},... | collective-permute-start | bytes 1179656 | tf_op jit(solution)/shard_map/ppermute | solution.py:31
  48.6 9.3 %collective-permute-start.4 = (bf16[4,32,1536]{2,1,0:T(8,128)(2,1)S(1)}, bf16[4,32,1536]{2,1,0:T(8,128)(2,1)S(1)}, u32[]{:S(2)}, u32[]{:S(2)}) collective-permute-start(bf16[4,32,1536]{2,1,0:T(8,128)(2,1)S(1)} %collective-permute-done.2), channel_id=1, source_target_pairs={{0,8},{8,16},{16,24},{24,32},{32,40},{40,48},{48,56},{56,0},{1,9},... | collective-permute-start | bytes 1179656 | tf_op jit(solution)/shard_map/ppermute | solution.py:28
  48.6 9.3 %collective-permute-start.5 = (bf16[4,32,1536]{2,1,0:T(8,128)(2,1)S(1)}, bf16[4,32,1536]{2,1,0:T(8,128)(2,1)S(1)}, u32[]{:S(2)}, u32[]{:S(2)}) collective-permute-start(bf16[4,32,1536]{2,1,0:T(8,128)(2,1)S(1)} %collective-permute-done.3), channel_id=1, source_target_pairs={{8,0},{16,8},{24,16},{32,24},{40,32},{48,40},{56,48},{0,56},{9,1},... | collective-permute-start | bytes 1179656 | tf_op jit(solution)/shard_map/ppermute | solution.py:31
  57.8 9.0 %collective-permute-start.6 = (bf16[4,32,1536]{2,1,0:T(8,128)(2,1)S(1)}, bf16[4,32,1536]{2,1,0:T(8,128)(2,1)S(1)}, u32[]{:S(2)}, u32[]{:S(2)}) collective-permute-start(bf16[4,32,1536]{2,1,0:T(8,128)(2,1)S(1)} %collective-permute-done.4), channel_id=1, source_target_pairs={{0,8},{8,16},{16,24},{24,32},{32,40},{40,48},{48,56},{56,0},{1,9},... | collective-permute-start | bytes 1179656 | tf_op jit(solution)/shard_map/ppermute | solution.py:28
  66.9 1.7 copy-start
  123.6 22.0 %collective-permute-start.7 = (bf16[512,512]{1,0:T(8,128)(2,1)S(1)}, bf16[512,512]{1,0:T(8,128)(2,1)S(1)}, u32[]{:S(2)}, u32[]{:S(2)}) collective-permute-start(bf16[512,512]{1,0:T(8,128)(2,1)S(1)} %get-tuple-element.31), channel_id=1, source_target_pairs={{0,64},{64,128},{128,192},{192,0},{1,65},{65,129},{129,193},{193,1... | collective-permute-start | bytes 1572872 | tf_op jit(solution)/shard_map/ppermute | solution.py:174
  125.1 20.5 %collective-permute-start.8 = (bf16[512,512]{1,0:T(8,128)(2,1)S(1)}, bf16[512,512]{1,0:T(8,128)(2,1)S(1)}, u32[]{:S(2)}, u32[]{:S(2)}) collective-permute-start(bf16[512,512]{1,0:T(8,128)(2,1)S(1)} %get-tuple-element.32), channel_id=1, source_target_pairs={{64,0},{128,64},{192,128},{0,192},{65,1},{129,65},{193,129},{1,193... | collective-permute-start | bytes 1572872 | tf_op jit(solution)/shard_map/ppermute | solution.py:174
  143.0 21.0 %collective-permute-start.10 = (bf16[512,512]{1,0:T(8,128)(2,1)S(1)}, bf16[512,512]{1,0:T(8,128)(2,1)S(1)}, u32[]{:S(2)}, u32[]{:S(2)}) collective-permute-start(bf16[512,512]{1,0:T(8,128)(2,1)S(1)} %slice.220), channel_id=1, source_target_pairs={{0,64},{64,128},{128,192},{192,0},{1,65},{65,129},{129,193},{193,1... | collective-permute-start | bytes 1572872 | tf_op jit(solution)/shard_map/ppermute | solution.py:174
  144.6 19.4 %collective-permute-start.11 = (bf16[512,512]{1,0:T(8,128)(2,1)S(1)}, bf16[512,512]{1,0:T(8,128)(2,1)S(1)}, u32[]{:S(2)}, u32[]{:S(2)}) collective-permute-start(bf16[512,512]{1,0:T(8,128)(2,1)S(1)} %slice.221), channel_id=1, source_target_pairs={{64,0},{128,64},{192,128},{0,192},{65,1},{129,65},{193,129},{1,193... | collective-permute-start | bytes 1572872 | tf_op jit(solution)/shard_map/ppermute | solution.py:174
  145.6 10.2 %copy-start.5 = (bf16[512,512]{1,0:T(8,128)(2,1)}, bf16[512,512]{1,0:T(8,128)(2,1)S(1)}, u32[]{:S(2)}) copy-start(bf16[512,512]{1,0:T(8,128)(2,1)S(1)} %collective-permute-done.7) | copy-start | bytes 1572868
  145.6 10.2 %copy-start.4 = (bf16[512,512]{1,0:T(8,128)(2,1)}, bf16[512,512]{1,0:T(8,128)(2,1)S(1)}, u32[]{:S(2)}) copy-start(bf16[512,512]{1,0:T(8,128)(2,1)S(1)} %collective-permute-done.8) | copy-start | bytes 1572868
  155.8 8.2 %copy-start.1 = (bf16[2048,1024]{1,0:T(8,128)(2,1)S(1)}, bf16[2048,1024]{1,0:T(8,128)(2,1)}, u32[]{:S(2)}) copy-start(bf16[2048,1024]{1,0:T(8,128)(2,1)} %get-tuple-element.57) | copy-start | bytes 12582916
  155.8 8.2 %copy-start.2 = (bf16[2048,512]{1,0:T(8,128)(2,1)S(1)}, bf16[2048,512]{1,0:T(8,128)(2,1)}, u32[]{:S(2)}) copy-start(bf16[2048,512]{1,0:T(8,128)(2,1)} %get-tuple-element.58) | copy-start | bytes 6291460
  164.0 2.4 copy-start.6
  164.1 2.4 copy-start.8
  168.7 2.5 %copy-start.3 = (bf16[1024,512]{1,0:T(8,128)(2,1)S(1)}, bf16[1024,512]{1,0:T(8,128)(2,1)}, u32[]{:S(2)}) copy-start(bf16[1024,512]{1,0:T(8,128)(2,1)} %get-tuple-element.49) | copy-start | bytes 3145732
  168.7 6.0 %copy-start.12 = (s32[192,2]{0,1:T(2,128)S(1)}, s32[192,2]{0,1:T(2,128)}, u32[]{:S(2)}) copy-start(s32[192,2]{0,1:T(2,128)} %param.9) | copy-start | bytes 4612
  168.7 15.8 %copy-start.9 = (bf16[512,512]{1,0:T(8,128)(2,1)S(1)}, bf16[512,512]{1,0:T(8,128)(2,1)}, u32[]{:S(2)}) copy-start(bf16[512,512]{1,0:T(8,128)(2,1)} %copy-done.8) | copy-start | bytes 1572868
  170.0 19.8 %copy-start.7 = (bf16[512,512]{1,0:T(8,128)(2,1)S(1)}, bf16[512,512]{1,0:T(8,128)(2,1)}, u32[]{:S(2)}) copy-start(bf16[512,512]{1,0:T(8,128)(2,1)} %copy-done.6) | copy-start | bytes 1572868
  170.0 14.5 %collective-permute-start.9 = (bf16[512,512]{1,0:T(8,128)(2,1)S(1)}, bf16[512,512]{1,0:T(8,128)(2,1)S(1)}, u32[]{:S(2)}, u32[]{:S(2)}) collective-permute-start(bf16[512,512]{1,0:T(8,128)(2,1)S(1)} %add_convert_fusion.3), channel_id=1, source_target_pairs={{0,64},{64,128},{128,192},{192,0},{1,65},{65,129},{129,193},{193,1... | collective-permute-start | bytes 1572872 | tf_op jit(solution)/shard_map/ppermute | solution.py:174
  172.4 17.4 %collective-permute-start.12 = (bf16[512,512]{1,0:T(8,128)(2,1)S(1)}, bf16[512,512]{1,0:T(8,128)(2,1)S(1)}, u32[]{:S(2)}, u32[]{:S(2)}) collective-permute-start(bf16[512,512]{1,0:T(8,128)(2,1)S(1)} %add_convert_fusion.1), channel_id=1, source_target_pairs={{64,0},{128,64},{192,128},{0,192},{65,1},{129,65},{193,129},{1,193... | collective-permute-start | bytes 1572872 | tf_op jit(solution)/shard_map/ppermute | solution.py:174
  184.6 19.2 %copy-start.11 = (bf16[31,1024]{1,0:T(8,128)(2,1)S(1)}, bf16[31,1024]{1,0:T(8,128)(2,1)}, u32[]{:S(2)}) copy-start(bf16[31,1024]{1,0:T(8,128)(2,1)} %param.10) | copy-start | bytes 190468
  184.6 29.3 %copy-start.10 = (bf16[192,1024]{1,0:T(8,128)(2,1)S(1)}, bf16[192,1024]{1,0:T(8,128)(2,1)}, u32[]{:S(2)}) copy-start(bf16[192,1024]{1,0:T(8,128)(2,1)} %param.7) | copy-start | bytes 1179652
  185.6 14.6 %all-to-all-start.1 = ((bf16[8,64,512]{2,1,0:T(8,128)(2,1)}), bf16[8,64,512]{2,1,0:T(8,128)(2,1)S(1)}, u32[]{:S(2)}, u32[]{:S(2)}) async-start(bf16[8,64,512]{2,1,0:T(8,128)(2,1)} %bitcast.35), calls=%async_computation.1 | async-start | bytes 1048576 | tf_op jit(solution)/shard_map/all_to_all | solution.py:213
  190.8 33.8 %copy-start.13 = (bf16[192,2]{0,1:T(2,128)(2,1)S(1)}, bf16[192,2]{0,1:T(2,128)(2,1)}, u32[]{:S(2)}) copy-start(bf16[192,2]{0,1:T(2,128)(2,1)} %param.8) | copy-start | bytes 2308
  200.1 13.8 %all-to-all-start.2 = ((bf16[8,64,512]{2,1,0:T(8,128)(2,1)}), bf16[8,64,512]{2,1,0:T(8,128)(2,1)S(1)}, u32[]{:S(2)}, u32[]{:S(2)}) async-start(bf16[8,64,512]{2,1,0:T(8,128)(2,1)} %bitcast.36), calls=%async_computation.2 | async-start | bytes 1048576 | tf_op jit(solution)/shard_map/all_to_all | solution.py:213
  214.3 10.9 %collective-permute-start.13 = (bf16[15,1024]{1,0:T(8,128)(2,1)S(1)}, bf16[15,1024]{1,0:T(8,128)(2,1)S(1)}, u32[]{:S(2)}, u32[]{:S(2)}) collective-permute-start(bf16[15,1024]{1,0:T(8,128)(2,1)S(1)} %get-tuple-element.59), channel_id=1, source_target_pairs={{0,1},{1,2},{2,3},{3,4},{4,5},{5,6},{6,7},{7,8},{8,9},{9,10},{10,1... | collective-permute-start | bytes 92168 | tf_op jit(solution)/shard_map/ppermute | solution.py:76
  216.3 9.4 %collective-permute-start.14 = (bf16[15,1024]{1,0:T(8,128)(2,1)S(1)}, bf16[15,1024]{1,0:T(8,128)(2,1)S(1)}, u32[]{:S(2)}, u32[]{:S(2)}) collective-permute-start(bf16[15,1024]{1,0:T(8,128)(2,1)S(1)} %get-tuple-element.60), channel_id=1, source_target_pairs={{1,0},{2,1},{3,2},{4,3},{5,4},{6,5},{7,6},{8,7},{9,8},{10,9},{11,1... | collective-permute-start | bytes 92168 | tf_op jit(solution)/shard_map/ppermute | solution.py:77
  225.9 9.9 %all-to-all-start.3 = ((bf16[4,32,1536]{2,1,0:T(8,128)(2,1)}), bf16[4,32,1536]{2,1,0:T(8,128)(2,1)S(1)}, u32[]{:S(2)}, u32[]{:S(2)}) async-start(bf16[4,32,1536]{2,1,0:T(8,128)(2,1)} %bitcast.127), calls=%async_computation.4 | async-start | bytes 786432 | tf_op jit(solution)/shard_map/all_to_all | solution.py:57
Sparse Core Ops, SparseCore 0:
  10.8 101.9 all-gather.2
  168.8 48.1 reduce-scatter.1

commit v5 on v4

v5 whole, which is shorter than its diff:
```python
import functools

import jax
import jax.numpy as jnp
from jax import lax
from jax.experimental import pallas as pl
from jax.experimental.pallas import tpu as pltpu
from jax.sharding import Mesh, PartitionSpec as P

BF = jnp.bfloat16
F32 = jnp.float32
SLOTS = 64
SPARE = 60
META = 8
STEP = 4
CHUNK = 256


def dot(a, b, contract, batch=((), ())):
    return lax.dot_general(a, b, (contract, batch), preferred_element_type=F32)


def ring_gather(shard, axis, place, buffer):
    count = lax.axis_size(axis)
    me = lax.axis_index(axis)
    up = [(i, (i + 1) % count) for i in range(count)]
    down = [(target, source) for source, target in up]
    buffer = place(buffer, shard, me)
    right = left = shard
    for step in range(1, count // 2 + 1):
        right = lax.ppermute(right, axis, up)
        buffer = place(buffer, right, (me - step) % count)
        if step < count - step:
            left = lax.ppermute(left, axis, down)
            buffer = place(buffer, left, (me + step) % count)
    return buffer


def gather_weights(expert_weights):
    ny, nz = lax.axis_size("y"), lax.axis_size("z")
    rows, width = expert_weights.shape[1], expert_weights.shape[2]
    part = width // (3 * ny)
    sliced = expert_weights[0].reshape(rows, 3, ny, part).transpose(2, 0, 1, 3)
    sliced = sliced.reshape(ny, rows, 3 * part)
    mine = lax.all_to_all(sliced, "y", 0, 0, tiled=True)

    def place(buffer, shard, z):
        return lax.dynamic_update_slice(buffer, shard[:, None], (0, z, 0, 0))

    buffer = ring_gather(mine, "z", place, jnp.zeros((ny, nz, rows, 3 * part), BF))
    return buffer.reshape(ny * nz * rows, 3 * part)


def scatter_weight_grad(term):
    ny, nz = lax.axis_size("y"), lax.axis_size("z")
    rows = term.shape[0] // (ny * nz)
    part = term.shape[1] // 3
    blocks = term.reshape(ny, nz, rows, 3 * part).transpose(1, 0, 2, 3)
    mine = lax.psum_scatter(blocks.reshape(nz * ny * rows, 3 * part), "z", scatter_dimension=0, tiled=True)
    back = lax.all_to_all(mine.reshape(ny, rows, 3 * part), "y", 0, 0, tiled=True)
    back = back.reshape(ny, rows, 3, part).transpose(1, 2, 0, 3)
    return back.reshape(1, rows, 3 * ny * part)


def slots_of(chosen):
    frames = chosen.shape[-1]
    before = (jnp.arange(frames)[:, None] < jnp.arange(frames)[None, :]).astype(BF)
    ranks = dot(chosen.astype(BF), before, ((chosen.ndim - 1,), (0,))).astype(jnp.int32)
    return chosen[..., None, :] & (ranks[..., None, :] == jnp.arange(SLOTS)[:, None])


def with_halo(block, width):
    axes = ("y", "z", "x", "c")
    count = 1
    for axis in axes:
        count *= lax.axis_size(axis)
    forward = [(i, i + 1) for i in range(count - 1)]
    backward = [(target, source) for source, target in forward]
    low = lax.ppermute(block[block.shape[0] - width :], axes, forward)
    high = lax.ppermute(block[:width], axes, backward)
    return jnp.concatenate([low, block, high], axis=0)


def route_kernel(scaled, x_ref, out_ref):
    rows, width = x_ref.shape[1:]
    frames, experts = rows - META, out_ref.shape[0]
    meta = x_ref[0, frames:rows, :frames].astype(F32)
    names = lax.broadcasted_iota(jnp.int32, (experts, frames), 0).astype(F32)
    first, second = (names == meta[0:1]).astype(F32), (names == meta[1:2]).astype(F32)
    chosen = first + second
    gate = first * meta[2:3] + second * meta[3:4] if scaled else chosen
    earlier = lax.broadcasted_iota(jnp.int32, (frames, frames), 0)
    before = (earlier < lax.broadcasted_iota(jnp.int32, (frames, frames), 1)).astype(F32).astype(BF)
    ranks = dot(chosen.astype(BF), before, ((1,), (0,)))
    slot = lax.broadcasted_iota(jnp.int32, (SLOTS, frames), 0).astype(F32)
    for e in range(experts):
        here = (slot == ranks[e : e + 1]) & (chosen[e : e + 1] > 0.0)
        placing = jnp.where(here, gate[e : e + 1], 0.0).astype(BF)
        out_ref[e, 0] = dot(placing, x_ref[0, :frames], ((1,), (0,))).astype(BF)


def route(packed, experts, scaled):
    groups, rows, width = packed.shape
    return pl.pallas_call(
        functools.partial(route_kernel, scaled),
        grid=(groups,),
        in_specs=[pl.BlockSpec((1, rows, width), lambda i: (i, 0, 0))],
        out_specs=pl.BlockSpec((experts, 1, SLOTS, width), lambda i: (0, i, 0, 0)),
        out_shape=jax.ShapeDtypeStruct((experts, groups, SLOTS, width), BF),
        compiler_params=pltpu.CompilerParams(vmem_limit_bytes=32 * 1024 * 1024),
    )(packed)


def rows_kernel(info, u_ref, q_ref, w_ref, *refs):
    low_ref, high_ref, pre_ref, h_ref = refs[-4:]
    steps, width, part, half = u_ref.shape[1], u_ref.shape[3], h_ref.shape[3], low_ref.shape[1]
    count = steps * SLOTS
    u, q = u_ref[0].reshape(count, width), q_ref[:, 0].reshape(count, width)
    gate_part = 0.0
    for c in range(0, part, CHUNK):
        gate_in = dot(u, w_ref[:, c : c + CHUNK], ((1,), (0,)))
        up_in = dot(u, w_ref[:, part + c : part + c + CHUNK], ((1,), (0,)))
        hidden_grad = dot(q, w_ref[:, 2 * part + c : 2 * part + c + CHUNK], ((1,), (0,)))
        sigmoid = jax.nn.sigmoid(gate_in)
        activated = gate_in * sigmoid
        hidden = (activated * up_in).astype(BF)
        h_ref[:, 0, :, c : c + CHUNK] = hidden.reshape(steps, SLOTS, CHUNK)
        slope = sigmoid * (1.0 + gate_in * (1.0 - sigmoid))
        pre_ref[:, c : c + CHUNK] = (hidden_grad * up_in * slope).astype(BF)
        pre_ref[:, part + c : part + c + CHUNK] = (hidden_grad * activated).astype(BF)
        gate_part += jnp.sum(hidden.astype(F32) * hidden_grad, axis=1, keepdims=True)
    row_grad = dot(pre_ref[...], w_ref[:, : 2 * part], ((1,), (1,)))
    high_ref[...] = row_grad[:, half:].astype(BF)
    low_ref[...] = row_grad[:, :half].astype(BF)
    row = lax.broadcasted_iota(jnp.int32, (SLOTS, 128), 0)
    lane = lax.broadcasted_iota(jnp.int32, (SLOTS, 128), 1)
    for j in range(steps):
        place = pl.ds(j * SLOTS, SLOTS)
        diagonal = jnp.where(row == lane, gate_part[j * SLOTS : (j + 1) * SLOTS], 0.0)
        line = jnp.sum(diagonal, axis=0, keepdims=True)
        low_ref[place, :128] = jnp.where(row == SPARE, line, low_ref[place, :128].astype(F32)).astype(BF)


def expert_rows(targets, rows_in, rows_q, weights, kept):
    groups, sources, _, width = rows_in.shape
    part = weights.shape[1] // 3
    steps = sources // STEP
    mine = len(targets) * sources * SLOTS
    info = jnp.stack(targets).astype(jnp.int32)
    by_group = lambda i, info: (info[i // steps], i % steps, 0, 0)
    by_source = lambda i, info: (i % steps, info[i // steps], 0, 0)
    in_order = lambda i, info: (i, 0)
    low, high, *kept = pl.pallas_call(
        rows_kernel,
        grid_spec=pltpu.PrefetchScalarGridSpec(
            num_scalar_prefetch=1,
            grid=(len(targets) * steps,),
            in_specs=[
                pl.BlockSpec((1, STEP, SLOTS, width), by_group),
                pl.BlockSpec((STEP, 1, SLOTS, width), by_source),
                pl.BlockSpec(weights.shape, lambda i, info: (0, 0)),
            ]
            + [pl.BlockSpec(memory_space=pl.ANY) for _ in kept],
            out_specs=[
                pl.BlockSpec((STEP * SLOTS, width // 2), in_order),
                pl.BlockSpec((STEP * SLOTS, width // 2), in_order),
                pl.BlockSpec((STEP * SLOTS, 2 * part), lambda i, info: (info[i // steps] * steps + i % steps, 0)),
                pl.BlockSpec((STEP, 1, SLOTS, part), by_source),
            ],
        ),
        out_shape=[
            jax.ShapeDtypeStruct((mine, width // 2), BF),
            jax.ShapeDtypeStruct((mine, width // 2), BF),
            jax.ShapeDtypeStruct((groups * sources * SLOTS, 2 * part), BF),
            jax.ShapeDtypeStruct((sources, groups, SLOTS, part), BF),
        ],
        input_output_aliases={4 + k: 2 + k for k in range(len(kept))},
        compiler_params=pltpu.CompilerParams(vmem_limit_bytes=52 * 1024 * 1024),
    )(info, rows_in, rows_q, weights, *kept)
    return low, high, kept


def add(*parts):
    return sum(part.astype(F32) for part in parts)


def rows_backward(rows_in, rows_q, weights):
    ny = lax.axis_size("y")
    me = lax.axis_index("y")
    width = rows_in.shape[3]
    up = [(i, (i + 1) % ny) for i in range(ny)]
    down = [(target, source) for source, target in up]

    def send(rows, way):
        return lax.ppermute(rows, "y", way)

    def run(offsets, kept):
        return expert_rows([(me + offset) % ny for offset in offsets], rows_in, rows_q, weights, kept)

    far_low, far_high, kept = run([2], [])
    low_via, high_via = send(far_low, up), send(far_high, down)
    near_low, near_high, kept = run([1, ny - 1], kept)
    low_via, high_via, kept = lax.optimization_barrier((low_via, high_via, kept))
    rows = far_low.shape[0]
    below_high, above_low = send(near_high[:rows], up), send(near_low[rows:], down)
    below_low = send(add(near_low[:rows], low_via).astype(BF), up)
    above_high = send(add(near_high[rows:], high_via).astype(BF), down)
    own_low, own_high, kept = run([0], kept)
    pre_grads, hidden = kept
    first = dot(rows_in.reshape(-1, width), pre_grads, ((0,), (0,))).astype(BF)
    rows_q, below_high, above_low, first = lax.optimization_barrier((rows_q, below_high, above_low, first))
    second = dot(rows_q.reshape(-1, width), hidden.reshape(-1, hidden.shape[3]), ((0,), (0,))).astype(BF)
    term = jnp.concatenate([first, second], axis=1)
    low = add(own_low, below_low, above_low).astype(BF)
    high = add(own_high, below_high, above_high).astype(BF)
    return low, high, term


def local(block_in, out_grad, gate_values, expert_ids, conv_kernel, expert_weights):
    frames, width = block_in.shape
    ny, experts = lax.axis_size("y"), lax.axis_size("x") * lax.axis_size("c")
    by_expert = ("x", "c")

    meta = jnp.concatenate([expert_ids.astype(BF).T, gate_values.T], axis=0)
    meta = jnp.pad(meta, ((0, META - 4), (0, width - frames)))
    all_grad = lax.all_gather(jnp.concatenate([out_grad, meta], axis=0), "y", axis=0, tiled=False)
    sent_in = route(jnp.concatenate([block_in, meta], axis=0)[None], experts, False)
    mine_in = lax.all_to_all(sent_in, by_expert, 0, 0, tiled=True)
    rows_in = lax.all_gather(mine_in[:, 0], "y", axis=0, tiled=False)
    sent_q = route(all_grad, experts, True)
    rows_q = lax.all_to_all(sent_q, by_expert, 0, 0, tiled=True)
    weights = gather_weights(expert_weights)
    low, high, term = rows_backward(rows_in, rows_q, weights)
    weight_grad = scatter_weight_grad(term)
    summed = jnp.concatenate([low, high], axis=1).reshape(experts, SLOTS, width)
    returned = lax.all_to_all(summed, by_expert, 0, 0, tiled=True)

    own_ids = expert_ids.T[None] == jnp.arange(experts, dtype=jnp.int32)[:, None, None]
    own = slots_of(own_ids[:, 0] | own_ids[:, 1])
    own_placing = own.astype(BF)
    flat = own_placing.reshape(experts * SLOTS, frames)
    frame_grad = out_grad.astype(F32) + dot(
        flat, returned.reshape(experts * SLOTS, width), ((0,), (0,))
    )
    gate_sums = jnp.einsum(
        "es,est,ekt->tk",
        returned[:, SPARE, :SLOTS].astype(F32),
        own.astype(F32),
        own_ids.astype(F32),
        precision="highest",
    )
    gate_out = (gate_sums / gate_values.astype(F32)).astype(BF)

    taps = conv_kernel.shape[0]
    half = (taps - 1) // 2
    kernel_rows = conv_kernel.astype(F32)
    padded = with_halo(frame_grad.astype(BF), half).astype(F32)
    conv_part = jnp.zeros((frames, width), F32)
    for offset in range(taps):
        conv_part = conv_part + kernel_rows[offset] * padded[2 * half - offset : 2 * half - offset + frames]
    input_grad = (frame_grad + conv_part).astype(BF)
    return input_grad, weight_grad, gate_out


def solution(mesh):
    grid = Mesh(mesh.devices.reshape(4, 8, 4, 2), ("y", "z", "x", "c"))
    frames = P(("y", "z", "x", "c"), None)
    weights = P(("x", "c"), ("y", "z"), None)
    in_specs = (frames, frames, frames, frames, P(), weights)
    out_specs = (frames, weights, frames)
    return jax.shard_map(local, mesh=grid, in_specs=in_specs, out_specs=out_specs, check_vma=False)
```

time: 248 us -> 229 us (0.923); the launches traced: 244 us -> 228 us
  waiting for transfers between devices: 108 us -> 85.1 us
  blocking collectives: 0 us -> 20.3 us
  Pallas kernels: 37.1 us -> 27.6 us
  starting transfers between devices: 47.5 us -> 42.5 us
    all_gather x1 -> x2, waiting for transfers between devices: 41.4 us -> 0.01 us  [the longest x1 0.01 us: local(): rows_in = lax.all_gather(mine_in[:, 0], 'y', axis=0, tiled=False)]
    all_to_all x0 -> x1, blocking collectives: none -> 20.3 us  [local(): mine_in = lax.all_to_all(sent_in, by_expert, 0, 0, tiled=True)]
    pallas_call x3, Pallas kernels: 37.1 us -> 23.2 us  [expert_rows(): pl.pallas_call(rows_kernel, grid_spec=pltpu.PrefetchScalarGridSpec(num_sc...]
    all_to_all x2, waiting for transfers between devices: 19.3 us -> 29 us  [the longest x1 15.6 us: local(): returned = lax.all_to_all(summed, by_expert, 0, 0, tiled=True)]
    ppermute x1, waiting for transfers between devices: 0.01 us -> 6.79 us  [with_halo(): low = lax.ppermute(block[block.shape[0] - width:], axes, forward)]
    pallas_call x0 -> x2, Pallas kernels: none -> 4.41 us  [route(): pl.pallas_call(functools.partial(route_kernel, scaled), grid=(groups,), i...]
    ppermute x1, starting transfers between devices: 8.08 us -> 4.69 us  [with_halo(): high = lax.ppermute(block[:width], axes, backward)]
  transfers between devices with their start and end apart: 21 -> 22, of which waited for: 11 -> 10; matrix products, arithmetic and copies ran while one was open for 10% -> 10% of each run, Pallas kernels for 11% -> 9%
where the time goes in v5:
time: 229 us; the launch traced here: 228 us
  waiting for transfers between devices  85.1 us (37%)
  starting transfers between devices  42.5 us (19%)
  Pallas kernels  27.6 us (12%)
  blocking collectives  20.3 us (9%)
  between operations  14.2 us (6%)
  local copies, waits for them, and re-layouts  13.9 us (6%)
  matrix products  12.8 us (6%)
  other arithmetic  12.1 us (5%)
    ppermute x4, waiting for transfers between devices, ring_gather(): right = lax.ppermute(right, axis, up)  27 us
    pallas_call x3, Pallas kernels, expert_rows(): pl.pallas_call(rows_kernel, grid_spec=pltpu.PrefetchScalarGridSpec(num_sc...  23.2 us
    all_to_all x1, blocking collectives, local(): mine_in = lax.all_to_all(sent_in, by_expert, 0, 0, tiled=True)  20.3 us
    all_to_all x1, waiting for transfers between devices, local(): returned = lax.all_to_all(summed, by_expert, 0, 0, tiled=True)  15.6 us
    all_to_all x1, waiting for transfers between devices, local(): rows_q = lax.all_to_all(sent_q, by_expert, 0, 0, tiled=True)  13.4 us
    dot_general x4, matrix products, dot(): return lax.dot_general(a, b, (contract, batch), preferred_element_type=F32)  12.6 us
    ppermute x6, waiting for transfers between devices, send(): return lax.ppermute(rows, 'y', way)  11.9 us
    ppermute x3, starting transfers between devices, ring_gather(): left = lax.ppermute(left, axis, down)  8.82 us
  transfers between devices with their start and end apart: 22, of which 10 were waited for; matrix products, arithmetic and copies ran while one was open for 10% of the time, Pallas kernels for 9%

profile of v5, /device:TPU:8, one launch (start us, length us, event | category | flops | bytes accessed | tf_op | source)
XLA Modules:
  0.0 228.4 jit_solution(2202262433756669135)
XLA Ops:
  7.2 0.7 convert_bitcast_fusion
  7.9 0.7 fusion.47
  8.6 2.0 pad_maximum_fusion.2
  10.7 0.8 shard_map.85
  11.5 20.3 %all_to_all.25 = bf16[8,1,64,1024]{3,2,1,0:T(8,128)(2,1)} all-to-all(bf16[8,1,64,1024]{3,2,1,0:T(8,128)(2,1)S(1)} %shard_map.85), channel_id=1, replica_groups=mesh['y'=4,'z'=8,'x'=4,'c'=2] {'x','c'}, dimensions={0} | all-to-all | bytes 2097152 | tf_op jit(solution)/shard_map/all_to_all | solution.py:228
  31.8 0.3 reshape_squeeze.3
  32.1 0.2 copy.72
  32.3 1.3 reshape.40
  33.6 4.9 %all-to-all-start.2 = ((bf16[4,32,1536]{2,1,0:T(8,128)(2,1)}), bf16[4,32,1536]{2,1,0:T(8,128)(2,1)S(1)}, u32[]{:S(2)}, u32[]{:S(2)}) async-start(bf16[4,32,1536]{2,1,0:T(8,128)(2,1)} %reshape.40), calls=%async_computation.2 | async-start | bytes 786432 | tf_op jit(solution)/shard_map/all_to_all | solution.py:45
  38.5 8.2 %all-to-all-done.2 = bf16[4,32,1536]{2,1,0:T(8,128)(2,1)S(1)} async-done(((bf16[4,32,1536]{2,1,0:T(8,128)(2,1)}), bf16[4,32,1536]{2,1,0:T(8,128)(2,1)S(1)}, u32[]{:S(2)}, u32[]{:S(2)}) %all-to-all-start.2) | async-done | bytes 393248 | tf_op jit(solution)/shard_map/all_to_all | solution.py:45
  46.7 1.6 collective-permute-start
  48.3 2.4 %collective-permute-start.1 = (bf16[4,32,1536]{2,1,0:T(8,128)(2,1)S(1)}, bf16[4,32,1536]{2,1,0:T(8,128)(2,1)}, u32[]{:S(2)}, u32[]{:S(2)}) collective-permute-start(bf16[4,32,1536]{2,1,0:T(8,128)(2,1)S(1)} %all-to-all-done.2), channel_id=1, source_target_pairs={{8,0},{16,8},{24,16},{32,24},{40,32},{48,40},{56,48},{0,56},{9,1},... | collective-permute-start | bytes 1179656 | tf_op jit(solution)/shard_map/ppermute | solution.py:34
  50.6 1.4 copy-done.1
  52.1 3.6 %shard_map.86 = bf16[8,4,64,1024]{3,2,1,0:T(8,128)(2,1)S(1)} custom-call(bf16[4,200,1024]{2,1,0:T(8,128)(2,1)S(1)} %bitcast.113), custom_call_target="tpu_custom_call" | custom-call | tf_op jit(solution)/shard_map/pallas_call | solution.py:104
  55.7 2.0 copy-done
  57.7 4.6 %all-to-all-start.1 = ((bf16[8,4,64,1024]{3,2,1,0:T(8,128)(2,1)}), bf16[8,4,64,1024]{3,2,1,0:T(8,128)(2,1)}, u32[]{:S(2)}, u32[]{:S(2)}) async-start(bf16[8,4,64,1024]{3,2,1,0:T(8,128)(2,1)} %copy-done), calls=%async_computation.1 | async-start | bytes 8388608 | tf_op jit(solution)/shard_map/all_to_all | solution.py:231
  62.4 0.3 broadcast_in_dim.37
  62.8 0.1 collective-permute-start.2
  62.9 3.2 %collective-permute-start.3 = (bf16[4,32,1536]{2,1,0:T(8,128)(2,1)}, bf16[4,32,1536]{2,1,0:T(8,128)(2,1)S(1)}, u32[]{:S(2)}, u32[]{:S(2)}) collective-permute-start(bf16[4,32,1536]{2,1,0:T(8,128)(2,1)} %collective-permute-done.1), channel_id=1, source_target_pairs={{8,0},{16,8},{24,16},{32,24},{40,32},{48,40},{56,48},{0,56},{9,1},... | collective-permute-start | bytes 1179656 | tf_op jit(solution)/shard_map/ppermute | solution.py:34
  66.1 1.0 bitcast_dynamic-update-slice_fusion.6
  67.1 1.0 bitcast_dynamic-update-slice_fusion.5
  68.2 7.5 %collective-permute-done.2 = bf16[4,32,1536]{2,1,0:T(8,128)(2,1)S(1)} collective-permute-done((bf16[4,32,1536]{2,1,0:T(8,128)(2,1)}, bf16[4,32,1536]{2,1,0:T(8,128)(2,1)S(1)}, u32[]{:S(2)}, u32[]{:S(2)}) %collective-permute-start.2) | collective-permute-done | bytes 393248 | tf_op jit(solution)/shard_map/ppermute | solution.py:31
  75.6 3.2 %collective-permute-start.5 = (bf16[4,32,1536]{2,1,0:T(8,128)(2,1)S(1)}, bf16[4,32,1536]{2,1,0:T(8,128)(2,1)S(1)}, u32[]{:S(2)}, u32[]{:S(2)}) collective-permute-start(bf16[4,32,1536]{2,1,0:T(8,128)(2,1)S(1)} %collective-permute-done.3), channel_id=1, source_target_pairs={{8,0},{16,8},{24,16},{32,24},{40,32},{48,40},{56,48},{0,56},{9,1},... | collective-permute-start | bytes 1179656 | tf_op jit(solution)/shard_map/ppermute | solution.py:34
  78.9 8.6 %collective-permute-done.4 = bf16[4,32,1536]{2,1,0:T(8,128)(2,1)S(1)} collective-permute-done((bf16[4,32,1536]{2,1,0:T(8,128)(2,1)S(1)}, bf16[4,32,1536]{2,1,0:T(8,128)(2,1)S(1)}, u32[]{:S(2)}, u32[]{:S(2)}) %collective-permute-start.4) | collective-permute-done | bytes 393248 | tf_op jit(solution)/shard_map/ppermute | solution.py:31
  87.6 11.0 %collective-permute-done.6 = bf16[4,32,1536]{2,1,0:T(8,128)(2,1)S(1)} collective-permute-done((bf16[4,32,1536]{2,1,0:T(8,128)(2,1)S(1)}, bf16[4,32,1536]{2,1,0:T(8,128)(2,1)S(1)}, u32[]{:S(2)}, u32[]{:S(2)}) %collective-permute-start.6) | collective-permute-done | bytes 393248 | tf_op jit(solution)/shard_map/ppermute | solution.py:31
  98.6 13.4 %all-to-all-done.1.q_ref = bf16[8,4,64,1024]{3,2,1,0:T(8,128)(2,1)} async-done(((bf16[8,4,64,1024]{3,2,1,0:T(8,128)(2,1)}), bf16[8,4,64,1024]{3,2,1,0:T(8,128)(2,1)}, u32[]{:S(2)}, u32[]{:S(2)}) %all-to-all-start.1) | async-done | bytes 4194336 | tf_op jit(solution)/shard_map/all_to_all | solution.py:231
  112.0 6.3 %shard_map.87 = (bf16[512,512]{1,0:T(8,128)(2,1)S(1)}, bf16[512,512]{1,0:T(8,128)(2,1)S(1)}, bf16[2048,1024]{1,0:T(8,128)(2,1)}, bf16[8,4,64,512]{3,2,1,0:T(8,128)(2,1)}) custom-call(s32[1]{0:T(128)} %bitcast.28.info, bf16[4,8,64,1024]{3,2,1,0:T(8,128)(2,1)} %bitcast.117, bf16[8,4,64,1024]{3,2,1,0:T(8,128)(2,1)} %all-to-all-done.1.q_ref, ...), custom_call_target="tpu_custom_call" | custom-call | tf_op jit(solution)/shard_map/pallas_call | solution.py:153
  118.3 0.3 collective-permute-start.7
  118.5 1.7 collective-permute-start.8
  120.4 10.3 %shard_map.88 = (bf16[1024,512]{1,0:T(8,128)(2,1)S(1)}, bf16[1024,512]{1,0:T(8,128)(2,1)}, bf16[2048,1024]{1,0:T(8,128)(2,1)}, bf16[8,4,64,512]{3,2,1,0:T(8,128)(2,1)}) custom-call(s32[2]{0:T(128)S(1)} %pad_add_fusion.info, bf16[4,8,64,1024]{3,2,1,0:T(8,128)(2,1)} %bitcast.118, ...), custom_call_target="tpu_custom_call", output_to_operand_aliasing={{2}: (4, {}), {3}: (5, {})} | custom-call | tf_op jit(solution)/shard_map/pallas_call | solution.py:153
  130.6 1.1 slice.216
  131.7 0.4 collective-permute-start.10
  132.1 2.5 %collective-permute-start.11 = (bf16[512,512]{1,0:T(8,128)(2,1)S(1)}, bf16[512,512]{1,0:T(8,128)(2,1)S(1)}, u32[]{:S(2)}, u32[]{:S(2)}) collective-permute-start(bf16[512,512]{1,0:T(8,128)(2,1)S(1)} %slice.217), channel_id=1, source_target_pairs={{64,0},{128,64},{192,128},{0,192},{65,1},{129,65},{193,129},{1,193... | collective-permute-start | bytes 1572872 | tf_op jit(solution)/shard_map/ppermute | solution.py:195
  134.7 6.7 %shard_map.89 = (bf16[512,512]{1,0:T(8,128)(2,1)S(1)}, bf16[512,512]{1,0:T(8,128)(2,1)S(1)}, bf16[2048,1024]{1,0:T(8,128)(2,1)}, bf16[8,4,64,512]{3,2,1,0:T(8,128)(2,1)}) custom-call(s32[1]{0:T(128)} %bitcast.4.info, bf16[4,8,64,1024]{3,2,1,0:T(8,128)(2,1)} %bitcast.119, ...), custom_call_target="tpu_custom_call", output_to_operand_aliasing={{2}: (4, {}), {3}: (5, {})} | custom-call | tf_op jit(solution)/shard_map/pallas_call | solution.py:153
  141.4 7.1 %convolution_convert_fusion = bf16[1024,1024]{1,0:T(8,128)(2,1)S(1)} fusion(bf16[2048,1024]{1,0:T(8,128)(2,1)S(1)} %bitcast.120, bf16[2048,1024]{1,0:T(8,128)(2,1)} %get-tuple-element.35), kind=kOutput, calls=%fused_computation.2 | convolution fusion | flops 4296015872 | bytes 10485760 | tf_op jit(solution)/shard_map/dot_general | solution.py:20
  148.5 4.9 %bitcast_convert_fusion = bf16[1024,512]{1,0:T(8,128)(2,1)S(1)} fusion(bf16[8,4,64,1024]{3,2,1,0:T(8,128)(2,1)} %all-to-all-done.1.q_ref, bf16[8,4,64,512]{3,2,1,0:T(8,128)(2,1)S(1)} %copy-done.4), kind=kOutput, calls=%fused_computation.1 | convolution fusion | flops 2148007936 | bytes 7340032 | tf_op jit(solution)/shard_map/dot_general | solution.py:20
  153.5 0.2 pad_maximum_fusion
  153.7 2.0 copy.55
  155.7 1.2 copy-done.5
  156.9 1.3 add_convert_fusion.1
  158.2 3.3 %collective-permute-start.12 = (bf16[512,512]{1,0:T(8,128)(2,1)S(1)}, bf16[512,512]{1,0:T(8,128)(2,1)S(1)}, u32[]{:S(2)}, u32[]{:S(2)}) collective-permute-start(bf16[512,512]{1,0:T(8,128)(2,1)S(1)} %add_convert_fusion.1), channel_id=1, source_target_pairs={{64,0},{128,64},{192,128},{0,192},{65,1},{129,65},{193,129},{1,193... | collective-permute-start | bytes 1572872 | tf_op jit(solution)/shard_map/ppermute | solution.py:195
  161.5 1.2 add_convert_fusion.3
  162.6 0.1 collective-permute-start.9
  162.7 8.6 %collective-permute-done.12 = bf16[512,512]{1,0:T(8,128)(2,1)S(1)} collective-permute-done((bf16[512,512]{1,0:T(8,128)(2,1)S(1)}, bf16[512,512]{1,0:T(8,128)(2,1)S(1)}, u32[]{:S(2)}, u32[]{:S(2)}) %collective-permute-start.12) | collective-permute-done | bytes 524320 | tf_op jit(solution)/shard_map/ppermute | solution.py:195
  171.3 0.2 add_convert_fusion
  171.5 3.2 %collective-permute-done.9 = bf16[512,512]{1,0:T(8,128)(2,1)S(1)} collective-permute-done((bf16[512,512]{1,0:T(8,128)(2,1)S(1)}, bf16[512,512]{1,0:T(8,128)(2,1)S(1)}, u32[]{:S(2)}, u32[]{:S(2)}) %collective-permute-start.9) | collective-permute-done | bytes 524320 | tf_op jit(solution)/shard_map/ppermute | solution.py:195
  174.8 0.2 add_convert_fusion.2
  175.0 1.1 pad_maximum_fusion.1
  176.1 3.7 %all-to-all-start.3 = ((bf16[8,64,1024]{2,1,0:T(8,128)(2,1)}), bf16[8,64,1024]{2,1,0:T(8,128)(2,1)S(1)}, u32[]{:S(2)}, u32[]{:S(2)}) async-start(bf16[8,64,1024]{2,1,0:T(8,128)(2,1)} %bitcast.32), calls=%async_computation.3 | async-start | bytes 2097152 | tf_op jit(solution)/shard_map/all_to_all | solution.py:236
  179.8 0.1 convolution_convert_fusion.1
  180.1 15.6 %all-to-all-done.3 = bf16[8,64,1024]{2,1,0:T(8,128)(2,1)S(1)} async-done(((bf16[8,64,1024]{2,1,0:T(8,128)(2,1)}), bf16[8,64,1024]{2,1,0:T(8,128)(2,1)S(1)}, u32[]{:S(2)}, u32[]{:S(2)}) %all-to-all-start.3) | async-done | bytes 1048608 | tf_op jit(solution)/shard_map/all_to_all | solution.py:236
  195.7 0.4 fusion.53
  196.1 4.7 %collective-permute-start.14 = (bf16[15,1024]{1,0:T(8,128)(2,1)S(1)}, bf16[15,1024]{1,0:T(8,128)(2,1)S(1)}, u32[]{:S(2)}, u32[]{:S(2)}) collective-permute-start(bf16[15,1024]{1,0:T(8,128)(2,1)S(1)} %get-tuple-element.44), channel_id=1, source_target_pairs={{1,0},{2,1},{3,2},{4,3},{5,4},{6,5},{7,6},{8,7},{9,8},{10,9},{11,1... | collective-permute-start | bytes 92168 | tf_op jit(solution)/shard_map/ppermute | solution.py:80
  200.8 1.9 collective-permute-start.13
  202.8 0.2 fusion.34
  203.0 0.6 fusion.49
  203.6 6.8 %collective-permute-done.13 = bf16[15,1024]{1,0:T(8,128)(2,1)S(1)} collective-permute-done((bf16[15,1024]{1,0:T(8,128)(2,1)S(1)}, bf16[15,1024]{1,0:T(8,128)(2,1)S(1)}, u32[]{:S(2)}, u32[]{:S(2)}) %collective-permute-start.13) | collective-permute-done | bytes 30752 | tf_op jit(solution)/shard_map/ppermute | solution.py:79
  210.4 0.1 maximum_convert_fusion
  210.6 3.7 %all-to-all-start.4 = ((bf16[4,32,1536]{2,1,0:T(8,128)(2,1)}), bf16[4,32,1536]{2,1,0:T(8,128)(2,1)S(1)}, u32[]{:S(2)}, u32[]{:S(2)}) async-start(bf16[4,32,1536]{2,1,0:T(8,128)(2,1)} %bitcast.125), calls=%async_computation.5 | async-start | bytes 786432 | tf_op jit(solution)/shard_map/all_to_all | solution.py:60
  214.3 3.7 %fusion.3 = bf16[192,1024]{1,0:T(8,128)(2,1)} fusion(f32[192,1024]{1,0:T(8,128)S(1)} %get-tuple-element.79, f32[222,1024]{1,0:T(8,128)S(1)} %maximum_convert_fusion, f32[1024]{0:T(1024)S(1)} %bitcast.140, f32[1024]{0:T(1024)S(1)} %bitcast.139, f32[1024]{0:T(1024)S(1)} %bitcast.138, f32[1024]{0:T(1024)S(1)} %bitcast.137, f32[1024]{0:T(1024)S(1)} %bitcast.136, ...), kind=kLoop, calls=%fused_computation.14 | loop fusion | flops 12386304 | bytes 25686016 | tf_op jit(solution)/shard_map/convert_element_type | solution.py:261
  218.0 2.2 all-to-all-done.4
  220.2 0.3 reshape.47
  220.5 0.4 copy.56
  220.9 1.0 reshape.48
  (66 shorter events, 0.7 us)
Async XLA Ops:
  7.2 43.5 %all-gather.7.cloned.1.call-start = ((), (), s32[]{:S(2)}) async-start(), calls=%async_computation.8 | async-start | bytes 2048000 | tf_op jit(solution)/shard_map/all_gather | solution.py:226
  8.6 23.3 %copy-start.12 = (bf16[1,32,6144]{2,1,0:T(8,128)(2,1)S(1)}, bf16[1,32,6144]{2,1,0:T(8,128)(2,1)}, u32[]{:S(2)}) copy-start(bf16[1,32,6144]{2,1,0:T(8,128)(2,1)} %param.11) | copy-start | bytes 1179652
  10.6 101.4 %all-gather.5.cloned.1.call-start = ((), (), s32[]{:S(2)}) async-start(), calls=%async_computation.7 | async-start | bytes 5242880 | tf_op jit(solution)/shard_map/all_gather | solution.py:229
  33.6 13.1 %all-to-all-start.2 = ((bf16[4,32,1536]{2,1,0:T(8,128)(2,1)}), bf16[4,32,1536]{2,1,0:T(8,128)(2,1)S(1)}, u32[]{:S(2)}, u32[]{:S(2)}) async-start(bf16[4,32,1536]{2,1,0:T(8,128)(2,1)} %reshape.40), calls=%async_computation.2 | async-start | bytes 786432 | tf_op jit(solution)/shard_map/all_to_all | solution.py:45
  46.7 16.1 %collective-permute-start = (bf16[4,32,1536]{2,1,0:T(8,128)(2,1)S(1)}, bf16[4,32,1536]{2,1,0:T(8,128)(2,1)}, u32[]{:S(2)}, u32[]{:S(2)}) collective-permute-start(bf16[4,32,1536]{2,1,0:T(8,128)(2,1)S(1)} %all-to-all-done.2), channel_id=1, source_target_pairs={{0,8},{8,16},{16,24},{24,32},{32,40},{40,48},{48,56},{56,0},{1,9},... | collective-permute-start | bytes 1179656 | tf_op jit(solution)/shard_map/ppermute | solution.py:31
  48.3 14.6 %collective-permute-start.1 = (bf16[4,32,1536]{2,1,0:T(8,128)(2,1)S(1)}, bf16[4,32,1536]{2,1,0:T(8,128)(2,1)}, u32[]{:S(2)}, u32[]{:S(2)}) collective-permute-start(bf16[4,32,1536]{2,1,0:T(8,128)(2,1)S(1)} %all-to-all-done.2), channel_id=1, source_target_pairs={{8,0},{16,8},{24,16},{32,24},{40,32},{48,40},{56,48},{0,56},{9,1},... | collective-permute-start | bytes 1179656 | tf_op jit(solution)/shard_map/ppermute | solution.py:34
  50.6 1.4 copy-start.1
  55.6 2.1 copy-start
  57.7 54.3 %all-to-all-start.1 = ((bf16[8,4,64,1024]{3,2,1,0:T(8,128)(2,1)}), bf16[8,4,64,1024]{3,2,1,0:T(8,128)(2,1)}, u32[]{:S(2)}, u32[]{:S(2)}) async-start(bf16[8,4,64,1024]{3,2,1,0:T(8,128)(2,1)} %copy-done), calls=%async_computation.1 | async-start | bytes 8388608 | tf_op jit(solution)/shard_map/all_to_all | solution.py:231
  62.3 148.2 %reduce-scatter.2.cloned.1.call-start = ((), (), s32[]{:S(2)}) async-start(), calls=%async_computation.6 | async-start | bytes 3538944 | tf_op jit(solution)/shard_map/reduce_scatter | solution.py:59
  62.8 12.8 %collective-permute-start.2 = (bf16[4,32,1536]{2,1,0:T(8,128)(2,1)}, bf16[4,32,1536]{2,1,0:T(8,128)(2,1)S(1)}, u32[]{:S(2)}, u32[]{:S(2)}) collective-permute-start(bf16[4,32,1536]{2,1,0:T(8,128)(2,1)} %collective-permute-done), channel_id=1, source_target_pairs={{0,8},{8,16},{16,24},{24,32},{32,40},{40,48},{48,56},{56,0},{1,9},... | collective-permute-start | bytes 1179656 | tf_op jit(solution)/shard_map/ppermute | solution.py:31
  62.9 12.8 %collective-permute-start.3 = (bf16[4,32,1536]{2,1,0:T(8,128)(2,1)}, bf16[4,32,1536]{2,1,0:T(8,128)(2,1)S(1)}, u32[]{:S(2)}, u32[]{:S(2)}) collective-permute-start(bf16[4,32,1536]{2,1,0:T(8,128)(2,1)} %collective-permute-done.1), channel_id=1, source_target_pairs={{8,0},{16,8},{24,16},{32,24},{40,32},{48,40},{56,48},{0,56},{9,1},... | collective-permute-start | bytes 1179656 | tf_op jit(solution)/shard_map/ppermute | solution.py:34
  75.6 11.9 %collective-permute-start.4 = (bf16[4,32,1536]{2,1,0:T(8,128)(2,1)S(1)}, bf16[4,32,1536]{2,1,0:T(8,128)(2,1)S(1)}, u32[]{:S(2)}, u32[]{:S(2)}) collective-permute-start(bf16[4,32,1536]{2,1,0:T(8,128)(2,1)S(1)} %collective-permute-done.2), channel_id=1, source_target_pairs={{0,8},{8,16},{16,24},{24,32},{32,40},{40,48},{48,56},{56,0},{1,9},... | collective-permute-start | bytes 1179656 | tf_op jit(solution)/shard_map/ppermute | solution.py:31
  75.6 11.9 %collective-permute-start.5 = (bf16[4,32,1536]{2,1,0:T(8,128)(2,1)S(1)}, bf16[4,32,1536]{2,1,0:T(8,128)(2,1)S(1)}, u32[]{:S(2)}, u32[]{:S(2)}) collective-permute-start(bf16[4,32,1536]{2,1,0:T(8,128)(2,1)S(1)} %collective-permute-done.3), channel_id=1, source_target_pairs={{8,0},{16,8},{24,16},{32,24},{40,32},{48,40},{56,48},{0,56},{9,1},... | collective-permute-start | bytes 1179656 | tf_op jit(solution)/shard_map/ppermute | solution.py:34
  87.5 11.1 %collective-permute-start.6 = (bf16[4,32,1536]{2,1,0:T(8,128)(2,1)S(1)}, bf16[4,32,1536]{2,1,0:T(8,128)(2,1)S(1)}, u32[]{:S(2)}, u32[]{:S(2)}) collective-permute-start(bf16[4,32,1536]{2,1,0:T(8,128)(2,1)S(1)} %collective-permute-done.4), channel_id=1, source_target_pairs={{0,8},{8,16},{16,24},{24,32},{32,40},{40,48},{48,56},{56,0},{1,9},... | collective-permute-start | bytes 1179656 | tf_op jit(solution)/shard_map/ppermute | solution.py:31
  98.6 13.4 %copy-start.2 = (bf16[4,8,32,1536]{3,2,1,0:T(8,128)(2,1)}, bf16[4,8,32,1536]{3,2,1,0:T(8,128)(2,1)S(1)}, u32[]{:S(2)}) copy-start(bf16[4,8,32,1536]{3,2,1,0:T(8,128)(2,1)S(1)} %bitcast_dynamic-update-slice_fusion) | copy-start | bytes 9437188
  118.3 16.4 %collective-permute-start.7 = (bf16[512,512]{1,0:T(8,128)(2,1)S(1)}, bf16[512,512]{1,0:T(8,128)(2,1)S(1)}, u32[]{:S(2)}, u32[]{:S(2)}) collective-permute-start(bf16[512,512]{1,0:T(8,128)(2,1)S(1)} %get-tuple-element.23), channel_id=1, source_target_pairs={{0,64},{64,128},{128,192},{192,0},{1,65},{65,129},{129,193},{193,1... | collective-permute-start | bytes 1572872 | tf_op jit(solution)/shard_map/ppermute | solution.py:195
  118.5 16.1 %collective-permute-start.8 = (bf16[512,512]{1,0:T(8,128)(2,1)S(1)}, bf16[512,512]{1,0:T(8,128)(2,1)S(1)}, u32[]{:S(2)}, u32[]{:S(2)}) collective-permute-start(bf16[512,512]{1,0:T(8,128)(2,1)S(1)} %get-tuple-element.24), channel_id=1, source_target_pairs={{64,0},{128,64},{192,128},{0,192},{65,1},{129,65},{193,129},{1,193... | collective-permute-start | bytes 1572872 | tf_op jit(solution)/shard_map/ppermute | solution.py:195
  131.7 16.8 %collective-permute-start.10 = (bf16[512,512]{1,0:T(8,128)(2,1)S(1)}, bf16[512,512]{1,0:T(8,128)(2,1)S(1)}, u32[]{:S(2)}, u32[]{:S(2)}) collective-permute-start(bf16[512,512]{1,0:T(8,128)(2,1)S(1)} %slice.216), channel_id=1, source_target_pairs={{0,64},{64,128},{128,192},{192,0},{1,65},{65,129},{129,193},{193,1... | collective-permute-start | bytes 1572872 | tf_op jit(solution)/shard_map/ppermute | solution.py:195
  132.1 16.4 %collective-permute-start.11 = (bf16[512,512]{1,0:T(8,128)(2,1)S(1)}, bf16[512,512]{1,0:T(8,128)(2,1)S(1)}, u32[]{:S(2)}, u32[]{:S(2)}) collective-permute-start(bf16[512,512]{1,0:T(8,128)(2,1)S(1)} %slice.217), channel_id=1, source_target_pairs={{64,0},{128,64},{192,128},{0,192},{65,1},{129,65},{193,129},{1,193... | collective-permute-start | bytes 1572872 | tf_op jit(solution)/shard_map/ppermute | solution.py:195
  134.7 6.7 %copy-start.6 = (bf16[512,512]{1,0:T(8,128)(2,1)}, bf16[512,512]{1,0:T(8,128)(2,1)S(1)}, u32[]{:S(2)}) copy-start(bf16[512,512]{1,0:T(8,128)(2,1)S(1)} %collective-permute-done.7) | copy-start | bytes 1572868
  134.7 13.8 %copy-start.7 = (bf16[512,512]{1,0:T(8,128)(2,1)}, bf16[512,512]{1,0:T(8,128)(2,1)S(1)}, u32[]{:S(2)}) copy-start(bf16[512,512]{1,0:T(8,128)(2,1)S(1)} %collective-permute-done.8) | copy-start | bytes 1572868
  134.7 6.7 %copy-start.3 = (bf16[32,1,64,1024]{3,2,1,0:T(8,128)(2,1)S(1)}, bf16[32,1,64,1024]{3,2,1,0:T(8,128)(2,1)}, u32[]{:S(2)}) copy-start(bf16[32,1,64,1024]{3,2,1,0:T(8,128)(2,1)} %all-gather.5.cloned.1.call-done) | copy-start | bytes 12582916
  141.3 7.2 %copy-start.4 = (bf16[8,4,64,512]{3,2,1,0:T(8,128)(2,1)S(1)}, bf16[8,4,64,512]{3,2,1,0:T(8,128)(2,1)}, u32[]{:S(2)}) copy-start(bf16[8,4,64,512]{3,2,1,0:T(8,128)(2,1)} %get-tuple-element.42) | copy-start | bytes 6291460
  148.5 4.9 %copy-start.10 = (bf16[512,512]{1,0:T(8,128)(2,1)}, bf16[512,512]{1,0:T(8,128)(2,1)S(1)}, u32[]{:S(2)}) copy-start(bf16[512,512]{1,0:T(8,128)(2,1)S(1)} %collective-permute-done.10) | copy-start | bytes 1572868
  148.5 4.9 %copy-start.8 = (bf16[512,512]{1,0:T(8,128)(2,1)}, bf16[512,512]{1,0:T(8,128)(2,1)S(1)}, u32[]{:S(2)}) copy-start(bf16[512,512]{1,0:T(8,128)(2,1)S(1)} %collective-permute-done.11) | copy-start | bytes 1572868
  155.7 1.2 copy-start.5
  156.9 14.4 %copy-start.11 = (bf16[512,512]{1,0:T(8,128)(2,1)S(1)}, bf16[512,512]{1,0:T(8,128)(2,1)}, u32[]{:S(2)}) copy-start(bf16[512,512]{1,0:T(8,128)(2,1)} %copy-done.10) | copy-start | bytes 1572868
  156.9 17.9 %copy-start.9 = (bf16[512,512]{1,0:T(8,128)(2,1)S(1)}, bf16[512,512]{1,0:T(8,128)(2,1)}, u32[]{:S(2)}) copy-start(bf16[512,512]{1,0:T(8,128)(2,1)} %copy-done.8) | copy-start | bytes 1572868
  158.2 13.2 %collective-permute-start.12 = (bf16[512,512]{1,0:T(8,128)(2,1)S(1)}, bf16[512,512]{1,0:T(8,128)(2,1)S(1)}, u32[]{:S(2)}, u32[]{:S(2)}) collective-permute-start(bf16[512,512]{1,0:T(8,128)(2,1)S(1)} %add_convert_fusion.1), channel_id=1, source_target_pairs={{64,0},{128,64},{192,128},{0,192},{65,1},{129,65},{193,129},{1,193... | collective-permute-start | bytes 1572872 | tf_op jit(solution)/shard_map/ppermute | solution.py:195
  162.6 12.1 %collective-permute-start.9 = (bf16[512,512]{1,0:T(8,128)(2,1)S(1)}, bf16[512,512]{1,0:T(8,128)(2,1)S(1)}, u32[]{:S(2)}, u32[]{:S(2)}) collective-permute-start(bf16[512,512]{1,0:T(8,128)(2,1)S(1)} %add_convert_fusion.3), channel_id=1, source_target_pairs={{0,64},{64,128},{128,192},{192,0},{1,65},{65,129},{129,193},{193,1... | collective-permute-start | bytes 1572872 | tf_op jit(solution)/shard_map/ppermute | solution.py:195
  174.8 5.0 %copy-start.15 = (s32[192,2]{0,1:T(2,128)S(1)}, s32[192,2]{0,1:T(2,128)}, u32[]{:S(2)}) copy-start(s32[192,2]{0,1:T(2,128)} %param.9) | copy-start | bytes 4612
  174.8 5.2 %copy-start.14 = (bf16[31,1024]{1,0:T(8,128)(2,1)S(1)}, bf16[31,1024]{1,0:T(8,128)(2,1)}, u32[]{:S(2)}) copy-start(bf16[31,1024]{1,0:T(8,128)(2,1)} %param.10) | copy-start | bytes 190468
  174.8 20.9 %copy-start.13 = (bf16[192,1024]{1,0:T(8,128)(2,1)S(1)}, bf16[192,1024]{1,0:T(8,128)(2,1)}, u32[]{:S(2)}) copy-start(bf16[192,1024]{1,0:T(8,128)(2,1)} %param.7) | copy-start | bytes 1179652
  176.1 26.9 %copy-start.16 = (bf16[192,2]{0,1:T(2,128)(2,1)S(1)}, bf16[192,2]{0,1:T(2,128)(2,1)}, u32[]{:S(2)}) copy-start(bf16[192,2]{0,1:T(2,128)(2,1)} %param.8) | copy-start | bytes 2308
  176.1 19.6 %all-to-all-start.3 = ((bf16[8,64,1024]{2,1,0:T(8,128)(2,1)}), bf16[8,64,1024]{2,1,0:T(8,128)(2,1)S(1)}, u32[]{:S(2)}, u32[]{:S(2)}) async-start(bf16[8,64,1024]{2,1,0:T(8,128)(2,1)} %bitcast.32), calls=%async_computation.3 | async-start | bytes 2097152 | tf_op jit(solution)/shard_map/all_to_all | solution.py:236
  196.1 7.5 %collective-permute-start.14 = (bf16[15,1024]{1,0:T(8,128)(2,1)S(1)}, bf16[15,1024]{1,0:T(8,128)(2,1)S(1)}, u32[]{:S(2)}, u32[]{:S(2)}) collective-permute-start(bf16[15,1024]{1,0:T(8,128)(2,1)S(1)} %get-tuple-element.44), channel_id=1, source_target_pairs={{1,0},{2,1},{3,2},{4,3},{5,4},{6,5},{7,6},{8,7},{9,8},{10,9},{11,1... | collective-permute-start | bytes 92168 | tf_op jit(solution)/shard_map/ppermute | solution.py:80
  200.8 9.6 %collective-permute-start.13 = (bf16[15,1024]{1,0:T(8,128)(2,1)S(1)}, bf16[15,1024]{1,0:T(8,128)(2,1)S(1)}, u32[]{:S(2)}, u32[]{:S(2)}) collective-permute-start(bf16[15,1024]{1,0:T(8,128)(2,1)S(1)} %get-tuple-element.43), channel_id=1, source_target_pairs={{0,1},{1,2},{2,3},{3,4},{4,5},{5,6},{6,7},{7,8},{8,9},{9,10},{10,1... | collective-permute-start | bytes 92168 | tf_op jit(solution)/shard_map/ppermute | solution.py:79
  210.6 9.7 %all-to-all-start.4 = ((bf16[4,32,1536]{2,1,0:T(8,128)(2,1)}), bf16[4,32,1536]{2,1,0:T(8,128)(2,1)S(1)}, u32[]{:S(2)}, u32[]{:S(2)}) async-start(bf16[4,32,1536]{2,1,0:T(8,128)(2,1)} %bitcast.125), calls=%async_computation.5 | async-start | bytes 786432 | tf_op jit(solution)/shard_map/all_to_all | solution.py:60
Sparse Core Ops, SparseCore 0:
  10.7 34.4 all-gather.6
  47.0 51.0 all-gather.4
  155.8 45.5 reduce-scatter.1

commit v6 on v5

--- a/solution.py
+++ b/solution.py
@@ -20,43 +20,48 @@
     return lax.dot_general(a, b, (contract, batch), preferred_element_type=F32)
 
 
-def ring_gather(shard, axis, place, buffer):
+def ring_ways(axis):
     count = lax.axis_size(axis)
-    me = lax.axis_index(axis)
     up = [(i, (i + 1) % count) for i in range(count)]
-    down = [(target, source) for source, target in up]
-    buffer = place(buffer, shard, me)
-    right = left = shard
-    for step in range(1, count // 2 + 1):
-        right = lax.ppermute(right, axis, up)
-        buffer = place(buffer, right, (me - step) % count)
-        if step < count - step:
-            left = lax.ppermute(left, axis, down)
-            buffer = place(buffer, left, (me + step) % count)
-    return buffer
-
-
-def gather_weights(expert_weights):
-    ny, nz = lax.axis_size("y"), lax.axis_size("z")
+    return up, [(target, source) for source, target in up]
+
+
+def ring_step(right, left, axis):
+    up, down = ring_ways(axis)
+    return lax.ppermute(right, axis, up), lax.ppermute(left, axis, down)
+
+
+def own_columns(expert_weights):
+    ny = lax.axis_size("y")
     rows, width = expert_weights.shape[1], expert_weights.shape[2]
     part = width // (3 * ny)
     sliced = expert_weights[0].reshape(rows, 3, ny, part).transpose(2, 0, 1, 3)
-    sliced = sliced.reshape(ny, rows, 3 * part)
-    mine = lax.all_to_all(sliced, "y", 0, 0, tiled=True)
+    return lax.all_to_all(sliced.reshape(ny, rows, 3 * part), "y", 0, 0, tiled=True)
+
+
+def gather_weights(mine, after):
+    ny, rows, width = mine.shape
+    nz = lax.axis_size("z")
+    me = lax.axis_index("z")
 
     def place(buffer, shard, z):
-        return lax.dynamic_update_slice(buffer, shard[:, None], (0, z, 0, 0))
-
-    buffer = ring_gather(mine, "z", place, jnp.zeros((ny, nz, rows, 3 * part), BF))
-    return buffer.reshape(ny * nz * rows, 3 * part)
+        return lax.dynamic_update_slice(buffer, shard[:, None], (0, z % nz, 0, 0))
+
+    buffer = place(jnp.zeros((ny, nz, rows, width), BF), mine, me)
+    mine, after = lax.optimization_barrier((mine, after))
+    right = left = mine
+    for step in range(1, nz // 2):
+        right, left = ring_step(right, left, "z")
+        buffer = place(place(buffer, right, me - step), left, me + step)
+    right = lax.ppermute(right, "z", ring_ways("z")[0])
+    buffer = place(buffer, right, me - nz // 2)
+    return buffer.reshape(ny * nz * rows, width)
 
 
 def scatter_weight_grad(term):
     ny, nz = lax.axis_size("y"), lax.axis_size("z")
-    rows = term.shape[0] // (ny * nz)
-    part = term.shape[1] // 3
-    blocks = term.reshape(ny, nz, rows, 3 * part).transpose(1, 0, 2, 3)
-    mine = lax.psum_scatter(blocks.reshape(nz * ny * rows, 3 * part), "z", scatter_dimension=0, tiled=True)
+    rows, part = term.shape[2], term.shape[3] // 3
+    mine = lax.psum_scatter(term.reshape(nz * ny * rows, 3 * part), "z", scatter_dimension=0, tiled=True)
     back = lax.all_to_all(mine.reshape(ny, rows, 3 * part), "y", 0, 0, tiled=True)
     back = back.reshape(ny, rows, 3, part).transpose(1, 2, 0, 3)
     return back.reshape(1, rows, 3 * ny * part)
@@ -111,11 +116,8 @@
     )(packed)
 
 
-def rows_kernel(info, u_ref, q_ref, w_ref, *refs):
-    low_ref, high_ref, pre_ref, h_ref = refs[-4:]
-    steps, width, part, half = u_ref.shape[1], u_ref.shape[3], h_ref.shape[3], low_ref.shape[1]
-    count = steps * SLOTS
-    u, q = u_ref[0].reshape(count, width), q_ref[:, 0].reshape(count, width)
+def rows_of(u, q, w_ref, low_ref, high_ref, pre_ref, h_ref):
+    steps, part, half = h_ref.shape[0], h_ref.shape[3], low_ref.shape[1]
     gate_part = 0.0
     for c in range(0, part, CHUNK):
         gate_in = dot(u, w_ref[:, c : c + CHUNK], ((1,), (0,)))
@@ -139,6 +141,76 @@
         diagonal = jnp.where(row == lane, gate_part[j * SLOTS : (j + 1) * SLOTS], 0.0)
         line = jnp.sum(diagonal, axis=0, keepdims=True)
         low_ref[place, :128] = jnp.where(row == SPARE, line, low_ref[place, :128].astype(F32)).astype(BF)
+
+
+def rows_kernel(info, u_ref, q_ref, w_ref, *refs):
+    count, width = u_ref.shape[1] * SLOTS, u_ref.shape[3]
+    rows_of(u_ref[0].reshape(count, width), q_ref[:, 0].reshape(count, width), w_ref, *refs[-4:])
+
+
+def last_kernel(info, u_ref, q_ref, w_ref, pre_ref, h_ref, low_ref, high_ref, term_ref, own_pre, own_h, total):
+    step, last = pl.program_id(0), pl.num_programs(0) - 1
+    count, width = u_ref.shape[1] * SLOTS, u_ref.shape[3]
+    part, wide = h_ref.shape[3], pre_ref.shape[1]
+    groups, each = term_ref.shape[1], term_ref.shape[0] * term_ref.shape[2]
+    u, q = u_ref[0].reshape(count, width), q_ref[:, 0].reshape(count, width)
+
+    @pl.when(step == 0)
+    def _():
+        rows_of(u, q, w_ref, low_ref, high_ref, own_pre, own_h)
+        total[:, :wide] = dot(u, own_pre[...], ((0,), (0,)))
+        total[:, wide:] = dot(q, own_h[:, 0].reshape(count, part), ((0,), (0,)))
+
+    @pl.when(step > 0)
+    def _():
+        total[:, :wide] += dot(u, pre_ref[...], ((0,), (0,)))
+        total[:, wide:] += dot(q, h_ref[:, 0].reshape(count, part), ((0,), (0,)))
+
+    @pl.when(step == last)
+    def _():
+        for g in range(groups):
+            block = total[g * each : (g + 1) * each].astype(BF)
+            term_ref[:, g] = block.reshape(term_ref.shape[0], term_ref.shape[2], term_ref.shape[3])
+
+
+def last_rows(targets, rows_in, rows_q, weights, pre_grads, hidden):
+    groups, sources, _, width = rows_in.shape
+    nz = lax.axis_size("z")
+    part = weights.shape[1] // 3
+    mine = sources * SLOTS
+    each = width // (groups * nz)
+    info = jnp.stack(targets).astype(jnp.int32)
+    fixed = lambda i, info: (0, 0)
+    return pl.pallas_call(
+        last_kernel,
+        grid_spec=pltpu.PrefetchScalarGridSpec(
+            num_scalar_prefetch=1,
+            grid=(groups,),
+            in_specs=[
+                pl.BlockSpec((1, sources, SLOTS, width), lambda i, info: (info[i], 0, 0, 0)),
+                pl.BlockSpec((sources, 1, SLOTS, width), lambda i, info: (0, info[i], 0, 0)),
+                pl.BlockSpec(weights.shape, fixed),
+                pl.BlockSpec((mine, 2 * part), lambda i, info: (info[jnp.maximum(i, 1)], 0)),
+                pl.BlockSpec((sources, 1, SLOTS, part), lambda i, info: (0, info[jnp.maximum(i, 1)], 0, 0)),
+            ],
+            out_specs=[
+                pl.BlockSpec((mine, width // 2), fixed),
+                pl.BlockSpec((mine, width // 2), fixed),
+                pl.BlockSpec((nz, groups, each, 3 * part), lambda i, info: (0, 0, 0, 0)),
+            ],
+            scratch_shapes=[
+                pltpu.VMEM((mine, 2 * part), BF),
+                pltpu.VMEM((sources, 1, SLOTS, part), BF),
+                pltpu.VMEM((width, 3 * part), F32),
+            ],
+        ),
+        out_shape=[
+            jax.ShapeDtypeStruct((mine, width // 2), BF),
+            jax.ShapeDtypeStruct((mine, width // 2), BF),
+            jax.ShapeDtypeStruct((nz, groups, each, 3 * part), BF),
+        ],
+        compiler_params=pltpu.CompilerParams(vmem_limit_bytes=56 * 1024 * 1024),
+    )(info, rows_in, rows_q, weights, pre_grads, hidden)
 
 
 def expert_rows(targets, rows_in, rows_q, weights, kept):
@@ -187,7 +259,6 @@
 def rows_backward(rows_in, rows_q, weights):
     ny = lax.axis_size("y")
     me = lax.axis_index("y")
-    width = rows_in.shape[3]
     up = [(i, (i + 1) % ny) for i in range(ny)]
     down = [(target, source) for source, target in up]
 
@@ -205,12 +276,9 @@
     below_high, above_low = send(near_high[:rows], up), send(near_low[rows:], down)
     below_low = send(add(near_low[:rows], low_via).astype(BF), up)
     above_high = send(add(near_high[rows:], high_via).astype(BF), down)
-    own_low, own_high, kept = run([0], kept)
-    pre_grads, hidden = kept
-    first = dot(rows_in.reshape(-1, width), pre_grads, ((0,), (0,))).astype(BF)
-    rows_q, below_high, above_low, first = lax.optimization_barrier((rows_q, below_high, above_low, first))
-    second = dot(rows_q.reshape(-1, width), hidden.reshape(-1, hidden.shape[3]), ((0,), (0,))).astype(BF)
-    term = jnp.concatenate([first, second], axis=1)
+    targets = [(me + offset) % ny for offset in (0, 2, 1, ny - 1)]
+    own_low, own_high, term = last_rows(targets, rows_in, rows_q, weights, *kept)
+    term, below_high, above_low = lax.optimization_barrier((term, below_high, above_low))
     low = add(own_low, below_low, above_low).astype(BF)
     high = add(own_high, below_high, above_high).astype(BF)
     return low, high, term
@@ -224,12 +292,14 @@
     meta = jnp.concatenate([expert_ids.astype(BF).T, gate_values.T], axis=0)
     meta = jnp.pad(meta, ((0, META - 4), (0, width - frames)))
     all_grad = lax.all_gather(jnp.concatenate([out_grad, meta], axis=0), "y", axis=0, tiled=False)
-    sent_in = route(jnp.concatenate([block_in, meta], axis=0)[None], experts, False)
+    columns = own_columns(expert_weights)
+    columns, packed_in = lax.optimization_barrier((columns, jnp.concatenate([block_in, meta], axis=0)))
+    sent_in = route(packed_in[None], experts, False)
     mine_in = lax.all_to_all(sent_in, by_expert, 0, 0, tiled=True)
     rows_in = lax.all_gather(mine_in[:, 0], "y", axis=0, tiled=False)
     sent_q = route(all_grad, experts, True)
+    weights = gather_weights(columns, sent_q)
     rows_q = lax.all_to_all(sent_q, by_expert, 0, 0, tiled=True)
-    weights = gather_weights(expert_weights)
     low, high, term = rows_backward(rows_in, rows_q, weights)
     weight_grad = scatter_weight_grad(term)
     summed = jnp.concatenate([low, high], axis=1).reshape(experts, SLOTS, width)

time: 229 us -> 225 us (0.983)
  waiting for transfers between devices: 85.1 us -> 64.2 us
  matrix products: 12.8 us -> 0.78 us
  blocking collectives: 20.3 us -> 31.6 us
  Pallas kernels: 27.6 us -> 38.1 us
  local copies, waits for them, and re-layouts: 13.9 us -> 19.4 us
    pallas_call x0 -> x1, Pallas kernels: none -> 17.1 us  [last_rows(): pl.pallas_call(last_kernel, grid_spec=pltpu.PrefetchScalarGridSpec(num_sc...]
    all_to_all x1, waiting for transfers between devices: 13.4 us -> 0.01 us  [local(): rows_q = lax.all_to_all(sent_q, by_expert, 0, 0, tiled=True)]
    dot_general x4 -> x2, matrix products: 12.6 us -> 0.56 us  [dot(): return lax.dot_general(a, b, (contract, batch), preferred_element_type=F32)]
    all_to_all x0 -> x1, blocking collectives: none -> 11.3 us  [own_columns(): lax.all_to_all(sliced.reshape(ny, rows, 3 * part), 'y', 0, 0, tiled=True)]
    all_to_all x1 -> x0, waiting for transfers between devices: 8.19 us -> none  [gather_weights(): mine = lax.all_to_all(sliced, 'y', 0, 0, tiled=True)]
    pallas_call x3 -> x2, Pallas kernels: 23.2 us -> 16.5 us  [expert_rows(): pl.pallas_call(rows_kernel, grid_spec=pltpu.PrefetchScalarGridSpec(num_sc...]
    all_to_all x1 -> x0, starting transfers between devices: 4.91 us -> none  [gather_weights(): mine = lax.all_to_all(sliced, 'y', 0, 0, tiled=True)]
    dynamic_update_slice x8, local copies, waits for them, and re-layouts: 2.24 us -> 6.26 us  [place(): return lax.dynamic_update_slice(buffer, shard[:, None], (0, z % nz, 0, 0))]
  transfers between devices with their start and end apart: 22 -> 21, of which waited for: 10 -> 9; matrix products, arithmetic and copies ran while one was open for 10% -> 10% of each run, Pallas kernels for 9% -> 14%
where the time goes in v6:
time: 225 us; the launch traced here: 224 us
  waiting for transfers between devices  64.2 us (29%)
  starting transfers between devices  43.3 us (19%)
  Pallas kernels  38.1 us (17%)
  blocking collectives  31.6 us (14%)
  local copies, waits for them, and re-layouts  19.4 us (9%)
  between operations  14.1 us (6%)
  other arithmetic  12.4 us (6%)
    ppermute x6, waiting for transfers between devices, ring_step(): return (lax.ppermute(right, axis, up), lax.ppermute(left, axis, down))  20.5 us
    all_to_all x1, blocking collectives, local(): mine_in = lax.all_to_all(sent_in, by_expert, 0, 0, tiled=True)  20.3 us
    pallas_call x1, Pallas kernels, last_rows(): pl.pallas_call(last_kernel, grid_spec=pltpu.PrefetchScalarGridSpec(num_sc...  17.1 us
    pallas_call x2, Pallas kernels, expert_rows(): pl.pallas_call(rows_kernel, grid_spec=pltpu.PrefetchScalarGridSpec(num_sc...  16.5 us
    all_to_all x1, waiting for transfers between devices, local(): returned = lax.all_to_all(summed, by_expert, 0, 0, tiled=True)  15.6 us
    ppermute x6, starting transfers between devices, ring_step(): return (lax.ppermute(right, axis, up), lax.ppermute(left, axis, down))  12.5 us
    all_to_all x1, blocking collectives, own_columns(): lax.all_to_all(sliced.reshape(ny, rows, 3 * part), 'y', 0, 0, tiled=True)  11.3 us
    ppermute x6, waiting for transfers between devices, send(): return lax.ppermute(rows, 'y', way)  10.2 us
  transfers between devices with their start and end apart: 21, of which 9 were waited for; matrix products, arithmetic and copies ran while one was open for 10% of the time, Pallas kernels for 14%

profile of v6, /device:TPU:8, one launch (start us, length us, event | category | flops | bytes accessed | tf_op | source)
XLA Modules:
  0.0 224.0 jit_solution(4771498553373342198)
XLA Ops:
  7.2 0.7 convert_bitcast_fusion
  7.9 0.7 fusion.46
  8.6 2.0 pad_maximum_fusion.1
  10.6 1.3 reshape_squeeze.3
  11.9 0.2 copy.61
  12.1 0.5 reshape.32
  12.7 11.3 %all_to_all.25 = bf16[4,32,1536]{2,1,0:T(8,128)(2,1)S(1)} all-to-all(bf16[4,32,1536]{2,1,0:T(8,128)(2,1)S(1)} %reshape.32), channel_id=1, replica_groups=mesh['y'=4,'z'=8,'x'=4,'c'=2] {'y'}, dimensions={0} | all-to-all | bytes 786432 | tf_op jit(solution)/shard_map/all_to_all | solution.py:39
  24.0 0.8 shard_map.85
  24.8 20.3 %all_to_all.26 = bf16[8,1,64,1024]{3,2,1,0:T(8,128)(2,1)} all-to-all(bf16[8,1,64,1024]{3,2,1,0:T(8,128)(2,1)S(1)} %shard_map.85), channel_id=1, replica_groups=mesh['y'=4,'z'=8,'x'=4,'c'=2] {'x','c'}, dimensions={0} | all-to-all | bytes 2097152 | tf_op jit(solution)/shard_map/all_to_all | solution.py:298
  45.4 1.4 copy-done.1
  46.8 3.6 %shard_map.86 = bf16[8,4,64,1024]{3,2,1,0:T(8,128)(2,1)S(1)} custom-call(bf16[4,200,1024]{2,1,0:T(8,128)(2,1)S(1)} %bitcast.102), custom_call_target="tpu_custom_call" | custom-call | tf_op jit(solution)/shard_map/pallas_call | solution.py:109
  50.4 2.0 copy-done
  52.4 4.6 %all-to-all-start.2 = ((bf16[8,4,64,1024]{3,2,1,0:T(8,128)(2,1)}), bf16[8,4,64,1024]{3,2,1,0:T(8,128)(2,1)}, u32[]{:S(2)}, u32[]{:S(2)}) async-start(bf16[8,4,64,1024]{3,2,1,0:T(8,128)(2,1)} %copy-done), calls=%async_computation.2 | async-start | bytes 8388608 | tf_op jit(solution)/shard_map/all_to_all | solution.py:302
  57.0 2.0 collective-permute-start
  59.0 4.1 %collective-permute-start.1 = (bf16[4,32,1536]{2,1,0:T(8,128)(2,1)S(1)}, bf16[4,32,1536]{2,1,0:T(8,128)(2,1)S(1)}, u32[]{:S(2)}, u32[]{:S(2)}) collective-permute-start(bf16[4,32,1536]{2,1,0:T(8,128)(2,1)S(1)} %all_to_all.25), channel_id=1, source_target_pairs={{8,0},{16,8},{24,16},{32,24},{40,32},{48,40},{56,48},{0,56},{9,1},... | collective-permute-start | bytes 1179656 | tf_op jit(solution)/shard_map/ppermute | solution.py:31
  63.1 2.0 broadcast_in_dim.37
  65.1 0.8 bitcast_dynamic-update-slice_fusion.7
  65.9 6.6 %collective-permute-done = bf16[4,32,1536]{2,1,0:T(8,128)(2,1)S(1)} collective-permute-done((bf16[4,32,1536]{2,1,0:T(8,128)(2,1)S(1)}, bf16[4,32,1536]{2,1,0:T(8,128)(2,1)S(1)}, u32[]{:S(2)}, u32[]{:S(2)}) %collective-permute-start) | collective-permute-done | bytes 393248 | tf_op jit(solution)/shard_map/ppermute | solution.py:31
  72.5 3.2 %collective-permute-start.3 = (bf16[4,32,1536]{2,1,0:T(8,128)(2,1)S(1)}, bf16[4,32,1536]{2,1,0:T(8,128)(2,1)S(1)}, u32[]{:S(2)}, u32[]{:S(2)}) collective-permute-start(bf16[4,32,1536]{2,1,0:T(8,128)(2,1)S(1)} %collective-permute-done.1), channel_id=1, source_target_pairs={{8,0},{16,8},{24,16},{32,24},{40,32},{48,40},{56,48},{0,56},{9,1},... | collective-permute-start | bytes 1179656 | tf_op jit(solution)/shard_map/ppermute | solution.py:31
  75.8 0.8 bitcast_dynamic-update-slice_fusion.6
  76.6 0.8 bitcast_dynamic-update-slice_fusion.5
  77.3 7.3 %collective-permute-done.2 = bf16[4,32,1536]{2,1,0:T(8,128)(2,1)S(1)} collective-permute-done((bf16[4,32,1536]{2,1,0:T(8,128)(2,1)S(1)}, bf16[4,32,1536]{2,1,0:T(8,128)(2,1)S(1)}, u32[]{:S(2)}, u32[]{:S(2)}) %collective-permute-start.2) | collective-permute-done | bytes 393248 | tf_op jit(solution)/shard_map/ppermute | solution.py:31
  84.6 3.2 %collective-permute-start.5 = (bf16[4,32,1536]{2,1,0:T(8,128)(2,1)S(1)}, bf16[4,32,1536]{2,1,0:T(8,128)(2,1)S(1)}, u32[]{:S(2)}, u32[]{:S(2)}) collective-permute-start(bf16[4,32,1536]{2,1,0:T(8,128)(2,1)S(1)} %collective-permute-done.3), channel_id=1, source_target_pairs={{8,0},{16,8},{24,16},{32,24},{40,32},{48,40},{56,48},{0,56},{9,1},... | collective-permute-start | bytes 1179656 | tf_op jit(solution)/shard_map/ppermute | solution.py:31
  87.9 0.8 bitcast_dynamic-update-slice_fusion.4
  88.6 0.8 bitcast_dynamic-update-slice_fusion.3
  89.4 6.5 %collective-permute-done.4 = bf16[4,32,1536]{2,1,0:T(8,128)(2,1)S(1)} collective-permute-done((bf16[4,32,1536]{2,1,0:T(8,128)(2,1)S(1)}, bf16[4,32,1536]{2,1,0:T(8,128)(2,1)S(1)}, u32[]{:S(2)}, u32[]{:S(2)}) %collective-permute-start.4) | collective-permute-done | bytes 393248 | tf_op jit(solution)/shard_map/ppermute | solution.py:31
  96.0 0.8 bitcast_dynamic-update-slice_fusion.2
  96.7 0.8 bitcast_dynamic-update-slice_fusion.1
  97.5 8.9 %collective-permute-done.6 = bf16[4,32,1536]{2,1,0:T(8,128)(2,1)S(1)} collective-permute-done((bf16[4,32,1536]{2,1,0:T(8,128)(2,1)S(1)}, bf16[4,32,1536]{2,1,0:T(8,128)(2,1)S(1)}, u32[]{:S(2)}, u32[]{:S(2)}) %collective-permute-start.6) | collective-permute-done | bytes 393248 | tf_op jit(solution)/shard_map/ppermute | solution.py:56
  106.5 0.8 bitcast_dynamic-update-slice_fusion
  107.2 6.3 %shard_map.87 = (bf16[512,512]{1,0:T(8,128)(2,1)S(1)}, bf16[512,512]{1,0:T(8,128)(2,1)S(1)}, bf16[2048,1024]{1,0:T(8,128)(2,1)}, bf16[8,4,64,512]{3,2,1,0:T(8,128)(2,1)}) custom-call(s32[1]{0:T(128)} %bitcast.5.info, bf16[4,8,64,1024]{3,2,1,0:T(8,128)(2,1)} %bitcast.104, bf16[8,4,64,1024]{3,2,1,0:T(8,128)(2,1)} %all-to-all-done.2.q_ref, ...), custom_call_target="tpu_custom_call" | custom-call | tf_op jit(solution)/shard_map/pallas_call | solution.py:225
  113.5 0.2 collective-permute-start.7
  113.7 1.8 collective-permute-start.8
  115.5 10.3 %shard_map.88 = (bf16[1024,512]{1,0:T(8,128)(2,1)S(1)}, bf16[1024,512]{1,0:T(8,128)(2,1)}, bf16[2048,1024]{1,0:T(8,128)(2,1)}, bf16[8,4,64,512]{3,2,1,0:T(8,128)(2,1)}) custom-call(s32[2]{0:T(128)S(1)} %pad_add_fusion.1.info, bf16[4,8,64,1024]{3,2,1,0:T(8,128)(2,1)} %bitcast.105, ...), custom_call_target="tpu_custom_call", output_to_operand_aliasing={{2}: (4, {}), {3}: (5, {})} | custom-call | tf_op jit(solution)/shard_map/pallas_call | solution.py:225
  125.8 1.9 slice.216
  127.7 0.2 collective-permute-start.10
  127.9 0.8 slice.217
  128.7 2.5 %collective-permute-start.11 = (bf16[512,512]{1,0:T(8,128)(2,1)}, bf16[512,512]{1,0:T(8,128)(2,1)}, u32[]{:S(2)}, u32[]{:S(2)}) collective-permute-start(bf16[512,512]{1,0:T(8,128)(2,1)} %slice.217), channel_id=1, source_target_pairs={{64,0},{128,64},{192,128},{0,192},{65,1},{129,65},{193,129},{1,193... | collective-permute-start | bytes 1572872 | tf_op jit(solution)/shard_map/ppermute | solution.py:266
  131.2 0.7 pad_add_fusion.info
  131.9 17.1 %shard_map.89 = (bf16[512,512]{1,0:T(8,128)(2,1)}, bf16[512,512]{1,0:T(8,128)(2,1)}, bf16[8,4,32,1536]{3,2,1,0:T(8,128)(2,1)}) custom-call(s32[4]{0:T(128)} %pad_add_fusion.info, bf16[4,8,64,1024]{3,2,1,0:T(8,128)(2,1)} %bitcast.106, bf16[8,4,64,1024]{3,2,1,0:T(8,128)(2,1)} %all-to-all-done.2.q_ref, bf16[1024,1536]{1,0:T(8,128)(2,1)} %bitcast.30.w_ref, ...), custom_call_target="tpu_custom_call" | custom-call | tf_op jit(solution)/shard_map/pallas_call | solution.py:184
  149.0 1.2 copy-done.2
  150.2 0.1 add_convert_fusion.1
  150.4 3.3 %collective-permute-start.12 = (bf16[512,512]{1,0:T(8,128)(2,1)S(1)}, bf16[512,512]{1,0:T(8,128)(2,1)S(1)}, u32[]{:S(2)}, u32[]{:S(2)}) collective-permute-start(bf16[512,512]{1,0:T(8,128)(2,1)S(1)} %add_convert_fusion.1), channel_id=1, source_target_pairs={{64,0},{128,64},{192,128},{0,192},{65,1},{129,65},{193,129},{1,193... | collective-permute-start | bytes 1572872 | tf_op jit(solution)/shard_map/ppermute | solution.py:266
  153.7 0.1 add_convert_fusion.3
  153.9 9.0 %collective-permute-done.12 = bf16[512,512]{1,0:T(8,128)(2,1)S(1)} collective-permute-done((bf16[512,512]{1,0:T(8,128)(2,1)S(1)}, bf16[512,512]{1,0:T(8,128)(2,1)S(1)}, u32[]{:S(2)}, u32[]{:S(2)}) %collective-permute-start.12) | collective-permute-done | bytes 524320 | tf_op jit(solution)/shard_map/ppermute | solution.py:266
  162.9 1.2 add_convert_fusion
  164.1 1.2 collective-permute-done.9
  165.3 1.3 add_convert_fusion.2
  166.6 1.1 pad_maximum_fusion
  167.8 3.7 %all-to-all-start.3 = ((bf16[8,64,1024]{2,1,0:T(8,128)(2,1)}), bf16[8,64,1024]{2,1,0:T(8,128)(2,1)S(1)}, u32[]{:S(2)}, u32[]{:S(2)}) async-start(bf16[8,64,1024]{2,1,0:T(8,128)(2,1)} %bitcast.31), calls=%async_computation.3 | async-start | bytes 2097152 | tf_op jit(solution)/shard_map/all_to_all | solution.py:306
  171.5 0.1 convolution_convert_fusion
  171.8 15.6 %all-to-all-done.3 = bf16[8,64,1024]{2,1,0:T(8,128)(2,1)S(1)} async-done(((bf16[8,64,1024]{2,1,0:T(8,128)(2,1)}), bf16[8,64,1024]{2,1,0:T(8,128)(2,1)S(1)}, u32[]{:S(2)}, u32[]{:S(2)}) %all-to-all-start.3) | async-done | bytes 1048608 | tf_op jit(solution)/shard_map/all_to_all | solution.py:306
  187.4 0.4 fusion.52
  187.8 8.6 %collective-permute-start.14 = (bf16[15,1024]{1,0:T(8,128)(2,1)S(1)}, bf16[15,1024]{1,0:T(8,128)(2,1)S(1)}, u32[]{:S(2)}, u32[]{:S(2)}) collective-permute-start(bf16[15,1024]{1,0:T(8,128)(2,1)S(1)} %get-tuple-element.46), channel_id=1, source_target_pairs={{1,0},{2,1},{3,2},{4,3},{5,4},{6,5},{7,6},{8,7},{9,8},{10,9},{11,1... | collective-permute-start | bytes 92168 | tf_op jit(solution)/shard_map/ppermute | solution.py:85
  196.4 1.9 collective-permute-start.13
  198.4 0.2 fusion.34
  198.6 0.6 fusion.48
  199.2 6.8 %collective-permute-done.13 = bf16[15,1024]{1,0:T(8,128)(2,1)S(1)} collective-permute-done((bf16[15,1024]{1,0:T(8,128)(2,1)S(1)}, bf16[15,1024]{1,0:T(8,128)(2,1)S(1)}, u32[]{:S(2)}, u32[]{:S(2)}) %collective-permute-start.13) | collective-permute-done | bytes 30752 | tf_op jit(solution)/shard_map/ppermute | solution.py:84
  206.1 3.8 %all-to-all-start.4 = ((bf16[4,32,1536]{2,1,0:T(8,128)(2,1)}), bf16[4,32,1536]{2,1,0:T(8,128)(2,1)S(1)}, u32[]{:S(2)}, u32[]{:S(2)}) async-start(bf16[4,32,1536]{2,1,0:T(8,128)(2,1)} %bitcast.110), calls=%async_computation.5 | async-start | bytes 786432 | tf_op jit(solution)/shard_map/all_to_all | solution.py:65
  209.9 3.7 %fusion.3 = bf16[192,1024]{1,0:T(8,128)(2,1)} fusion(f32[192,1024]{1,0:T(8,128)S(1)} %get-tuple-element.81, f32[222,1024]{1,0:T(8,128)S(1)} %maximum_convert_fusion, f32[1024]{0:T(1024)S(1)} %bitcast.125, f32[1024]{0:T(1024)S(1)} %bitcast.124, f32[1024]{0:T(1024)S(1)} %bitcast.123, f32[1024]{0:T(1024)S(1)} %bitcast.122, f32[1024]{0:T(1024)S(1)} %bitcast.121, ...), kind=kLoop, calls=%fused_computation.11 | loop fusion | flops 12386304 | bytes 25686016 | tf_op jit(solution)/shard_map/convert_element_type | solution.py:331
  213.6 2.2 all-to-all-done.4
  215.8 0.3 reshape.37
  216.1 0.4 copy.47
  216.5 1.0 reshape.38
  (46 shorter events, 0.7 us)
Async XLA Ops:
  7.2 38.2 %all-gather.7.cloned.1.call-start = ((), (), s32[]{:S(2)}) async-start(), calls=%async_computation.8 | async-start | bytes 2048000 | tf_op jit(solution)/shard_map/all_gather | solution.py:294
  10.6 96.7 %all-gather.5.cloned.1.call-start = ((), (), s32[]{:S(2)}) async-start(), calls=%async_computation.7 | async-start | bytes 5242880 | tf_op jit(solution)/shard_map/all_gather | solution.py:299
  45.4 1.4 copy-start.1
  50.4 2.0 copy-start
  52.4 54.8 %all-to-all-start.2 = ((bf16[8,4,64,1024]{3,2,1,0:T(8,128)(2,1)}), bf16[8,4,64,1024]{3,2,1,0:T(8,128)(2,1)}, u32[]{:S(2)}, u32[]{:S(2)}) async-start(bf16[8,4,64,1024]{3,2,1,0:T(8,128)(2,1)} %copy-done), calls=%async_computation.2 | async-start | bytes 8388608 | tf_op jit(solution)/shard_map/all_to_all | solution.py:302
  57.0 149.2 %reduce-scatter.2.cloned.1.call-start = ((), (), s32[]{:S(2)}) async-start(), calls=%async_computation.6 | async-start | bytes 3538944 | tf_op jit(solution)/shard_map/reduce_scatter | solution.py:64
  57.0 15.5 %collective-permute-start = (bf16[4,32,1536]{2,1,0:T(8,128)(2,1)S(1)}, bf16[4,32,1536]{2,1,0:T(8,128)(2,1)S(1)}, u32[]{:S(2)}, u32[]{:S(2)}) collective-permute-start(bf16[4,32,1536]{2,1,0:T(8,128)(2,1)S(1)} %all_to_all.25), channel_id=1, source_target_pairs={{0,8},{8,16},{16,24},{24,32},{32,40},{40,48},{48,56},{56,0},{1,9},... | collective-permute-start | bytes 1179656 | tf_op jit(solution)/shard_map/ppermute | solution.py:31
  59.0 13.5 %collective-permute-start.1 = (bf16[4,32,1536]{2,1,0:T(8,128)(2,1)S(1)}, bf16[4,32,1536]{2,1,0:T(8,128)(2,1)S(1)}, u32[]{:S(2)}, u32[]{:S(2)}) collective-permute-start(bf16[4,32,1536]{2,1,0:T(8,128)(2,1)S(1)} %all_to_all.25), channel_id=1, source_target_pairs={{8,0},{16,8},{24,16},{32,24},{40,32},{48,40},{56,48},{0,56},{9,1},... | collective-permute-start | bytes 1179656 | tf_op jit(solution)/shard_map/ppermute | solution.py:31
  72.5 12.1 %collective-permute-start.2 = (bf16[4,32,1536]{2,1,0:T(8,128)(2,1)S(1)}, bf16[4,32,1536]{2,1,0:T(8,128)(2,1)S(1)}, u32[]{:S(2)}, u32[]{:S(2)}) collective-permute-start(bf16[4,32,1536]{2,1,0:T(8,128)(2,1)S(1)} %collective-permute-done), channel_id=1, source_target_pairs={{0,8},{8,16},{16,24},{24,32},{32,40},{40,48},{48,56},{56,0},{1,9},... | collective-permute-start | bytes 1179656 | tf_op jit(solution)/shard_map/ppermute | solution.py:31
  72.5 12.1 %collective-permute-start.3 = (bf16[4,32,1536]{2,1,0:T(8,128)(2,1)S(1)}, bf16[4,32,1536]{2,1,0:T(8,128)(2,1)S(1)}, u32[]{:S(2)}, u32[]{:S(2)}) collective-permute-start(bf16[4,32,1536]{2,1,0:T(8,128)(2,1)S(1)} %collective-permute-done.1), channel_id=1, source_target_pairs={{8,0},{16,8},{24,16},{32,24},{40,32},{48,40},{56,48},{0,56},{9,1},... | collective-permute-start | bytes 1179656 | tf_op jit(solution)/shard_map/ppermute | solution.py:31
  84.6 11.3 %collective-permute-start.4 = (bf16[4,32,1536]{2,1,0:T(8,128)(2,1)S(1)}, bf16[4,32,1536]{2,1,0:T(8,128)(2,1)S(1)}, u32[]{:S(2)}, u32[]{:S(2)}) collective-permute-start(bf16[4,32,1536]{2,1,0:T(8,128)(2,1)S(1)} %collective-permute-done.2), channel_id=1, source_target_pairs={{0,8},{8,16},{16,24},{24,32},{32,40},{40,48},{48,56},{56,0},{1,9},... | collective-permute-start | bytes 1179656 | tf_op jit(solution)/shard_map/ppermute | solution.py:31
  84.6 12.1 %collective-permute-start.5 = (bf16[4,32,1536]{2,1,0:T(8,128)(2,1)S(1)}, bf16[4,32,1536]{2,1,0:T(8,128)(2,1)S(1)}, u32[]{:S(2)}, u32[]{:S(2)}) collective-permute-start(bf16[4,32,1536]{2,1,0:T(8,128)(2,1)S(1)} %collective-permute-done.3), channel_id=1, source_target_pairs={{8,0},{16,8},{24,16},{32,24},{40,32},{48,40},{56,48},{0,56},{9,1},... | collective-permute-start | bytes 1179656 | tf_op jit(solution)/shard_map/ppermute | solution.py:31
  95.9 10.5 %collective-permute-start.6 = (bf16[4,32,1536]{2,1,0:T(8,128)(2,1)S(1)}, bf16[4,32,1536]{2,1,0:T(8,128)(2,1)S(1)}, u32[]{:S(2)}, u32[]{:S(2)}) collective-permute-start(bf16[4,32,1536]{2,1,0:T(8,128)(2,1)S(1)} %collective-permute-done.4), channel_id=1, source_target_pairs={{0,8},{8,16},{16,24},{24,32},{32,40},{40,48},{48,56},{56,0},{1,9},... | collective-permute-start | bytes 1179656 | tf_op jit(solution)/shard_map/ppermute | solution.py:56
  113.5 18.4 %collective-permute-start.7 = (bf16[512,512]{1,0:T(8,128)(2,1)S(1)}, bf16[512,512]{1,0:T(8,128)(2,1)S(1)}, u32[]{:S(2)}, u32[]{:S(2)}) collective-permute-start(bf16[512,512]{1,0:T(8,128)(2,1)S(1)} %get-tuple-element.27), channel_id=1, source_target_pairs={{0,64},{64,128},{128,192},{192,0},{1,65},{65,129},{129,193},{193,1... | collective-permute-start | bytes 1572872 | tf_op jit(solution)/shard_map/ppermute | solution.py:266
  113.7 18.2 %collective-permute-start.8 = (bf16[512,512]{1,0:T(8,128)(2,1)S(1)}, bf16[512,512]{1,0:T(8,128)(2,1)S(1)}, u32[]{:S(2)}, u32[]{:S(2)}) collective-permute-start(bf16[512,512]{1,0:T(8,128)(2,1)S(1)} %get-tuple-element.28), channel_id=1, source_target_pairs={{64,0},{128,64},{192,128},{0,192},{65,1},{129,65},{193,129},{1,193... | collective-permute-start | bytes 1572872 | tf_op jit(solution)/shard_map/ppermute | solution.py:266
  127.7 21.3 %collective-permute-start.10 = (bf16[512,512]{1,0:T(8,128)(2,1)}, bf16[512,512]{1,0:T(8,128)(2,1)}, u32[]{:S(2)}, u32[]{:S(2)}) collective-permute-start(bf16[512,512]{1,0:T(8,128)(2,1)} %slice.216), channel_id=1, source_target_pairs={{0,64},{64,128},{128,192},{192,0},{1,65},{65,129},{129,193},{193,1... | collective-permute-start | bytes 1572872 | tf_op jit(solution)/shard_map/ppermute | solution.py:266
  128.7 20.3 %collective-permute-start.11 = (bf16[512,512]{1,0:T(8,128)(2,1)}, bf16[512,512]{1,0:T(8,128)(2,1)}, u32[]{:S(2)}, u32[]{:S(2)}) collective-permute-start(bf16[512,512]{1,0:T(8,128)(2,1)} %slice.217), channel_id=1, source_target_pairs={{64,0},{128,64},{192,128},{0,192},{65,1},{129,65},{193,129},{1,193... | collective-permute-start | bytes 1572872 | tf_op jit(solution)/shard_map/ppermute | solution.py:266
  149.0 1.2 copy-start.2
  150.2 12.7 %copy-start.4 = (bf16[512,512]{1,0:T(8,128)(2,1)S(1)}, bf16[512,512]{1,0:T(8,128)(2,1)}, u32[]{:S(2)}) copy-start(bf16[512,512]{1,0:T(8,128)(2,1)} %get-tuple-element.41) | copy-start | bytes 1572868
  150.2 15.1 %copy-start.3 = (bf16[512,512]{1,0:T(8,128)(2,1)S(1)}, bf16[512,512]{1,0:T(8,128)(2,1)}, u32[]{:S(2)}) copy-start(bf16[512,512]{1,0:T(8,128)(2,1)} %get-tuple-element.35) | copy-start | bytes 1572868
  150.4 12.5 %collective-permute-start.12 = (bf16[512,512]{1,0:T(8,128)(2,1)S(1)}, bf16[512,512]{1,0:T(8,128)(2,1)S(1)}, u32[]{:S(2)}, u32[]{:S(2)}) collective-permute-start(bf16[512,512]{1,0:T(8,128)(2,1)S(1)} %add_convert_fusion.1), channel_id=1, source_target_pairs={{64,0},{128,64},{192,128},{0,192},{65,1},{129,65},{193,129},{1,193... | collective-permute-start | bytes 1572872 | tf_op jit(solution)/shard_map/ppermute | solution.py:266
  153.8 11.5 %collective-permute-start.9 = (bf16[512,512]{1,0:T(8,128)(2,1)S(1)}, bf16[512,512]{1,0:T(8,128)(2,1)S(1)}, u32[]{:S(2)}, u32[]{:S(2)}) collective-permute-start(bf16[512,512]{1,0:T(8,128)(2,1)S(1)} %add_convert_fusion.3), channel_id=1, source_target_pairs={{0,64},{64,128},{128,192},{192,0},{1,65},{65,129},{129,193},{193,1... | collective-permute-start | bytes 1572872 | tf_op jit(solution)/shard_map/ppermute | solution.py:266
  165.3 6.2 %copy-start.7 = (s32[192,2]{0,1:T(2,128)S(1)}, s32[192,2]{0,1:T(2,128)}, u32[]{:S(2)}) copy-start(s32[192,2]{0,1:T(2,128)} %param.9) | copy-start | bytes 4612
  165.3 6.3 %copy-start.6 = (bf16[31,1024]{1,0:T(8,128)(2,1)S(1)}, bf16[31,1024]{1,0:T(8,128)(2,1)}, u32[]{:S(2)}) copy-start(bf16[31,1024]{1,0:T(8,128)(2,1)} %param.10) | copy-start | bytes 190468
  165.3 22.0 %copy-start.5 = (bf16[192,1024]{1,0:T(8,128)(2,1)S(1)}, bf16[192,1024]{1,0:T(8,128)(2,1)}, u32[]{:S(2)}) copy-start(bf16[192,1024]{1,0:T(8,128)(2,1)} %param.7) | copy-start | bytes 1179652
  167.8 30.8 %copy-start.8 = (bf16[192,2]{0,1:T(2,128)(2,1)S(1)}, bf16[192,2]{0,1:T(2,128)(2,1)}, u32[]{:S(2)}) copy-start(bf16[192,2]{0,1:T(2,128)(2,1)} %param.8) | copy-start | bytes 2308
  167.8 19.6 %all-to-all-start.3 = ((bf16[8,64,1024]{2,1,0:T(8,128)(2,1)}), bf16[8,64,1024]{2,1,0:T(8,128)(2,1)S(1)}, u32[]{:S(2)}, u32[]{:S(2)}) async-start(bf16[8,64,1024]{2,1,0:T(8,128)(2,1)} %bitcast.31), calls=%async_computation.3 | async-start | bytes 2097152 | tf_op jit(solution)/shard_map/all_to_all | solution.py:306
  187.8 11.4 %collective-permute-start.14 = (bf16[15,1024]{1,0:T(8,128)(2,1)S(1)}, bf16[15,1024]{1,0:T(8,128)(2,1)S(1)}, u32[]{:S(2)}, u32[]{:S(2)}) collective-permute-start(bf16[15,1024]{1,0:T(8,128)(2,1)S(1)} %get-tuple-element.46), channel_id=1, source_target_pairs={{1,0},{2,1},{3,2},{4,3},{5,4},{6,5},{7,6},{8,7},{9,8},{10,9},{11,1... | collective-permute-start | bytes 92168 | tf_op jit(solution)/shard_map/ppermute | solution.py:85
  196.4 9.6 %collective-permute-start.13 = (bf16[15,1024]{1,0:T(8,128)(2,1)S(1)}, bf16[15,1024]{1,0:T(8,128)(2,1)S(1)}, u32[]{:S(2)}, u32[]{:S(2)}) collective-permute-start(bf16[15,1024]{1,0:T(8,128)(2,1)S(1)} %get-tuple-element.45), channel_id=1, source_target_pairs={{0,1},{1,2},{2,3},{3,4},{4,5},{5,6},{6,7},{7,8},{8,9},{9,10},{10,1... | collective-permute-start | bytes 92168 | tf_op jit(solution)/shard_map/ppermute | solution.py:84
  206.1 9.7 %all-to-all-start.4 = ((bf16[4,32,1536]{2,1,0:T(8,128)(2,1)}), bf16[4,32,1536]{2,1,0:T(8,128)(2,1)S(1)}, u32[]{:S(2)}, u32[]{:S(2)}) async-start(bf16[4,32,1536]{2,1,0:T(8,128)(2,1)} %bitcast.110), calls=%async_computation.5 | async-start | bytes 786432 | tf_op jit(solution)/shard_map/all_to_all | solution.py:65
Sparse Core Ops, SparseCore 0:
  10.7 31.4 all-gather.6
  45.3 50.1 all-gather.4
  149.2 47.2 reduce-scatter.1

commit v7 on v6

--- a/solution.py
+++ b/solution.py
@@ -14,6 +14,7 @@
 META = 8
 STEP = 4
 CHUNK = 256
+EDGE = 16
 
 
 def dot(a, b, contract, batch=((), ())):
@@ -74,7 +75,7 @@
     return chosen[..., None, :] & (ranks[..., None, :] == jnp.arange(SLOTS)[:, None])
 
 
-def with_halo(block, width):
+def halo_of(block, width):
     axes = ("y", "z", "x", "c")
     count = 1
     for axis in axes:
@@ -82,8 +83,16 @@
     forward = [(i, i + 1) for i in range(count - 1)]
     backward = [(target, source) for source, target in forward]
     low = lax.ppermute(block[block.shape[0] - width :], axes, forward)
-    high = lax.ppermute(block[:width], axes, backward)
-    return jnp.concatenate([low, block, high], axis=0)
+    return low, lax.ppermute(block[:width], axes, backward)
+
+
+def convolved(centre, rows, taps):
+    total = centre
+    count = taps.shape[0]
+    for offset in range(count):
+        first = count - 1 - offset
+        total = total + taps[offset] * rows[first : first + centre.shape[0]]
+    return total.astype(BF)
 
 
 def route_kernel(scaled, x_ref, out_ref):
@@ -111,7 +120,7 @@
         grid=(groups,),
         in_specs=[pl.BlockSpec((1, rows, width), lambda i: (i, 0, 0))],
         out_specs=pl.BlockSpec((experts, 1, SLOTS, width), lambda i: (0, i, 0, 0)),
-        out_shape=jax.ShapeDtypeStruct((experts, groups, SLOTS, width), BF),
+        out_shape=pltpu.HBM((experts, groups, SLOTS, width), BF),
         compiler_params=pltpu.CompilerParams(vmem_limit_bytes=32 * 1024 * 1024),
     )(packed)
 
@@ -143,9 +152,16 @@
         low_ref[place, :128] = jnp.where(row == SPARE, line, low_ref[place, :128].astype(F32)).astype(BF)
 
 
-def rows_kernel(info, u_ref, q_ref, w_ref, *refs):
+def rows_kernel(targets, steps, info, u_ref, q_ref, w_ref, *refs):
     count, width = u_ref.shape[1] * SLOTS, u_ref.shape[3]
-    rows_of(u_ref[0].reshape(count, width), q_ref[:, 0].reshape(count, width), w_ref, *refs[-4:])
+    pre_ref, h_ref = refs[-2:]
+    pairs = refs[-2 - 2 * targets : -2]
+    for t in range(targets):
+
+        @pl.when(pl.program_id(0) // steps == t)
+        def _():
+            u, q = u_ref[0].reshape(count, width), q_ref[:, 0].reshape(count, width)
+            rows_of(u, q, w_ref, pairs[2 * t], pairs[2 * t + 1], pre_ref, h_ref)
 
 
 def last_kernel(info, u_ref, q_ref, w_ref, pre_ref, h_ref, low_ref, high_ref, term_ref, own_pre, own_h, total):
@@ -217,39 +233,41 @@
     groups, sources, _, width = rows_in.shape
     part = weights.shape[1] // 3
     steps = sources // STEP
-    mine = len(targets) * sources * SLOTS
+    count = len(targets)
     info = jnp.stack(targets).astype(jnp.int32)
     by_group = lambda i, info: (info[i // steps], i % steps, 0, 0)
     by_source = lambda i, info: (i % steps, info[i // steps], 0, 0)
-    in_order = lambda i, info: (i, 0)
-    low, high, *kept = pl.pallas_call(
-        rows_kernel,
+    half_rows = [
+        pl.BlockSpec((STEP * SLOTS, width // 2), lambda i, info, t=t: (jnp.clip(i - t * steps, 0, steps - 1), 0))
+        for t in range(count)
+        for _ in range(2)
+    ]
+    *halves, pre_grads, hidden = pl.pallas_call(
+        functools.partial(rows_kernel, count, steps),
         grid_spec=pltpu.PrefetchScalarGridSpec(
             num_scalar_prefetch=1,
-            grid=(len(targets) * steps,),
+            grid=(count * steps,),
             in_specs=[
                 pl.BlockSpec((1, STEP, SLOTS, width), by_group),
                 pl.BlockSpec((STEP, 1, SLOTS, width), by_source),
                 pl.BlockSpec(weights.shape, lambda i, info: (0, 0)),
             ]
             + [pl.BlockSpec(memory_space=pl.ANY) for _ in kept],
-            out_specs=[
-                pl.BlockSpec((STEP * SLOTS, width // 2), in_order),
-                pl.BlockSpec((STEP * SLOTS, width // 2), in_order),
+            out_specs=half_rows
+            + [
                 pl.BlockSpec((STEP * SLOTS, 2 * part), lambda i, info: (info[i // steps] * steps + i % steps, 0)),
                 pl.BlockSpec((STEP, 1, SLOTS, part), by_source),
             ],
         ),
-        out_shape=[
-            jax.ShapeDtypeStruct((mine, width // 2), BF),
-            jax.ShapeDtypeStruct((mine, width // 2), BF),
+        out_shape=[jax.ShapeDtypeStruct((sources * SLOTS, width // 2), BF)] * (2 * count)
+        + [
             jax.ShapeDtypeStruct((groups * sources * SLOTS, 2 * part), BF),
             jax.ShapeDtypeStruct((sources, groups, SLOTS, part), BF),
         ],
-        input_output_aliases={4 + k: 2 + k for k in range(len(kept))},
+        input_output_aliases={4 + k: 2 * count + k for k in range(len(kept))},
         compiler_params=pltpu.CompilerParams(vmem_limit_bytes=52 * 1024 * 1024),
     )(info, rows_in, rows_q, weights, *kept)
-    return low, high, kept
+    return halves, [pre_grads, hidden]
 
 
 def add(*parts):
@@ -268,14 +286,13 @@
     def run(offsets, kept):
         return expert_rows([(me + offset) % ny for offset in offsets], rows_in, rows_q, weights, kept)
 
-    far_low, far_high, kept = run([2], [])
+    (far_low, far_high), kept = run([2], [])
     low_via, high_via = send(far_low, up), send(far_high, down)
-    near_low, near_high, kept = run([1, ny - 1], kept)
+    (up_low, up_high, down_low, down_high), kept = run([1, ny - 1], kept)
     low_via, high_via, kept = lax.optimization_barrier((low_via, high_via, kept))
-    rows = far_low.shape[0]
-    below_high, above_low = send(near_high[:rows], up), send(near_low[rows:], down)
-    below_low = send(add(near_low[:rows], low_via).astype(BF), up)
-    above_high = send(add(near_high[rows:], high_via).astype(BF), down)
+    below_high, above_low = send(up_high, up), send(down_low, down)
+    below_low = send(add(up_low, low_via).astype(BF), up)
+    above_high = send(add(down_high, high_via).astype(BF), down)
     targets = [(me + offset) % ny for offset in (0, 2, 1, ny - 1)]
     own_low, own_high, term = last_rows(targets, rows_in, rows_q, weights, *kept)
     term, below_high, above_low = lax.optimization_barrier((term, below_high, above_low))
@@ -321,14 +338,18 @@
     )
     gate_out = (gate_sums / gate_values.astype(F32)).astype(BF)
 
-    taps = conv_kernel.shape[0]
-    half = (taps - 1) // 2
-    kernel_rows = conv_kernel.astype(F32)
-    padded = with_halo(frame_grad.astype(BF), half).astype(F32)
-    conv_part = jnp.zeros((frames, width), F32)
-    for offset in range(taps):
-        conv_part = conv_part + kernel_rows[offset] * padded[2 * half - offset : 2 * half - offset + frames]
-    input_grad = (frame_grad + conv_part).astype(BF)
+    taps = conv_kernel.astype(F32)
+    half = taps.shape[0] // 2
+    rounded = frame_grad.astype(BF)
+    low, high = halo_of(rounded, half)
+    rows = rounded.astype(F32)
+    inner = convolved(frame_grad[EDGE : frames - EDGE], rows[EDGE - half : frames - EDGE + half], taps)
+    low, high, inner, weight_grad = lax.optimization_barrier((low, high, inner, weight_grad))
+    top = jnp.concatenate([low.astype(F32), rows[: EDGE + half]], axis=0)
+    bottom = jnp.concatenate([rows[frames - EDGE - half :], high.astype(F32)], axis=0)
+    first = convolved(frame_grad[:EDGE], top, taps)
+    final = convolved(frame_grad[frames - EDGE :], bottom, taps)
+    input_grad = jnp.concatenate([first, inner, final], axis=0)
     return input_grad, weight_grad, gate_out
 
 

time: 225 us -> 221 us (0.982)
  local copies, waits for them, and re-layouts: 19.4 us -> 8.31 us
  Pallas kernels: 38.1 us -> 40.5 us
  waiting for transfers between devices: 64.2 us -> 66.6 us
    ppermute x2, waiting for transfers between devices: 6.79 us -> 0.01 us  [the longest x1 0.01 us: halo_of(): low = lax.ppermute(block[block.shape[0] - width:], axes, forward)]
    dynamic_update_slice x8, local copies, waits for them, and re-layouts: 6.26 us -> 0.25 us  [place(): return lax.dynamic_update_slice(buffer, shard[:, None], (0, z % nz, 0, 0))]
    ppermute x6, waiting for transfers between devices: 20.5 us -> 25.8 us  [ring_step(): return (lax.ppermute(right, axis, up), lax.ppermute(left, axis, down))]
    all_to_all x1, waiting for transfers between devices: 2.23 us -> 5.32 us  [scatter_weight_grad(): lax.all_to_all(mine.reshape(ny, rows, 3 * part), 'y', 0, 0, tiled=True)]
    slice x5 -> x4, local copies, waits for them, and re-layouts: 2.8 us -> 0.13 us  [the longest x2 0.09 us: convolved(): total = total + taps[offset] * rows[first:first + centre.shape[0]]]
    convert_element_type x4 -> x7, other arithmetic: 4.09 us -> 4.61 us  [the longest x3 3.29 us: convolved(): return total.astype(BF)]
  transfers between devices with their start and end apart: 21 -> 21, of which waited for: 9 -> 9; matrix products, arithmetic and copies ran while one was open for 10% -> 6% of each run, Pallas kernels for 14% -> 16%
where the time goes in v7:
time: 221 us; the launch traced here: 219 us
  waiting for transfers between devices  66.6 us (30%)
  starting transfers between devices  43.5 us (20%)
  Pallas kernels  40.5 us (18%)
  blocking collectives  31.8 us (14%)
  between operations  14.2 us (6%)
  other arithmetic  13.7 us (6%)
  local copies, waits for them, and re-layouts  8.31 us (4%)
    ppermute x6, waiting for transfers between devices, ring_step(): return (lax.ppermute(right, axis, up), lax.ppermute(left, axis, down))  25.8 us
    all_to_all x1, blocking collectives, local(): mine_in = lax.all_to_all(sent_in, by_expert, 0, 0, tiled=True)  20.5 us
    pallas_call x1, Pallas kernels, last_rows(): pl.pallas_call(last_kernel, grid_spec=pltpu.PrefetchScalarGridSpec(num_sc...  17.1 us
    pallas_call x2, Pallas kernels, expert_rows(): pl.pallas_call(functools.partial(rows_kernel, count, steps), grid_spec=pl...  17 us
    all_to_all x1, waiting for transfers between devices, local(): returned = lax.all_to_all(summed, by_expert, 0, 0, tiled=True)  15.4 us
    ppermute x6, starting transfers between devices, ring_step(): return (lax.ppermute(right, axis, up), lax.ppermute(left, axis, down))  12.5 us
    all_to_all x1, blocking collectives, own_columns(): lax.all_to_all(sliced.reshape(ny, rows, 3 * part), 'y', 0, 0, tiled=True)  11.3 us
    ppermute x1, waiting for transfers between devices, gather_weights(): right = lax.ppermute(right, 'z', ring_ways('z')[0])  10.4 us
  transfers between devices with their start and end apart: 21, of which 9 were waited for; matrix products, arithmetic and copies ran while one was open for 6% of the time, Pallas kernels for 16%

profile of v7, /device:TPU:8, one launch (start us, length us, event | category | flops | bytes accessed | tf_op | source)
XLA Modules:
  0.0 219.4 jit_solution(7086848907811177611)
XLA Ops:
  7.2 0.0 all-gather.7.cloned.1.call-start
  7.2 0.7 convert_bitcast_fusion
  7.9 0.7 fusion.168
  8.6 1.9 pad_maximum_fusion.1
  10.6 0.0 all-gather.5.cloned.1.call-start
  10.6 1.3 reshape_squeeze.3
  11.9 0.2 copy.61
  12.1 0.5 reshape.32
  12.6 11.3 %all_to_all.25 = bf16[4,32,1536]{2,1,0:T(8,128)(2,1)S(1)} all-to-all(bf16[4,32,1536]{2,1,0:T(8,128)(2,1)S(1)} %reshape.32), channel_id=1, replica_groups=mesh['y'=4,'z'=8,'x'=4,'c'=2] {'y'}, dimensions={0} | all-to-all | bytes 786432 | tf_op jit(solution)/shard_map/all_to_all | solution.py:40
  24.0 1.8 shard_map.85
  25.8 20.5 %all_to_all.26 = bf16[8,1,64,1024]{3,2,1,0:T(8,128)(2,1)} all-to-all(bf16[8,1,64,1024]{3,2,1,0:T(8,128)(2,1)} %shard_map.85), channel_id=1, replica_groups=mesh['y'=4,'z'=8,'x'=4,'c'=2] {'x','c'}, dimensions={0} | all-to-all | bytes 2097152 | tf_op jit(solution)/shard_map/all_to_all | solution.py:315
  46.5 0.0 all-gather.7.cloned.1.call-done
  46.5 1.4 copy-done
  48.0 4.6 %shard_map.86 = bf16[8,4,64,1024]{3,2,1,0:T(8,128)(2,1)} custom-call(bf16[4,200,1024]{2,1,0:T(8,128)(2,1)S(1)} %bitcast.102), custom_call_target="tpu_custom_call" | custom-call | tf_op jit(solution)/shard_map/pallas_call | solution.py:118
  52.6 4.5 %all-to-all-start.2 = ((bf16[8,4,64,1024]{3,2,1,0:T(8,128)(2,1)}), bf16[8,4,64,1024]{3,2,1,0:T(8,128)(2,1)}, u32[]{:S(2)}, u32[]{:S(2)}) async-start(bf16[8,4,64,1024]{3,2,1,0:T(8,128)(2,1)} %shard_map.86), calls=%async_computation.2 | async-start | bytes 8388608 | tf_op jit(solution)/shard_map/all_to_all | solution.py:319
  57.1 0.0 reduce-scatter.2.cloned.1.call-start
  57.2 2.0 collective-permute-start
  59.2 4.1 %collective-permute-start.1 = (bf16[4,32,1536]{2,1,0:T(8,128)(2,1)S(1)}, bf16[4,32,1536]{2,1,0:T(8,128)(2,1)S(1)}, u32[]{:S(2)}, u32[]{:S(2)}) collective-permute-start(bf16[4,32,1536]{2,1,0:T(8,128)(2,1)S(1)} %all_to_all.25), channel_id=1, source_target_pairs={{8,0},{16,8},{24,16},{32,24},{40,32},{48,40},{56,48},{0,56},{9,1},... | collective-permute-start | bytes 1179656 | tf_op jit(solution)/shard_map/ppermute | solution.py:32
  63.2 0.3 broadcast_in_dim.37
  63.6 9.0 %collective-permute-done = bf16[4,32,1536]{2,1,0:T(8,128)(2,1)S(1)} collective-permute-done((bf16[4,32,1536]{2,1,0:T(8,128)(2,1)S(1)}, bf16[4,32,1536]{2,1,0:T(8,128)(2,1)S(1)}, u32[]{:S(2)}, u32[]{:S(2)}) %collective-permute-start) | collective-permute-done | bytes 393248 | tf_op jit(solution)/shard_map/ppermute | solution.py:32
  72.7 3.2 %collective-permute-start.3 = (bf16[4,32,1536]{2,1,0:T(8,128)(2,1)S(1)}, bf16[4,32,1536]{2,1,0:T(8,128)(2,1)S(1)}, u32[]{:S(2)}, u32[]{:S(2)}) collective-permute-start(bf16[4,32,1536]{2,1,0:T(8,128)(2,1)S(1)} %collective-permute-done.1), channel_id=1, source_target_pairs={{8,0},{16,8},{24,16},{32,24},{40,32},{48,40},{56,48},{0,56},{9,1},... | collective-permute-start | bytes 1179656 | tf_op jit(solution)/shard_map/ppermute | solution.py:32
  76.0 8.8 %collective-permute-done.2 = bf16[4,32,1536]{2,1,0:T(8,128)(2,1)S(1)} collective-permute-done((bf16[4,32,1536]{2,1,0:T(8,128)(2,1)S(1)}, bf16[4,32,1536]{2,1,0:T(8,128)(2,1)S(1)}, u32[]{:S(2)}, u32[]{:S(2)}) %collective-permute-start.2) | collective-permute-done | bytes 393248 | tf_op jit(solution)/shard_map/ppermute | solution.py:32
  84.8 3.2 %collective-permute-start.5 = (bf16[4,32,1536]{2,1,0:T(8,128)(2,1)S(1)}, bf16[4,32,1536]{2,1,0:T(8,128)(2,1)S(1)}, u32[]{:S(2)}, u32[]{:S(2)}) collective-permute-start(bf16[4,32,1536]{2,1,0:T(8,128)(2,1)S(1)} %collective-permute-done.3), channel_id=1, source_target_pairs={{8,0},{16,8},{24,16},{32,24},{40,32},{48,40},{56,48},{0,56},{9,1},... | collective-permute-start | bytes 1179656 | tf_op jit(solution)/shard_map/ppermute | solution.py:32
  88.1 8.0 %collective-permute-done.4 = bf16[4,32,1536]{2,1,0:T(8,128)(2,1)S(1)} collective-permute-done((bf16[4,32,1536]{2,1,0:T(8,128)(2,1)S(1)}, bf16[4,32,1536]{2,1,0:T(8,128)(2,1)S(1)}, u32[]{:S(2)}, u32[]{:S(2)}) %collective-permute-start.4) | collective-permute-done | bytes 393248 | tf_op jit(solution)/shard_map/ppermute | solution.py:32
  96.2 10.4 %collective-permute-done.6 = bf16[4,32,1536]{2,1,0:T(8,128)(2,1)S(1)} collective-permute-done((bf16[4,32,1536]{2,1,0:T(8,128)(2,1)S(1)}, bf16[4,32,1536]{2,1,0:T(8,128)(2,1)S(1)}, u32[]{:S(2)}, u32[]{:S(2)}) %collective-permute-start.6) | collective-permute-done | bytes 393248 | tf_op jit(solution)/shard_map/ppermute | solution.py:57
  106.6 0.1 all-to-all-done.2.q_ref
  106.8 1.5 copy-done.1
  108.3 6.4 %shard_map.87 = (bf16[512,512]{1,0:T(8,128)(2,1)S(1)}, bf16[512,512]{1,0:T(8,128)(2,1)S(1)}, bf16[2048,1024]{1,0:T(8,128)(2,1)}, bf16[8,4,64,512]{3,2,1,0:T(8,128)(2,1)}) custom-call(s32[1]{0:T(128)} %bitcast.5.info, bf16[4,8,64,1024]{3,2,1,0:T(8,128)(2,1)} %bitcast.107, bf16[8,4,64,1024]{3,2,1,0:T(8,128)(2,1)} %all-to-all-done.2.q_ref, ...), custom_call_target="tpu_custom_call" | custom-call | tf_op jit(solution)/shard_map/pallas_call | solution.py:245
  114.7 0.2 collective-permute-start.7
  114.8 1.9 collective-permute-start.8
  116.7 0.1 pad_add_fusion.1.info
  116.8 10.6 %shard_map.88 = (bf16[512,512]{1,0:T(8,128)(2,1)S(1)}, bf16[512,512]{1,0:T(8,128)(2,1)S(1)}, bf16[512,512]{1,0:T(8,128)(2,1)S(1)}, bf16[512,512]{1,0:T(8,128)(2,...) custom-call(s32[2]{0:T(128)S(1)} %pad_add_fusion.1.info, ...), custom_call_target="tpu_custom_call", output_to_operand_aliasing={{4}: (4, {}), {5}: (5, {})} | custom-call | tf_op jit(solution)/shard_map/pallas_call | solution.py:245
  127.3 0.3 collective-permute-start.10
  127.6 2.5 %collective-permute-start.11 = (bf16[512,512]{1,0:T(8,128)(2,1)S(1)}, bf16[512,512]{1,0:T(8,128)(2,1)}, u32[]{:S(2)}, u32[]{:S(2)}) collective-permute-start(bf16[512,512]{1,0:T(8,128)(2,1)S(1)} %get-tuple-element.46), channel_id=1, source_target_pairs={{64,0},{128,64},{192,128},{0,192},{65,1},{129,65},{193,129},{1,193... | collective-permute-start | bytes 1572872 | tf_op jit(solution)/shard_map/ppermute | solution.py:284
  130.1 0.6 pad_add_fusion.info
  130.7 17.1 %shard_map.89 = (bf16[512,512]{1,0:T(8,128)(2,1)}, bf16[512,512]{1,0:T(8,128)(2,1)}, bf16[8,4,32,1536]{3,2,1,0:T(8,128)(2,1)}) custom-call(s32[4]{0:T(128)} %pad_add_fusion.info, bf16[4,8,64,1024]{3,2,1,0:T(8,128)(2,1)} %bitcast.109, bf16[8,4,64,1024]{3,2,1,0:T(8,128)(2,1)} %all-to-all-done.2.q_ref, bf16[1024,1536]{1,0:T(8,128)(2,1)} %bitcast.106, ...), custom_call_target="tpu_custom_call" | custom-call | tf_op jit(solution)/shard_map/pallas_call | solution.py:200
  147.9 1.0 copy-done.3
  148.9 1.2 add_convert_fusion.1
  150.0 3.3 %collective-permute-start.12 = (bf16[512,512]{1,0:T(8,128)(2,1)S(1)}, bf16[512,512]{1,0:T(8,128)(2,1)S(1)}, u32[]{:S(2)}, u32[]{:S(2)}) collective-permute-start(bf16[512,512]{1,0:T(8,128)(2,1)S(1)} %add_convert_fusion.1), channel_id=1, source_target_pairs={{64,0},{128,64},{192,128},{0,192},{65,1},{129,65},{193,129},{1,193... | collective-permute-start | bytes 1572872 | tf_op jit(solution)/shard_map/ppermute | solution.py:284
  153.3 0.1 add_convert_fusion.3
  153.4 0.1 collective-permute-start.9
  153.5 8.2 %collective-permute-done.12 = bf16[512,512]{1,0:T(8,128)(2,1)S(1)} collective-permute-done((bf16[512,512]{1,0:T(8,128)(2,1)S(1)}, bf16[512,512]{1,0:T(8,128)(2,1)S(1)}, u32[]{:S(2)}, u32[]{:S(2)}) %collective-permute-start.12) | collective-permute-done | bytes 524320 | tf_op jit(solution)/shard_map/ppermute | solution.py:284
  161.7 1.2 add_convert_fusion
  163.0 1.2 collective-permute-done.9
  164.2 1.3 add_convert_fusion.2
  165.5 1.1 pad_maximum_fusion
  166.6 3.8 %all-to-all-start.3 = ((bf16[8,64,1024]{2,1,0:T(8,128)(2,1)}), bf16[8,64,1024]{2,1,0:T(8,128)(2,1)S(1)}, u32[]{:S(2)}, u32[]{:S(2)}) async-start(bf16[8,64,1024]{2,1,0:T(8,128)(2,1)} %bitcast.31), calls=%async_computation.3 | async-start | bytes 2097152 | tf_op jit(solution)/shard_map/all_to_all | solution.py:323
  170.4 0.1 convolution_convert_fusion
  170.6 0.1 fusion.174
  170.7 15.4 %all-to-all-done.3 = bf16[8,64,1024]{2,1,0:T(8,128)(2,1)S(1)} async-done(((bf16[8,64,1024]{2,1,0:T(8,128)(2,1)}), bf16[8,64,1024]{2,1,0:T(8,128)(2,1)S(1)}, u32[]{:S(2)}, u32[]{:S(2)}) %all-to-all-start.3) | async-done | bytes 1048608 | tf_op jit(solution)/shard_map/all_to_all | solution.py:323
  186.1 0.4 fusion.171
  186.5 1.9 collective-permute-start.13
  188.5 8.6 %collective-permute-start.14 = (bf16[15,1024]{1,0:T(8,128)(2,1)S(1)}, bf16[15,1024]{1,0:T(8,128)(2,1)S(1)}, u32[]{:S(2)}, u32[]{:S(2)}) collective-permute-start(bf16[15,1024]{1,0:T(8,128)(2,1)S(1)} %get-tuple-element.61), channel_id=1, source_target_pairs={{1,0},{2,1},{3,2},{4,3},{5,4},{6,5},{7,6},{8,7},{9,8},{10,9},{11,1... | collective-permute-start | bytes 92168 | tf_op jit(solution)/shard_map/ppermute | solution.py:86
  197.1 0.2 fusion.34
  197.3 2.7 %fusion.2 = bf16[160,1024]{1,0:T(8,128)(2,1)S(1)} fusion(f32[192,1024]{1,0:T(8,128)S(1)} %get-tuple-element.57, f32[192,1024]{1,0:T(8,128)S(1)} %get-tuple-element.96, f32[1024]{0:T(1024)S(1)} %bitcast.147, f32[1024]{0:T(1024)S(1)} %bitcast.144, f32[1024]{0:T(1024)S(1)} %bitcast.141, f32[1024]{0:T(1024)S(1)} %bitcast.138, f32[1024]{0:T(1024)S(1)} %bitcast.135, ...), kind=kLoop, calls=%fused_computation.38 | loop fusion | flops 10321920 | bytes 21426176 | tf_op jit(solution)/shard_map/convert_element_type | solution.py:95
  200.0 3.9 %all-to-all-start.4 = ((bf16[4,32,1536]{2,1,0:T(8,128)(2,1)}), bf16[4,32,1536]{2,1,0:T(8,128)(2,1)S(1)}, u32[]{:S(2)}, u32[]{:S(2)}) async-start(bf16[4,32,1536]{2,1,0:T(8,128)(2,1)} %bitcast.113), calls=%async_computation.5 | async-start | bytes 786432 | tf_op jit(solution)/shard_map/all_to_all | solution.py:66
  203.9 0.6 fusion.170
  204.5 5.3 %all-to-all-done.4 = bf16[4,32,1536]{2,1,0:T(8,128)(2,1)S(1)} async-done(((bf16[4,32,1536]{2,1,0:T(8,128)(2,1)}), bf16[4,32,1536]{2,1,0:T(8,128)(2,1)S(1)}, u32[]{:S(2)}, u32[]{:S(2)}) %all-to-all-start.4) | async-done | bytes 393248 | tf_op jit(solution)/shard_map/all_to_all | solution.py:66
  209.8 0.3 reshape.37
  210.1 0.4 copy.47
  210.4 1.0 reshape.38
  211.5 0.3 fusion.162
  211.8 0.3 fusion.104
  212.1 0.8 pad_maximum_fusion.3
  (49 shorter events, 0.5 us)
Async XLA Ops:
  7.2 39.4 %all-gather.7.cloned.1.call-start = ((), (), s32[]{:S(2)}) async-start(), calls=%async_computation.8 | async-start | bytes 2048000 | tf_op jit(solution)/shard_map/all_gather | solution.py:311
  10.6 96.2 %all-gather.5.cloned.1.call-start = ((), (), s32[]{:S(2)}) async-start(), calls=%async_computation.7 | async-start | bytes 5242880 | tf_op jit(solution)/shard_map/all_gather | solution.py:316
  46.5 1.4 copy-start
  52.6 54.2 %all-to-all-start.2 = ((bf16[8,4,64,1024]{3,2,1,0:T(8,128)(2,1)}), bf16[8,4,64,1024]{3,2,1,0:T(8,128)(2,1)}, u32[]{:S(2)}, u32[]{:S(2)}) async-start(bf16[8,4,64,1024]{3,2,1,0:T(8,128)(2,1)} %shard_map.86), calls=%async_computation.2 | async-start | bytes 8388608 | tf_op jit(solution)/shard_map/all_to_all | solution.py:319
  57.1 142.9 %reduce-scatter.2.cloned.1.call-start = ((), (), s32[]{:S(2)}) async-start(), calls=%async_computation.6 | async-start | bytes 3538944 | tf_op jit(solution)/shard_map/reduce_scatter | solution.py:65
  57.2 15.5 %collective-permute-start = (bf16[4,32,1536]{2,1,0:T(8,128)(2,1)S(1)}, bf16[4,32,1536]{2,1,0:T(8,128)(2,1)S(1)}, u32[]{:S(2)}, u32[]{:S(2)}) collective-permute-start(bf16[4,32,1536]{2,1,0:T(8,128)(2,1)S(1)} %all_to_all.25), channel_id=1, source_target_pairs={{0,8},{8,16},{16,24},{24,32},{32,40},{40,48},{48,56},{56,0},{1,9},... | collective-permute-start | bytes 1179656 | tf_op jit(solution)/shard_map/ppermute | solution.py:32
  59.2 13.5 %collective-permute-start.1 = (bf16[4,32,1536]{2,1,0:T(8,128)(2,1)S(1)}, bf16[4,32,1536]{2,1,0:T(8,128)(2,1)S(1)}, u32[]{:S(2)}, u32[]{:S(2)}) collective-permute-start(bf16[4,32,1536]{2,1,0:T(8,128)(2,1)S(1)} %all_to_all.25), channel_id=1, source_target_pairs={{8,0},{16,8},{24,16},{32,24},{40,32},{48,40},{56,48},{0,56},{9,1},... | collective-permute-start | bytes 1179656 | tf_op jit(solution)/shard_map/ppermute | solution.py:32
  72.7 12.1 %collective-permute-start.2 = (bf16[4,32,1536]{2,1,0:T(8,128)(2,1)S(1)}, bf16[4,32,1536]{2,1,0:T(8,128)(2,1)S(1)}, u32[]{:S(2)}, u32[]{:S(2)}) collective-permute-start(bf16[4,32,1536]{2,1,0:T(8,128)(2,1)S(1)} %collective-permute-done), channel_id=1, source_target_pairs={{0,8},{8,16},{16,24},{24,32},{32,40},{40,48},{48,56},{56,0},{1,9},... | collective-permute-start | bytes 1179656 | tf_op jit(solution)/shard_map/ppermute | solution.py:32
  72.7 12.1 %collective-permute-start.3 = (bf16[4,32,1536]{2,1,0:T(8,128)(2,1)S(1)}, bf16[4,32,1536]{2,1,0:T(8,128)(2,1)S(1)}, u32[]{:S(2)}, u32[]{:S(2)}) collective-permute-start(bf16[4,32,1536]{2,1,0:T(8,128)(2,1)S(1)} %collective-permute-done.1), channel_id=1, source_target_pairs={{8,0},{16,8},{24,16},{32,24},{40,32},{48,40},{56,48},{0,56},{9,1},... | collective-permute-start | bytes 1179656 | tf_op jit(solution)/shard_map/ppermute | solution.py:32
  84.8 11.3 %collective-permute-start.4 = (bf16[4,32,1536]{2,1,0:T(8,128)(2,1)S(1)}, bf16[4,32,1536]{2,1,0:T(8,128)(2,1)S(1)}, u32[]{:S(2)}, u32[]{:S(2)}) collective-permute-start(bf16[4,32,1536]{2,1,0:T(8,128)(2,1)S(1)} %collective-permute-done.2), channel_id=1, source_target_pairs={{0,8},{8,16},{16,24},{24,32},{32,40},{40,48},{48,56},{56,0},{1,9},... | collective-permute-start | bytes 1179656 | tf_op jit(solution)/shard_map/ppermute | solution.py:32
  84.8 11.4 %collective-permute-start.5 = (bf16[4,32,1536]{2,1,0:T(8,128)(2,1)S(1)}, bf16[4,32,1536]{2,1,0:T(8,128)(2,1)S(1)}, u32[]{:S(2)}, u32[]{:S(2)}) collective-permute-start(bf16[4,32,1536]{2,1,0:T(8,128)(2,1)S(1)} %collective-permute-done.3), channel_id=1, source_target_pairs={{8,0},{16,8},{24,16},{32,24},{40,32},{48,40},{56,48},{0,56},{9,1},... | collective-permute-start | bytes 1179656 | tf_op jit(solution)/shard_map/ppermute | solution.py:32
  96.1 10.5 %collective-permute-start.6 = (bf16[4,32,1536]{2,1,0:T(8,128)(2,1)S(1)}, bf16[4,32,1536]{2,1,0:T(8,128)(2,1)S(1)}, u32[]{:S(2)}, u32[]{:S(2)}) collective-permute-start(bf16[4,32,1536]{2,1,0:T(8,128)(2,1)S(1)} %collective-permute-done.4), channel_id=1, source_target_pairs={{0,8},{8,16},{16,24},{24,32},{32,40},{40,48},{48,56},{56,0},{1,9},... | collective-permute-start | bytes 1179656 | tf_op jit(solution)/shard_map/ppermute | solution.py:57
  106.6 1.6 copy-start.1
  114.7 16.1 %collective-permute-start.7 = (bf16[512,512]{1,0:T(8,128)(2,1)S(1)}, bf16[512,512]{1,0:T(8,128)(2,1)S(1)}, u32[]{:S(2)}, u32[]{:S(2)}) collective-permute-start(bf16[512,512]{1,0:T(8,128)(2,1)S(1)} %get-tuple-element.33), channel_id=1, source_target_pairs={{0,64},{64,128},{128,192},{192,0},{1,65},{65,129},{129,193},{193,1... | collective-permute-start | bytes 1572872 | tf_op jit(solution)/shard_map/ppermute | solution.py:284
  114.8 15.9 %collective-permute-start.8 = (bf16[512,512]{1,0:T(8,128)(2,1)S(1)}, bf16[512,512]{1,0:T(8,128)(2,1)}, u32[]{:S(2)}, u32[]{:S(2)}) collective-permute-start(bf16[512,512]{1,0:T(8,128)(2,1)S(1)} %get-tuple-element.34), channel_id=1, source_target_pairs={{64,0},{128,64},{192,128},{0,192},{65,1},{129,65},{193,129},{1,193... | collective-permute-start | bytes 1572872 | tf_op jit(solution)/shard_map/ppermute | solution.py:284
  127.3 20.5 %collective-permute-start.10 = (bf16[512,512]{1,0:T(8,128)(2,1)S(1)}, bf16[512,512]{1,0:T(8,128)(2,1)}, u32[]{:S(2)}, u32[]{:S(2)}) collective-permute-start(bf16[512,512]{1,0:T(8,128)(2,1)S(1)} %get-tuple-element.45), channel_id=1, source_target_pairs={{0,64},{64,128},{128,192},{192,0},{1,65},{65,129},{129,193},{193,1... | collective-permute-start | bytes 1572872 | tf_op jit(solution)/shard_map/ppermute | solution.py:284
  127.6 20.2 %collective-permute-start.11 = (bf16[512,512]{1,0:T(8,128)(2,1)S(1)}, bf16[512,512]{1,0:T(8,128)(2,1)}, u32[]{:S(2)}, u32[]{:S(2)}) collective-permute-start(bf16[512,512]{1,0:T(8,128)(2,1)S(1)} %get-tuple-element.46), channel_id=1, source_target_pairs={{64,0},{128,64},{192,128},{0,192},{65,1},{129,65},{193,129},{1,193... | collective-permute-start | bytes 1572872 | tf_op jit(solution)/shard_map/ppermute | solution.py:284
  147.8 1.0 copy-start.3
  147.8 13.9 %copy-start.5 = (bf16[512,512]{1,0:T(8,128)(2,1)S(1)}, bf16[512,512]{1,0:T(8,128)(2,1)}, u32[]{:S(2)}) copy-start(bf16[512,512]{1,0:T(8,128)(2,1)} %get-tuple-element.48) | copy-start | bytes 1572868
  147.9 16.3 %copy-start.4 = (bf16[512,512]{1,0:T(8,128)(2,1)S(1)}, bf16[512,512]{1,0:T(8,128)(2,1)}, u32[]{:S(2)}) copy-start(bf16[512,512]{1,0:T(8,128)(2,1)} %get-tuple-element.41) | copy-start | bytes 1572868
  150.0 11.7 %collective-permute-start.12 = (bf16[512,512]{1,0:T(8,128)(2,1)S(1)}, bf16[512,512]{1,0:T(8,128)(2,1)S(1)}, u32[]{:S(2)}, u32[]{:S(2)}) collective-permute-start(bf16[512,512]{1,0:T(8,128)(2,1)S(1)} %add_convert_fusion.1), channel_id=1, source_target_pairs={{64,0},{128,64},{192,128},{0,192},{65,1},{129,65},{193,129},{1,193... | collective-permute-start | bytes 1572872 | tf_op jit(solution)/shard_map/ppermute | solution.py:284
  153.4 10.7 %collective-permute-start.9 = (bf16[512,512]{1,0:T(8,128)(2,1)S(1)}, bf16[512,512]{1,0:T(8,128)(2,1)S(1)}, u32[]{:S(2)}, u32[]{:S(2)}) collective-permute-start(bf16[512,512]{1,0:T(8,128)(2,1)S(1)} %add_convert_fusion.3), channel_id=1, source_target_pairs={{0,64},{64,128},{128,192},{192,0},{1,65},{65,129},{129,193},{193,1... | collective-permute-start | bytes 1572872 | tf_op jit(solution)/shard_map/ppermute | solution.py:284
  164.2 6.2 %copy-start.7 = (s32[192,2]{0,1:T(2,128)S(1)}, s32[192,2]{0,1:T(2,128)}, u32[]{:S(2)}) copy-start(s32[192,2]{0,1:T(2,128)} %param.9) | copy-start | bytes 4612
  164.2 6.4 %copy-start.6 = (bf16[31,1024]{1,0:T(8,128)(2,1)S(1)}, bf16[31,1024]{1,0:T(8,128)(2,1)}, u32[]{:S(2)}) copy-start(bf16[31,1024]{1,0:T(8,128)(2,1)} %param.10) | copy-start | bytes 190468
  164.2 21.9 %copy-start.2 = (bf16[192,1024]{1,0:T(8,128)(2,1)S(1)}, bf16[192,1024]{1,0:T(8,128)(2,1)}, u32[]{:S(2)}) copy-start(bf16[192,1024]{1,0:T(8,128)(2,1)} %param.7) | copy-start | bytes 1179652
  166.6 19.5 %all-to-all-start.3 = ((bf16[8,64,1024]{2,1,0:T(8,128)(2,1)}), bf16[8,64,1024]{2,1,0:T(8,128)(2,1)S(1)}, u32[]{:S(2)}, u32[]{:S(2)}) async-start(bf16[8,64,1024]{2,1,0:T(8,128)(2,1)} %bitcast.31), calls=%async_computation.3 | async-start | bytes 2097152 | tf_op jit(solution)/shard_map/all_to_all | solution.py:323
  186.5 25.0 %collective-permute-start.13 = (bf16[15,1024]{1,0:T(8,128)(2,1)S(1)}, bf16[15,1024]{1,0:T(8,128)(2,1)S(1)}, u32[]{:S(2)}, u32[]{:S(2)}) collective-permute-start(bf16[15,1024]{1,0:T(8,128)(2,1)S(1)} %get-tuple-element.62), channel_id=1, source_target_pairs={{0,1},{1,2},{2,3},{3,4},{4,5},{5,6},{6,7},{7,8},{8,9},{9,10},{10,1... | collective-permute-start | bytes 92168 | tf_op jit(solution)/shard_map/ppermute | solution.py:85
  188.5 23.0 %collective-permute-start.14 = (bf16[15,1024]{1,0:T(8,128)(2,1)S(1)}, bf16[15,1024]{1,0:T(8,128)(2,1)S(1)}, u32[]{:S(2)}, u32[]{:S(2)}) collective-permute-start(bf16[15,1024]{1,0:T(8,128)(2,1)S(1)} %get-tuple-element.61), channel_id=1, source_target_pairs={{1,0},{2,1},{3,2},{4,3},{5,4},{6,5},{7,6},{8,7},{9,8},{10,9},{11,1... | collective-permute-start | bytes 92168 | tf_op jit(solution)/shard_map/ppermute | solution.py:86
  197.3 6.6 %copy-start.8 = (bf16[192,2]{0,1:T(2,128)(2,1)S(1)}, bf16[192,2]{0,1:T(2,128)(2,1)}, u32[]{:S(2)}) copy-start(bf16[192,2]{0,1:T(2,128)(2,1)} %param.8) | copy-start | bytes 2308
  200.0 9.8 %all-to-all-start.4 = ((bf16[4,32,1536]{2,1,0:T(8,128)(2,1)}), bf16[4,32,1536]{2,1,0:T(8,128)(2,1)S(1)}, u32[]{:S(2)}, u32[]{:S(2)}) async-start(bf16[4,32,1536]{2,1,0:T(8,128)(2,1)} %bitcast.113), calls=%async_computation.5 | async-start | bytes 786432 | tf_op jit(solution)/shard_map/all_to_all | solution.py:66
Sparse Core Ops, SparseCore 0:
  10.7 31.4 all-gather.6
  46.5 50.1 all-gather.4
  148.0 46.4 reduce-scatter.1

commit v8 on v7

--- a/solution.py
+++ b/solution.py
@@ -15,6 +15,7 @@
 STEP = 4
 CHUNK = 256
 EDGE = 16
+EXTRA = 128
 
 
 def dot(a, b, contract, batch=((), ())):
@@ -59,13 +60,41 @@
     return buffer.reshape(ny * nz * rows, width)
 
 
+def merge_kernel(parts_ref, out_ref):
+    ny, rows, wide = parts_ref.shape
+    part = wide // 3
+    for k in range(3):
+        for y in range(ny):
+            first = (k * ny + y) * part
+            out_ref[:, first : first + part] = parts_ref[y, :, k * part : (k + 1) * part]
+
+
+def merged(parts):
+    ny, rows, wide = parts.shape
+    return pl.pallas_call(merge_kernel, out_shape=jax.ShapeDtypeStruct((rows, ny * wide), BF))(parts)
+
+
+def sum_kernel(*refs):
+    out_ref = refs[-1]
+    half = refs[0].shape[1]
+    for side in range(2):
+        own, below, above = (ref[...].astype(F32) for ref in refs[3 * side : 3 * side + 3])
+        out_ref[:, side * half : (side + 1) * half] = (own + below + above).astype(BF)
+
+
+def summed(*parts):
+    rows, half = parts[0].shape
+    shape = jax.ShapeDtypeStruct((rows, 2 * half), BF)
+    limit = pltpu.CompilerParams(vmem_limit_bytes=32 * 1024 * 1024)
+    return pl.pallas_call(sum_kernel, out_shape=shape, compiler_params=limit)(*parts)
+
+
 def scatter_weight_grad(term):
     ny, nz = lax.axis_size("y"), lax.axis_size("z")
     rows, part = term.shape[2], term.shape[3] // 3
     mine = lax.psum_scatter(term.reshape(nz * ny * rows, 3 * part), "z", scatter_dimension=0, tiled=True)
     back = lax.all_to_all(mine.reshape(ny, rows, 3 * part), "y", 0, 0, tiled=True)
-    back = back.reshape(ny, rows, 3, part).transpose(1, 2, 0, 3)
-    return back.reshape(1, rows, 3 * ny * part)
+    return mine, merged(back)[None]
 
 
 def slots_of(chosen):
@@ -95,28 +124,31 @@
     return total.astype(BF)
 
 
-def route_kernel(scaled, x_ref, out_ref):
+def route_kernel(plain, x_ref, out_ref):
     rows, width = x_ref.shape[1:]
     frames, experts = rows - META, out_ref.shape[0]
     meta = x_ref[0, frames:rows, :frames].astype(F32)
     names = lax.broadcasted_iota(jnp.int32, (experts, frames), 0).astype(F32)
     first, second = (names == meta[0:1]).astype(F32), (names == meta[1:2]).astype(F32)
     chosen = first + second
-    gate = first * meta[2:3] + second * meta[3:4] if scaled else chosen
+    gate = first * meta[2:3] + second * meta[3:4]
     earlier = lax.broadcasted_iota(jnp.int32, (frames, frames), 0)
     before = (earlier < lax.broadcasted_iota(jnp.int32, (frames, frames), 1)).astype(F32).astype(BF)
     ranks = dot(chosen.astype(BF), before, ((1,), (0,)))
     slot = lax.broadcasted_iota(jnp.int32, (SLOTS, frames), 0).astype(F32)
     for e in range(experts):
         here = (slot == ranks[e : e + 1]) & (chosen[e : e + 1] > 0.0)
+        if plain:
+            placing = jnp.where(here, 1.0, 0.0).astype(BF)
+            out_ref[e, 0, :, :plain] = dot(placing, x_ref[0, :frames, :plain], ((1,), (0,))).astype(BF)
         placing = jnp.where(here, gate[e : e + 1], 0.0).astype(BF)
-        out_ref[e, 0] = dot(placing, x_ref[0, :frames], ((1,), (0,))).astype(BF)
-
-
-def route(packed, experts, scaled):
+        out_ref[e, 0, :, plain:] = dot(placing, x_ref[0, :frames, plain:], ((1,), (0,))).astype(BF)
+
+
+def route(packed, experts, plain):
     groups, rows, width = packed.shape
     return pl.pallas_call(
-        functools.partial(route_kernel, scaled),
+        functools.partial(route_kernel, plain),
         grid=(groups,),
         in_specs=[pl.BlockSpec((1, rows, width), lambda i: (i, 0, 0))],
         out_specs=pl.BlockSpec((experts, 1, SLOTS, width), lambda i: (0, i, 0, 0)),
@@ -152,24 +184,30 @@
         low_ref[place, :128] = jnp.where(row == SPARE, line, low_ref[place, :128].astype(F32)).astype(BF)
 
 
+def both_rows(u_ref, q_ref, width):
+    count = u_ref.shape[1] * SLOTS
+    rows = u_ref[0].reshape(count, u_ref.shape[3])
+    q = jnp.concatenate([rows[:, width:], q_ref[:, 0].reshape(count, q_ref.shape[3])], axis=1)
+    return rows[:, :width], q
+
+
 def rows_kernel(targets, steps, info, u_ref, q_ref, w_ref, *refs):
-    count, width = u_ref.shape[1] * SLOTS, u_ref.shape[3]
     pre_ref, h_ref = refs[-2:]
     pairs = refs[-2 - 2 * targets : -2]
     for t in range(targets):
 
         @pl.when(pl.program_id(0) // steps == t)
         def _():
-            u, q = u_ref[0].reshape(count, width), q_ref[:, 0].reshape(count, width)
+            u, q = both_rows(u_ref, q_ref, w_ref.shape[0])
             rows_of(u, q, w_ref, pairs[2 * t], pairs[2 * t + 1], pre_ref, h_ref)
 
 
 def last_kernel(info, u_ref, q_ref, w_ref, pre_ref, h_ref, low_ref, high_ref, term_ref, own_pre, own_h, total):
     step, last = pl.program_id(0), pl.num_programs(0) - 1
-    count, width = u_ref.shape[1] * SLOTS, u_ref.shape[3]
+    count = u_ref.shape[1] * SLOTS
     part, wide = h_ref.shape[3], pre_ref.shape[1]
     groups, each = term_ref.shape[1], term_ref.shape[0] * term_ref.shape[2]
-    u, q = u_ref[0].reshape(count, width), q_ref[:, 0].reshape(count, width)
+    u, q = both_rows(u_ref, q_ref, w_ref.shape[0])
 
     @pl.when(step == 0)
     def _():
@@ -190,7 +228,8 @@
 
 
 def last_rows(targets, rows_in, rows_q, weights, pre_grads, hidden):
-    groups, sources, _, width = rows_in.shape
+    groups, sources = rows_in.shape[:2]
+    width = weights.shape[0]
     nz = lax.axis_size("z")
     part = weights.shape[1] // 3
     mine = sources * SLOTS
@@ -203,8 +242,8 @@
             num_scalar_prefetch=1,
             grid=(groups,),
             in_specs=[
-                pl.BlockSpec((1, sources, SLOTS, width), lambda i, info: (info[i], 0, 0, 0)),
-                pl.BlockSpec((sources, 1, SLOTS, width), lambda i, info: (0, info[i], 0, 0)),
+                pl.BlockSpec((1, sources, SLOTS, rows_in.shape[3]), lambda i, info: (info[i], 0, 0, 0)),
+                pl.BlockSpec((sources, 1, SLOTS, rows_q.shape[3]), lambda i, info: (0, info[i], 0, 0)),
                 pl.BlockSpec(weights.shape, fixed),
                 pl.BlockSpec((mine, 2 * part), lambda i, info: (info[jnp.maximum(i, 1)], 0)),
                 pl.BlockSpec((sources, 1, SLOTS, part), lambda i, info: (0, info[jnp.maximum(i, 1)], 0, 0)),
@@ -230,8 +269,8 @@
 
 
 def expert_rows(targets, rows_in, rows_q, weights, kept):
-    groups, sources, _, width = rows_in.shape
-    part = weights.shape[1] // 3
+    groups, sources = rows_in.shape[:2]
+    width, part = weights.shape[0], weights.shape[1] // 3
     steps = sources // STEP
     count = len(targets)
     info = jnp.stack(targets).astype(jnp.int32)
@@ -248,8 +287,8 @@
             num_scalar_prefetch=1,
             grid=(count * steps,),
             in_specs=[
-                pl.BlockSpec((1, STEP, SLOTS, width), by_group),
-                pl.BlockSpec((STEP, 1, SLOTS, width), by_source),
+                pl.BlockSpec((1, STEP, SLOTS, rows_in.shape[3]), by_group),
+                pl.BlockSpec((STEP, 1, SLOTS, rows_q.shape[3]), by_source),
                 pl.BlockSpec(weights.shape, lambda i, info: (0, 0)),
             ]
             + [pl.BlockSpec(memory_space=pl.ANY) for _ in kept],
@@ -296,9 +335,7 @@
     targets = [(me + offset) % ny for offset in (0, 2, 1, ny - 1)]
     own_low, own_high, term = last_rows(targets, rows_in, rows_q, weights, *kept)
     term, below_high, above_low = lax.optimization_barrier((term, below_high, above_low))
-    low = add(own_low, below_low, above_low).astype(BF)
-    high = add(own_high, below_high, above_high).astype(BF)
-    return low, high, term
+    return summed(own_low, below_low, above_low, own_high, below_high, above_high), term
 
 
 def local(block_in, out_grad, gate_values, expert_ids, conv_kernel, expert_weights):
@@ -307,20 +344,23 @@
     by_expert = ("x", "c")
 
     meta = jnp.concatenate([expert_ids.astype(BF).T, gate_values.T], axis=0)
-    meta = jnp.pad(meta, ((0, META - 4), (0, width - frames)))
-    all_grad = lax.all_gather(jnp.concatenate([out_grad, meta], axis=0), "y", axis=0, tiled=False)
+
+    def packed(*arrays):
+        rows = jnp.concatenate(arrays, axis=1)
+        return jnp.concatenate([rows, jnp.pad(meta, ((0, META - 4), (0, rows.shape[1] - frames)))], axis=0)
+
+    all_grad = lax.all_gather(packed(out_grad[:, EXTRA:]), "y", axis=0, tiled=False)
     columns = own_columns(expert_weights)
-    columns, packed_in = lax.optimization_barrier((columns, jnp.concatenate([block_in, meta], axis=0)))
-    sent_in = route(packed_in[None], experts, False)
+    columns, packed_in = lax.optimization_barrier((columns, packed(block_in, out_grad[:, :EXTRA])))
+    sent_in = route(packed_in[None], experts, width)
     mine_in = lax.all_to_all(sent_in, by_expert, 0, 0, tiled=True)
     rows_in = lax.all_gather(mine_in[:, 0], "y", axis=0, tiled=False)
-    sent_q = route(all_grad, experts, True)
+    sent_q = route(all_grad, experts, 0)
     weights = gather_weights(columns, sent_q)
     rows_q = lax.all_to_all(sent_q, by_expert, 0, 0, tiled=True)
-    low, high, term = rows_backward(rows_in, rows_q, weights)
-    weight_grad = scatter_weight_grad(term)
-    summed = jnp.concatenate([low, high], axis=1).reshape(experts, SLOTS, width)
-    returned = lax.all_to_all(summed, by_expert, 0, 0, tiled=True)
+    row_sums, term = rows_backward(rows_in, rows_q, weights)
+    reduced, weight_grad = scatter_weight_grad(term)
+    returned = lax.all_to_all(row_sums.reshape(experts, SLOTS, width), by_expert, 0, 0, tiled=True)
 
     own_ids = expert_ids.T[None] == jnp.arange(experts, dtype=jnp.int32)[:, None, None]
     own = slots_of(own_ids[:, 0] | own_ids[:, 1])
@@ -342,6 +382,7 @@
     half = taps.shape[0] // 2
     rounded = frame_grad.astype(BF)
     low, high = halo_of(rounded, half)
+    frame_grad, rounded, reduced = lax.optimization_barrier((frame_grad, rounded, reduced))
     rows = rounded.astype(F32)
     inner = convolved(frame_grad[EDGE : frames - EDGE], rows[EDGE - half : frames - EDGE + half], taps)
     low, high, inner, weight_grad = lax.optimization_barrier((low, high, inner, weight_grad))

time: 221 us -> 222 us (level)
  blocking collectives: 31.8 us -> 21.9 us
  starting transfers between devices: 43.5 us -> 52.2 us
  other arithmetic: 13.7 us -> 10.1 us
  Pallas kernels: 40.5 us -> 44 us
  waiting for transfers between devices: 66.6 us -> 69.9 us
    all_to_all x1 -> x0, blocking collectives: 11.3 us -> none  [own_columns(): lax.all_to_all(sliced.reshape(ny, rows, 3 * part), 'y', 0, 0, tiled=True)]
    ppermute x6, waiting for transfers between devices: 25.8 us -> 17.4 us  [ring_step(): return (lax.ppermute(right, axis, up), lax.ppermute(left, axis, down))]
    all_to_all x1, waiting for transfers between devices: 0.15 us -> 8.33 us  [local(): rows_q = lax.all_to_all(sent_q, by_expert, 0, 0, tiled=True)]
    all_to_all x1 -> x2, waiting for transfers between devices: 15.4 us -> 21.2 us  [the longest x1 15.4 us: local(): lax.all_to_all(row_sums.reshape(experts, SLOTS, width), by_expert, 0, 0,...]
    all_to_all x1 -> x2, starting transfers between devices: 3.78 us -> 9.52 us  [the longest x1 5.61 us: own_columns(): lax.all_to_all(sliced.reshape(ny, rows, 3 * part), 'y', 0, 0, tiled=True)]
    all_to_all x1, starting transfers between devices: 3.86 us -> 7.79 us  [scatter_weight_grad(): lax.all_to_all(mine.reshape(ny, rows, 3 * part), 'y', 0, 0, tiled=True)]
    pallas_call x2 -> x4, Pallas kernels: 6.45 us -> 9.72 us  [the longest x2 6.57 us: route(): pl.pallas_call(functools.partial(route_kernel, plain), grid=(groups,), in...]
    convert_element_type x2 -> x1, other arithmetic: 2.55 us -> 0.07 us  [local(): rows = rounded.astype(F32)]
  transfers between devices with their start and end apart: 21 -> 22, of which waited for: 9 -> 10; matrix products, arithmetic and copies ran while one was open for 6% -> 6% of each run, Pallas kernels for 16% -> 17%
where the time goes in v8:
time: 222 us
  waiting for transfers between devices  69.9 us (31%)
  starting transfers between devices  52.2 us (24%)
  Pallas kernels  44 us (20%)
  blocking collectives  21.9 us (10%)
  between operations  14.2 us (6%)
  other arithmetic  10.1 us (5%)
  local copies, waits for them, and re-layouts  8.63 us (4%)
    all_to_all x1, blocking collectives, local(): mine_in = lax.all_to_all(sent_in, by_expert, 0, 0, tiled=True)  21.9 us
    ppermute x6, waiting for transfers between devices, ring_step(): return (lax.ppermute(right, axis, up), lax.ppermute(left, axis, down))  17.4 us
    pallas_call x2, Pallas kernels, expert_rows(): pl.pallas_call(functools.partial(rows_kernel, count, steps), grid_spec=pl...  17.2 us
    pallas_call x1, Pallas kernels, last_rows(): pl.pallas_call(last_kernel, grid_spec=pltpu.PrefetchScalarGridSpec(num_sc...  17 us
    all_to_all x1, waiting for transfers between devices, local(): lax.all_to_all(row_sums.reshape(experts, SLOTS, width), by_expert, 0, 0,...  15.4 us
    ppermute x6, starting transfers between devices, ring_step(): return (lax.ppermute(right, axis, up), lax.ppermute(left, axis, down))  12.3 us
    ppermute x6, waiting for transfers between devices, send(): return lax.ppermute(rows, 'y', way)  9.99 us
    ppermute x1, waiting for transfers between devices, gather_weights(): right = lax.ppermute(right, 'z', ring_ways('z')[0])  9.57 us
  transfers between devices with their start and end apart: 22, of which 10 were waited for; matrix products, arithmetic and copies ran while one was open for 6% of the time, Pallas kernels for 17%

profile of v8, /device:TPU:8, one launch (start us, length us, event | category | flops | bytes accessed | tf_op | source)
XLA Modules:
  0.0 221.7 jit_solution(10978178438606908270)
XLA Ops:
  7.2 0.0 all-gather.7.cloned.1.call-start
  7.2 0.7 convert_bitcast_fusion
  8.0 1.0 slice.537
  9.0 0.7 pad_maximum_fusion.3
  9.7 0.8 fusion.40
  10.5 1.3 reshape_squeeze.3
  11.7 0.2 copy.50
  12.0 1.3 reshape.26
  13.2 5.6 %all-to-all-start = ((bf16[4,32,1536]{2,1,0:T(8,128)(2,1)}), bf16[4,32,1536]{2,1,0:T(8,128)(2,1)S(1)}, u32[]{:S(2)}, u32[]{:S(2)}) async-start(bf16[4,32,1536]{2,1,0:T(8,128)(2,1)} %reshape.26), calls=%async_computation | async-start | bytes 786432 | tf_op jit(solution)/shard_map/all_to_all | solution.py:41
  18.9 5.9 %all-to-all-done = bf16[4,32,1536]{2,1,0:T(8,128)(2,1)S(1)} async-done(((bf16[4,32,1536]{2,1,0:T(8,128)(2,1)}), bf16[4,32,1536]{2,1,0:T(8,128)(2,1)S(1)}, u32[]{:S(2)}, u32[]{:S(2)}) %all-to-all-start) | async-done | bytes 393248 | tf_op jit(solution)/shard_map/all_to_all | solution.py:41
  24.8 2.1 shard_map.85
  26.8 21.9 %all_to_all.25 = bf16[8,1,64,1152]{3,2,1,0:T(8,128)(2,1)} all-to-all(bf16[8,1,64,1152]{3,2,1,0:T(8,128)(2,1)} %shard_map.85), channel_id=1, replica_groups=mesh['y'=4,'z'=8,'x'=4,'c'=2] {'x','c'}, dimensions={0} | all-to-all | bytes 2359296 | tf_op jit(solution)/shard_map/all_to_all | solution.py:356
  48.7 0.0 all-gather.5.cloned.1.call-update
  48.9 0.0 all-gather.7.cloned.1.call-done
  49.0 1.4 copy-done
  50.3 4.5 %shard_map.86 = bf16[8,4,64,896]{3,2,1,0:T(8,128)(2,1)} custom-call(bf16[4,200,896]{2,1,0:T(8,128)(2,1)S(1)} %bitcast.103), custom_call_target="tpu_custom_call" | custom-call | tf_op jit(solution)/shard_map/pallas_call | solution.py:150
  54.8 1.9 collective-permute-start
  56.7 3.9 %collective-permute-start.1 = (bf16[4,32,1536]{2,1,0:T(8,128)(2,1)S(1)}, bf16[4,32,1536]{2,1,0:T(8,128)(2,1)}, u32[]{:S(2)}, u32[]{:S(2)}) collective-permute-start(bf16[4,32,1536]{2,1,0:T(8,128)(2,1)S(1)} %all-to-all-done), channel_id=1, source_target_pairs={{8,0},{16,8},{24,16},{32,24},{40,32},{48,40},{56,48},{0,56},{9,1},... | collective-permute-start | bytes 1179656 | tf_op jit(solution)/shard_map/ppermute | solution.py:33
  60.7 0.3 broadcast_in_dim.40
  61.1 4.6 %all-to-all-start.2 = ((bf16[8,4,64,896]{3,2,1,0:T(8,128)(2,1)}), bf16[8,4,64,896]{3,2,1,0:T(8,128)(2,1)}, u32[]{:S(2)}, u32[]{:S(2)}) async-start(bf16[8,4,64,896]{3,2,1,0:T(8,128)(2,1)} %shard_map.86), calls=%async_computation.2 | async-start | bytes 7340032 | tf_op jit(solution)/shard_map/all_to_all | solution.py:360
  65.6 0.0 reduce-scatter.2.cloned.1.call-start
  65.7 4.0 %collective-permute-done = bf16[4,32,1536]{2,1,0:T(8,128)(2,1)} collective-permute-done((bf16[4,32,1536]{2,1,0:T(8,128)(2,1)S(1)}, bf16[4,32,1536]{2,1,0:T(8,128)(2,1)}, u32[]{:S(2)}, u32[]{:S(2)}) %collective-permute-start) | collective-permute-done | bytes 393248 | tf_op jit(solution)/shard_map/ppermute | solution.py:33
  69.7 3.2 %collective-permute-start.3 = (bf16[4,32,1536]{2,1,0:T(8,128)(2,1)}, bf16[4,32,1536]{2,1,0:T(8,128)(2,1)S(1)}, u32[]{:S(2)}, u32[]{:S(2)}) collective-permute-start(bf16[4,32,1536]{2,1,0:T(8,128)(2,1)} %collective-permute-done.1), channel_id=1, source_target_pairs={{8,0},{16,8},{24,16},{32,24},{40,32},{48,40},{56,48},{0,56},{9,1},... | collective-permute-start | bytes 1179656 | tf_op jit(solution)/shard_map/ppermute | solution.py:33
  72.9 1.0 bitcast_dynamic-update-slice_fusion.6
  74.0 1.0 bitcast_dynamic-update-slice_fusion.5
  75.0 6.2 %collective-permute-done.2 = bf16[4,32,1536]{2,1,0:T(8,128)(2,1)S(1)} collective-permute-done((bf16[4,32,1536]{2,1,0:T(8,128)(2,1)}, bf16[4,32,1536]{2,1,0:T(8,128)(2,1)S(1)}, u32[]{:S(2)}, u32[]{:S(2)}) %collective-permute-start.2) | collective-permute-done | bytes 393248 | tf_op jit(solution)/shard_map/ppermute | solution.py:33
  81.2 3.2 %collective-permute-start.5 = (bf16[4,32,1536]{2,1,0:T(8,128)(2,1)S(1)}, bf16[4,32,1536]{2,1,0:T(8,128)(2,1)S(1)}, u32[]{:S(2)}, u32[]{:S(2)}) collective-permute-start(bf16[4,32,1536]{2,1,0:T(8,128)(2,1)S(1)} %collective-permute-done.3), channel_id=1, source_target_pairs={{8,0},{16,8},{24,16},{32,24},{40,32},{48,40},{56,48},{0,56},{9,1},... | collective-permute-start | bytes 1179656 | tf_op jit(solution)/shard_map/ppermute | solution.py:33
  84.5 7.2 %collective-permute-done.4 = bf16[4,32,1536]{2,1,0:T(8,128)(2,1)S(1)} collective-permute-done((bf16[4,32,1536]{2,1,0:T(8,128)(2,1)S(1)}, bf16[4,32,1536]{2,1,0:T(8,128)(2,1)S(1)}, u32[]{:S(2)}, u32[]{:S(2)}) %collective-permute-start.4) | collective-permute-done | bytes 393248 | tf_op jit(solution)/shard_map/ppermute | solution.py:33
  91.8 9.6 %collective-permute-done.6 = bf16[4,32,1536]{2,1,0:T(8,128)(2,1)S(1)} collective-permute-done((bf16[4,32,1536]{2,1,0:T(8,128)(2,1)S(1)}, bf16[4,32,1536]{2,1,0:T(8,128)(2,1)S(1)}, u32[]{:S(2)}, u32[]{:S(2)}) %collective-permute-start.6) | collective-permute-done | bytes 393248 | tf_op jit(solution)/shard_map/ppermute | solution.py:58
  101.4 8.3 %all-to-all-done.2.q_ref = bf16[8,4,64,896]{3,2,1,0:T(8,128)(2,1)} async-done(((bf16[8,4,64,896]{3,2,1,0:T(8,128)(2,1)}), bf16[8,4,64,896]{3,2,1,0:T(8,128)(2,1)}, u32[]{:S(2)}, u32[]{:S(2)}) %all-to-all-start.2) | async-done | bytes 3670048 | tf_op jit(solution)/shard_map/all_to_all | solution.py:360
  109.7 6.6 %shard_map.87 = (bf16[512,512]{1,0:T(8,128)(2,1)}, bf16[512,512]{1,0:T(8,128)(2,1)S(1)}, bf16[2048,1024]{1,0:T(8,128)(2,1)}, bf16[8,4,64,512]{3,2,1,0:T(8,128)(2,1)}) custom-call(s32[1]{0:T(128)} %bitcast.5.info, bf16[4,8,64,1152]{3,2,1,0:T(8,128)(2,1)} %bitcast.107, bf16[8,4,64,896]{3,2,1,0:T(8,128)(2,1)} %all-to-all-done.2.q_ref, bf16[1024,1536]{1,0:T(8,128)(2,1)} %bitcast.104), custom_call_target="tpu_custom_call" | custom-call | tf_op jit(solution)/shard_map/pallas_call | solution.py:284
  116.3 2.0 collective-permute-start.8
  118.3 0.1 pad_add_fusion.1.info
  118.4 10.6 %shard_map.88 = (bf16[512,512]{1,0:T(8,128)(2,1)S(1)}, bf16[512,512]{1,0:T(8,128)(2,1)S(1)}, bf16[512,512]{1,0:T(8,128)(2,1)S(1)}, bf16[512,512]{1,0:T(8,128)(2,...) custom-call(s32[2]{0:T(128)S(1)} %pad_add_fusion.1.info, ...), custom_call_target="tpu_custom_call", output_to_operand_aliasing={{4}: (4, {}), {5}: (5, {})} | custom-call | tf_op jit(solution)/shard_map/pallas_call | solution.py:284
  129.0 0.2 collective-permute-start.10
  129.3 2.5 %collective-permute-start.11 = (bf16[512,512]{1,0:T(8,128)(2,1)S(1)}, bf16[512,512]{1,0:T(8,128)(2,1)S(1)}, u32[]{:S(2)}, u32[]{:S(2)}) collective-permute-start(bf16[512,512]{1,0:T(8,128)(2,1)S(1)} %get-tuple-element.48), channel_id=1, source_target_pairs={{64,0},{128,64},{192,128},{0,192},{65,1},{129,65},{193,129},{1,193... | collective-permute-start | bytes 1572872 | tf_op jit(solution)/shard_map/ppermute | solution.py:323
  131.8 0.6 pad_add_fusion.info
  132.4 17.0 %shard_map.89 = (bf16[512,512]{1,0:T(8,128)(2,1)}, bf16[512,512]{1,0:T(8,128)(2,1)}, bf16[8,4,32,1536]{3,2,1,0:T(8,128)(2,1)}) custom-call(s32[4]{0:T(128)} %pad_add_fusion.info, bf16[4,8,64,1152]{3,2,1,0:T(8,128)(2,1)} %bitcast.109, bf16[8,4,64,896]{3,2,1,0:T(8,128)(2,1)} %all-to-all-done.2.q_ref, bf16[1024,1536]{1,0:T(8,128)(2,1)} %bitcast.106, ...), custom_call_target="tpu_custom_call" | custom-call | tf_op jit(solution)/shard_map/pallas_call | solution.py:239
  149.5 0.0 reduce-scatter.2.cloned.1.call-update
  149.5 1.3 add_convert_fusion.1
  150.8 0.1 collective-permute-start.9
  150.9 1.2 add_convert_fusion
  152.1 3.3 %collective-permute-start.12 = (bf16[512,512]{1,0:T(8,128)(2,1)S(1)}, bf16[512,512]{1,0:T(8,128)(2,1)S(1)}, u32[]{:S(2)}, u32[]{:S(2)}) collective-permute-start(bf16[512,512]{1,0:T(8,128)(2,1)S(1)} %add_convert_fusion), channel_id=1, source_target_pairs={{64,0},{128,64},{192,128},{0,192},{65,1},{129,65},{193,129},{1,193... | collective-permute-start | bytes 1572872 | tf_op jit(solution)/shard_map/ppermute | solution.py:323
  155.3 9.3 %collective-permute-done.9.refs_1_ = bf16[512,512]{1,0:T(8,128)(2,1)S(1)} collective-permute-done((bf16[512,512]{1,0:T(8,128)(2,1)S(1)}, bf16[512,512]{1,0:T(8,128)(2,1)S(1)}, u32[]{:S(2)}, u32[]{:S(2)}) %collective-permute-start.9) | collective-permute-done | bytes 524320 | tf_op jit(solution)/shard_map/ppermute | solution.py:323
  164.7 0.7 collective-permute-done.12.refs_5_
  165.3 1.4 shard_map.90
  166.7 3.9 %all-to-all-start.3 = ((bf16[8,64,1024]{2,1,0:T(8,128)(2,1)}), bf16[8,64,1024]{2,1,0:T(8,128)(2,1)S(1)}, u32[]{:S(2)}, u32[]{:S(2)}) async-start(bf16[8,64,1024]{2,1,0:T(8,128)(2,1)} %bitcast.31), calls=%async_computation.3 | async-start | bytes 2097152 | tf_op jit(solution)/shard_map/all_to_all | solution.py:363
  170.7 0.1 convolution_convert_fusion
  170.9 0.1 fusion.171
  170.9 15.4 %all-to-all-done.3 = bf16[8,64,1024]{2,1,0:T(8,128)(2,1)S(1)} async-done(((bf16[8,64,1024]{2,1,0:T(8,128)(2,1)}), bf16[8,64,1024]{2,1,0:T(8,128)(2,1)S(1)}, u32[]{:S(2)}, u32[]{:S(2)}) %all-to-all-start.3) | async-done | bytes 1048608 | tf_op jit(solution)/shard_map/all_to_all | solution.py:363
  186.3 0.4 fusion.173
  186.8 1.9 collective-permute-start.13
  188.7 7.9 %collective-permute-start.14 = (bf16[15,1024]{1,0:T(8,128)(2,1)S(1)}, bf16[15,1024]{1,0:T(8,128)(2,1)S(1)}, u32[]{:S(2)}, u32[]{:S(2)}) collective-permute-start(bf16[15,1024]{1,0:T(8,128)(2,1)S(1)} %get-tuple-element.63), channel_id=1, source_target_pairs={{1,0},{2,1},{3,2},{4,3},{5,4},{6,5},{7,6},{8,7},{9,8},{10,9},{11,1... | collective-permute-start | bytes 92168 | tf_op jit(solution)/shard_map/ppermute | solution.py:115
  196.5 0.2 fusion.36
  196.8 0.6 fusion.168
  197.4 0.1 convert_element_type.78
  197.5 7.8 %all-to-all-start.4 = ((bf16[4,32,1536]{2,1,0:T(8,128)(2,1)}), bf16[4,32,1536]{2,1,0:T(8,128)(2,1)S(1)}, u32[]{:S(2)}, u32[]{:S(2)}) async-start(bf16[4,32,1536]{2,1,0:T(8,128)(2,1)} %bitcast.112), calls=%async_computation.5 | async-start | bytes 786432 | tf_op jit(solution)/shard_map/all_to_all | solution.py:96
  205.3 2.6 %fusion.4 = bf16[160,1024]{1,0:T(8,128)(2,1)S(1)} fusion(f32[192,1024]{1,0:T(8,128)S(1)} %convert_element_type.78, f32[192,1024]{1,0:T(8,128)S(1)} %get-tuple-element.55, f32[1024]{0:T(1024)S(1)} %bitcast.147, f32[1024]{0:T(1024)S(1)} %bitcast.144, f32[1024]{0:T(1024)S(1)} %bitcast.141, f32[1024]{0:T(1024)S(1)} %bitcast.138, f32[1024]{0:T(1024)S(1)} %bitcast.135, ...), kind=kLoop, calls=%fused_computation.39 | loop fusion | flops 10321920 | bytes 21426176 | tf_op jit(solution)/shard_map/convert_element_type | solution.py:124
  207.9 3.3 %all-to-all-done.4.parts_ref = bf16[4,32,1536]{2,1,0:T(8,128)(2,1)S(1)} async-done(((bf16[4,32,1536]{2,1,0:T(8,128)(2,1)}), bf16[4,32,1536]{2,1,0:T(8,128)(2,1)S(1)}, u32[]{:S(2)}, u32[]{:S(2)}) %all-to-all-start.4) | async-done | bytes 393248 | tf_op jit(solution)/shard_map/all_to_all | solution.py:96
  211.2 0.7 copy-done.4
  211.9 1.8 shard_map.91
  213.7 0.3 fusion.166
  214.0 0.3 fusion.108
  214.4 0.8 pad_maximum_fusion
  (55 shorter events, 0.5 us)
Async XLA Ops:
  7.2 11.7 %slice-start = ((bf16[192,1024]{1,0:T(8,128)(2,1)}), bf16[192,128]{1,0:T(8,128)(2,1)S(1)}, s32[]{:S(2)}) async-start(bf16[192,1024]{1,0:T(8,128)(2,1)} %param.7), calls=%async_computation.9 | async-start | bytes 98304 | tf_op jit(solution)/shard_map/slice | solution.py:354
  7.2 11.7 %copy-start.6 = (bf16[192,1024]{1,0:T(8,128)(2,1)S(1)}, bf16[192,1024]{1,0:T(8,128)(2,1)}, u32[]{:S(2)}) copy-start(bf16[192,1024]{1,0:T(8,128)(2,1)} %param.6) | copy-start | bytes 1179652
  7.2 41.7 %all-gather.7.cloned.1.call-start = ((), (), s32[]{:S(2)}) async-start(), calls=%async_computation.8 | async-start | bytes 1792000 | tf_op jit(solution)/shard_map/all_gather | solution.py:352
  13.2 11.5 %all-to-all-start = ((bf16[4,32,1536]{2,1,0:T(8,128)(2,1)}), bf16[4,32,1536]{2,1,0:T(8,128)(2,1)S(1)}, u32[]{:S(2)}, u32[]{:S(2)}) async-start(bf16[4,32,1536]{2,1,0:T(8,128)(2,1)} %reshape.26), calls=%async_computation | async-start | bytes 786432 | tf_op jit(solution)/shard_map/all_to_all | solution.py:41
  18.8 90.9 %all-gather.5.cloned.1.call-start = ((), (), s32[]{:S(2)}) async-start(), calls=%async_computation.7 | async-start | bytes 5898240 | tf_op jit(solution)/shard_map/all_gather | solution.py:357
  48.9 1.4 copy-start
  54.8 14.9 %collective-permute-start = (bf16[4,32,1536]{2,1,0:T(8,128)(2,1)S(1)}, bf16[4,32,1536]{2,1,0:T(8,128)(2,1)}, u32[]{:S(2)}, u32[]{:S(2)}) collective-permute-start(bf16[4,32,1536]{2,1,0:T(8,128)(2,1)S(1)} %all-to-all-done), channel_id=1, source_target_pairs={{0,8},{8,16},{16,24},{24,32},{32,40},{40,48},{48,56},{56,0},{1,9},... | collective-permute-start | bytes 1179656 | tf_op jit(solution)/shard_map/ppermute | solution.py:33
  56.7 13.0 %collective-permute-start.1 = (bf16[4,32,1536]{2,1,0:T(8,128)(2,1)S(1)}, bf16[4,32,1536]{2,1,0:T(8,128)(2,1)}, u32[]{:S(2)}, u32[]{:S(2)}) collective-permute-start(bf16[4,32,1536]{2,1,0:T(8,128)(2,1)S(1)} %all-to-all-done), channel_id=1, source_target_pairs={{8,0},{16,8},{24,16},{32,24},{40,32},{48,40},{56,48},{0,56},{9,1},... | collective-permute-start | bytes 1179656 | tf_op jit(solution)/shard_map/ppermute | solution.py:33
  61.1 48.6 %all-to-all-start.2 = ((bf16[8,4,64,896]{3,2,1,0:T(8,128)(2,1)}), bf16[8,4,64,896]{3,2,1,0:T(8,128)(2,1)}, u32[]{:S(2)}, u32[]{:S(2)}) async-start(bf16[8,4,64,896]{3,2,1,0:T(8,128)(2,1)} %shard_map.86), calls=%async_computation.2 | async-start | bytes 7340032 | tf_op jit(solution)/shard_map/all_to_all | solution.py:360
  65.6 131.7 %reduce-scatter.2.cloned.1.call-start = ((), (), s32[]{:S(2)}) async-start(), calls=%async_computation.6 | async-start | bytes 3538944 | tf_op jit(solution)/shard_map/reduce_scatter | solution.py:95
  69.7 11.5 %collective-permute-start.2 = (bf16[4,32,1536]{2,1,0:T(8,128)(2,1)}, bf16[4,32,1536]{2,1,0:T(8,128)(2,1)S(1)}, u32[]{:S(2)}, u32[]{:S(2)}) collective-permute-start(bf16[4,32,1536]{2,1,0:T(8,128)(2,1)} %collective-permute-done), channel_id=1, source_target_pairs={{0,8},{8,16},{16,24},{24,32},{32,40},{40,48},{48,56},{56,0},{1,9},... | collective-permute-start | bytes 1179656 | tf_op jit(solution)/shard_map/ppermute | solution.py:33
  69.7 11.5 %collective-permute-start.3 = (bf16[4,32,1536]{2,1,0:T(8,128)(2,1)}, bf16[4,32,1536]{2,1,0:T(8,128)(2,1)S(1)}, u32[]{:S(2)}, u32[]{:S(2)}) collective-permute-start(bf16[4,32,1536]{2,1,0:T(8,128)(2,1)} %collective-permute-done.1), channel_id=1, source_target_pairs={{8,0},{16,8},{24,16},{32,24},{40,32},{48,40},{56,48},{0,56},{9,1},... | collective-permute-start | bytes 1179656 | tf_op jit(solution)/shard_map/ppermute | solution.py:33
  81.2 10.5 %collective-permute-start.4 = (bf16[4,32,1536]{2,1,0:T(8,128)(2,1)S(1)}, bf16[4,32,1536]{2,1,0:T(8,128)(2,1)S(1)}, u32[]{:S(2)}, u32[]{:S(2)}) collective-permute-start(bf16[4,32,1536]{2,1,0:T(8,128)(2,1)S(1)} %collective-permute-done.2), channel_id=1, source_target_pairs={{0,8},{8,16},{16,24},{24,32},{32,40},{40,48},{48,56},{56,0},{1,9},... | collective-permute-start | bytes 1179656 | tf_op jit(solution)/shard_map/ppermute | solution.py:33
  81.2 10.5 %collective-permute-start.5 = (bf16[4,32,1536]{2,1,0:T(8,128)(2,1)S(1)}, bf16[4,32,1536]{2,1,0:T(8,128)(2,1)S(1)}, u32[]{:S(2)}, u32[]{:S(2)}) collective-permute-start(bf16[4,32,1536]{2,1,0:T(8,128)(2,1)S(1)} %collective-permute-done.3), channel_id=1, source_target_pairs={{8,0},{16,8},{24,16},{32,24},{40,32},{48,40},{56,48},{0,56},{9,1},... | collective-permute-start | bytes 1179656 | tf_op jit(solution)/shard_map/ppermute | solution.py:33
  91.7 9.7 %collective-permute-start.6 = (bf16[4,32,1536]{2,1,0:T(8,128)(2,1)S(1)}, bf16[4,32,1536]{2,1,0:T(8,128)(2,1)S(1)}, u32[]{:S(2)}, u32[]{:S(2)}) collective-permute-start(bf16[4,32,1536]{2,1,0:T(8,128)(2,1)S(1)} %collective-permute-done.4), channel_id=1, source_target_pairs={{0,8},{8,16},{16,24},{24,32},{32,40},{40,48},{48,56},{56,0},{1,9},... | collective-permute-start | bytes 1179656 | tf_op jit(solution)/shard_map/ppermute | solution.py:58
  101.4 8.3 %copy-start.3 = (bf16[4,8,32,1536]{3,2,1,0:T(8,128)(2,1)}, bf16[4,8,32,1536]{3,2,1,0:T(8,128)(2,1)S(1)}, u32[]{:S(2)}) copy-start(bf16[4,8,32,1536]{3,2,1,0:T(8,128)(2,1)S(1)} %bitcast_dynamic-update-slice_fusion) | copy-start | bytes 9437188
  116.3 16.1 %collective-permute-start.7 = (bf16[512,512]{1,0:T(8,128)(2,1)}, bf16[512,512]{1,0:T(8,128)(2,1)}, u32[]{:S(2)}, u32[]{:S(2)}) collective-permute-start(bf16[512,512]{1,0:T(8,128)(2,1)} %get-tuple-element.35), channel_id=1, source_target_pairs={{0,64},{64,128},{128,192},{192,0},{1,65},{65,129},{129,193},{193,1... | collective-permute-start | bytes 1572872 | tf_op jit(solution)/shard_map/ppermute | solution.py:323
  116.3 16.1 %collective-permute-start.8 = (bf16[512,512]{1,0:T(8,128)(2,1)S(1)}, bf16[512,512]{1,0:T(8,128)(2,1)}, u32[]{:S(2)}, u32[]{:S(2)}) collective-permute-start(bf16[512,512]{1,0:T(8,128)(2,1)S(1)} %get-tuple-element.36), channel_id=1, source_target_pairs={{64,0},{128,64},{192,128},{0,192},{65,1},{129,65},{193,129},{1,193... | collective-permute-start | bytes 1572872 | tf_op jit(solution)/shard_map/ppermute | solution.py:323
  129.0 20.4 %collective-permute-start.10 = (bf16[512,512]{1,0:T(8,128)(2,1)S(1)}, bf16[512,512]{1,0:T(8,128)(2,1)S(1)}, u32[]{:S(2)}, u32[]{:S(2)}) collective-permute-start(bf16[512,512]{1,0:T(8,128)(2,1)S(1)} %get-tuple-element.47), channel_id=1, source_target_pairs={{0,64},{64,128},{128,192},{192,0},{1,65},{65,129},{129,193},{193,1... | collective-permute-start | bytes 1572872 | tf_op jit(solution)/shard_map/ppermute | solution.py:323
  129.3 20.2 %collective-permute-start.11 = (bf16[512,512]{1,0:T(8,128)(2,1)S(1)}, bf16[512,512]{1,0:T(8,128)(2,1)S(1)}, u32[]{:S(2)}, u32[]{:S(2)}) collective-permute-start(bf16[512,512]{1,0:T(8,128)(2,1)S(1)} %get-tuple-element.48), channel_id=1, source_target_pairs={{64,0},{128,64},{192,128},{0,192},{65,1},{129,65},{193,129},{1,193... | collective-permute-start | bytes 1572872 | tf_op jit(solution)/shard_map/ppermute | solution.py:323
  149.4 1.4 copy-start.5
  149.5 15.9 %copy-start.1 = (bf16[512,512]{1,0:T(8,128)(2,1)S(1)}, bf16[512,512]{1,0:T(8,128)(2,1)}, u32[]{:S(2)}) copy-start(bf16[512,512]{1,0:T(8,128)(2,1)} %get-tuple-element.43.refs_0_) | copy-start | bytes 1572868
  149.5 15.9 %copy-start.2 = (bf16[512,512]{1,0:T(8,128)(2,1)S(1)}, bf16[512,512]{1,0:T(8,128)(2,1)}, u32[]{:S(2)}) copy-start(bf16[512,512]{1,0:T(8,128)(2,1)} %get-tuple-element.50.refs_3_) | copy-start | bytes 1572868
  150.8 13.9 %collective-permute-start.9 = (bf16[512,512]{1,0:T(8,128)(2,1)S(1)}, bf16[512,512]{1,0:T(8,128)(2,1)S(1)}, u32[]{:S(2)}, u32[]{:S(2)}) collective-permute-start(bf16[512,512]{1,0:T(8,128)(2,1)S(1)} %add_convert_fusion.1), channel_id=1, source_target_pairs={{0,64},{64,128},{128,192},{192,0},{1,65},{65,129},{129,193},{193,1... | collective-permute-start | bytes 1572872 | tf_op jit(solution)/shard_map/ppermute | solution.py:323
  152.1 13.2 %collective-permute-start.12 = (bf16[512,512]{1,0:T(8,128)(2,1)S(1)}, bf16[512,512]{1,0:T(8,128)(2,1)S(1)}, u32[]{:S(2)}, u32[]{:S(2)}) collective-permute-start(bf16[512,512]{1,0:T(8,128)(2,1)S(1)} %add_convert_fusion), channel_id=1, source_target_pairs={{64,0},{128,64},{192,128},{0,192},{65,1},{129,65},{193,129},{1,193... | collective-permute-start | bytes 1572872 | tf_op jit(solution)/shard_map/ppermute | solution.py:323
  165.3 5.3 %copy-start.9 = (s32[192,2]{0,1:T(2,128)S(1)}, s32[192,2]{0,1:T(2,128)}, u32[]{:S(2)}) copy-start(s32[192,2]{0,1:T(2,128)} %param.9) | copy-start | bytes 4612
  165.3 5.5 %copy-start.8 = (bf16[31,1024]{1,0:T(8,128)(2,1)S(1)}, bf16[31,1024]{1,0:T(8,128)(2,1)}, u32[]{:S(2)}) copy-start(bf16[31,1024]{1,0:T(8,128)(2,1)} %param.10) | copy-start | bytes 190468
  165.3 21.0 %copy-start.7 = (bf16[192,1024]{1,0:T(8,128)(2,1)S(1)}, bf16[192,1024]{1,0:T(8,128)(2,1)}, u32[]{:S(2)}) copy-start(bf16[192,1024]{1,0:T(8,128)(2,1)} %param.7) | copy-start | bytes 1179652
  166.7 30.1 %copy-start.10 = (bf16[192,2]{0,1:T(2,128)(2,1)S(1)}, bf16[192,2]{0,1:T(2,128)(2,1)}, u32[]{:S(2)}) copy-start(bf16[192,2]{0,1:T(2,128)(2,1)} %param.8) | copy-start | bytes 2308
  166.7 19.6 %all-to-all-start.3 = ((bf16[8,64,1024]{2,1,0:T(8,128)(2,1)}), bf16[8,64,1024]{2,1,0:T(8,128)(2,1)S(1)}, u32[]{:S(2)}, u32[]{:S(2)}) async-start(bf16[8,64,1024]{2,1,0:T(8,128)(2,1)} %bitcast.31), calls=%async_computation.3 | async-start | bytes 2097152 | tf_op jit(solution)/shard_map/all_to_all | solution.py:363
  186.8 26.9 %collective-permute-start.13 = (bf16[15,1024]{1,0:T(8,128)(2,1)S(1)}, bf16[15,1024]{1,0:T(8,128)(2,1)S(1)}, u32[]{:S(2)}, u32[]{:S(2)}) collective-permute-start(bf16[15,1024]{1,0:T(8,128)(2,1)S(1)} %get-tuple-element.64), channel_id=1, source_target_pairs={{0,1},{1,2},{2,3},{3,4},{4,5},{5,6},{6,7},{7,8},{8,9},{9,10},{10,1... | collective-permute-start | bytes 92168 | tf_op jit(solution)/shard_map/ppermute | solution.py:114
  188.7 25.0 %collective-permute-start.14 = (bf16[15,1024]{1,0:T(8,128)(2,1)S(1)}, bf16[15,1024]{1,0:T(8,128)(2,1)S(1)}, u32[]{:S(2)}, u32[]{:S(2)}) collective-permute-start(bf16[15,1024]{1,0:T(8,128)(2,1)S(1)} %get-tuple-element.63), channel_id=1, source_target_pairs={{1,0},{2,1},{3,2},{4,3},{5,4},{6,5},{7,6},{8,7},{9,8},{10,9},{11,1... | collective-permute-start | bytes 92168 | tf_op jit(solution)/shard_map/ppermute | solution.py:115
  197.5 13.7 %all-to-all-start.4 = ((bf16[4,32,1536]{2,1,0:T(8,128)(2,1)}), bf16[4,32,1536]{2,1,0:T(8,128)(2,1)S(1)}, u32[]{:S(2)}, u32[]{:S(2)}) async-start(bf16[4,32,1536]{2,1,0:T(8,128)(2,1)} %bitcast.112), calls=%async_computation.5 | async-start | bytes 786432 | tf_op jit(solution)/shard_map/all_to_all | solution.py:96
  211.2 0.7 copy-start.4
Sparse Core Ops, SparseCore 0:
  10.6 30.0 all-gather.6
  48.9 54.6 all-gather.4
  149.6 45.2 reduce-scatter.1

commit v9 on v7

--- a/solution.py
+++ b/solution.py
@@ -54,9 +54,39 @@
     for step in range(1, nz // 2):
         right, left = ring_step(right, left, "z")
         buffer = place(place(buffer, right, me - step), left, me + step)
-    right = lax.ppermute(right, "z", ring_ways("z")[0])
-    buffer = place(buffer, right, me - nz // 2)
+    up, down = ring_ways("z")
+    across = [lax.ppermute(right[: ny // 2], "z", up), lax.ppermute(left[ny // 2 :], "z", down)]
+    buffer = place(buffer, jnp.concatenate(across, axis=0), me + nz // 2)
     return buffer.reshape(ny * nz * rows, width)
+
+
+def merge_kernel(parts_ref, out_ref):
+    ny, rows, wide = parts_ref.shape
+    part = wide // 3
+    for k in range(3):
+        for y in range(ny):
+            first = (k * ny + y) * part
+            out_ref[:, first : first + part] = parts_ref[y, :, k * part : (k + 1) * part]
+
+
+def merged(parts):
+    ny, rows, wide = parts.shape
+    return pl.pallas_call(merge_kernel, out_shape=jax.ShapeDtypeStruct((rows, ny * wide), BF))(parts)
+
+
+def sum_kernel(*refs):
+    out_ref = refs[-1]
+    half = refs[0].shape[1]
+    for side in range(2):
+        own, below, above = (ref[...].astype(F32) for ref in refs[3 * side : 3 * side + 3])
+        out_ref[:, side * half : (side + 1) * half] = (own + below + above).astype(BF)
+
+
+def summed(*parts):
+    rows, half = parts[0].shape
+    shape = jax.ShapeDtypeStruct((rows, 2 * half), BF)
+    limit = pltpu.CompilerParams(vmem_limit_bytes=32 * 1024 * 1024)
+    return pl.pallas_call(sum_kernel, out_shape=shape, compiler_params=limit)(*parts)
 
 
 def scatter_weight_grad(term):
@@ -64,8 +94,7 @@
     rows, part = term.shape[2], term.shape[3] // 3
     mine = lax.psum_scatter(term.reshape(nz * ny * rows, 3 * part), "z", scatter_dimension=0, tiled=True)
     back = lax.all_to_all(mine.reshape(ny, rows, 3 * part), "y", 0, 0, tiled=True)
-    back = back.reshape(ny, rows, 3, part).transpose(1, 2, 0, 3)
-    return back.reshape(1, rows, 3 * ny * part)
+    return mine, merged(back)[None]
 
 
 def slots_of(chosen):
@@ -296,9 +325,7 @@
     targets = [(me + offset) % ny for offset in (0, 2, 1, ny - 1)]
     own_low, own_high, term = last_rows(targets, rows_in, rows_q, weights, *kept)
     term, below_high, above_low = lax.optimization_barrier((term, below_high, above_low))
-    low = add(own_low, below_low, above_low).astype(BF)
-    high = add(own_high, below_high, above_high).astype(BF)
-    return low, high, term
+    return summed(own_low, below_low, above_low, own_high, below_high, above_high), term
 
 
 def local(block_in, out_grad, gate_values, expert_ids, conv_kernel, expert_weights):
@@ -317,10 +344,9 @@
     sent_q = route(all_grad, experts, True)
     weights = gather_weights(columns, sent_q)
     rows_q = lax.all_to_all(sent_q, by_expert, 0, 0, tiled=True)
-    low, high, term = rows_backward(rows_in, rows_q, weights)
-    weight_grad = scatter_weight_grad(term)
-    summed = jnp.concatenate([low, high], axis=1).reshape(experts, SLOTS, width)
-    returned = lax.all_to_all(summed, by_expert, 0, 0, tiled=True)
+    row_sums, term = rows_backward(rows_in, rows_q, weights)
+    reduced, weight_grad = scatter_weight_grad(term)
+    returned = lax.all_to_all(row_sums.reshape(experts, SLOTS, width), by_expert, 0, 0, tiled=True)
 
     own_ids = expert_ids.T[None] == jnp.arange(experts, dtype=jnp.int32)[:, None, None]
     own = slots_of(own_ids[:, 0] | own_ids[:, 1])
@@ -342,6 +368,7 @@
     half = taps.shape[0] // 2
     rounded = frame_grad.astype(BF)
     low, high = halo_of(rounded, half)
+    frame_grad, rounded, reduced = lax.optimization_barrier((frame_grad, rounded, reduced))
     rows = rounded.astype(F32)
     inner = convolved(frame_grad[EDGE : frames - EDGE], rows[EDGE - half : frames - EDGE + half], taps)
     low, high, inner, weight_grad = lax.optimization_barrier((low, high, inner, weight_grad))

time: 221 us -> 219 us (level)
  starting transfers between devices: 43.5 us -> 50.6 us
  waiting for transfers between devices: 66.6 us -> 60.8 us
  Pallas kernels: 40.5 us -> 43.7 us
  local copies, waits for them, and re-layouts: 8.31 us -> 5.58 us
  other arithmetic: 13.7 us -> 11.1 us
    ppermute x1 -> x2, starting transfers between devices: 0.01 us -> 3.85 us  [the longest x1 3.77 us: gather_weights(): lax.ppermute(left[ny // 2:], 'z', down)]
    ppermute x1 -> x2, waiting for transfers between devices: 10.4 us -> 6.78 us  [the longest x1 3.79 us: gather_weights(): lax.ppermute(right[:ny // 2], 'z', up)]
    pallas_call x0 -> x2, Pallas kernels: none -> 3.13 us  [the longest x1 1.77 us: merged(): pl.pallas_call(merge_kernel, out_shape=jax.ShapeDtypeStruct((rows, ny * w...]
    convert_element_type x2 -> x1, other arithmetic: 2.55 us -> 0.07 us  [local(): rows = rounded.astype(F32)]
  transfers between devices with their start and end apart: 21 -> 22, of which waited for: 9 -> 10; matrix products, arithmetic and copies ran while one was open for 6% -> 5% of each run, Pallas kernels for 16% -> 17%
where the time goes in v9:
time: 219 us
  waiting for transfers between devices  60.8 us (28%)
  starting transfers between devices  50.6 us (23%)
  Pallas kernels  43.7 us (20%)
  blocking collectives  31.8 us (15%)
  between operations  14.2 us (6%)
  other arithmetic  11.1 us (5%)
  local copies, waits for them, and re-layouts  5.58 us (3%)
    ppermute x6, waiting for transfers between devices, ring_step(): return (lax.ppermute(right, axis, up), lax.ppermute(left, axis, down))  24.6 us
    all_to_all x1, blocking collectives, local(): mine_in = lax.all_to_all(sent_in, by_expert, 0, 0, tiled=True)  20.5 us
    pallas_call x2, Pallas kernels, expert_rows(): pl.pallas_call(functools.partial(rows_kernel, count, steps), grid_spec=pl...  17.1 us
    pallas_call x1, Pallas kernels, last_rows(): pl.pallas_call(last_kernel, grid_spec=pltpu.PrefetchScalarGridSpec(num_sc...  17 us
    all_to_all x1, waiting for transfers between devices, local(): lax.all_to_all(row_sums.reshape(experts, SLOTS, width), by_expert, 0, 0,...  15.6 us
    ppermute x6, starting transfers between devices, ring_step(): return (lax.ppermute(right, axis, up), lax.ppermute(left, axis, down))  12.5 us
    all_to_all x1, blocking collectives, own_columns(): lax.all_to_all(sliced.reshape(ny, rows, 3 * part), 'y', 0, 0, tiled=True)  11.3 us
    ppermute x1, starting transfers between devices, halo_of(): return (low, lax.ppermute(block[:width], axes, backward))  9.89 us
  transfers between devices with their start and end apart: 22, of which 10 were waited for; matrix products, arithmetic and copies ran while one was open for 5% of the time, Pallas kernels for 17%

profile of v9, /device:TPU:8, one launch (start us, length us, event | category | flops | bytes accessed | tf_op | source)
XLA Modules:
  0.0 218.6 jit_solution(2740868482917795590)
XLA Ops:
  7.2 0.0 all-gather.7.cloned.1.call-start
  7.2 0.7 convert_bitcast_fusion
  7.9 0.7 fusion.169
  8.6 1.9 pad_maximum_fusion
  10.6 0.0 all-gather.5.cloned.1.call-start
  10.6 1.3 reshape_squeeze.3
  11.9 0.2 copy.50
  12.1 0.5 reshape.26
  12.6 11.3 %all_to_all.25 = bf16[4,32,1536]{2,1,0:T(8,128)(2,1)S(1)} all-to-all(bf16[4,32,1536]{2,1,0:T(8,128)(2,1)S(1)} %reshape.26), channel_id=1, replica_groups=mesh['y'=4,'z'=8,'x'=4,'c'=2] {'y'}, dimensions={0} | all-to-all | bytes 786432 | tf_op jit(solution)/shard_map/all_to_all | solution.py:40
  24.0 1.8 shard_map.85
  25.8 20.5 %all_to_all.26 = bf16[8,1,64,1024]{3,2,1,0:T(8,128)(2,1)} all-to-all(bf16[8,1,64,1024]{3,2,1,0:T(8,128)(2,1)} %shard_map.85), channel_id=1, replica_groups=mesh['y'=4,'z'=8,'x'=4,'c'=2] {'x','c'}, dimensions={0} | all-to-all | bytes 2097152 | tf_op jit(solution)/shard_map/all_to_all | solution.py:342
  46.3 0.0 all-gather.7.cloned.1.call-done
  46.4 1.4 copy-done
  47.8 4.6 %shard_map.86 = bf16[8,4,64,1024]{3,2,1,0:T(8,128)(2,1)} custom-call(bf16[4,200,1024]{2,1,0:T(8,128)(2,1)S(1)} %bitcast.104), custom_call_target="tpu_custom_call" | custom-call | tf_op jit(solution)/shard_map/pallas_call | solution.py:147
  52.4 4.6 %all-to-all-start.2 = ((bf16[8,4,64,1024]{3,2,1,0:T(8,128)(2,1)}), bf16[8,4,64,1024]{3,2,1,0:T(8,128)(2,1)}, u32[]{:S(2)}, u32[]{:S(2)}) async-start(bf16[8,4,64,1024]{3,2,1,0:T(8,128)(2,1)} %shard_map.86), calls=%async_computation.2 | async-start | bytes 8388608 | tf_op jit(solution)/shard_map/all_to_all | solution.py:346
  56.9 0.0 reduce-scatter.2.cloned.1.call-start
  57.1 2.0 collective-permute-start
  59.1 4.1 %collective-permute-start.1 = (bf16[4,32,1536]{2,1,0:T(8,128)(2,1)S(1)}, bf16[4,32,1536]{2,1,0:T(8,128)(2,1)S(1)}, u32[]{:S(2)}, u32[]{:S(2)}) collective-permute-start(bf16[4,32,1536]{2,1,0:T(8,128)(2,1)S(1)} %all_to_all.25), channel_id=1, source_target_pairs={{8,0},{16,8},{24,16},{32,24},{40,32},{48,40},{56,48},{0,56},{9,1},... | collective-permute-start | bytes 1179656 | tf_op jit(solution)/shard_map/ppermute | solution.py:32
  63.2 0.3 broadcast_in_dim.40
  63.6 8.9 %collective-permute-done = bf16[4,32,1536]{2,1,0:T(8,128)(2,1)S(1)} collective-permute-done((bf16[4,32,1536]{2,1,0:T(8,128)(2,1)S(1)}, bf16[4,32,1536]{2,1,0:T(8,128)(2,1)S(1)}, u32[]{:S(2)}, u32[]{:S(2)}) %collective-permute-start) | collective-permute-done | bytes 393248 | tf_op jit(solution)/shard_map/ppermute | solution.py:32
  72.5 3.2 %collective-permute-start.3 = (bf16[4,32,1536]{2,1,0:T(8,128)(2,1)S(1)}, bf16[4,32,1536]{2,1,0:T(8,128)(2,1)S(1)}, u32[]{:S(2)}, u32[]{:S(2)}) collective-permute-start(bf16[4,32,1536]{2,1,0:T(8,128)(2,1)S(1)} %collective-permute-done.1), channel_id=1, source_target_pairs={{8,0},{16,8},{24,16},{32,24},{40,32},{48,40},{56,48},{0,56},{9,1},... | collective-permute-start | bytes 1179656 | tf_op jit(solution)/shard_map/ppermute | solution.py:32
  75.8 8.6 %collective-permute-done.2 = bf16[4,32,1536]{2,1,0:T(8,128)(2,1)S(1)} collective-permute-done((bf16[4,32,1536]{2,1,0:T(8,128)(2,1)S(1)}, bf16[4,32,1536]{2,1,0:T(8,128)(2,1)S(1)}, u32[]{:S(2)}, u32[]{:S(2)}) %collective-permute-start.2) | collective-permute-done | bytes 393248 | tf_op jit(solution)/shard_map/ppermute | solution.py:32
  84.4 3.2 %collective-permute-start.5 = (bf16[4,32,1536]{2,1,0:T(8,128)(2,1)S(1)}, bf16[4,32,1536]{2,1,0:T(8,128)(2,1)S(1)}, u32[]{:S(2)}, u32[]{:S(2)}) collective-permute-start(bf16[4,32,1536]{2,1,0:T(8,128)(2,1)S(1)} %collective-permute-done.3), channel_id=1, source_target_pairs={{8,0},{16,8},{24,16},{32,24},{40,32},{48,40},{56,48},{0,56},{9,1},... | collective-permute-start | bytes 1179656 | tf_op jit(solution)/shard_map/ppermute | solution.py:32
  87.7 7.1 %collective-permute-done.5 = bf16[4,32,1536]{2,1,0:T(8,128)(2,1)S(1)} collective-permute-done((bf16[4,32,1536]{2,1,0:T(8,128)(2,1)S(1)}, bf16[4,32,1536]{2,1,0:T(8,128)(2,1)S(1)}, u32[]{:S(2)}, u32[]{:S(2)}) %collective-permute-start.5) | collective-permute-done | bytes 393248 | tf_op jit(solution)/shard_map/ppermute | solution.py:32
  94.8 3.8 %collective-permute-start.7 = (bf16[2,32,1536]{2,1,0:T(8,128)(2,1)S(1)}, bf16[2,32,1536]{2,1,0:T(8,128)(2,1)S(1)}, u32[]{:S(2)}, u32[]{:S(2)}) collective-permute-start(bf16[2,32,1536]{2,1,0:T(8,128)(2,1)S(1)} %slice.673), channel_id=1, source_target_pairs={{8,0},{16,8},{24,16},{32,24},{40,32},{48,40},{56,48},{0,56},{9,1},... | collective-permute-start | bytes 589832 | tf_op jit(solution)/shard_map/ppermute | solution.py:58
  98.6 0.1 collective-permute-start.6
  98.8 3.0 %collective-permute-done.7 = bf16[2,32,1536]{2,1,0:T(8,128)(2,1)S(1)} collective-permute-done((bf16[2,32,1536]{2,1,0:T(8,128)(2,1)S(1)}, bf16[2,32,1536]{2,1,0:T(8,128)(2,1)S(1)}, u32[]{:S(2)}, u32[]{:S(2)}) %collective-permute-start.7) | collective-permute-done | bytes 196640 | tf_op jit(solution)/shard_map/ppermute | solution.py:58
  101.8 3.8 %collective-permute-done.6 = bf16[2,32,1536]{2,1,0:T(8,128)(2,1)S(1)} collective-permute-done((bf16[2,32,1536]{2,1,0:T(8,128)(2,1)S(1)}, bf16[2,32,1536]{2,1,0:T(8,128)(2,1)S(1)}, u32[]{:S(2)}, u32[]{:S(2)}) %collective-permute-start.6) | collective-permute-done | bytes 196640 | tf_op jit(solution)/shard_map/ppermute | solution.py:58
  105.6 1.0 all-to-all-done.2.q_ref
  106.6 0.6 copy-done.3
  107.2 6.5 %shard_map.87 = (bf16[512,512]{1,0:T(8,128)(2,1)}, bf16[512,512]{1,0:T(8,128)(2,1)S(1)}, bf16[2048,1024]{1,0:T(8,128)(2,1)}, bf16[8,4,64,512]{3,2,1,0:T(8,128)(2,1)}) custom-call(s32[1]{0:T(128)} %bitcast.5.info, bf16[4,8,64,1024]{3,2,1,0:T(8,128)(2,1)} %bitcast.109, bf16[8,4,64,1024]{3,2,1,0:T(8,128)(2,1)} %all-to-all-done.2.q_ref, bf16[1024,1536]{1,0:T(8,128)(2,1)} %bitcast.106), custom_call_target="tpu_custom_call" | custom-call | tf_op jit(solution)/shard_map/pallas_call | solution.py:274
  113.8 0.1 collective-permute-start.8
  113.9 1.9 collective-permute-start.9
  115.8 0.1 pad_add_fusion.1.info
  115.9 10.6 %shard_map.88 = (bf16[512,512]{1,0:T(8,128)(2,1)S(1)}, bf16[512,512]{1,0:T(8,128)(2,1)S(1)}, bf16[512,512]{1,0:T(8,128)(2,1)S(1)}, bf16[512,512]{1,0:T(8,128)(2,...) custom-call(s32[2]{0:T(128)S(1)} %pad_add_fusion.1.info, ...), custom_call_target="tpu_custom_call", output_to_operand_aliasing={{4}: (4, {}), {5}: (5, {})} | custom-call | tf_op jit(solution)/shard_map/pallas_call | solution.py:274
  126.5 0.2 collective-permute-start.11
  126.7 2.5 %collective-permute-start.12 = (bf16[512,512]{1,0:T(8,128)(2,1)S(1)}, bf16[512,512]{1,0:T(8,128)(2,1)S(1)}, u32[]{:S(2)}, u32[]{:S(2)}) collective-permute-start(bf16[512,512]{1,0:T(8,128)(2,1)S(1)} %get-tuple-element.48), channel_id=1, source_target_pairs={{64,0},{128,64},{192,128},{0,192},{65,1},{129,65},{193,129},{1,193... | collective-permute-start | bytes 1572872 | tf_op jit(solution)/shard_map/ppermute | solution.py:313
  129.2 0.6 pad_add_fusion.info
  129.7 17.0 %shard_map.89 = (bf16[512,512]{1,0:T(8,128)(2,1)}, bf16[512,512]{1,0:T(8,128)(2,1)}, bf16[8,4,32,1536]{3,2,1,0:T(8,128)(2,1)}) custom-call(s32[4]{0:T(128)} %pad_add_fusion.info, bf16[4,8,64,1024]{3,2,1,0:T(8,128)(2,1)} %bitcast.111, bf16[8,4,64,1024]{3,2,1,0:T(8,128)(2,1)} %all-to-all-done.2.q_ref, bf16[1024,1536]{1,0:T(8,128)(2,1)} %bitcast.108, ...), custom_call_target="tpu_custom_call" | custom-call | tf_op jit(solution)/shard_map/pallas_call | solution.py:229
  146.8 1.3 add_convert_fusion.1
  148.1 0.1 collective-permute-start.10
  148.2 1.2 add_convert_fusion
  149.4 3.5 %collective-permute-start.13 = (bf16[512,512]{1,0:T(8,128)(2,1)S(1)}, bf16[512,512]{1,0:T(8,128)(2,1)S(1)}, u32[]{:S(2)}, u32[]{:S(2)}) collective-permute-start(bf16[512,512]{1,0:T(8,128)(2,1)S(1)} %add_convert_fusion), channel_id=1, source_target_pairs={{64,0},{128,64},{192,128},{0,192},{65,1},{129,65},{193,129},{1,193... | collective-permute-start | bytes 1572872 | tf_op jit(solution)/shard_map/ppermute | solution.py:313
  152.9 8.5 %collective-permute-done.10.refs_1_ = bf16[512,512]{1,0:T(8,128)(2,1)S(1)} collective-permute-done((bf16[512,512]{1,0:T(8,128)(2,1)S(1)}, bf16[512,512]{1,0:T(8,128)(2,1)S(1)}, u32[]{:S(2)}, u32[]{:S(2)}) %collective-permute-start.10) | collective-permute-done | bytes 524320 | tf_op jit(solution)/shard_map/ppermute | solution.py:313
  161.4 0.9 collective-permute-done.13.refs_5_
  162.3 1.4 shard_map.90
  163.7 3.7 %all-to-all-start.3 = ((bf16[8,64,1024]{2,1,0:T(8,128)(2,1)}), bf16[8,64,1024]{2,1,0:T(8,128)(2,1)S(1)}, u32[]{:S(2)}, u32[]{:S(2)}) async-start(bf16[8,64,1024]{2,1,0:T(8,128)(2,1)} %bitcast.31), calls=%async_computation.3 | async-start | bytes 2097152 | tf_op jit(solution)/shard_map/all_to_all | solution.py:349
  167.4 0.1 convolution_convert_fusion
  167.6 0.1 fusion.174
  167.7 15.6 %all-to-all-done.3 = bf16[8,64,1024]{2,1,0:T(8,128)(2,1)S(1)} async-done(((bf16[8,64,1024]{2,1,0:T(8,128)(2,1)}), bf16[8,64,1024]{2,1,0:T(8,128)(2,1)S(1)}, u32[]{:S(2)}, u32[]{:S(2)}) %all-to-all-start.3) | async-done | bytes 1048608 | tf_op jit(solution)/shard_map/all_to_all | solution.py:349
  183.3 0.4 fusion.176
  183.7 1.9 collective-permute-start.14
  185.7 9.9 %collective-permute-start.15 = (bf16[15,1024]{1,0:T(8,128)(2,1)S(1)}, bf16[15,1024]{1,0:T(8,128)(2,1)S(1)}, u32[]{:S(2)}, u32[]{:S(2)}) collective-permute-start(bf16[15,1024]{1,0:T(8,128)(2,1)S(1)} %get-tuple-element.63), channel_id=1, source_target_pairs={{1,0},{2,1},{3,2},{4,3},{5,4},{6,5},{7,6},{8,7},{9,8},{10,9},{11,1... | collective-permute-start | bytes 92168 | tf_op jit(solution)/shard_map/ppermute | solution.py:115
  195.6 0.2 fusion.34
  195.8 0.6 fusion.171
  196.4 0.1 convert_element_type.76
  196.5 5.8 %all-to-all-start.4 = ((bf16[4,32,1536]{2,1,0:T(8,128)(2,1)}), bf16[4,32,1536]{2,1,0:T(8,128)(2,1)S(1)}, u32[]{:S(2)}, u32[]{:S(2)}) async-start(bf16[4,32,1536]{2,1,0:T(8,128)(2,1)} %bitcast.114), calls=%async_computation.5 | async-start | bytes 786432 | tf_op jit(solution)/shard_map/all_to_all | solution.py:96
  202.2 2.6 %fusion.2 = bf16[160,1024]{1,0:T(8,128)(2,1)S(1)} fusion(f32[192,1024]{1,0:T(8,128)S(1)} %convert_element_type.76, f32[192,1024]{1,0:T(8,128)S(1)} %get-tuple-element.55, f32[1024]{0:T(1024)S(1)} %bitcast.149, f32[1024]{0:T(1024)S(1)} %bitcast.146, f32[1024]{0:T(1024)S(1)} %bitcast.143, f32[1024]{0:T(1024)S(1)} %bitcast.140, f32[1024]{0:T(1024)S(1)} %bitcast.137, ...), kind=kLoop, calls=%fused_computation.35 | loop fusion | flops 10321920 | bytes 21426176 | tf_op jit(solution)/shard_map/convert_element_type | solution.py:124
  204.8 3.3 %all-to-all-done.4.parts_ref = bf16[4,32,1536]{2,1,0:T(8,128)(2,1)S(1)} async-done(((bf16[4,32,1536]{2,1,0:T(8,128)(2,1)}), bf16[4,32,1536]{2,1,0:T(8,128)(2,1)S(1)}, u32[]{:S(2)}, u32[]{:S(2)}) %all-to-all-start.4) | async-done | bytes 393248 | tf_op jit(solution)/shard_map/all_to_all | solution.py:96
  208.2 0.7 copy-done.4
  208.9 1.8 shard_map.91
  210.7 0.3 fusion.163
  211.0 0.3 fusion.105
  211.3 0.8 pad_maximum_fusion.2
  (52 shorter events, 0.5 us)
Async XLA Ops:
  7.2 39.2 %all-gather.7.cloned.1.call-start = ((), (), s32[]{:S(2)}) async-start(), calls=%async_computation.8 | async-start | bytes 2048000 | tf_op jit(solution)/shard_map/all_gather | solution.py:338
  10.6 96.0 %all-gather.5.cloned.1.call-start = ((), (), s32[]{:S(2)}) async-start(), calls=%async_computation.7 | async-start | bytes 5242880 | tf_op jit(solution)/shard_map/all_gather | solution.py:343
  46.4 1.4 copy-start
  52.4 54.2 %all-to-all-start.2 = ((bf16[8,4,64,1024]{3,2,1,0:T(8,128)(2,1)}), bf16[8,4,64,1024]{3,2,1,0:T(8,128)(2,1)}, u32[]{:S(2)}, u32[]{:S(2)}) async-start(bf16[8,4,64,1024]{3,2,1,0:T(8,128)(2,1)} %shard_map.86), calls=%async_computation.2 | async-start | bytes 8388608 | tf_op jit(solution)/shard_map/all_to_all | solution.py:346
  56.9 139.5 %reduce-scatter.2.cloned.1.call-start = ((), (), s32[]{:S(2)}) async-start(), calls=%async_computation.6 | async-start | bytes 3538944 | tf_op jit(solution)/shard_map/reduce_scatter | solution.py:95
  57.1 15.3 %collective-permute-start = (bf16[4,32,1536]{2,1,0:T(8,128)(2,1)S(1)}, bf16[4,32,1536]{2,1,0:T(8,128)(2,1)S(1)}, u32[]{:S(2)}, u32[]{:S(2)}) collective-permute-start(bf16[4,32,1536]{2,1,0:T(8,128)(2,1)S(1)} %all_to_all.25), channel_id=1, source_target_pairs={{0,8},{8,16},{16,24},{24,32},{32,40},{40,48},{48,56},{56,0},{1,9},... | collective-permute-start | bytes 1179656 | tf_op jit(solution)/shard_map/ppermute | solution.py:32
  59.1 13.4 %collective-permute-start.1 = (bf16[4,32,1536]{2,1,0:T(8,128)(2,1)S(1)}, bf16[4,32,1536]{2,1,0:T(8,128)(2,1)S(1)}, u32[]{:S(2)}, u32[]{:S(2)}) collective-permute-start(bf16[4,32,1536]{2,1,0:T(8,128)(2,1)S(1)} %all_to_all.25), channel_id=1, source_target_pairs={{8,0},{16,8},{24,16},{32,24},{40,32},{48,40},{56,48},{0,56},{9,1},... | collective-permute-start | bytes 1179656 | tf_op jit(solution)/shard_map/ppermute | solution.py:32
  72.5 11.9 %collective-permute-start.2 = (bf16[4,32,1536]{2,1,0:T(8,128)(2,1)S(1)}, bf16[4,32,1536]{2,1,0:T(8,128)(2,1)S(1)}, u32[]{:S(2)}, u32[]{:S(2)}) collective-permute-start(bf16[4,32,1536]{2,1,0:T(8,128)(2,1)S(1)} %collective-permute-done), channel_id=1, source_target_pairs={{0,8},{8,16},{16,24},{24,32},{32,40},{40,48},{48,56},{56,0},{1,9},... | collective-permute-start | bytes 1179656 | tf_op jit(solution)/shard_map/ppermute | solution.py:32
  72.5 11.9 %collective-permute-start.3 = (bf16[4,32,1536]{2,1,0:T(8,128)(2,1)S(1)}, bf16[4,32,1536]{2,1,0:T(8,128)(2,1)S(1)}, u32[]{:S(2)}, u32[]{:S(2)}) collective-permute-start(bf16[4,32,1536]{2,1,0:T(8,128)(2,1)S(1)} %collective-permute-done.1), channel_id=1, source_target_pairs={{8,0},{16,8},{24,16},{32,24},{40,32},{48,40},{56,48},{0,56},{9,1},... | collective-permute-start | bytes 1179656 | tf_op jit(solution)/shard_map/ppermute | solution.py:32
  84.4 14.2 %collective-permute-start.4 = (bf16[4,32,1536]{2,1,0:T(8,128)(2,1)S(1)}, bf16[4,32,1536]{2,1,0:T(8,128)(2,1)S(1)}, u32[]{:S(2)}, u32[]{:S(2)}) collective-permute-start(bf16[4,32,1536]{2,1,0:T(8,128)(2,1)S(1)} %collective-permute-done.2), channel_id=1, source_target_pairs={{0,8},{8,16},{16,24},{24,32},{32,40},{40,48},{48,56},{56,0},{1,9},... | collective-permute-start | bytes 1179656 | tf_op jit(solution)/shard_map/ppermute | solution.py:32
  84.4 10.4 %collective-permute-start.5 = (bf16[4,32,1536]{2,1,0:T(8,128)(2,1)S(1)}, bf16[4,32,1536]{2,1,0:T(8,128)(2,1)S(1)}, u32[]{:S(2)}, u32[]{:S(2)}) collective-permute-start(bf16[4,32,1536]{2,1,0:T(8,128)(2,1)S(1)} %collective-permute-done.3), channel_id=1, source_target_pairs={{8,0},{16,8},{24,16},{32,24},{40,32},{48,40},{56,48},{0,56},{9,1},... | collective-permute-start | bytes 1179656 | tf_op jit(solution)/shard_map/ppermute | solution.py:32
  94.8 7.0 %collective-permute-start.7 = (bf16[2,32,1536]{2,1,0:T(8,128)(2,1)S(1)}, bf16[2,32,1536]{2,1,0:T(8,128)(2,1)S(1)}, u32[]{:S(2)}, u32[]{:S(2)}) collective-permute-start(bf16[2,32,1536]{2,1,0:T(8,128)(2,1)S(1)} %slice.673), channel_id=1, source_target_pairs={{8,0},{16,8},{24,16},{32,24},{40,32},{48,40},{56,48},{0,56},{9,1},... | collective-permute-start | bytes 589832 | tf_op jit(solution)/shard_map/ppermute | solution.py:58
  98.6 7.0 %collective-permute-start.6 = (bf16[2,32,1536]{2,1,0:T(8,128)(2,1)S(1)}, bf16[2,32,1536]{2,1,0:T(8,128)(2,1)S(1)}, u32[]{:S(2)}, u32[]{:S(2)}) collective-permute-start(bf16[2,32,1536]{2,1,0:T(8,128)(2,1)S(1)} %slice.672), channel_id=1, source_target_pairs={{0,8},{8,16},{16,24},{24,32},{32,40},{40,48},{48,56},{56,0},{1,9},... | collective-permute-start | bytes 589832 | tf_op jit(solution)/shard_map/ppermute | solution.py:58
  105.6 1.6 copy-start.3
  113.8 16.0 %collective-permute-start.8 = (bf16[512,512]{1,0:T(8,128)(2,1)}, bf16[512,512]{1,0:T(8,128)(2,1)}, u32[]{:S(2)}, u32[]{:S(2)}) collective-permute-start(bf16[512,512]{1,0:T(8,128)(2,1)} %get-tuple-element.35), channel_id=1, source_target_pairs={{0,64},{64,128},{128,192},{192,0},{1,65},{65,129},{129,193},{193,1... | collective-permute-start | bytes 1572872 | tf_op jit(solution)/shard_map/ppermute | solution.py:313
  113.9 15.8 %collective-permute-start.9 = (bf16[512,512]{1,0:T(8,128)(2,1)S(1)}, bf16[512,512]{1,0:T(8,128)(2,1)}, u32[]{:S(2)}, u32[]{:S(2)}) collective-permute-start(bf16[512,512]{1,0:T(8,128)(2,1)S(1)} %get-tuple-element.36), channel_id=1, source_target_pairs={{64,0},{128,64},{192,128},{0,192},{65,1},{129,65},{193,129},{1,193... | collective-permute-start | bytes 1572872 | tf_op jit(solution)/shard_map/ppermute | solution.py:313
  126.5 20.3 %collective-permute-start.11 = (bf16[512,512]{1,0:T(8,128)(2,1)S(1)}, bf16[512,512]{1,0:T(8,128)(2,1)S(1)}, u32[]{:S(2)}, u32[]{:S(2)}) collective-permute-start(bf16[512,512]{1,0:T(8,128)(2,1)S(1)} %get-tuple-element.47), channel_id=1, source_target_pairs={{0,64},{64,128},{128,192},{192,0},{1,65},{65,129},{129,193},{193,1... | collective-permute-start | bytes 1572872 | tf_op jit(solution)/shard_map/ppermute | solution.py:313
  126.7 20.1 %collective-permute-start.12 = (bf16[512,512]{1,0:T(8,128)(2,1)S(1)}, bf16[512,512]{1,0:T(8,128)(2,1)S(1)}, u32[]{:S(2)}, u32[]{:S(2)}) collective-permute-start(bf16[512,512]{1,0:T(8,128)(2,1)S(1)} %get-tuple-element.48), channel_id=1, source_target_pairs={{64,0},{128,64},{192,128},{0,192},{65,1},{129,65},{193,129},{1,193... | collective-permute-start | bytes 1572872 | tf_op jit(solution)/shard_map/ppermute | solution.py:313
  146.8 1.4 copy-start.5
  146.8 15.5 %copy-start.1 = (bf16[512,512]{1,0:T(8,128)(2,1)S(1)}, bf16[512,512]{1,0:T(8,128)(2,1)}, u32[]{:S(2)}) copy-start(bf16[512,512]{1,0:T(8,128)(2,1)} %get-tuple-element.43.refs_0_) | copy-start | bytes 1572868
  146.8 15.5 %copy-start.2 = (bf16[512,512]{1,0:T(8,128)(2,1)S(1)}, bf16[512,512]{1,0:T(8,128)(2,1)}, u32[]{:S(2)}) copy-start(bf16[512,512]{1,0:T(8,128)(2,1)} %get-tuple-element.50.refs_3_) | copy-start | bytes 1572868
  148.1 13.3 %collective-permute-start.10 = (bf16[512,512]{1,0:T(8,128)(2,1)S(1)}, bf16[512,512]{1,0:T(8,128)(2,1)S(1)}, u32[]{:S(2)}, u32[]{:S(2)}) collective-permute-start(bf16[512,512]{1,0:T(8,128)(2,1)S(1)} %add_convert_fusion.1), channel_id=1, source_target_pairs={{0,64},{64,128},{128,192},{192,0},{1,65},{65,129},{129,193},{193,1... | collective-permute-start | bytes 1572872 | tf_op jit(solution)/shard_map/ppermute | solution.py:313
  149.4 12.9 %collective-permute-start.13 = (bf16[512,512]{1,0:T(8,128)(2,1)S(1)}, bf16[512,512]{1,0:T(8,128)(2,1)S(1)}, u32[]{:S(2)}, u32[]{:S(2)}) collective-permute-start(bf16[512,512]{1,0:T(8,128)(2,1)S(1)} %add_convert_fusion), channel_id=1, source_target_pairs={{64,0},{128,64},{192,128},{0,192},{65,1},{129,65},{193,129},{1,193... | collective-permute-start | bytes 1572872 | tf_op jit(solution)/shard_map/ppermute | solution.py:313
  162.3 5.1 %copy-start.8 = (s32[192,2]{0,1:T(2,128)S(1)}, s32[192,2]{0,1:T(2,128)}, u32[]{:S(2)}) copy-start(s32[192,2]{0,1:T(2,128)} %param.9) | copy-start | bytes 4612
  162.3 5.3 %copy-start.7 = (bf16[31,1024]{1,0:T(8,128)(2,1)S(1)}, bf16[31,1024]{1,0:T(8,128)(2,1)}, u32[]{:S(2)}) copy-start(bf16[31,1024]{1,0:T(8,128)(2,1)} %param.10) | copy-start | bytes 190468
  162.3 21.0 %copy-start.6 = (bf16[192,1024]{1,0:T(8,128)(2,1)S(1)}, bf16[192,1024]{1,0:T(8,128)(2,1)}, u32[]{:S(2)}) copy-start(bf16[192,1024]{1,0:T(8,128)(2,1)} %param.7) | copy-start | bytes 1179652
  163.7 32.1 %copy-start.9 = (bf16[192,2]{0,1:T(2,128)(2,1)S(1)}, bf16[192,2]{0,1:T(2,128)(2,1)}, u32[]{:S(2)}) copy-start(bf16[192,2]{0,1:T(2,128)(2,1)} %param.8) | copy-start | bytes 2308
  163.7 19.6 %all-to-all-start.3 = ((bf16[8,64,1024]{2,1,0:T(8,128)(2,1)}), bf16[8,64,1024]{2,1,0:T(8,128)(2,1)S(1)}, u32[]{:S(2)}, u32[]{:S(2)}) async-start(bf16[8,64,1024]{2,1,0:T(8,128)(2,1)} %bitcast.31), calls=%async_computation.3 | async-start | bytes 2097152 | tf_op jit(solution)/shard_map/all_to_all | solution.py:349
  183.7 26.9 %collective-permute-start.14 = (bf16[15,1024]{1,0:T(8,128)(2,1)S(1)}, bf16[15,1024]{1,0:T(8,128)(2,1)S(1)}, u32[]{:S(2)}, u32[]{:S(2)}) collective-permute-start(bf16[15,1024]{1,0:T(8,128)(2,1)S(1)} %get-tuple-element.64), channel_id=1, source_target_pairs={{0,1},{1,2},{2,3},{3,4},{4,5},{5,6},{6,7},{7,8},{8,9},{9,10},{10,1... | collective-permute-start | bytes 92168 | tf_op jit(solution)/shard_map/ppermute | solution.py:114
  185.7 25.0 %collective-permute-start.15 = (bf16[15,1024]{1,0:T(8,128)(2,1)S(1)}, bf16[15,1024]{1,0:T(8,128)(2,1)S(1)}, u32[]{:S(2)}, u32[]{:S(2)}) collective-permute-start(bf16[15,1024]{1,0:T(8,128)(2,1)S(1)} %get-tuple-element.63), channel_id=1, source_target_pairs={{1,0},{2,1},{3,2},{4,3},{5,4},{6,5},{7,6},{8,7},{9,8},{10,9},{11,1... | collective-permute-start | bytes 92168 | tf_op jit(solution)/shard_map/ppermute | solution.py:115
  196.5 11.7 %all-to-all-start.4 = ((bf16[4,32,1536]{2,1,0:T(8,128)(2,1)}), bf16[4,32,1536]{2,1,0:T(8,128)(2,1)S(1)}, u32[]{:S(2)}, u32[]{:S(2)}) async-start(bf16[4,32,1536]{2,1,0:T(8,128)(2,1)} %bitcast.114), calls=%async_computation.5 | async-start | bytes 786432 | tf_op jit(solution)/shard_map/all_to_all | solution.py:96
  208.2 0.7 copy-start.4
Sparse Core Ops, SparseCore 0:
  10.7 31.4 all-gather.6
  46.5 50.1 all-gather.4
  146.9 47.2 reduce-scatter.1

commit v10 on v8

--- a/solution.py
+++ b/solution.py
@@ -55,8 +55,9 @@
     for step in range(1, nz // 2):
         right, left = ring_step(right, left, "z")
         buffer = place(place(buffer, right, me - step), left, me + step)
-    right = lax.ppermute(right, "z", ring_ways("z")[0])
-    buffer = place(buffer, right, me - nz // 2)
+    up, down = ring_ways("z")
+    across = [lax.ppermute(right[: ny // 2], "z", up), lax.ppermute(left[ny // 2 :], "z", down)]
+    buffer = place(buffer, jnp.concatenate(across, axis=0), me + nz // 2)
     return buffer.reshape(ny * nz * rows, width)
 
 
@@ -350,10 +351,11 @@
         return jnp.concatenate([rows, jnp.pad(meta, ((0, META - 4), (0, rows.shape[1] - frames)))], axis=0)
 
     all_grad = lax.all_gather(packed(out_grad[:, EXTRA:]), "y", axis=0, tiled=False)
+    sent_in = route(packed(block_in, out_grad[:, :EXTRA])[None], experts, width)
+    mine_in = lax.all_to_all(sent_in, by_expert, 0, 0, tiled=True)
+    mine_in, expert_weights = lax.optimization_barrier((mine_in, expert_weights))
     columns = own_columns(expert_weights)
-    columns, packed_in = lax.optimization_barrier((columns, packed(block_in, out_grad[:, :EXTRA])))
-    sent_in = route(packed_in[None], experts, width)
-    mine_in = lax.all_to_all(sent_in, by_expert, 0, 0, tiled=True)
+    all_grad, columns = lax.optimization_barrier((all_grad, columns))
     rows_in = lax.all_gather(mine_in[:, 0], "y", axis=0, tiled=False)
     sent_q = route(all_grad, experts, 0)
     weights = gather_weights(columns, sent_q)

time: 222 us -> 221 us (level)
  waiting for transfers between devices: 69.9 us -> 65 us
  starting transfers between devices: 52.2 us -> 55.4 us
    all_to_all x1, waiting for transfers between devices: 8.33 us -> 0.01 us  [local(): rows_q = lax.all_to_all(sent_q, by_expert, 0, 0, tiled=True)]
    ppermute x6, waiting for transfers between devices: 17.4 us -> 24.9 us  [ring_step(): return (lax.ppermute(right, axis, up), lax.ppermute(left, axis, down))]
    ppermute x1 -> x2, starting transfers between devices: 0.01 us -> 3.85 us  [the longest x1 3.77 us: gather_weights(): lax.ppermute(left[ny // 2:], 'z', down)]
    ppermute x6, waiting for transfers between devices: 9.99 us -> 6.92 us  [send(): return lax.ppermute(rows, 'y', way)]
    ppermute x1 -> x2, waiting for transfers between devices: 9.57 us -> 6.78 us  [the longest x1 3.79 us: gather_weights(): lax.ppermute(right[:ny // 2], 'z', up)]
  transfers between devices with their start and end apart: 22 -> 23, of which waited for: 10 -> 11; matrix products, arithmetic and copies ran while one was open for 6% -> 5% of each run, Pallas kernels for 17% -> 17%
where the time goes in v10:
time: 221 us; the launch traced here: 220 us
  waiting for transfers between devices  65 us (29%)
  starting transfers between devices  55.4 us (25%)
  Pallas kernels  43.9 us (20%)
  blocking collectives  21.9 us (10%)
  between operations  14.1 us (6%)
  other arithmetic  11 us (5%)
  local copies, waits for them, and re-layouts  8.07 us (4%)
    ppermute x6, waiting for transfers between devices, ring_step(): return (lax.ppermute(right, axis, up), lax.ppermute(left, axis, down))  24.9 us
    all_to_all x1, blocking collectives, local(): mine_in = lax.all_to_all(sent_in, by_expert, 0, 0, tiled=True)  21.9 us
    pallas_call x2, Pallas kernels, expert_rows(): pl.pallas_call(functools.partial(rows_kernel, count, steps), grid_spec=pl...  17.2 us
    pallas_call x1, Pallas kernels, last_rows(): pl.pallas_call(last_kernel, grid_spec=pltpu.PrefetchScalarGridSpec(num_sc...  17 us
    all_to_all x1, waiting for transfers between devices, local(): lax.all_to_all(row_sums.reshape(experts, SLOTS, width), by_expert, 0, 0,...  15.7 us
    ppermute x6, starting transfers between devices, ring_step(): return (lax.ppermute(right, axis, up), lax.ppermute(left, axis, down))  11.6 us
    ppermute x6, starting transfers between devices, send(): return lax.ppermute(rows, 'y', way)  8.32 us
    ppermute x1, starting transfers between devices, halo_of(): return (low, lax.ppermute(block[:width], axes, backward))  7.86 us
  transfers between devices with their start and end apart: 23, of which 11 were waited for; matrix products, arithmetic and copies ran while one was open for 5% of the time, Pallas kernels for 17%

profile of v10, /device:TPU:8, one launch (start us, length us, event | category | flops | bytes accessed | tf_op | source)
XLA Modules:
  0.0 220.2 jit_solution(11597875774291703426)
XLA Ops:
  7.2 0.7 convert_bitcast_fusion
  7.9 1.0 slice.543
  8.9 0.7 pad_maximum_fusion.3
  9.6 0.8 fusion.42
  10.4 0.8 slice.542
  11.3 1.0 fusion.40.x_ref
  12.3 2.0 shard_map.85
  14.4 21.9 %all_to_all.25 = bf16[8,1,64,1152]{3,2,1,0:T(8,128)(2,1)} all-to-all(bf16[8,1,64,1152]{3,2,1,0:T(8,128)(2,1)} %shard_map.85), channel_id=1, replica_groups=mesh['y'=4,'z'=8,'x'=4,'c'=2] {'x','c'}, dimensions={0} | all-to-all | bytes 2359296 | tf_op jit(solution)/shard_map/all_to_all | solution.py:355
  36.3 0.3 reshape_squeeze.3
  36.6 0.2 copy.50
  36.8 1.3 reshape.26
  38.1 5.4 %all-to-all-start.1 = ((bf16[4,32,1536]{2,1,0:T(8,128)(2,1)}), bf16[4,32,1536]{2,1,0:T(8,128)(2,1)S(1)}, u32[]{:S(2)}, u32[]{:S(2)}) async-start(bf16[4,32,1536]{2,1,0:T(8,128)(2,1)} %reshape.26), calls=%async_computation.1 | async-start | bytes 786432 | tf_op jit(solution)/shard_map/all_to_all | solution.py:41
  43.5 6.7 %all-to-all-done.1 = bf16[4,32,1536]{2,1,0:T(8,128)(2,1)S(1)} async-done(((bf16[4,32,1536]{2,1,0:T(8,128)(2,1)}), bf16[4,32,1536]{2,1,0:T(8,128)(2,1)S(1)}, u32[]{:S(2)}, u32[]{:S(2)}) %all-to-all-start.1) | async-done | bytes 393248 | tf_op jit(solution)/shard_map/all_to_all | solution.py:41
  50.2 1.4 copy-done
  51.6 4.5 %shard_map.86 = bf16[8,4,64,896]{3,2,1,0:T(8,128)(2,1)} custom-call(bf16[4,200,896]{2,1,0:T(8,128)(2,1)S(1)} %bitcast.105), custom_call_target="tpu_custom_call" | custom-call | tf_op jit(solution)/shard_map/pallas_call | solution.py:151
  56.1 4.6 %all-to-all-start.2 = ((bf16[8,4,64,896]{3,2,1,0:T(8,128)(2,1)}), bf16[8,4,64,896]{3,2,1,0:T(8,128)(2,1)}, u32[]{:S(2)}, u32[]{:S(2)}) async-start(bf16[8,4,64,896]{3,2,1,0:T(8,128)(2,1)} %shard_map.86), calls=%async_computation.2 | async-start | bytes 7340032 | tf_op jit(solution)/shard_map/all_to_all | solution.py:362
  60.7 0.0 reduce-scatter.2.cloned.1.call-start
  60.7 1.2 collective-permute-start
  61.9 4.0 %collective-permute-start.1 = (bf16[4,32,1536]{2,1,0:T(8,128)(2,1)S(1)}, bf16[4,32,1536]{2,1,0:T(8,128)(2,1)S(1)}, u32[]{:S(2)}, u32[]{:S(2)}) collective-permute-start(bf16[4,32,1536]{2,1,0:T(8,128)(2,1)S(1)} %all-to-all-done.1), channel_id=1, source_target_pairs={{8,0},{16,8},{24,16},{32,24},{40,32},{48,40},{56,48},{0,56},{9,1},... | collective-permute-start | bytes 1179656 | tf_op jit(solution)/shard_map/ppermute | solution.py:33
  65.9 0.3 broadcast_in_dim.40
  66.3 9.0 %collective-permute-done = bf16[4,32,1536]{2,1,0:T(8,128)(2,1)S(1)} collective-permute-done((bf16[4,32,1536]{2,1,0:T(8,128)(2,1)S(1)}, bf16[4,32,1536]{2,1,0:T(8,128)(2,1)S(1)}, u32[]{:S(2)}, u32[]{:S(2)}) %collective-permute-start) | collective-permute-done | bytes 393248 | tf_op jit(solution)/shard_map/ppermute | solution.py:33
  75.4 3.2 %collective-permute-start.3 = (bf16[4,32,1536]{2,1,0:T(8,128)(2,1)S(1)}, bf16[4,32,1536]{2,1,0:T(8,128)(2,1)S(1)}, u32[]{:S(2)}, u32[]{:S(2)}) collective-permute-start(bf16[4,32,1536]{2,1,0:T(8,128)(2,1)S(1)} %collective-permute-done.1), channel_id=1, source_target_pairs={{8,0},{16,8},{24,16},{32,24},{40,32},{48,40},{56,48},{0,56},{9,1},... | collective-permute-start | bytes 1179656 | tf_op jit(solution)/shard_map/ppermute | solution.py:33
  78.7 8.7 %collective-permute-done.2 = bf16[4,32,1536]{2,1,0:T(8,128)(2,1)S(1)} collective-permute-done((bf16[4,32,1536]{2,1,0:T(8,128)(2,1)S(1)}, bf16[4,32,1536]{2,1,0:T(8,128)(2,1)S(1)}, u32[]{:S(2)}, u32[]{:S(2)}) %collective-permute-start.2) | collective-permute-done | bytes 393248 | tf_op jit(solution)/shard_map/ppermute | solution.py:33
  87.3 3.2 %collective-permute-start.5 = (bf16[4,32,1536]{2,1,0:T(8,128)(2,1)S(1)}, bf16[4,32,1536]{2,1,0:T(8,128)(2,1)S(1)}, u32[]{:S(2)}, u32[]{:S(2)}) collective-permute-start(bf16[4,32,1536]{2,1,0:T(8,128)(2,1)S(1)} %collective-permute-done.3), channel_id=1, source_target_pairs={{8,0},{16,8},{24,16},{32,24},{40,32},{48,40},{56,48},{0,56},{9,1},... | collective-permute-start | bytes 1179656 | tf_op jit(solution)/shard_map/ppermute | solution.py:33
  90.6 7.2 %collective-permute-done.5 = bf16[4,32,1536]{2,1,0:T(8,128)(2,1)S(1)} collective-permute-done((bf16[4,32,1536]{2,1,0:T(8,128)(2,1)S(1)}, bf16[4,32,1536]{2,1,0:T(8,128)(2,1)S(1)}, u32[]{:S(2)}, u32[]{:S(2)}) %collective-permute-start.5) | collective-permute-done | bytes 393248 | tf_op jit(solution)/shard_map/ppermute | solution.py:33
  97.8 3.8 %collective-permute-start.7 = (bf16[2,32,1536]{2,1,0:T(8,128)(2,1)S(1)}, bf16[2,32,1536]{2,1,0:T(8,128)(2,1)S(1)}, u32[]{:S(2)}, u32[]{:S(2)}) collective-permute-start(bf16[2,32,1536]{2,1,0:T(8,128)(2,1)S(1)} %slice.681), channel_id=1, source_target_pairs={{8,0},{16,8},{24,16},{32,24},{40,32},{48,40},{56,48},{0,56},{9,1},... | collective-permute-start | bytes 589832 | tf_op jit(solution)/shard_map/ppermute | solution.py:59
  101.6 0.1 collective-permute-start.6
  101.8 3.0 %collective-permute-done.7 = bf16[2,32,1536]{2,1,0:T(8,128)(2,1)S(1)} collective-permute-done((bf16[2,32,1536]{2,1,0:T(8,128)(2,1)S(1)}, bf16[2,32,1536]{2,1,0:T(8,128)(2,1)S(1)}, u32[]{:S(2)}, u32[]{:S(2)}) %collective-permute-start.7) | collective-permute-done | bytes 196640 | tf_op jit(solution)/shard_map/ppermute | solution.py:59
  104.8 3.8 %collective-permute-done.6 = bf16[2,32,1536]{2,1,0:T(8,128)(2,1)S(1)} collective-permute-done((bf16[2,32,1536]{2,1,0:T(8,128)(2,1)S(1)}, bf16[2,32,1536]{2,1,0:T(8,128)(2,1)S(1)}, u32[]{:S(2)}, u32[]{:S(2)}) %collective-permute-start.6) | collective-permute-done | bytes 196640 | tf_op jit(solution)/shard_map/ppermute | solution.py:59
  108.7 1.6 copy-done.3
  110.3 6.5 %shard_map.87 = (bf16[512,512]{1,0:T(8,128)(2,1)}, bf16[512,512]{1,0:T(8,128)(2,1)S(1)}, bf16[2048,1024]{1,0:T(8,128)(2,1)}, bf16[8,4,64,512]{3,2,1,0:T(8,128)(2,1)}) custom-call(s32[1]{0:T(128)} %bitcast.5.info, bf16[4,8,64,1152]{3,2,1,0:T(8,128)(2,1)} %bitcast.109, bf16[8,4,64,896]{3,2,1,0:T(8,128)(2,1)} %all-to-all-done.2.q_ref, bf16[1024,1536]{1,0:T(8,128)(2,1)} %bitcast.106), custom_call_target="tpu_custom_call" | custom-call | tf_op jit(solution)/shard_map/pallas_call | solution.py:285
  116.8 2.0 collective-permute-start.9
  118.8 0.1 pad_add_fusion.1.info
  118.9 10.6 %shard_map.88 = (bf16[512,512]{1,0:T(8,128)(2,1)S(1)}, bf16[512,512]{1,0:T(8,128)(2,1)S(1)}, bf16[512,512]{1,0:T(8,128)(2,1)S(1)}, bf16[512,512]{1,0:T(8,128)(2,...) custom-call(s32[2]{0:T(128)S(1)} %pad_add_fusion.1.info, ...), custom_call_target="tpu_custom_call", output_to_operand_aliasing={{4}: (4, {}), {5}: (5, {})} | custom-call | tf_op jit(solution)/shard_map/pallas_call | solution.py:285
  129.5 0.3 collective-permute-start.11
  129.8 2.6 %collective-permute-start.12 = (bf16[512,512]{1,0:T(8,128)(2,1)S(1)}, bf16[512,512]{1,0:T(8,128)(2,1)S(1)}, u32[]{:S(2)}, u32[]{:S(2)}) collective-permute-start(bf16[512,512]{1,0:T(8,128)(2,1)S(1)} %get-tuple-element.52), channel_id=1, source_target_pairs={{64,0},{128,64},{192,128},{0,192},{65,1},{129,65},{193,129},{1,193... | collective-permute-start | bytes 1572872 | tf_op jit(solution)/shard_map/ppermute | solution.py:324
  132.5 0.6 pad_add_fusion.info
  133.1 17.0 %shard_map.89 = (bf16[512,512]{1,0:T(8,128)(2,1)}, bf16[512,512]{1,0:T(8,128)(2,1)}, bf16[8,4,32,1536]{3,2,1,0:T(8,128)(2,1)}) custom-call(s32[4]{0:T(128)} %pad_add_fusion.info, bf16[4,8,64,1152]{3,2,1,0:T(8,128)(2,1)} %bitcast.111, bf16[8,4,64,896]{3,2,1,0:T(8,128)(2,1)} %all-to-all-done.2.q_ref, bf16[1024,1536]{1,0:T(8,128)(2,1)} %bitcast.108, ...), custom_call_target="tpu_custom_call" | custom-call | tf_op jit(solution)/shard_map/pallas_call | solution.py:240
  150.2 1.3 add_convert_fusion.1
  151.4 0.1 collective-permute-start.10
  151.5 1.2 add_convert_fusion
  152.7 3.3 %collective-permute-start.13 = (bf16[512,512]{1,0:T(8,128)(2,1)S(1)}, bf16[512,512]{1,0:T(8,128)(2,1)S(1)}, u32[]{:S(2)}, u32[]{:S(2)}) collective-permute-start(bf16[512,512]{1,0:T(8,128)(2,1)S(1)} %add_convert_fusion), channel_id=1, source_target_pairs={{64,0},{128,64},{192,128},{0,192},{65,1},{129,65},{193,129},{1,193... | collective-permute-start | bytes 1572872 | tf_op jit(solution)/shard_map/ppermute | solution.py:324
  156.0 6.3 %collective-permute-done.10.refs_1_ = bf16[512,512]{1,0:T(8,128)(2,1)S(1)} collective-permute-done((bf16[512,512]{1,0:T(8,128)(2,1)S(1)}, bf16[512,512]{1,0:T(8,128)(2,1)S(1)}, u32[]{:S(2)}, u32[]{:S(2)}) %collective-permute-start.10) | collective-permute-done | bytes 524320 | tf_op jit(solution)/shard_map/ppermute | solution.py:324
  162.2 0.7 collective-permute-done.13.refs_5_
  162.9 1.4 shard_map.90
  164.3 4.2 %all-to-all-start.3 = ((bf16[8,64,1024]{2,1,0:T(8,128)(2,1)}), bf16[8,64,1024]{2,1,0:T(8,128)(2,1)S(1)}, u32[]{:S(2)}, u32[]{:S(2)}) async-start(bf16[8,64,1024]{2,1,0:T(8,128)(2,1)} %bitcast.31), calls=%async_computation.3 | async-start | bytes 2097152 | tf_op jit(solution)/shard_map/all_to_all | solution.py:365
  168.6 0.1 convolution_convert_fusion
  168.7 0.1 fusion.173
  168.8 15.7 %all-to-all-done.3 = bf16[8,64,1024]{2,1,0:T(8,128)(2,1)S(1)} async-done(((bf16[8,64,1024]{2,1,0:T(8,128)(2,1)}), bf16[8,64,1024]{2,1,0:T(8,128)(2,1)S(1)}, u32[]{:S(2)}, u32[]{:S(2)}) %all-to-all-start.3) | async-done | bytes 1048608 | tf_op jit(solution)/shard_map/all_to_all | solution.py:365
  184.5 0.4 fusion.175
  184.9 1.9 collective-permute-start.14
  186.9 7.9 %collective-permute-start.15 = (bf16[15,1024]{1,0:T(8,128)(2,1)S(1)}, bf16[15,1024]{1,0:T(8,128)(2,1)S(1)}, u32[]{:S(2)}, u32[]{:S(2)}) collective-permute-start(bf16[15,1024]{1,0:T(8,128)(2,1)S(1)} %get-tuple-element.67), channel_id=1, source_target_pairs={{1,0},{2,1},{3,2},{4,3},{5,4},{6,5},{7,6},{8,7},{9,8},{10,9},{11,1... | collective-permute-start | bytes 92168 | tf_op jit(solution)/shard_map/ppermute | solution.py:116
  194.7 0.2 fusion.36
  195.0 0.6 fusion.170
  195.6 0.6 reduce-scatter.2.cloned.1.call-done
  196.2 0.1 convert_element_type.78
  196.3 7.5 %all-to-all-start.4 = ((bf16[4,32,1536]{2,1,0:T(8,128)(2,1)}), bf16[4,32,1536]{2,1,0:T(8,128)(2,1)S(1)}, u32[]{:S(2)}, u32[]{:S(2)}) async-start(bf16[4,32,1536]{2,1,0:T(8,128)(2,1)} %bitcast.114), calls=%async_computation.5 | async-start | bytes 786432 | tf_op jit(solution)/shard_map/all_to_all | solution.py:97
  203.8 2.6 %fusion.4 = bf16[160,1024]{1,0:T(8,128)(2,1)S(1)} fusion(f32[192,1024]{1,0:T(8,128)S(1)} %convert_element_type.78, f32[192,1024]{1,0:T(8,128)S(1)} %get-tuple-element.59, f32[1024]{0:T(1024)S(1)} %bitcast.149, f32[1024]{0:T(1024)S(1)} %bitcast.146, f32[1024]{0:T(1024)S(1)} %bitcast.143, f32[1024]{0:T(1024)S(1)} %bitcast.140, f32[1024]{0:T(1024)S(1)} %bitcast.137, ...), kind=kLoop, calls=%fused_computation.39 | loop fusion | flops 10321920 | bytes 21426176 | tf_op jit(solution)/shard_map/convert_element_type | solution.py:125
  206.4 3.3 %all-to-all-done.4.parts_ref = bf16[4,32,1536]{2,1,0:T(8,128)(2,1)S(1)} async-done(((bf16[4,32,1536]{2,1,0:T(8,128)(2,1)}), bf16[4,32,1536]{2,1,0:T(8,128)(2,1)S(1)}, u32[]{:S(2)}, u32[]{:S(2)}) %all-to-all-start.4) | async-done | bytes 393248 | tf_op jit(solution)/shard_map/all_to_all | solution.py:97
  209.7 0.7 copy-done.4
  210.4 1.8 shard_map.91
  212.2 0.3 fusion.168
  212.5 0.3 fusion.110
  212.9 0.8 pad_maximum_fusion
  (58 shorter events, 0.6 us)
Async XLA Ops:
  7.2 43.1 %all-gather.7.cloned.1.call-start = ((), (), s32[]{:S(2)}) async-start(), calls=%async_computation.8 | async-start | bytes 1792000 | tf_op jit(solution)/shard_map/all_gather | solution.py:353
  10.4 25.9 %copy-start.6 = (bf16[1,32,6144]{2,1,0:T(8,128)(2,1)S(1)}, bf16[1,32,6144]{2,1,0:T(8,128)(2,1)}, u32[]{:S(2)}) copy-start(bf16[1,32,6144]{2,1,0:T(8,128)(2,1)} %param.11) | copy-start | bytes 1179652
  10.4 98.3 %all-gather.5.cloned.1.call-start = ((), (), s32[]{:S(2)}) async-start(), calls=%async_computation.7 | async-start | bytes 5898240 | tf_op jit(solution)/shard_map/all_gather | solution.py:359
  38.1 12.1 %all-to-all-start.1 = ((bf16[4,32,1536]{2,1,0:T(8,128)(2,1)}), bf16[4,32,1536]{2,1,0:T(8,128)(2,1)S(1)}, u32[]{:S(2)}, u32[]{:S(2)}) async-start(bf16[4,32,1536]{2,1,0:T(8,128)(2,1)} %reshape.26), calls=%async_computation.1 | async-start | bytes 786432 | tf_op jit(solution)/shard_map/all_to_all | solution.py:41
  50.2 1.4 copy-start
  56.1 52.5 %all-to-all-start.2 = ((bf16[8,4,64,896]{3,2,1,0:T(8,128)(2,1)}), bf16[8,4,64,896]{3,2,1,0:T(8,128)(2,1)}, u32[]{:S(2)}, u32[]{:S(2)}) async-start(bf16[8,4,64,896]{3,2,1,0:T(8,128)(2,1)} %shard_map.86), calls=%async_computation.2 | async-start | bytes 7340032 | tf_op jit(solution)/shard_map/all_to_all | solution.py:362
  60.7 135.5 %reduce-scatter.2.cloned.1.call-start = ((), (), s32[]{:S(2)}) async-start(), calls=%async_computation.6 | async-start | bytes 3538944 | tf_op jit(solution)/shard_map/reduce_scatter | solution.py:96
  60.7 14.6 %collective-permute-start = (bf16[4,32,1536]{2,1,0:T(8,128)(2,1)S(1)}, bf16[4,32,1536]{2,1,0:T(8,128)(2,1)S(1)}, u32[]{:S(2)}, u32[]{:S(2)}) collective-permute-start(bf16[4,32,1536]{2,1,0:T(8,128)(2,1)S(1)} %all-to-all-done.1), channel_id=1, source_target_pairs={{0,8},{8,16},{16,24},{24,32},{32,40},{40,48},{48,56},{56,0},{1,9},... | collective-permute-start | bytes 1179656 | tf_op jit(solution)/shard_map/ppermute | solution.py:33
  61.9 13.5 %collective-permute-start.1 = (bf16[4,32,1536]{2,1,0:T(8,128)(2,1)S(1)}, bf16[4,32,1536]{2,1,0:T(8,128)(2,1)S(1)}, u32[]{:S(2)}, u32[]{:S(2)}) collective-permute-start(bf16[4,32,1536]{2,1,0:T(8,128)(2,1)S(1)} %all-to-all-done.1), channel_id=1, source_target_pairs={{8,0},{16,8},{24,16},{32,24},{40,32},{48,40},{56,48},{0,56},{9,1},... | collective-permute-start | bytes 1179656 | tf_op jit(solution)/shard_map/ppermute | solution.py:33
  75.3 12.0 %collective-permute-start.2 = (bf16[4,32,1536]{2,1,0:T(8,128)(2,1)S(1)}, bf16[4,32,1536]{2,1,0:T(8,128)(2,1)S(1)}, u32[]{:S(2)}, u32[]{:S(2)}) collective-permute-start(bf16[4,32,1536]{2,1,0:T(8,128)(2,1)S(1)} %collective-permute-done), channel_id=1, source_target_pairs={{0,8},{8,16},{16,24},{24,32},{32,40},{40,48},{48,56},{56,0},{1,9},... | collective-permute-start | bytes 1179656 | tf_op jit(solution)/shard_map/ppermute | solution.py:33
  75.4 12.0 %collective-permute-start.3 = (bf16[4,32,1536]{2,1,0:T(8,128)(2,1)S(1)}, bf16[4,32,1536]{2,1,0:T(8,128)(2,1)S(1)}, u32[]{:S(2)}, u32[]{:S(2)}) collective-permute-start(bf16[4,32,1536]{2,1,0:T(8,128)(2,1)S(1)} %collective-permute-done.1), channel_id=1, source_target_pairs={{8,0},{16,8},{24,16},{32,24},{40,32},{48,40},{56,48},{0,56},{9,1},... | collective-permute-start | bytes 1179656 | tf_op jit(solution)/shard_map/ppermute | solution.py:33
  87.3 14.3 %collective-permute-start.4 = (bf16[4,32,1536]{2,1,0:T(8,128)(2,1)S(1)}, bf16[4,32,1536]{2,1,0:T(8,128)(2,1)S(1)}, u32[]{:S(2)}, u32[]{:S(2)}) collective-permute-start(bf16[4,32,1536]{2,1,0:T(8,128)(2,1)S(1)} %collective-permute-done.2), channel_id=1, source_target_pairs={{0,8},{8,16},{16,24},{24,32},{32,40},{40,48},{48,56},{56,0},{1,9},... | collective-permute-start | bytes 1179656 | tf_op jit(solution)/shard_map/ppermute | solution.py:33
  87.3 10.5 %collective-permute-start.5 = (bf16[4,32,1536]{2,1,0:T(8,128)(2,1)S(1)}, bf16[4,32,1536]{2,1,0:T(8,128)(2,1)S(1)}, u32[]{:S(2)}, u32[]{:S(2)}) collective-permute-start(bf16[4,32,1536]{2,1,0:T(8,128)(2,1)S(1)} %collective-permute-done.3), channel_id=1, source_target_pairs={{8,0},{16,8},{24,16},{32,24},{40,32},{48,40},{56,48},{0,56},{9,1},... | collective-permute-start | bytes 1179656 | tf_op jit(solution)/shard_map/ppermute | solution.py:33
  97.8 7.0 %collective-permute-start.7 = (bf16[2,32,1536]{2,1,0:T(8,128)(2,1)S(1)}, bf16[2,32,1536]{2,1,0:T(8,128)(2,1)S(1)}, u32[]{:S(2)}, u32[]{:S(2)}) collective-permute-start(bf16[2,32,1536]{2,1,0:T(8,128)(2,1)S(1)} %slice.681), channel_id=1, source_target_pairs={{8,0},{16,8},{24,16},{32,24},{40,32},{48,40},{56,48},{0,56},{9,1},... | collective-permute-start | bytes 589832 | tf_op jit(solution)/shard_map/ppermute | solution.py:59
  101.6 7.0 %collective-permute-start.6 = (bf16[2,32,1536]{2,1,0:T(8,128)(2,1)S(1)}, bf16[2,32,1536]{2,1,0:T(8,128)(2,1)S(1)}, u32[]{:S(2)}, u32[]{:S(2)}) collective-permute-start(bf16[2,32,1536]{2,1,0:T(8,128)(2,1)S(1)} %slice.680), channel_id=1, source_target_pairs={{0,8},{8,16},{16,24},{24,32},{32,40},{40,48},{48,56},{56,0},{1,9},... | collective-permute-start | bytes 589832 | tf_op jit(solution)/shard_map/ppermute | solution.py:59
  108.6 1.6 copy-start.3
  116.8 16.3 %collective-permute-start.8 = (bf16[512,512]{1,0:T(8,128)(2,1)}, bf16[512,512]{1,0:T(8,128)(2,1)}, u32[]{:S(2)}, u32[]{:S(2)}) collective-permute-start(bf16[512,512]{1,0:T(8,128)(2,1)} %get-tuple-element.39), channel_id=1, source_target_pairs={{0,64},{64,128},{128,192},{192,0},{1,65},{65,129},{129,193},{193,1... | collective-permute-start | bytes 1572872 | tf_op jit(solution)/shard_map/ppermute | solution.py:324
  116.8 16.3 %collective-permute-start.9 = (bf16[512,512]{1,0:T(8,128)(2,1)S(1)}, bf16[512,512]{1,0:T(8,128)(2,1)}, u32[]{:S(2)}, u32[]{:S(2)}) collective-permute-start(bf16[512,512]{1,0:T(8,128)(2,1)S(1)} %get-tuple-element.40), channel_id=1, source_target_pairs={{64,0},{128,64},{192,128},{0,192},{65,1},{129,65},{193,129},{1,193... | collective-permute-start | bytes 1572872 | tf_op jit(solution)/shard_map/ppermute | solution.py:324
  129.5 20.6 %collective-permute-start.11 = (bf16[512,512]{1,0:T(8,128)(2,1)S(1)}, bf16[512,512]{1,0:T(8,128)(2,1)S(1)}, u32[]{:S(2)}, u32[]{:S(2)}) collective-permute-start(bf16[512,512]{1,0:T(8,128)(2,1)S(1)} %get-tuple-element.51), channel_id=1, source_target_pairs={{0,64},{64,128},{128,192},{192,0},{1,65},{65,129},{129,193},{193,1... | collective-permute-start | bytes 1572872 | tf_op jit(solution)/shard_map/ppermute | solution.py:324
  129.8 20.3 %collective-permute-start.12 = (bf16[512,512]{1,0:T(8,128)(2,1)S(1)}, bf16[512,512]{1,0:T(8,128)(2,1)S(1)}, u32[]{:S(2)}, u32[]{:S(2)}) collective-permute-start(bf16[512,512]{1,0:T(8,128)(2,1)S(1)} %get-tuple-element.52), channel_id=1, source_target_pairs={{64,0},{128,64},{192,128},{0,192},{65,1},{129,65},{193,129},{1,193... | collective-permute-start | bytes 1572872 | tf_op jit(solution)/shard_map/ppermute | solution.py:324
  150.1 1.4 copy-start.5
  150.1 12.8 %copy-start.1 = (bf16[512,512]{1,0:T(8,128)(2,1)S(1)}, bf16[512,512]{1,0:T(8,128)(2,1)}, u32[]{:S(2)}) copy-start(bf16[512,512]{1,0:T(8,128)(2,1)} %get-tuple-element.47.refs_0_) | copy-start | bytes 1572868
  150.1 12.8 %copy-start.2 = (bf16[512,512]{1,0:T(8,128)(2,1)S(1)}, bf16[512,512]{1,0:T(8,128)(2,1)}, u32[]{:S(2)}) copy-start(bf16[512,512]{1,0:T(8,128)(2,1)} %get-tuple-element.54.refs_3_) | copy-start | bytes 1572868
  151.4 10.8 %collective-permute-start.10 = (bf16[512,512]{1,0:T(8,128)(2,1)S(1)}, bf16[512,512]{1,0:T(8,128)(2,1)S(1)}, u32[]{:S(2)}, u32[]{:S(2)}) collective-permute-start(bf16[512,512]{1,0:T(8,128)(2,1)S(1)} %add_convert_fusion.1), channel_id=1, source_target_pairs={{0,64},{64,128},{128,192},{192,0},{1,65},{65,129},{129,193},{193,1... | collective-permute-start | bytes 1572872 | tf_op jit(solution)/shard_map/ppermute | solution.py:324
  152.7 10.2 %collective-permute-start.13 = (bf16[512,512]{1,0:T(8,128)(2,1)S(1)}, bf16[512,512]{1,0:T(8,128)(2,1)S(1)}, u32[]{:S(2)}, u32[]{:S(2)}) collective-permute-start(bf16[512,512]{1,0:T(8,128)(2,1)S(1)} %add_convert_fusion), channel_id=1, source_target_pairs={{64,0},{128,64},{192,128},{0,192},{65,1},{129,65},{193,129},{1,193... | collective-permute-start | bytes 1572872 | tf_op jit(solution)/shard_map/ppermute | solution.py:324
  162.9 5.6 %copy-start.9 = (s32[192,2]{0,1:T(2,128)S(1)}, s32[192,2]{0,1:T(2,128)}, u32[]{:S(2)}) copy-start(s32[192,2]{0,1:T(2,128)} %param.9) | copy-start | bytes 4612
  162.9 5.8 %copy-start.8 = (bf16[31,1024]{1,0:T(8,128)(2,1)S(1)}, bf16[31,1024]{1,0:T(8,128)(2,1)}, u32[]{:S(2)}) copy-start(bf16[31,1024]{1,0:T(8,128)(2,1)} %param.10) | copy-start | bytes 190468
  162.9 21.6 %copy-start.7 = (bf16[192,1024]{1,0:T(8,128)(2,1)S(1)}, bf16[192,1024]{1,0:T(8,128)(2,1)}, u32[]{:S(2)}) copy-start(bf16[192,1024]{1,0:T(8,128)(2,1)} %param.7) | copy-start | bytes 1179652
  164.3 30.7 %copy-start.10 = (bf16[192,2]{0,1:T(2,128)(2,1)S(1)}, bf16[192,2]{0,1:T(2,128)(2,1)}, u32[]{:S(2)}) copy-start(bf16[192,2]{0,1:T(2,128)(2,1)} %param.8) | copy-start | bytes 2308
  164.3 20.2 %all-to-all-start.3 = ((bf16[8,64,1024]{2,1,0:T(8,128)(2,1)}), bf16[8,64,1024]{2,1,0:T(8,128)(2,1)S(1)}, u32[]{:S(2)}, u32[]{:S(2)}) async-start(bf16[8,64,1024]{2,1,0:T(8,128)(2,1)} %bitcast.31), calls=%async_computation.3 | async-start | bytes 2097152 | tf_op jit(solution)/shard_map/all_to_all | solution.py:365
  184.9 27.3 %collective-permute-start.14 = (bf16[15,1024]{1,0:T(8,128)(2,1)S(1)}, bf16[15,1024]{1,0:T(8,128)(2,1)S(1)}, u32[]{:S(2)}, u32[]{:S(2)}) collective-permute-start(bf16[15,1024]{1,0:T(8,128)(2,1)S(1)} %get-tuple-element.68), channel_id=1, source_target_pairs={{0,1},{1,2},{2,3},{3,4},{4,5},{5,6},{6,7},{7,8},{8,9},{9,10},{10,1... | collective-permute-start | bytes 92168 | tf_op jit(solution)/shard_map/ppermute | solution.py:115
  186.9 25.3 %collective-permute-start.15 = (bf16[15,1024]{1,0:T(8,128)(2,1)S(1)}, bf16[15,1024]{1,0:T(8,128)(2,1)S(1)}, u32[]{:S(2)}, u32[]{:S(2)}) collective-permute-start(bf16[15,1024]{1,0:T(8,128)(2,1)S(1)} %get-tuple-element.67), channel_id=1, source_target_pairs={{1,0},{2,1},{3,2},{4,3},{5,4},{6,5},{7,6},{8,7},{9,8},{10,9},{11,1... | collective-permute-start | bytes 92168 | tf_op jit(solution)/shard_map/ppermute | solution.py:116
  196.3 13.4 %all-to-all-start.4 = ((bf16[4,32,1536]{2,1,0:T(8,128)(2,1)}), bf16[4,32,1536]{2,1,0:T(8,128)(2,1)S(1)}, u32[]{:S(2)}, u32[]{:S(2)}) async-start(bf16[4,32,1536]{2,1,0:T(8,128)(2,1)} %bitcast.114), calls=%async_computation.5 | async-start | bytes 786432 | tf_op jit(solution)/shard_map/all_to_all | solution.py:97
  209.7 0.7 copy-start.4
Sparse Core Ops, SparseCore 0:
  10.5 30.0 all-gather.6
  42.4 55.9 all-gather.4
  150.3 45.8 reduce-scatter.1

commit v11 on v10

--- a/solution.py
+++ b/solution.py
@@ -49,15 +49,21 @@
     def place(buffer, shard, z):
         return lax.dynamic_update_slice(buffer, shard[:, None], (0, z % nz, 0, 0))
 
-    buffer = place(jnp.zeros((ny, nz, rows, width), BF), mine, me)
+    up, down = ring_ways("z")
     mine, after = lax.optimization_barrier((mine, after))
-    right = left = mine
+    halves = [[mine[: ny // 2]] * 2, [mine[ny // 2 :]] * 2]
+    held = {0: mine}
     for step in range(1, nz // 2):
-        right, left = ring_step(right, left, "z")
-        buffer = place(place(buffer, right, me - step), left, me + step)
-    up, down = ring_ways("z")
-    across = [lax.ppermute(right[: ny // 2], "z", up), lax.ppermute(left[ny // 2 :], "z", down)]
-    buffer = place(buffer, jnp.concatenate(across, axis=0), me + nz // 2)
+        halves = [list(ring_step(right, left, "z")) for right, left in halves]
+        for way, sign in enumerate((-1, 1)):
+            held[sign * step] = jnp.concatenate([half[way] for half in halves], axis=0)
+    across = [
+        lax.ppermute(half[way][way : way + 1], "z", (up, down)[way]) for half in halves for way in range(2)
+    ]
+    held[nz // 2] = jnp.concatenate(across, axis=0)
+    buffer = jnp.zeros((ny, nz, rows, width), BF)
+    for offset, shard in held.items():
+        buffer = place(buffer, shard, me + offset)
     return buffer.reshape(ny * nz * rows, width)
 
 

time: 221 us -> 218 us (0.986)
  waiting for transfers between devices: 65 us -> 44.7 us
  blocking collectives: 21.9 us -> 33 us
  starting transfers between devices: 55.4 us -> 61.8 us
    ppermute x6 -> x12, waiting for transfers between devices: 24.9 us -> 12.2 us  [ring_step(): return (lax.ppermute(right, axis, up), lax.ppermute(left, axis, down))]
    all_to_all x0 -> x1, blocking collectives: none -> 11.1 us  [own_columns(): lax.all_to_all(sliced.reshape(ny, rows, 3 * part), 'y', 0, 0, tiled=True)]
    ppermute x6 -> x12, starting transfers between devices: 11.6 us -> 20.1 us  [ring_step(): return (lax.ppermute(right, axis, up), lax.ppermute(left, axis, down))]
    all_to_all x1 -> x0, waiting for transfers between devices: 6.71 us -> none  [own_columns(): lax.all_to_all(sliced.reshape(ny, rows, 3 * part), 'y', 0, 0, tiled=True)]
    all_to_all x1 -> x0, starting transfers between devices: 5.43 us -> none  [own_columns(): lax.all_to_all(sliced.reshape(ny, rows, 3 * part), 'y', 0, 0, tiled=True)]
    ppermute x2 -> x4, starting transfers between devices: 3.85 us -> 7.26 us  [gather_weights(): lax.ppermute(half[way][way:way + 1], 'z', (up, down)[way])]
    ppermute x2 -> x4, waiting for transfers between devices: 6.78 us -> 5.72 us  [gather_weights(): lax.ppermute(half[way][way:way + 1], 'z', (up, down)[way])]
  transfers between devices with their start and end apart: 23 -> 30, of which waited for: 11 -> 12; matrix products, arithmetic and copies ran while one was open for 5% -> 5% of each run, Pallas kernels for 17% -> 17%
where the time goes in v11:
time: 218 us; the launch traced here: 217 us
  starting transfers between devices  61.8 us (28%)
  waiting for transfers between devices  44.7 us (21%)
  Pallas kernels  43.9 us (20%)
  blocking collectives  33 us (15%)
  between operations  14.3 us (7%)
  other arithmetic  11.3 us (5%)
  local copies, waits for them, and re-layouts  7.15 us (3%)
    all_to_all x1, blocking collectives, local(): mine_in = lax.all_to_all(sent_in, by_expert, 0, 0, tiled=True)  21.9 us
    ppermute x12, starting transfers between devices, ring_step(): return (lax.ppermute(right, axis, up), lax.ppermute(left, axis, down))  20.1 us
    pallas_call x2, Pallas kernels, expert_rows(): pl.pallas_call(functools.partial(rows_kernel, count, steps), grid_spec=pl...  17.2 us
    pallas_call x1, Pallas kernels, last_rows(): pl.pallas_call(last_kernel, grid_spec=pltpu.PrefetchScalarGridSpec(num_sc...  17 us
    all_to_all x1, waiting for transfers between devices, local(): lax.all_to_all(row_sums.reshape(experts, SLOTS, width), by_expert, 0, 0,...  15.7 us
    ppermute x12, waiting for transfers between devices, ring_step(): return (lax.ppermute(right, axis, up), lax.ppermute(left, axis, down))  12.2 us
    all_to_all x1, blocking collectives, own_columns(): lax.all_to_all(sliced.reshape(ny, rows, 3 * part), 'y', 0, 0, tiled=True)  11.1 us
    ppermute x1, starting transfers between devices, halo_of(): return (low, lax.ppermute(block[:width], axes, backward))  8.28 us
  transfers between devices with their start and end apart: 30, of which 12 were waited for; matrix products, arithmetic and copies ran while one was open for 5% of the time, Pallas kernels for 17%

profile of v11, /device:TPU:8, one launch (start us, length us, event | category | flops | bytes accessed | tf_op | source)
XLA Modules:
  0.0 216.9 jit_solution(11486496978447576529)
XLA Ops:
  7.2 0.7 convert_bitcast_fusion
  7.9 1.0 slice.555
  8.9 0.7 pad_maximum_fusion.3
  9.6 0.8 fusion.48
  10.5 0.8 slice.554
  11.3 1.0 fusion.40.x_ref
  12.3 2.1 shard_map.85
  14.4 21.9 %all_to_all.25 = bf16[8,1,64,1152]{3,2,1,0:T(8,128)(2,1)} all-to-all(bf16[8,1,64,1152]{3,2,1,0:T(8,128)(2,1)} %shard_map.85), channel_id=1, replica_groups=mesh['y'=4,'z'=8,'x'=4,'c'=2] {'x','c'}, dimensions={0} | all-to-all | bytes 2359296 | tf_op jit(solution)/shard_map/all_to_all | solution.py:361
  36.4 0.3 reshape_squeeze.3
  36.6 0.2 copy.50
  36.9 0.5 reshape.26
  37.4 11.1 %all_to_all.26 = bf16[4,32,1536]{2,1,0:T(8,128)(2,1)S(1)} all-to-all(bf16[4,32,1536]{2,1,0:T(8,128)(2,1)S(1)} %reshape.26), channel_id=1, replica_groups=mesh['y'=4,'z'=8,'x'=4,'c'=2] {'y'}, dimensions={0} | all-to-all | bytes 786432 | tf_op jit(solution)/shard_map/all_to_all | solution.py:41
  48.5 1.4 copy-done
  49.9 4.5 %shard_map.86 = bf16[8,4,64,896]{3,2,1,0:T(8,128)(2,1)} custom-call(bf16[4,200,896]{2,1,0:T(8,128)(2,1)S(1)} %bitcast.117), custom_call_target="tpu_custom_call" | custom-call | tf_op jit(solution)/shard_map/pallas_call | solution.py:157
  54.4 4.6 %all-to-all-start.2 = ((bf16[8,4,64,896]{3,2,1,0:T(8,128)(2,1)}), bf16[8,4,64,896]{3,2,1,0:T(8,128)(2,1)}, u32[]{:S(2)}, u32[]{:S(2)}) async-start(bf16[8,4,64,896]{3,2,1,0:T(8,128)(2,1)} %shard_map.86), calls=%async_computation.2 | async-start | bytes 7340032 | tf_op jit(solution)/shard_map/all_to_all | solution.py:368
  59.2 2.0 collective-permute-start.1
  61.2 4.0 %collective-permute-start.3 = (bf16[2,32,1536]{2,1,0:T(8,128)(2,1)S(1)}, bf16[2,32,1536]{2,1,0:T(8,128)(2,1)S(1)}, u32[]{:S(2)}, u32[]{:S(2)}) collective-permute-start(bf16[2,32,1536]{2,1,0:T(8,128)(2,1)S(1)} %get-tuple-element.70), channel_id=1, source_target_pairs={{8,0},{16,8},{24,16},{32,24},{40,32},{48,40},{56,48},{0,56},{9,1},... | collective-permute-start | bytes 589832 | tf_op jit(solution)/shard_map/ppermute | solution.py:33
  65.2 3.2 %collective-permute-start.2 = (bf16[2,32,1536]{2,1,0:T(8,128)(2,1)S(1)}, bf16[2,32,1536]{2,1,0:T(8,128)(2,1)S(1)}, u32[]{:S(2)}, u32[]{:S(2)}) collective-permute-start(bf16[2,32,1536]{2,1,0:T(8,128)(2,1)S(1)} %get-tuple-element.69), channel_id=1, source_target_pairs={{8,0},{16,8},{24,16},{32,24},{40,32},{48,40},{56,48},{0,56},{9,1},... | collective-permute-start | bytes 589832 | tf_op jit(solution)/shard_map/ppermute | solution.py:33
  68.4 0.3 broadcast_in_dim.40
  68.8 2.0 collective-permute-done.1
  70.8 4.2 %collective-permute-done = bf16[2,32,1536]{2,1,0:T(8,128)(2,1)S(1)} collective-permute-done((bf16[2,32,1536]{2,1,0:T(8,128)(2,1)S(1)}, bf16[2,32,1536]{2,1,0:T(8,128)(2,1)S(1)}, u32[]{:S(2)}, u32[]{:S(2)}) %collective-permute-start) | collective-permute-done | bytes 196640 | tf_op jit(solution)/shard_map/ppermute | solution.py:33
  75.0 3.2 %collective-permute-start.7 = (bf16[2,32,1536]{2,1,0:T(8,128)(2,1)S(1)}, bf16[2,32,1536]{2,1,0:T(8,128)(2,1)S(1)}, u32[]{:S(2)}, u32[]{:S(2)}) collective-permute-start(bf16[2,32,1536]{2,1,0:T(8,128)(2,1)S(1)} %collective-permute-done.3), channel_id=1, source_target_pairs={{8,0},{16,8},{24,16},{32,24},{40,32},{48,40},{56,48},{0,56},{9,1},... | collective-permute-start | bytes 589832 | tf_op jit(solution)/shard_map/ppermute | solution.py:33
  78.2 0.9 collective-permute-start.6
  79.2 0.3 collective-permute-done.5
  79.4 1.0 collective-permute-start.9
  80.4 3.6 %collective-permute-done.4 = bf16[2,32,1536]{2,1,0:T(8,128)(2,1)S(1)} collective-permute-done((bf16[2,32,1536]{2,1,0:T(8,128)(2,1)S(1)}, bf16[2,32,1536]{2,1,0:T(8,128)(2,1)S(1)}, u32[]{:S(2)}, u32[]{:S(2)}) %collective-permute-start.4) | collective-permute-done | bytes 196640 | tf_op jit(solution)/shard_map/ppermute | solution.py:33
  84.0 3.2 %collective-permute-start.11 = (bf16[2,32,1536]{2,1,0:T(8,128)(2,1)S(1)}, bf16[2,32,1536]{2,1,0:T(8,128)(2,1)S(1)}, u32[]{:S(2)}, u32[]{:S(2)}) collective-permute-start(bf16[2,32,1536]{2,1,0:T(8,128)(2,1)S(1)} %collective-permute-done.7), channel_id=1, source_target_pairs={{8,0},{16,8},{24,16},{32,24},{40,32},{48,40},{56,48},{0,56},{9,1},... | collective-permute-start | bytes 589832 | tf_op jit(solution)/shard_map/ppermute | solution.py:33
  87.3 2.6 %collective-permute-start.10 = (bf16[2,32,1536]{2,1,0:T(8,128)(2,1)S(1)}, bf16[2,32,1536]{2,1,0:T(8,128)(2,1)S(1)}, u32[]{:S(2)}, u32[]{:S(2)}) collective-permute-start(bf16[2,32,1536]{2,1,0:T(8,128)(2,1)S(1)} %collective-permute-done.6), channel_id=1, source_target_pairs={{8,0},{16,8},{24,16},{32,24},{40,32},{48,40},{56,48},{0,56},{9,1},... | collective-permute-start | bytes 589832 | tf_op jit(solution)/shard_map/ppermute | solution.py:33
  89.9 2.1 collective-permute-done.11
  92.0 3.8 %collective-permute-start.15 = (bf16[1,32,1536]{2,1,0:T(8,128)(2,1)S(1)}, bf16[1,32,1536]{2,1,0:T(8,128)(2,1)S(1)}, u32[]{:S(2)}, u32[]{:S(2)}) collective-permute-start(bf16[1,32,1536]{2,1,0:T(8,128)(2,1)S(1)} %slice.699), channel_id=1, source_target_pairs={{8,0},{16,8},{24,16},{32,24},{40,32},{48,40},{56,48},{0,56},{9,1},... | collective-permute-start | bytes 294920 | tf_op jit(solution)/shard_map/ppermute | solution.py:61
  96.0 3.3 %collective-permute-start.13 = (bf16[1,32,1536]{2,1,0:T(8,128)(2,1)S(1)}, bf16[1,32,1536]{2,1,0:T(8,128)(2,1)S(1)}, u32[]{:S(2)}, u32[]{:S(2)}) collective-permute-start(bf16[1,32,1536]{2,1,0:T(8,128)(2,1)S(1)} %slice.697), channel_id=1, source_target_pairs={{8,0},{16,8},{24,16},{32,24},{40,32},{48,40},{56,48},{0,56},{9,1},... | collective-permute-start | bytes 294920 | tf_op jit(solution)/shard_map/ppermute | solution.py:61
  99.4 2.3 %collective-permute-done.14 = bf16[1,32,1536]{2,1,0:T(8,128)(2,1)S(1)} collective-permute-done((bf16[1,32,1536]{2,1,0:T(8,128)(2,1)S(1)}, bf16[1,32,1536]{2,1,0:T(8,128)(2,1)S(1)}, u32[]{:S(2)}, u32[]{:S(2)}) %collective-permute-start.14) | collective-permute-done | bytes 98336 | tf_op jit(solution)/shard_map/ppermute | solution.py:61
  101.7 3.4 %collective-permute-done.12 = bf16[1,32,1536]{2,1,0:T(8,128)(2,1)S(1)} collective-permute-done((bf16[1,32,1536]{2,1,0:T(8,128)(2,1)S(1)}, bf16[1,32,1536]{2,1,0:T(8,128)(2,1)S(1)}, u32[]{:S(2)}, u32[]{:S(2)}) %collective-permute-start.12) | collective-permute-done | bytes 98336 | tf_op jit(solution)/shard_map/ppermute | solution.py:61
  105.2 1.6 copy-done.3
  106.8 6.5 %shard_map.87 = (bf16[512,512]{1,0:T(8,128)(2,1)}, bf16[512,512]{1,0:T(8,128)(2,1)S(1)}, bf16[2048,1024]{1,0:T(8,128)(2,1)}, bf16[8,4,64,512]{3,2,1,0:T(8,128)(2,1)}) custom-call(s32[1]{0:T(128)} %bitcast.5.info, bf16[4,8,64,1152]{3,2,1,0:T(8,128)(2,1)} %bitcast.121, bf16[8,4,64,896]{3,2,1,0:T(8,128)(2,1)} %all-to-all-done.2.q_ref, bf16[1024,1536]{1,0:T(8,128)(2,1)} %bitcast.118), custom_call_target="tpu_custom_call" | custom-call | tf_op jit(solution)/shard_map/pallas_call | solution.py:291
  113.4 0.2 collective-permute-start.16
  113.5 1.9 collective-permute-start.17
  115.5 10.6 %shard_map.88 = (bf16[512,512]{1,0:T(8,128)(2,1)S(1)}, bf16[512,512]{1,0:T(8,128)(2,1)S(1)}, bf16[512,512]{1,0:T(8,128)(2,1)S(1)}, bf16[512,512]{1,0:T(8,128)(2,...) custom-call(s32[2]{0:T(128)S(1)} %pad_add_fusion.1.info, ...), custom_call_target="tpu_custom_call", output_to_operand_aliasing={{4}: (4, {}), {5}: (5, {})} | custom-call | tf_op jit(solution)/shard_map/pallas_call | solution.py:291
  126.2 2.9 %collective-permute-start.20 = (bf16[512,512]{1,0:T(8,128)(2,1)S(1)}, bf16[512,512]{1,0:T(8,128)(2,1)S(1)}, u32[]{:S(2)}, u32[]{:S(2)}) collective-permute-start(bf16[512,512]{1,0:T(8,128)(2,1)S(1)} %get-tuple-element.52), channel_id=1, source_target_pairs={{64,0},{128,64},{192,128},{0,192},{65,1},{129,65},{193,129},{1,193... | collective-permute-start | bytes 1572872 | tf_op jit(solution)/shard_map/ppermute | solution.py:330
  129.1 0.7 pad_add_fusion.info
  129.8 17.0 %shard_map.89 = (bf16[512,512]{1,0:T(8,128)(2,1)}, bf16[512,512]{1,0:T(8,128)(2,1)}, bf16[8,4,32,1536]{3,2,1,0:T(8,128)(2,1)}) custom-call(s32[4]{0:T(128)} %pad_add_fusion.info, bf16[4,8,64,1152]{3,2,1,0:T(8,128)(2,1)} %bitcast.123, bf16[8,4,64,896]{3,2,1,0:T(8,128)(2,1)} %all-to-all-done.2.q_ref, bf16[1024,1536]{1,0:T(8,128)(2,1)} %bitcast.120, ...), custom_call_target="tpu_custom_call" | custom-call | tf_op jit(solution)/shard_map/pallas_call | solution.py:246
  146.9 1.3 add_convert_fusion.1
  148.3 1.2 add_convert_fusion
  149.4 3.0 %collective-permute-start.21 = (bf16[512,512]{1,0:T(8,128)(2,1)S(1)}, bf16[512,512]{1,0:T(8,128)(2,1)S(1)}, u32[]{:S(2)}, u32[]{:S(2)}) collective-permute-start(bf16[512,512]{1,0:T(8,128)(2,1)S(1)} %add_convert_fusion), channel_id=1, source_target_pairs={{64,0},{128,64},{192,128},{0,192},{65,1},{129,65},{193,129},{1,193... | collective-permute-start | bytes 1572872 | tf_op jit(solution)/shard_map/ppermute | solution.py:330
  152.5 5.9 %collective-permute-done.18.refs_1_ = bf16[512,512]{1,0:T(8,128)(2,1)S(1)} collective-permute-done((bf16[512,512]{1,0:T(8,128)(2,1)S(1)}, bf16[512,512]{1,0:T(8,128)(2,1)S(1)}, u32[]{:S(2)}, u32[]{:S(2)}) %collective-permute-start.18) | collective-permute-done | bytes 524320 | tf_op jit(solution)/shard_map/ppermute | solution.py:330
  158.4 0.8 collective-permute-done.21.refs_5_
  159.2 1.4 shard_map.90
  160.6 4.6 %all-to-all-start.3 = ((bf16[8,64,1024]{2,1,0:T(8,128)(2,1)}), bf16[8,64,1024]{2,1,0:T(8,128)(2,1)S(1)}, u32[]{:S(2)}, u32[]{:S(2)}) async-start(bf16[8,64,1024]{2,1,0:T(8,128)(2,1)} %bitcast.31), calls=%async_computation.3 | async-start | bytes 2097152 | tf_op jit(solution)/shard_map/all_to_all | solution.py:371
  165.2 0.1 convolution_convert_fusion
  165.4 15.7 %all-to-all-done.3 = bf16[8,64,1024]{2,1,0:T(8,128)(2,1)S(1)} async-done(((bf16[8,64,1024]{2,1,0:T(8,128)(2,1)}), bf16[8,64,1024]{2,1,0:T(8,128)(2,1)S(1)}, u32[]{:S(2)}, u32[]{:S(2)}) %all-to-all-start.3) | async-done | bytes 1048608 | tf_op jit(solution)/shard_map/all_to_all | solution.py:371
  181.1 0.4 fusion.182
  181.6 1.9 collective-permute-start.22
  183.5 8.3 %collective-permute-start.23 = (bf16[15,1024]{1,0:T(8,128)(2,1)S(1)}, bf16[15,1024]{1,0:T(8,128)(2,1)S(1)}, u32[]{:S(2)}, u32[]{:S(2)}) collective-permute-start(bf16[15,1024]{1,0:T(8,128)(2,1)S(1)} %get-tuple-element.67), channel_id=1, source_target_pairs={{1,0},{2,1},{3,2},{4,3},{5,4},{6,5},{7,6},{8,7},{9,8},{10,9},{11,1... | collective-permute-start | bytes 92168 | tf_op jit(solution)/shard_map/ppermute | solution.py:122
  191.8 0.2 fusion.36
  192.0 0.6 fusion.176
  192.6 1.0 reduce-scatter.2.cloned.1.call-done
  193.7 6.7 %all-to-all-start.4 = ((bf16[4,32,1536]{2,1,0:T(8,128)(2,1)}), bf16[4,32,1536]{2,1,0:T(8,128)(2,1)S(1)}, u32[]{:S(2)}, u32[]{:S(2)}) async-start(bf16[4,32,1536]{2,1,0:T(8,128)(2,1)} %bitcast.126), calls=%async_computation.5 | async-start | bytes 786432 | tf_op jit(solution)/shard_map/all_to_all | solution.py:103
  200.5 2.6 %fusion.4 = bf16[160,1024]{1,0:T(8,128)(2,1)S(1)} fusion(f32[192,1024]{1,0:T(8,128)S(1)} %convert_element_type.78, f32[192,1024]{1,0:T(8,128)S(1)} %get-tuple-element.59, f32[1024]{0:T(1024)S(1)} %bitcast.161, f32[1024]{0:T(1024)S(1)} %bitcast.158, f32[1024]{0:T(1024)S(1)} %bitcast.155, f32[1024]{0:T(1024)S(1)} %bitcast.152, f32[1024]{0:T(1024)S(1)} %bitcast.149, ...), kind=kLoop, calls=%fused_computation.39 | loop fusion | flops 10321920 | bytes 21426176 | tf_op jit(solution)/shard_map/convert_element_type | solution.py:131
  203.1 3.3 %all-to-all-done.4.parts_ref = bf16[4,32,1536]{2,1,0:T(8,128)(2,1)S(1)} async-done(((bf16[4,32,1536]{2,1,0:T(8,128)(2,1)}), bf16[4,32,1536]{2,1,0:T(8,128)(2,1)S(1)}, u32[]{:S(2)}, u32[]{:S(2)}) %all-to-all-start.4) | async-done | bytes 393248 | tf_op jit(solution)/shard_map/all_to_all | solution.py:103
  206.4 0.7 copy-done.4
  207.1 1.8 shard_map.91
  208.9 0.3 fusion.174
  209.3 0.3 fusion.116
  209.6 0.8 pad_maximum_fusion
  (76 shorter events, 1.3 us)
Async XLA Ops:
  7.2 41.4 %all-gather.7.cloned.1.call-start = ((), (), s32[]{:S(2)}) async-start(), calls=%async_computation.8 | async-start | bytes 1792000 | tf_op jit(solution)/shard_map/all_gather | solution.py:359
  10.4 26.0 %copy-start.6 = (bf16[1,32,6144]{2,1,0:T(8,128)(2,1)S(1)}, bf16[1,32,6144]{2,1,0:T(8,128)(2,1)}, u32[]{:S(2)}) copy-start(bf16[1,32,6144]{2,1,0:T(8,128)(2,1)} %param.11) | copy-start | bytes 1179652
  10.4 94.8 %all-gather.5.cloned.1.call-start = ((), (), s32[]{:S(2)}) async-start(), calls=%async_computation.7 | async-start | bytes 5898240 | tf_op jit(solution)/shard_map/all_gather | solution.py:365
  48.5 1.4 copy-start
  54.4 50.9 %all-to-all-start.2 = ((bf16[8,4,64,896]{3,2,1,0:T(8,128)(2,1)}), bf16[8,4,64,896]{3,2,1,0:T(8,128)(2,1)}, u32[]{:S(2)}, u32[]{:S(2)}) async-start(bf16[8,4,64,896]{3,2,1,0:T(8,128)(2,1)} %shard_map.86), calls=%async_computation.2 | async-start | bytes 7340032 | tf_op jit(solution)/shard_map/all_to_all | solution.py:368
  58.9 134.7 %reduce-scatter.2.cloned.1.call-start = ((), (), s32[]{:S(2)}) async-start(), calls=%async_computation.6 | async-start | bytes 3538944 | tf_op jit(solution)/shard_map/reduce_scatter | solution.py:102
  59.2 11.6 %collective-permute-start.1 = (bf16[2,32,1536]{2,1,0:T(8,128)(2,1)S(1)}, bf16[2,32,1536]{2,1,0:T(8,128)(2,1)S(1)}, u32[]{:S(2)}, u32[]{:S(2)}) collective-permute-start(bf16[2,32,1536]{2,1,0:T(8,128)(2,1)S(1)} %get-tuple-element.70), channel_id=1, source_target_pairs={{0,8},{8,16},{16,24},{24,32},{32,40},{40,48},{48,56},{56,0},{1,9},... | collective-permute-start | bytes 589832 | tf_op jit(solution)/shard_map/ppermute | solution.py:33
  61.2 13.8 %collective-permute-start.3 = (bf16[2,32,1536]{2,1,0:T(8,128)(2,1)S(1)}, bf16[2,32,1536]{2,1,0:T(8,128)(2,1)S(1)}, u32[]{:S(2)}, u32[]{:S(2)}) collective-permute-start(bf16[2,32,1536]{2,1,0:T(8,128)(2,1)S(1)} %get-tuple-element.70), channel_id=1, source_target_pairs={{8,0},{16,8},{24,16},{32,24},{40,32},{48,40},{56,48},{0,56},{9,1},... | collective-permute-start | bytes 589832 | tf_op jit(solution)/shard_map/ppermute | solution.py:33
  65.2 9.8 %collective-permute-start = (bf16[2,32,1536]{2,1,0:T(8,128)(2,1)S(1)}, bf16[2,32,1536]{2,1,0:T(8,128)(2,1)S(1)}, u32[]{:S(2)}, u32[]{:S(2)}) collective-permute-start(bf16[2,32,1536]{2,1,0:T(8,128)(2,1)S(1)} %get-tuple-element.69), channel_id=1, source_target_pairs={{0,8},{8,16},{16,24},{24,32},{32,40},{40,48},{48,56},{56,0},{1,9},... | collective-permute-start | bytes 589832 | tf_op jit(solution)/shard_map/ppermute | solution.py:33
  65.2 13.0 %collective-permute-start.2 = (bf16[2,32,1536]{2,1,0:T(8,128)(2,1)S(1)}, bf16[2,32,1536]{2,1,0:T(8,128)(2,1)S(1)}, u32[]{:S(2)}, u32[]{:S(2)}) collective-permute-start(bf16[2,32,1536]{2,1,0:T(8,128)(2,1)S(1)} %get-tuple-element.69), channel_id=1, source_target_pairs={{8,0},{16,8},{24,16},{32,24},{40,32},{48,40},{56,48},{0,56},{9,1},... | collective-permute-start | bytes 589832 | tf_op jit(solution)/shard_map/ppermute | solution.py:33
  70.8 8.7 %collective-permute-start.5 = (bf16[2,32,1536]{2,1,0:T(8,128)(2,1)S(1)}, bf16[2,32,1536]{2,1,0:T(8,128)(2,1)S(1)}, u32[]{:S(2)}, u32[]{:S(2)}) collective-permute-start(bf16[2,32,1536]{2,1,0:T(8,128)(2,1)S(1)} %collective-permute-done.1), channel_id=1, source_target_pairs={{0,8},{8,16},{16,24},{24,32},{32,40},{40,48},{48,56},{56,0},{1,9},... | collective-permute-start | bytes 589832 | tf_op jit(solution)/shard_map/ppermute | solution.py:33
  75.0 9.1 %collective-permute-start.4 = (bf16[2,32,1536]{2,1,0:T(8,128)(2,1)S(1)}, bf16[2,32,1536]{2,1,0:T(8,128)(2,1)S(1)}, u32[]{:S(2)}, u32[]{:S(2)}) collective-permute-start(bf16[2,32,1536]{2,1,0:T(8,128)(2,1)S(1)} %collective-permute-done), channel_id=1, source_target_pairs={{0,8},{8,16},{16,24},{24,32},{32,40},{40,48},{48,56},{56,0},{1,9},... | collective-permute-start | bytes 589832 | tf_op jit(solution)/shard_map/ppermute | solution.py:33
  75.0 9.1 %collective-permute-start.7 = (bf16[2,32,1536]{2,1,0:T(8,128)(2,1)S(1)}, bf16[2,32,1536]{2,1,0:T(8,128)(2,1)S(1)}, u32[]{:S(2)}, u32[]{:S(2)}) collective-permute-start(bf16[2,32,1536]{2,1,0:T(8,128)(2,1)S(1)} %collective-permute-done.3), channel_id=1, source_target_pairs={{8,0},{16,8},{24,16},{32,24},{40,32},{48,40},{56,48},{0,56},{9,1},... | collective-permute-start | bytes 589832 | tf_op jit(solution)/shard_map/ppermute | solution.py:33
  78.2 9.1 %collective-permute-start.6 = (bf16[2,32,1536]{2,1,0:T(8,128)(2,1)S(1)}, bf16[2,32,1536]{2,1,0:T(8,128)(2,1)S(1)}, u32[]{:S(2)}, u32[]{:S(2)}) collective-permute-start(bf16[2,32,1536]{2,1,0:T(8,128)(2,1)S(1)} %collective-permute-done.2), channel_id=1, source_target_pairs={{8,0},{16,8},{24,16},{32,24},{40,32},{48,40},{56,48},{0,56},{9,1},... | collective-permute-start | bytes 589832 | tf_op jit(solution)/shard_map/ppermute | solution.py:33
  79.4 16.4 %collective-permute-start.9 = (bf16[2,32,1536]{2,1,0:T(8,128)(2,1)S(1)}, bf16[2,32,1536]{2,1,0:T(8,128)(2,1)S(1)}, u32[]{:S(2)}, u32[]{:S(2)}) collective-permute-start(bf16[2,32,1536]{2,1,0:T(8,128)(2,1)S(1)} %collective-permute-done.5), channel_id=1, source_target_pairs={{0,8},{8,16},{16,24},{24,32},{32,40},{40,48},{48,56},{56,0},{1,9},... | collective-permute-start | bytes 589832 | tf_op jit(solution)/shard_map/ppermute | solution.py:33
  84.0 15.2 %collective-permute-start.8 = (bf16[2,32,1536]{2,1,0:T(8,128)(2,1)S(1)}, bf16[2,32,1536]{2,1,0:T(8,128)(2,1)S(1)}, u32[]{:S(2)}, u32[]{:S(2)}) collective-permute-start(bf16[2,32,1536]{2,1,0:T(8,128)(2,1)S(1)} %collective-permute-done.4), channel_id=1, source_target_pairs={{0,8},{8,16},{16,24},{24,32},{32,40},{40,48},{48,56},{56,0},{1,9},... | collective-permute-start | bytes 589832 | tf_op jit(solution)/shard_map/ppermute | solution.py:33
  84.0 8.0 %collective-permute-start.11 = (bf16[2,32,1536]{2,1,0:T(8,128)(2,1)S(1)}, bf16[2,32,1536]{2,1,0:T(8,128)(2,1)S(1)}, u32[]{:S(2)}, u32[]{:S(2)}) collective-permute-start(bf16[2,32,1536]{2,1,0:T(8,128)(2,1)S(1)} %collective-permute-done.7), channel_id=1, source_target_pairs={{8,0},{16,8},{24,16},{32,24},{40,32},{48,40},{56,48},{0,56},{9,1},... | collective-permute-start | bytes 589832 | tf_op jit(solution)/shard_map/ppermute | solution.py:33
  87.3 8.7 %collective-permute-start.10 = (bf16[2,32,1536]{2,1,0:T(8,128)(2,1)S(1)}, bf16[2,32,1536]{2,1,0:T(8,128)(2,1)S(1)}, u32[]{:S(2)}, u32[]{:S(2)}) collective-permute-start(bf16[2,32,1536]{2,1,0:T(8,128)(2,1)S(1)} %collective-permute-done.6), channel_id=1, source_target_pairs={{8,0},{16,8},{24,16},{32,24},{40,32},{48,40},{56,48},{0,56},{9,1},... | collective-permute-start | bytes 589832 | tf_op jit(solution)/shard_map/ppermute | solution.py:33
  92.0 7.4 %collective-permute-start.15 = (bf16[1,32,1536]{2,1,0:T(8,128)(2,1)S(1)}, bf16[1,32,1536]{2,1,0:T(8,128)(2,1)S(1)}, u32[]{:S(2)}, u32[]{:S(2)}) collective-permute-start(bf16[1,32,1536]{2,1,0:T(8,128)(2,1)S(1)} %slice.699), channel_id=1, source_target_pairs={{8,0},{16,8},{24,16},{32,24},{40,32},{48,40},{56,48},{0,56},{9,1},... | collective-permute-start | bytes 294920 | tf_op jit(solution)/shard_map/ppermute | solution.py:61
  95.8 5.9 %collective-permute-start.14 = (bf16[1,32,1536]{2,1,0:T(8,128)(2,1)S(1)}, bf16[1,32,1536]{2,1,0:T(8,128)(2,1)S(1)}, u32[]{:S(2)}, u32[]{:S(2)}) collective-permute-start(bf16[1,32,1536]{2,1,0:T(8,128)(2,1)S(1)} %slice.698), channel_id=1, source_target_pairs={{0,8},{8,16},{16,24},{24,32},{32,40},{40,48},{48,56},{56,0},{1,9},... | collective-permute-start | bytes 294920 | tf_op jit(solution)/shard_map/ppermute | solution.py:61
  96.0 5.8 %collective-permute-start.13 = (bf16[1,32,1536]{2,1,0:T(8,128)(2,1)S(1)}, bf16[1,32,1536]{2,1,0:T(8,128)(2,1)S(1)}, u32[]{:S(2)}, u32[]{:S(2)}) collective-permute-start(bf16[1,32,1536]{2,1,0:T(8,128)(2,1)S(1)} %slice.697), channel_id=1, source_target_pairs={{8,0},{16,8},{24,16},{32,24},{40,32},{48,40},{56,48},{0,56},{9,1},... | collective-permute-start | bytes 294920 | tf_op jit(solution)/shard_map/ppermute | solution.py:61
  99.3 5.9 %collective-permute-start.12 = (bf16[1,32,1536]{2,1,0:T(8,128)(2,1)S(1)}, bf16[1,32,1536]{2,1,0:T(8,128)(2,1)S(1)}, u32[]{:S(2)}, u32[]{:S(2)}) collective-permute-start(bf16[1,32,1536]{2,1,0:T(8,128)(2,1)S(1)} %slice.696), channel_id=1, source_target_pairs={{0,8},{8,16},{16,24},{24,32},{32,40},{40,48},{48,56},{56,0},{1,9},... | collective-permute-start | bytes 294920 | tf_op jit(solution)/shard_map/ppermute | solution.py:61
  105.2 1.6 copy-start.3
  113.4 16.4 %collective-permute-start.16 = (bf16[512,512]{1,0:T(8,128)(2,1)}, bf16[512,512]{1,0:T(8,128)(2,1)}, u32[]{:S(2)}, u32[]{:S(2)}) collective-permute-start(bf16[512,512]{1,0:T(8,128)(2,1)} %get-tuple-element.39), channel_id=1, source_target_pairs={{0,64},{64,128},{128,192},{192,0},{1,65},{65,129},{129,193},{193,1... | collective-permute-start | bytes 1572872 | tf_op jit(solution)/shard_map/ppermute | solution.py:330
  113.5 16.3 %collective-permute-start.17 = (bf16[512,512]{1,0:T(8,128)(2,1)S(1)}, bf16[512,512]{1,0:T(8,128)(2,1)}, u32[]{:S(2)}, u32[]{:S(2)}) collective-permute-start(bf16[512,512]{1,0:T(8,128)(2,1)S(1)} %get-tuple-element.40), channel_id=1, source_target_pairs={{64,0},{128,64},{192,128},{0,192},{65,1},{129,65},{193,129},{1,193... | collective-permute-start | bytes 1572872 | tf_op jit(solution)/shard_map/ppermute | solution.py:330
  126.1 20.7 %collective-permute-start.19 = (bf16[512,512]{1,0:T(8,128)(2,1)S(1)}, bf16[512,512]{1,0:T(8,128)(2,1)S(1)}, u32[]{:S(2)}, u32[]{:S(2)}) collective-permute-start(bf16[512,512]{1,0:T(8,128)(2,1)S(1)} %get-tuple-element.51), channel_id=1, source_target_pairs={{0,64},{64,128},{128,192},{192,0},{1,65},{65,129},{129,193},{193,1... | collective-permute-start | bytes 1572872 | tf_op jit(solution)/shard_map/ppermute | solution.py:330
  126.2 20.6 %collective-permute-start.20 = (bf16[512,512]{1,0:T(8,128)(2,1)S(1)}, bf16[512,512]{1,0:T(8,128)(2,1)S(1)}, u32[]{:S(2)}, u32[]{:S(2)}) collective-permute-start(bf16[512,512]{1,0:T(8,128)(2,1)S(1)} %get-tuple-element.52), channel_id=1, source_target_pairs={{64,0},{128,64},{192,128},{0,192},{65,1},{129,65},{193,129},{1,193... | collective-permute-start | bytes 1572872 | tf_op jit(solution)/shard_map/ppermute | solution.py:330
  146.8 1.4 copy-start.5
  146.8 12.4 %copy-start.1 = (bf16[512,512]{1,0:T(8,128)(2,1)S(1)}, bf16[512,512]{1,0:T(8,128)(2,1)}, u32[]{:S(2)}) copy-start(bf16[512,512]{1,0:T(8,128)(2,1)} %get-tuple-element.47.refs_0_) | copy-start | bytes 1572868
  146.8 12.4 %copy-start.2 = (bf16[512,512]{1,0:T(8,128)(2,1)S(1)}, bf16[512,512]{1,0:T(8,128)(2,1)}, u32[]{:S(2)}) copy-start(bf16[512,512]{1,0:T(8,128)(2,1)} %get-tuple-element.54.refs_3_) | copy-start | bytes 1572868
  148.2 10.2 %collective-permute-start.18 = (bf16[512,512]{1,0:T(8,128)(2,1)S(1)}, bf16[512,512]{1,0:T(8,128)(2,1)S(1)}, u32[]{:S(2)}, u32[]{:S(2)}) collective-permute-start(bf16[512,512]{1,0:T(8,128)(2,1)S(1)} %add_convert_fusion.1), channel_id=1, source_target_pairs={{0,64},{64,128},{128,192},{192,0},{1,65},{65,129},{129,193},{193,1... | collective-permute-start | bytes 1572872 | tf_op jit(solution)/shard_map/ppermute | solution.py:330
  149.4 9.7 %collective-permute-start.21 = (bf16[512,512]{1,0:T(8,128)(2,1)S(1)}, bf16[512,512]{1,0:T(8,128)(2,1)S(1)}, u32[]{:S(2)}, u32[]{:S(2)}) collective-permute-start(bf16[512,512]{1,0:T(8,128)(2,1)S(1)} %add_convert_fusion), channel_id=1, source_target_pairs={{64,0},{128,64},{192,128},{0,192},{65,1},{129,65},{193,129},{1,193... | collective-permute-start | bytes 1572872 | tf_op jit(solution)/shard_map/ppermute | solution.py:330
  159.2 6.0 %copy-start.9 = (s32[192,2]{0,1:T(2,128)S(1)}, s32[192,2]{0,1:T(2,128)}, u32[]{:S(2)}) copy-start(s32[192,2]{0,1:T(2,128)} %param.9) | copy-start | bytes 4612
  159.2 6.1 %copy-start.8 = (bf16[31,1024]{1,0:T(8,128)(2,1)S(1)}, bf16[31,1024]{1,0:T(8,128)(2,1)}, u32[]{:S(2)}) copy-start(bf16[31,1024]{1,0:T(8,128)(2,1)} %param.10) | copy-start | bytes 190468
  159.2 21.9 %copy-start.7 = (bf16[192,1024]{1,0:T(8,128)(2,1)S(1)}, bf16[192,1024]{1,0:T(8,128)(2,1)}, u32[]{:S(2)}) copy-start(bf16[192,1024]{1,0:T(8,128)(2,1)} %param.7) | copy-start | bytes 1179652
  160.6 31.5 %copy-start.10 = (bf16[192,2]{0,1:T(2,128)(2,1)S(1)}, bf16[192,2]{0,1:T(2,128)(2,1)}, u32[]{:S(2)}) copy-start(bf16[192,2]{0,1:T(2,128)(2,1)} %param.8) | copy-start | bytes 2308
  160.6 20.5 %all-to-all-start.3 = ((bf16[8,64,1024]{2,1,0:T(8,128)(2,1)}), bf16[8,64,1024]{2,1,0:T(8,128)(2,1)S(1)}, u32[]{:S(2)}, u32[]{:S(2)}) async-start(bf16[8,64,1024]{2,1,0:T(8,128)(2,1)} %bitcast.31), calls=%async_computation.3 | async-start | bytes 2097152 | tf_op jit(solution)/shard_map/all_to_all | solution.py:371
  181.6 27.3 %collective-permute-start.22 = (bf16[15,1024]{1,0:T(8,128)(2,1)S(1)}, bf16[15,1024]{1,0:T(8,128)(2,1)S(1)}, u32[]{:S(2)}, u32[]{:S(2)}) collective-permute-start(bf16[15,1024]{1,0:T(8,128)(2,1)S(1)} %get-tuple-element.68), channel_id=1, source_target_pairs={{0,1},{1,2},{2,3},{3,4},{4,5},{5,6},{6,7},{7,8},{8,9},{9,10},{10,1... | collective-permute-start | bytes 92168 | tf_op jit(solution)/shard_map/ppermute | solution.py:121
  183.5 25.4 %collective-permute-start.23 = (bf16[15,1024]{1,0:T(8,128)(2,1)S(1)}, bf16[15,1024]{1,0:T(8,128)(2,1)S(1)}, u32[]{:S(2)}, u32[]{:S(2)}) collective-permute-start(bf16[15,1024]{1,0:T(8,128)(2,1)S(1)} %get-tuple-element.67), channel_id=1, source_target_pairs={{1,0},{2,1},{3,2},{4,3},{5,4},{6,5},{7,6},{8,7},{9,8},{10,9},{11,1... | collective-permute-start | bytes 92168 | tf_op jit(solution)/shard_map/ppermute | solution.py:122
  193.7 12.7 %all-to-all-start.4 = ((bf16[4,32,1536]{2,1,0:T(8,128)(2,1)}), bf16[4,32,1536]{2,1,0:T(8,128)(2,1)S(1)}, u32[]{:S(2)}, u32[]{:S(2)}) async-start(bf16[4,32,1536]{2,1,0:T(8,128)(2,1)} %bitcast.126), calls=%async_computation.5 | async-start | bytes 786432 | tf_op jit(solution)/shard_map/all_to_all | solution.py:103
  206.4 0.7 copy-start.4
Sparse Core Ops, SparseCore 0:
  10.5 30.0 all-gather.6
  42.4 55.9 all-gather.4
  147.0 46.6 reduce-scatter.1

commit v12 on v11

--- a/solution.py
+++ b/solution.py
@@ -361,9 +361,9 @@
     mine_in = lax.all_to_all(sent_in, by_expert, 0, 0, tiled=True)
     mine_in, expert_weights = lax.optimization_barrier((mine_in, expert_weights))
     columns = own_columns(expert_weights)
-    all_grad, columns = lax.optimization_barrier((all_grad, columns))
     rows_in = lax.all_gather(mine_in[:, 0], "y", axis=0, tiled=False)
     sent_q = route(all_grad, experts, 0)
+    columns, sent_q = lax.optimization_barrier((columns, sent_q))
     weights = gather_weights(columns, sent_q)
     rows_q = lax.all_to_all(sent_q, by_expert, 0, 0, tiled=True)
     row_sums, term = rows_backward(rows_in, rows_q, weights)

time: 218 us -> 213 us (0.977)
  blocking collectives: 33 us -> 21.9 us
  starting transfers between devices: 61.8 us -> 66.6 us
    all_to_all x1 -> x0, blocking collectives: 11.1 us -> none  [own_columns(): lax.all_to_all(sliced.reshape(ny, rows, 3 * part), 'y', 0, 0, tiled=True)]
    all_to_all x0 -> x1, starting transfers between devices: none -> 5.45 us  [own_columns(): lax.all_to_all(sliced.reshape(ny, rows, 3 * part), 'y', 0, 0, tiled=True)]
  transfers between devices with their start and end apart: 30 -> 31, of which waited for: 12 -> 13; matrix products, arithmetic and copies ran while one was open for 5% -> 5% of each run, Pallas kernels for 17% -> 18%
where the time goes in v12:
time: 213 us; the launch traced here: 212 us
  starting transfers between devices  66.6 us (31%)
  waiting for transfers between devices  45.4 us (21%)
  Pallas kernels  43.9 us (21%)
  blocking collectives  21.9 us (10%)
  between operations  14.3 us (7%)
  other arithmetic  11.3 us (5%)
  local copies, waits for them, and re-layouts  7.9 us (4%)
    all_to_all x1, blocking collectives, local(): mine_in = lax.all_to_all(sent_in, by_expert, 0, 0, tiled=True)  21.9 us
    ppermute x12, starting transfers between devices, ring_step(): return (lax.ppermute(right, axis, up), lax.ppermute(left, axis, down))  19.3 us
    pallas_call x2, Pallas kernels, expert_rows(): pl.pallas_call(functools.partial(rows_kernel, count, steps), grid_spec=pl...  17.2 us
    pallas_call x1, Pallas kernels, last_rows(): pl.pallas_call(last_kernel, grid_spec=pltpu.PrefetchScalarGridSpec(num_sc...  17 us
    all_to_all x1, waiting for transfers between devices, local(): lax.all_to_all(row_sums.reshape(experts, SLOTS, width), by_expert, 0, 0,...  15.7 us
    ppermute x12, waiting for transfers between devices, ring_step(): return (lax.ppermute(right, axis, up), lax.ppermute(left, axis, down))  12.2 us
    ppermute x6, starting transfers between devices, send(): return lax.ppermute(rows, 'y', way)  8.32 us
    ppermute x1, starting transfers between devices, halo_of(): return (low, lax.ppermute(block[:width], axes, backward))  8.28 us
  transfers between devices with their start and end apart: 31, of which 13 were waited for; matrix products, arithmetic and copies ran while one was open for 5% of the time, Pallas kernels for 18%

profile of v12, /device:TPU:8, one launch (start us, length us, event | category | flops | bytes accessed | tf_op | source)
XLA Modules:
  0.0 212.1 jit_solution(16338776766496674265)
XLA Ops:
  7.2 0.7 convert_bitcast_fusion
  7.9 1.0 slice.555
  8.9 0.7 pad_maximum_fusion.3
  9.6 0.8 fusion.48
  10.4 0.8 slice.554
  11.3 1.0 fusion.40.x_ref
  12.3 2.1 shard_map.85
  14.4 21.9 %all_to_all.25 = bf16[8,1,64,1152]{3,2,1,0:T(8,128)(2,1)} all-to-all(bf16[8,1,64,1152]{3,2,1,0:T(8,128)(2,1)} %shard_map.85), channel_id=1, replica_groups=mesh['y'=4,'z'=8,'x'=4,'c'=2] {'x','c'}, dimensions={0} | all-to-all | bytes 2359296 | tf_op jit(solution)/shard_map/all_to_all | solution.py:361
  36.4 0.3 reshape_squeeze.3
  36.9 1.3 reshape.26
  38.1 5.5 %all-to-all-start.1 = ((bf16[4,32,1536]{2,1,0:T(8,128)(2,1)}), bf16[4,32,1536]{2,1,0:T(8,128)(2,1)S(1)}, u32[]{:S(2)}, u32[]{:S(2)}) async-start(bf16[4,32,1536]{2,1,0:T(8,128)(2,1)} %reshape.26), calls=%async_computation.1 | async-start | bytes 786432 | tf_op jit(solution)/shard_map/all_to_all | solution.py:41
  43.6 1.4 copy-done
  45.0 4.5 %shard_map.86 = bf16[8,4,64,896]{3,2,1,0:T(8,128)(2,1)} custom-call(bf16[4,200,896]{2,1,0:T(8,128)(2,1)S(1)} %bitcast.117), custom_call_target="tpu_custom_call" | custom-call | tf_op jit(solution)/shard_map/pallas_call | solution.py:157
  49.5 0.8 all-to-all-done.1
  50.3 4.5 %all-to-all-start.2 = ((bf16[8,4,64,896]{3,2,1,0:T(8,128)(2,1)}), bf16[8,4,64,896]{3,2,1,0:T(8,128)(2,1)}, u32[]{:S(2)}, u32[]{:S(2)}) async-start(bf16[8,4,64,896]{3,2,1,0:T(8,128)(2,1)} %shard_map.86), calls=%async_computation.2 | async-start | bytes 7340032 | tf_op jit(solution)/shard_map/all_to_all | solution.py:368
  55.1 1.2 collective-permute-start.1
  56.2 4.0 %collective-permute-start.3 = (bf16[2,32,1536]{2,1,0:T(8,128)(2,1)S(1)}, bf16[2,32,1536]{2,1,0:T(8,128)(2,1)S(1)}, u32[]{:S(2)}, u32[]{:S(2)}) collective-permute-start(bf16[2,32,1536]{2,1,0:T(8,128)(2,1)S(1)} %get-tuple-element.69), channel_id=1, source_target_pairs={{8,0},{16,8},{24,16},{32,24},{40,32},{48,40},{56,48},{0,56},{9,1},... | collective-permute-start | bytes 589832 | tf_op jit(solution)/shard_map/ppermute | solution.py:33
  60.3 3.2 %collective-permute-start.2 = (bf16[2,32,1536]{2,1,0:T(8,128)(2,1)S(1)}, bf16[2,32,1536]{2,1,0:T(8,128)(2,1)S(1)}, u32[]{:S(2)}, u32[]{:S(2)}) collective-permute-start(bf16[2,32,1536]{2,1,0:T(8,128)(2,1)S(1)} %get-tuple-element.68), channel_id=1, source_target_pairs={{8,0},{16,8},{24,16},{32,24},{40,32},{48,40},{56,48},{0,56},{9,1},... | collective-permute-start | bytes 589832 | tf_op jit(solution)/shard_map/ppermute | solution.py:33
  63.5 0.3 broadcast_in_dim.40
  63.9 2.0 collective-permute-done.1
  65.9 4.2 %collective-permute-done = bf16[2,32,1536]{2,1,0:T(8,128)(2,1)S(1)} collective-permute-done((bf16[2,32,1536]{2,1,0:T(8,128)(2,1)S(1)}, bf16[2,32,1536]{2,1,0:T(8,128)(2,1)S(1)}, u32[]{:S(2)}, u32[]{:S(2)}) %collective-permute-start) | collective-permute-done | bytes 196640 | tf_op jit(solution)/shard_map/ppermute | solution.py:33
  70.1 3.2 %collective-permute-start.7 = (bf16[2,32,1536]{2,1,0:T(8,128)(2,1)S(1)}, bf16[2,32,1536]{2,1,0:T(8,128)(2,1)S(1)}, u32[]{:S(2)}, u32[]{:S(2)}) collective-permute-start(bf16[2,32,1536]{2,1,0:T(8,128)(2,1)S(1)} %collective-permute-done.3), channel_id=1, source_target_pairs={{8,0},{16,8},{24,16},{32,24},{40,32},{48,40},{56,48},{0,56},{9,1},... | collective-permute-start | bytes 589832 | tf_op jit(solution)/shard_map/ppermute | solution.py:33
  73.3 0.9 collective-permute-start.6
  74.2 0.3 collective-permute-done.5
  74.5 1.0 collective-permute-start.9
  75.5 3.6 %collective-permute-done.4 = bf16[2,32,1536]{2,1,0:T(8,128)(2,1)S(1)} collective-permute-done((bf16[2,32,1536]{2,1,0:T(8,128)(2,1)S(1)}, bf16[2,32,1536]{2,1,0:T(8,128)(2,1)S(1)}, u32[]{:S(2)}, u32[]{:S(2)}) %collective-permute-start.4) | collective-permute-done | bytes 196640 | tf_op jit(solution)/shard_map/ppermute | solution.py:33
  79.1 3.2 %collective-permute-start.11 = (bf16[2,32,1536]{2,1,0:T(8,128)(2,1)S(1)}, bf16[2,32,1536]{2,1,0:T(8,128)(2,1)S(1)}, u32[]{:S(2)}, u32[]{:S(2)}) collective-permute-start(bf16[2,32,1536]{2,1,0:T(8,128)(2,1)S(1)} %collective-permute-done.7), channel_id=1, source_target_pairs={{8,0},{16,8},{24,16},{32,24},{40,32},{48,40},{56,48},{0,56},{9,1},... | collective-permute-start | bytes 589832 | tf_op jit(solution)/shard_map/ppermute | solution.py:33
  82.4 2.6 %collective-permute-start.10 = (bf16[2,32,1536]{2,1,0:T(8,128)(2,1)S(1)}, bf16[2,32,1536]{2,1,0:T(8,128)(2,1)S(1)}, u32[]{:S(2)}, u32[]{:S(2)}) collective-permute-start(bf16[2,32,1536]{2,1,0:T(8,128)(2,1)S(1)} %collective-permute-done.6), channel_id=1, source_target_pairs={{8,0},{16,8},{24,16},{32,24},{40,32},{48,40},{56,48},{0,56},{9,1},... | collective-permute-start | bytes 589832 | tf_op jit(solution)/shard_map/ppermute | solution.py:33
  85.0 2.1 collective-permute-done.11
  87.1 3.8 %collective-permute-start.15 = (bf16[1,32,1536]{2,1,0:T(8,128)(2,1)S(1)}, bf16[1,32,1536]{2,1,0:T(8,128)(2,1)S(1)}, u32[]{:S(2)}, u32[]{:S(2)}) collective-permute-start(bf16[1,32,1536]{2,1,0:T(8,128)(2,1)S(1)} %slice.701), channel_id=1, source_target_pairs={{8,0},{16,8},{24,16},{32,24},{40,32},{48,40},{56,48},{0,56},{9,1},... | collective-permute-start | bytes 294920 | tf_op jit(solution)/shard_map/ppermute | solution.py:61
  91.0 3.3 %collective-permute-start.13 = (bf16[1,32,1536]{2,1,0:T(8,128)(2,1)S(1)}, bf16[1,32,1536]{2,1,0:T(8,128)(2,1)S(1)}, u32[]{:S(2)}, u32[]{:S(2)}) collective-permute-start(bf16[1,32,1536]{2,1,0:T(8,128)(2,1)S(1)} %slice.699), channel_id=1, source_target_pairs={{8,0},{16,8},{24,16},{32,24},{40,32},{48,40},{56,48},{0,56},{9,1},... | collective-permute-start | bytes 294920 | tf_op jit(solution)/shard_map/ppermute | solution.py:61
  94.5 2.3 %collective-permute-done.14 = bf16[1,32,1536]{2,1,0:T(8,128)(2,1)S(1)} collective-permute-done((bf16[1,32,1536]{2,1,0:T(8,128)(2,1)S(1)}, bf16[1,32,1536]{2,1,0:T(8,128)(2,1)S(1)}, u32[]{:S(2)}, u32[]{:S(2)}) %collective-permute-start.14) | collective-permute-done | bytes 98336 | tf_op jit(solution)/shard_map/ppermute | solution.py:61
  96.8 3.4 %collective-permute-done.12 = bf16[1,32,1536]{2,1,0:T(8,128)(2,1)S(1)} collective-permute-done((bf16[1,32,1536]{2,1,0:T(8,128)(2,1)S(1)}, bf16[1,32,1536]{2,1,0:T(8,128)(2,1)S(1)}, u32[]{:S(2)}, u32[]{:S(2)}) %collective-permute-start.12) | collective-permute-done | bytes 98336 | tf_op jit(solution)/shard_map/ppermute | solution.py:61
  100.3 1.6 copy-done.3
  101.9 6.5 %shard_map.87 = (bf16[512,512]{1,0:T(8,128)(2,1)}, bf16[512,512]{1,0:T(8,128)(2,1)S(1)}, bf16[2048,1024]{1,0:T(8,128)(2,1)}, bf16[8,4,64,512]{3,2,1,0:T(8,128)(2,1)}) custom-call(s32[1]{0:T(128)} %bitcast.5.info, bf16[4,8,64,1152]{3,2,1,0:T(8,128)(2,1)} %bitcast.121, bf16[8,4,64,896]{3,2,1,0:T(8,128)(2,1)} %all-to-all-done.2.q_ref, bf16[1024,1536]{1,0:T(8,128)(2,1)} %bitcast.118), custom_call_target="tpu_custom_call" | custom-call | tf_op jit(solution)/shard_map/pallas_call | solution.py:291
  108.4 0.9 collective-permute-start.16
  109.3 1.1 collective-permute-start.17
  110.5 10.6 %shard_map.88 = (bf16[512,512]{1,0:T(8,128)(2,1)S(1)}, bf16[512,512]{1,0:T(8,128)(2,1)S(1)}, bf16[512,512]{1,0:T(8,128)(2,1)S(1)}, bf16[512,512]{1,0:T(8,128)(2,...) custom-call(s32[2]{0:T(128)S(1)} %pad_add_fusion.1.info, ...), custom_call_target="tpu_custom_call", output_to_operand_aliasing={{4}: (4, {}), {5}: (5, {})} | custom-call | tf_op jit(solution)/shard_map/pallas_call | solution.py:291
  121.2 0.9 collective-permute-start.19
  122.1 2.3 %collective-permute-start.20 = (bf16[512,512]{1,0:T(8,128)(2,1)S(1)}, bf16[512,512]{1,0:T(8,128)(2,1)S(1)}, u32[]{:S(2)}, u32[]{:S(2)}) collective-permute-start(bf16[512,512]{1,0:T(8,128)(2,1)S(1)} %get-tuple-element.51), channel_id=1, source_target_pairs={{64,0},{128,64},{192,128},{0,192},{65,1},{129,65},{193,129},{1,193... | collective-permute-start | bytes 1572872 | tf_op jit(solution)/shard_map/ppermute | solution.py:330
  124.3 0.6 pad_add_fusion.info
  125.0 17.0 %shard_map.89 = (bf16[512,512]{1,0:T(8,128)(2,1)}, bf16[512,512]{1,0:T(8,128)(2,1)}, bf16[8,4,32,1536]{3,2,1,0:T(8,128)(2,1)}) custom-call(s32[4]{0:T(128)} %pad_add_fusion.info, bf16[4,8,64,1152]{3,2,1,0:T(8,128)(2,1)} %bitcast.123, bf16[8,4,64,896]{3,2,1,0:T(8,128)(2,1)} %all-to-all-done.2.q_ref, bf16[1024,1536]{1,0:T(8,128)(2,1)} %bitcast.120, ...), custom_call_target="tpu_custom_call" | custom-call | tf_op jit(solution)/shard_map/pallas_call | solution.py:246
  142.1 1.3 add_convert_fusion.1
  143.5 1.2 add_convert_fusion
  144.6 3.1 %collective-permute-start.21 = (bf16[512,512]{1,0:T(8,128)(2,1)S(1)}, bf16[512,512]{1,0:T(8,128)(2,1)S(1)}, u32[]{:S(2)}, u32[]{:S(2)}) collective-permute-start(bf16[512,512]{1,0:T(8,128)(2,1)S(1)} %add_convert_fusion), channel_id=1, source_target_pairs={{64,0},{128,64},{192,128},{0,192},{65,1},{129,65},{193,129},{1,193... | collective-permute-start | bytes 1572872 | tf_op jit(solution)/shard_map/ppermute | solution.py:330
  147.7 6.2 %collective-permute-done.18.refs_1_ = bf16[512,512]{1,0:T(8,128)(2,1)S(1)} collective-permute-done((bf16[512,512]{1,0:T(8,128)(2,1)S(1)}, bf16[512,512]{1,0:T(8,128)(2,1)S(1)}, u32[]{:S(2)}, u32[]{:S(2)}) %collective-permute-start.18) | collective-permute-done | bytes 524320 | tf_op jit(solution)/shard_map/ppermute | solution.py:330
  153.9 0.7 collective-permute-done.21.refs_5_
  154.6 1.4 shard_map.90
  156.0 4.4 %all-to-all-start.3 = ((bf16[8,64,1024]{2,1,0:T(8,128)(2,1)}), bf16[8,64,1024]{2,1,0:T(8,128)(2,1)S(1)}, u32[]{:S(2)}, u32[]{:S(2)}) async-start(bf16[8,64,1024]{2,1,0:T(8,128)(2,1)} %bitcast.31), calls=%async_computation.3 | async-start | bytes 2097152 | tf_op jit(solution)/shard_map/all_to_all | solution.py:371
  160.7 15.7 %all-to-all-done.3 = bf16[8,64,1024]{2,1,0:T(8,128)(2,1)S(1)} async-done(((bf16[8,64,1024]{2,1,0:T(8,128)(2,1)}), bf16[8,64,1024]{2,1,0:T(8,128)(2,1)S(1)}, u32[]{:S(2)}, u32[]{:S(2)}) %all-to-all-start.3) | async-done | bytes 1048608 | tf_op jit(solution)/shard_map/all_to_all | solution.py:371
  176.3 0.4 fusion.182
  176.8 1.9 collective-permute-start.22
  178.7 8.3 %collective-permute-start.23 = (bf16[15,1024]{1,0:T(8,128)(2,1)S(1)}, bf16[15,1024]{1,0:T(8,128)(2,1)S(1)}, u32[]{:S(2)}, u32[]{:S(2)}) collective-permute-start(bf16[15,1024]{1,0:T(8,128)(2,1)S(1)} %get-tuple-element.66), channel_id=1, source_target_pairs={{1,0},{2,1},{3,2},{4,3},{5,4},{6,5},{7,6},{8,7},{9,8},{10,9},{11,1... | collective-permute-start | bytes 92168 | tf_op jit(solution)/shard_map/ppermute | solution.py:122
  187.0 0.2 fusion.36
  187.3 0.6 fusion.176
  187.8 0.8 reduce-scatter.2.cloned.1.call-done
  188.7 7.0 %all-to-all-start.4 = ((bf16[4,32,1536]{2,1,0:T(8,128)(2,1)}), bf16[4,32,1536]{2,1,0:T(8,128)(2,1)S(1)}, u32[]{:S(2)}, u32[]{:S(2)}) async-start(bf16[4,32,1536]{2,1,0:T(8,128)(2,1)} %bitcast.126), calls=%async_computation.5 | async-start | bytes 786432 | tf_op jit(solution)/shard_map/all_to_all | solution.py:103
  195.7 2.6 %fusion.4 = bf16[160,1024]{1,0:T(8,128)(2,1)S(1)} fusion(f32[192,1024]{1,0:T(8,128)S(1)} %convert_element_type.78, f32[192,1024]{1,0:T(8,128)S(1)} %get-tuple-element.58, f32[1024]{0:T(1024)S(1)} %bitcast.161, f32[1024]{0:T(1024)S(1)} %bitcast.158, f32[1024]{0:T(1024)S(1)} %bitcast.155, f32[1024]{0:T(1024)S(1)} %bitcast.152, f32[1024]{0:T(1024)S(1)} %bitcast.149, ...), kind=kLoop, calls=%fused_computation.39 | loop fusion | flops 10321920 | bytes 21426176 | tf_op jit(solution)/shard_map/convert_element_type | solution.py:131
  198.3 3.3 %all-to-all-done.4.parts_ref = bf16[4,32,1536]{2,1,0:T(8,128)(2,1)S(1)} async-done(((bf16[4,32,1536]{2,1,0:T(8,128)(2,1)}), bf16[4,32,1536]{2,1,0:T(8,128)(2,1)S(1)}, u32[]{:S(2)}, u32[]{:S(2)}) %all-to-all-start.4) | async-done | bytes 393248 | tf_op jit(solution)/shard_map/all_to_all | solution.py:103
  201.6 0.7 copy-done.4
  202.3 1.8 shard_map.91
  204.1 0.3 fusion.174
  204.5 0.3 fusion.116
  204.8 0.8 pad_maximum_fusion
  (77 shorter events, 1.5 us)
Async XLA Ops:
  7.2 36.4 %all-gather.7.cloned.1.call-start = ((), (), s32[]{:S(2)}) async-start(), calls=%async_computation.8 | async-start | bytes 1792000 | tf_op jit(solution)/shard_map/all_gather | solution.py:359
  10.4 26.0 %copy-start.6 = (bf16[1,32,6144]{2,1,0:T(8,128)(2,1)S(1)}, bf16[1,32,6144]{2,1,0:T(8,128)(2,1)}, u32[]{:S(2)}) copy-start(bf16[1,32,6144]{2,1,0:T(8,128)(2,1)} %param.11) | copy-start | bytes 1179652
  10.4 89.9 %all-gather.5.cloned.1.call-start = ((), (), s32[]{:S(2)}) async-start(), calls=%async_computation.7 | async-start | bytes 5898240 | tf_op jit(solution)/shard_map/all_gather | solution.py:364
  38.1 12.2 %all-to-all-start.1 = ((bf16[4,32,1536]{2,1,0:T(8,128)(2,1)}), bf16[4,32,1536]{2,1,0:T(8,128)(2,1)S(1)}, u32[]{:S(2)}, u32[]{:S(2)}) async-start(bf16[4,32,1536]{2,1,0:T(8,128)(2,1)} %reshape.26), calls=%async_computation.1 | async-start | bytes 786432 | tf_op jit(solution)/shard_map/all_to_all | solution.py:41
  43.6 1.4 copy-start
  50.3 50.0 %all-to-all-start.2 = ((bf16[8,4,64,896]{3,2,1,0:T(8,128)(2,1)}), bf16[8,4,64,896]{3,2,1,0:T(8,128)(2,1)}, u32[]{:S(2)}, u32[]{:S(2)}) async-start(bf16[8,4,64,896]{3,2,1,0:T(8,128)(2,1)} %shard_map.86), calls=%async_computation.2 | async-start | bytes 7340032 | tf_op jit(solution)/shard_map/all_to_all | solution.py:368
  54.8 133.8 %reduce-scatter.2.cloned.1.call-start = ((), (), s32[]{:S(2)}) async-start(), calls=%async_computation.6 | async-start | bytes 3538944 | tf_op jit(solution)/shard_map/reduce_scatter | solution.py:102
  55.1 10.8 %collective-permute-start.1 = (bf16[2,32,1536]{2,1,0:T(8,128)(2,1)S(1)}, bf16[2,32,1536]{2,1,0:T(8,128)(2,1)S(1)}, u32[]{:S(2)}, u32[]{:S(2)}) collective-permute-start(bf16[2,32,1536]{2,1,0:T(8,128)(2,1)S(1)} %get-tuple-element.69), channel_id=1, source_target_pairs={{0,8},{8,16},{16,24},{24,32},{32,40},{40,48},{48,56},{56,0},{1,9},... | collective-permute-start | bytes 589832 | tf_op jit(solution)/shard_map/ppermute | solution.py:33
  56.2 13.8 %collective-permute-start.3 = (bf16[2,32,1536]{2,1,0:T(8,128)(2,1)S(1)}, bf16[2,32,1536]{2,1,0:T(8,128)(2,1)S(1)}, u32[]{:S(2)}, u32[]{:S(2)}) collective-permute-start(bf16[2,32,1536]{2,1,0:T(8,128)(2,1)S(1)} %get-tuple-element.69), channel_id=1, source_target_pairs={{8,0},{16,8},{24,16},{32,24},{40,32},{48,40},{56,48},{0,56},{9,1},... | collective-permute-start | bytes 589832 | tf_op jit(solution)/shard_map/ppermute | solution.py:33
  60.3 9.8 %collective-permute-start = (bf16[2,32,1536]{2,1,0:T(8,128)(2,1)S(1)}, bf16[2,32,1536]{2,1,0:T(8,128)(2,1)S(1)}, u32[]{:S(2)}, u32[]{:S(2)}) collective-permute-start(bf16[2,32,1536]{2,1,0:T(8,128)(2,1)S(1)} %get-tuple-element.68), channel_id=1, source_target_pairs={{0,8},{8,16},{16,24},{24,32},{32,40},{40,48},{48,56},{56,0},{1,9},... | collective-permute-start | bytes 589832 | tf_op jit(solution)/shard_map/ppermute | solution.py:33
  60.3 13.0 %collective-permute-start.2 = (bf16[2,32,1536]{2,1,0:T(8,128)(2,1)S(1)}, bf16[2,32,1536]{2,1,0:T(8,128)(2,1)S(1)}, u32[]{:S(2)}, u32[]{:S(2)}) collective-permute-start(bf16[2,32,1536]{2,1,0:T(8,128)(2,1)S(1)} %get-tuple-element.68), channel_id=1, source_target_pairs={{8,0},{16,8},{24,16},{32,24},{40,32},{48,40},{56,48},{0,56},{9,1},... | collective-permute-start | bytes 589832 | tf_op jit(solution)/shard_map/ppermute | solution.py:33
  65.9 8.7 %collective-permute-start.5 = (bf16[2,32,1536]{2,1,0:T(8,128)(2,1)S(1)}, bf16[2,32,1536]{2,1,0:T(8,128)(2,1)S(1)}, u32[]{:S(2)}, u32[]{:S(2)}) collective-permute-start(bf16[2,32,1536]{2,1,0:T(8,128)(2,1)S(1)} %collective-permute-done.1), channel_id=1, source_target_pairs={{0,8},{8,16},{16,24},{24,32},{32,40},{40,48},{48,56},{56,0},{1,9},... | collective-permute-start | bytes 589832 | tf_op jit(solution)/shard_map/ppermute | solution.py:33
  70.1 9.1 %collective-permute-start.4 = (bf16[2,32,1536]{2,1,0:T(8,128)(2,1)S(1)}, bf16[2,32,1536]{2,1,0:T(8,128)(2,1)S(1)}, u32[]{:S(2)}, u32[]{:S(2)}) collective-permute-start(bf16[2,32,1536]{2,1,0:T(8,128)(2,1)S(1)} %collective-permute-done), channel_id=1, source_target_pairs={{0,8},{8,16},{16,24},{24,32},{32,40},{40,48},{48,56},{56,0},{1,9},... | collective-permute-start | bytes 589832 | tf_op jit(solution)/shard_map/ppermute | solution.py:33
  70.1 9.1 %collective-permute-start.7 = (bf16[2,32,1536]{2,1,0:T(8,128)(2,1)S(1)}, bf16[2,32,1536]{2,1,0:T(8,128)(2,1)S(1)}, u32[]{:S(2)}, u32[]{:S(2)}) collective-permute-start(bf16[2,32,1536]{2,1,0:T(8,128)(2,1)S(1)} %collective-permute-done.3), channel_id=1, source_target_pairs={{8,0},{16,8},{24,16},{32,24},{40,32},{48,40},{56,48},{0,56},{9,1},... | collective-permute-start | bytes 589832 | tf_op jit(solution)/shard_map/ppermute | solution.py:33
  73.3 9.1 %collective-permute-start.6 = (bf16[2,32,1536]{2,1,0:T(8,128)(2,1)S(1)}, bf16[2,32,1536]{2,1,0:T(8,128)(2,1)S(1)}, u32[]{:S(2)}, u32[]{:S(2)}) collective-permute-start(bf16[2,32,1536]{2,1,0:T(8,128)(2,1)S(1)} %collective-permute-done.2), channel_id=1, source_target_pairs={{8,0},{16,8},{24,16},{32,24},{40,32},{48,40},{56,48},{0,56},{9,1},... | collective-permute-start | bytes 589832 | tf_op jit(solution)/shard_map/ppermute | solution.py:33
  74.5 16.4 %collective-permute-start.9 = (bf16[2,32,1536]{2,1,0:T(8,128)(2,1)S(1)}, bf16[2,32,1536]{2,1,0:T(8,128)(2,1)S(1)}, u32[]{:S(2)}, u32[]{:S(2)}) collective-permute-start(bf16[2,32,1536]{2,1,0:T(8,128)(2,1)S(1)} %collective-permute-done.5), channel_id=1, source_target_pairs={{0,8},{8,16},{16,24},{24,32},{32,40},{40,48},{48,56},{56,0},{1,9},... | collective-permute-start | bytes 589832 | tf_op jit(solution)/shard_map/ppermute | solution.py:33
  79.1 15.2 %collective-permute-start.8 = (bf16[2,32,1536]{2,1,0:T(8,128)(2,1)S(1)}, bf16[2,32,1536]{2,1,0:T(8,128)(2,1)S(1)}, u32[]{:S(2)}, u32[]{:S(2)}) collective-permute-start(bf16[2,32,1536]{2,1,0:T(8,128)(2,1)S(1)} %collective-permute-done.4), channel_id=1, source_target_pairs={{0,8},{8,16},{16,24},{24,32},{32,40},{40,48},{48,56},{56,0},{1,9},... | collective-permute-start | bytes 589832 | tf_op jit(solution)/shard_map/ppermute | solution.py:33
  79.1 8.0 %collective-permute-start.11 = (bf16[2,32,1536]{2,1,0:T(8,128)(2,1)S(1)}, bf16[2,32,1536]{2,1,0:T(8,128)(2,1)S(1)}, u32[]{:S(2)}, u32[]{:S(2)}) collective-permute-start(bf16[2,32,1536]{2,1,0:T(8,128)(2,1)S(1)} %collective-permute-done.7), channel_id=1, source_target_pairs={{8,0},{16,8},{24,16},{32,24},{40,32},{48,40},{56,48},{0,56},{9,1},... | collective-permute-start | bytes 589832 | tf_op jit(solution)/shard_map/ppermute | solution.py:33
  82.4 8.7 %collective-permute-start.10 = (bf16[2,32,1536]{2,1,0:T(8,128)(2,1)S(1)}, bf16[2,32,1536]{2,1,0:T(8,128)(2,1)S(1)}, u32[]{:S(2)}, u32[]{:S(2)}) collective-permute-start(bf16[2,32,1536]{2,1,0:T(8,128)(2,1)S(1)} %collective-permute-done.6), channel_id=1, source_target_pairs={{8,0},{16,8},{24,16},{32,24},{40,32},{48,40},{56,48},{0,56},{9,1},... | collective-permute-start | bytes 589832 | tf_op jit(solution)/shard_map/ppermute | solution.py:33
  87.1 7.4 %collective-permute-start.15 = (bf16[1,32,1536]{2,1,0:T(8,128)(2,1)S(1)}, bf16[1,32,1536]{2,1,0:T(8,128)(2,1)S(1)}, u32[]{:S(2)}, u32[]{:S(2)}) collective-permute-start(bf16[1,32,1536]{2,1,0:T(8,128)(2,1)S(1)} %slice.701), channel_id=1, source_target_pairs={{8,0},{16,8},{24,16},{32,24},{40,32},{48,40},{56,48},{0,56},{9,1},... | collective-permute-start | bytes 294920 | tf_op jit(solution)/shard_map/ppermute | solution.py:61
  90.9 5.9 %collective-permute-start.14 = (bf16[1,32,1536]{2,1,0:T(8,128)(2,1)S(1)}, bf16[1,32,1536]{2,1,0:T(8,128)(2,1)S(1)}, u32[]{:S(2)}, u32[]{:S(2)}) collective-permute-start(bf16[1,32,1536]{2,1,0:T(8,128)(2,1)S(1)} %slice.700), channel_id=1, source_target_pairs={{0,8},{8,16},{16,24},{24,32},{32,40},{40,48},{48,56},{56,0},{1,9},... | collective-permute-start | bytes 294920 | tf_op jit(solution)/shard_map/ppermute | solution.py:61
  91.0 5.8 %collective-permute-start.13 = (bf16[1,32,1536]{2,1,0:T(8,128)(2,1)S(1)}, bf16[1,32,1536]{2,1,0:T(8,128)(2,1)S(1)}, u32[]{:S(2)}, u32[]{:S(2)}) collective-permute-start(bf16[1,32,1536]{2,1,0:T(8,128)(2,1)S(1)} %slice.699), channel_id=1, source_target_pairs={{8,0},{16,8},{24,16},{32,24},{40,32},{48,40},{56,48},{0,56},{9,1},... | collective-permute-start | bytes 294920 | tf_op jit(solution)/shard_map/ppermute | solution.py:61
  94.3 5.9 %collective-permute-start.12 = (bf16[1,32,1536]{2,1,0:T(8,128)(2,1)S(1)}, bf16[1,32,1536]{2,1,0:T(8,128)(2,1)S(1)}, u32[]{:S(2)}, u32[]{:S(2)}) collective-permute-start(bf16[1,32,1536]{2,1,0:T(8,128)(2,1)S(1)} %slice.698), channel_id=1, source_target_pairs={{0,8},{8,16},{16,24},{24,32},{32,40},{40,48},{48,56},{56,0},{1,9},... | collective-permute-start | bytes 294920 | tf_op jit(solution)/shard_map/ppermute | solution.py:61
  100.3 1.6 copy-start.3
  108.4 16.5 %collective-permute-start.16 = (bf16[512,512]{1,0:T(8,128)(2,1)}, bf16[512,512]{1,0:T(8,128)(2,1)}, u32[]{:S(2)}, u32[]{:S(2)}) collective-permute-start(bf16[512,512]{1,0:T(8,128)(2,1)} %get-tuple-element.38), channel_id=1, source_target_pairs={{0,64},{64,128},{128,192},{192,0},{1,65},{65,129},{129,193},{193,1... | collective-permute-start | bytes 1572872 | tf_op jit(solution)/shard_map/ppermute | solution.py:330
  109.3 15.7 %collective-permute-start.17 = (bf16[512,512]{1,0:T(8,128)(2,1)S(1)}, bf16[512,512]{1,0:T(8,128)(2,1)}, u32[]{:S(2)}, u32[]{:S(2)}) collective-permute-start(bf16[512,512]{1,0:T(8,128)(2,1)S(1)} %get-tuple-element.39), channel_id=1, source_target_pairs={{64,0},{128,64},{192,128},{0,192},{65,1},{129,65},{193,129},{1,193... | collective-permute-start | bytes 1572872 | tf_op jit(solution)/shard_map/ppermute | solution.py:330
  121.2 20.8 %collective-permute-start.19 = (bf16[512,512]{1,0:T(8,128)(2,1)S(1)}, bf16[512,512]{1,0:T(8,128)(2,1)S(1)}, u32[]{:S(2)}, u32[]{:S(2)}) collective-permute-start(bf16[512,512]{1,0:T(8,128)(2,1)S(1)} %get-tuple-element.50), channel_id=1, source_target_pairs={{0,64},{64,128},{128,192},{192,0},{1,65},{65,129},{129,193},{193,1... | collective-permute-start | bytes 1572872 | tf_op jit(solution)/shard_map/ppermute | solution.py:330
  122.1 19.9 %collective-permute-start.20 = (bf16[512,512]{1,0:T(8,128)(2,1)S(1)}, bf16[512,512]{1,0:T(8,128)(2,1)S(1)}, u32[]{:S(2)}, u32[]{:S(2)}) collective-permute-start(bf16[512,512]{1,0:T(8,128)(2,1)S(1)} %get-tuple-element.51), channel_id=1, source_target_pairs={{64,0},{128,64},{192,128},{0,192},{65,1},{129,65},{193,129},{1,193... | collective-permute-start | bytes 1572872 | tf_op jit(solution)/shard_map/ppermute | solution.py:330
  142.0 1.4 copy-start.5
  142.0 12.5 %copy-start.1 = (bf16[512,512]{1,0:T(8,128)(2,1)S(1)}, bf16[512,512]{1,0:T(8,128)(2,1)}, u32[]{:S(2)}) copy-start(bf16[512,512]{1,0:T(8,128)(2,1)} %get-tuple-element.46.refs_0_) | copy-start | bytes 1572868
  142.0 12.5 %copy-start.2 = (bf16[512,512]{1,0:T(8,128)(2,1)S(1)}, bf16[512,512]{1,0:T(8,128)(2,1)}, u32[]{:S(2)}) copy-start(bf16[512,512]{1,0:T(8,128)(2,1)} %get-tuple-element.53.refs_3_) | copy-start | bytes 1572868
  143.4 10.5 %collective-permute-start.18 = (bf16[512,512]{1,0:T(8,128)(2,1)S(1)}, bf16[512,512]{1,0:T(8,128)(2,1)S(1)}, u32[]{:S(2)}, u32[]{:S(2)}) collective-permute-start(bf16[512,512]{1,0:T(8,128)(2,1)S(1)} %add_convert_fusion.1), channel_id=1, source_target_pairs={{0,64},{64,128},{128,192},{192,0},{1,65},{65,129},{129,193},{193,1... | collective-permute-start | bytes 1572872 | tf_op jit(solution)/shard_map/ppermute | solution.py:330
  144.6 9.9 %collective-permute-start.21 = (bf16[512,512]{1,0:T(8,128)(2,1)S(1)}, bf16[512,512]{1,0:T(8,128)(2,1)S(1)}, u32[]{:S(2)}, u32[]{:S(2)}) collective-permute-start(bf16[512,512]{1,0:T(8,128)(2,1)S(1)} %add_convert_fusion), channel_id=1, source_target_pairs={{64,0},{128,64},{192,128},{0,192},{65,1},{129,65},{193,129},{1,193... | collective-permute-start | bytes 1572872 | tf_op jit(solution)/shard_map/ppermute | solution.py:330
  154.6 5.8 %copy-start.9 = (s32[192,2]{0,1:T(2,128)S(1)}, s32[192,2]{0,1:T(2,128)}, u32[]{:S(2)}) copy-start(s32[192,2]{0,1:T(2,128)} %param.9) | copy-start | bytes 4612
  154.6 6.0 %copy-start.8 = (bf16[31,1024]{1,0:T(8,128)(2,1)S(1)}, bf16[31,1024]{1,0:T(8,128)(2,1)}, u32[]{:S(2)}) copy-start(bf16[31,1024]{1,0:T(8,128)(2,1)} %param.10) | copy-start | bytes 190468
  154.6 21.8 %copy-start.7 = (bf16[192,1024]{1,0:T(8,128)(2,1)S(1)}, bf16[192,1024]{1,0:T(8,128)(2,1)}, u32[]{:S(2)}) copy-start(bf16[192,1024]{1,0:T(8,128)(2,1)} %param.7) | copy-start | bytes 1179652
  156.0 31.3 %copy-start.10 = (bf16[192,2]{0,1:T(2,128)(2,1)S(1)}, bf16[192,2]{0,1:T(2,128)(2,1)}, u32[]{:S(2)}) copy-start(bf16[192,2]{0,1:T(2,128)(2,1)} %param.8) | copy-start | bytes 2308
  156.0 20.4 %all-to-all-start.3 = ((bf16[8,64,1024]{2,1,0:T(8,128)(2,1)}), bf16[8,64,1024]{2,1,0:T(8,128)(2,1)S(1)}, u32[]{:S(2)}, u32[]{:S(2)}) async-start(bf16[8,64,1024]{2,1,0:T(8,128)(2,1)} %bitcast.31), calls=%async_computation.3 | async-start | bytes 2097152 | tf_op jit(solution)/shard_map/all_to_all | solution.py:371
  176.8 27.3 %collective-permute-start.22 = (bf16[15,1024]{1,0:T(8,128)(2,1)S(1)}, bf16[15,1024]{1,0:T(8,128)(2,1)S(1)}, u32[]{:S(2)}, u32[]{:S(2)}) collective-permute-start(bf16[15,1024]{1,0:T(8,128)(2,1)S(1)} %get-tuple-element.67), channel_id=1, source_target_pairs={{0,1},{1,2},{2,3},{3,4},{4,5},{5,6},{6,7},{7,8},{8,9},{9,10},{10,1... | collective-permute-start | bytes 92168 | tf_op jit(solution)/shard_map/ppermute | solution.py:121
  178.7 25.4 %collective-permute-start.23 = (bf16[15,1024]{1,0:T(8,128)(2,1)S(1)}, bf16[15,1024]{1,0:T(8,128)(2,1)S(1)}, u32[]{:S(2)}, u32[]{:S(2)}) collective-permute-start(bf16[15,1024]{1,0:T(8,128)(2,1)S(1)} %get-tuple-element.66), channel_id=1, source_target_pairs={{1,0},{2,1},{3,2},{4,3},{5,4},{6,5},{7,6},{8,7},{9,8},{10,9},{11,1... | collective-permute-start | bytes 92168 | tf_op jit(solution)/shard_map/ppermute | solution.py:122
  188.7 12.9 %all-to-all-start.4 = ((bf16[4,32,1536]{2,1,0:T(8,128)(2,1)}), bf16[4,32,1536]{2,1,0:T(8,128)(2,1)S(1)}, u32[]{:S(2)}, u32[]{:S(2)}) async-start(bf16[4,32,1536]{2,1,0:T(8,128)(2,1)} %bitcast.126), calls=%async_computation.5 | async-start | bytes 786432 | tf_op jit(solution)/shard_map/all_to_all | solution.py:103
  201.6 0.7 copy-start.4
Sparse Core Ops, SparseCore 0:
  10.5 30.0 all-gather.6
  42.4 55.9 all-gather.4
  142.2 46.3 reduce-scatter.1
